TPU v7x, 32 devices: a whole 2x2x4 slice. The times are simulated.
32 devices in a mesh: dp: 16 (over z, y, core), mp: 2 (over x).
Axes of the slice: x: 2, y: 2, z: 4, core: 2. Of those that a mesh axis runs over, the one named last changes fastest.
Arguments:
- tokens: bfloat16 [6272, 768], P(('dp', 'mp')), may hold values from -6 to 6
- ln1_gain: bfloat16 [768], replicated, may hold values from 0.5 to 1.5
- ln1_bias: bfloat16 [768], replicated, may hold values from -1.75 to 1.75
- qkv_weight: bfloat16 [768, 2304], P(('dp', 'mp')), may hold values from -0.21875 to 0.21875
- qv_bias: bfloat16 [2, 768], replicated, may hold values from -1.75 to 1.75
- rel_pos_h: bfloat16 [27, 64], replicated, may hold values from -0.625 to 0.625
- rel_pos_w: bfloat16 [27, 64], replicated, may hold values from -0.625 to 0.625
- proj_weight: bfloat16 [768, 768], P(('dp', 'mp')), may hold values from -1.5 to 1.5
- proj_bias: bfloat16 [768], replicated, may hold values from -1.75 to 1.75
- ln2_gain: bfloat16 [768], replicated, may hold values from 0.5 to 1.5
- ln2_bias: bfloat16 [768], replicated, may hold values from -1.75 to 1.75
- fc1_weight: bfloat16 [768, 3072], P(None, 'mp'), may hold values from -0.21875 to 0.21875
- fc1_bias: bfloat16 [3072], P('mp'), may hold values from -1.75 to 1.75
- fc2_weight: bfloat16 [3072, 768], P('mp'), may hold values from -0.109375 to 0.109375
- fc2_bias: bfloat16 [768], replicated, may hold values from -1.75 to 1.75
- keep_mask: int32 [32, 2], P(('dp', 'mp')), may hold values from 0 to 1, as said below
- key_mask: int32 [32, 196], P(('dp', 'mp')), may hold values from 0 to 1, as said below
- out_grad: bfloat16 [6272, 768], P(('dp', 'mp')), may hold values from -6 to 6
Outputs:
- result: bfloat16 [6272, 768], P(('dp', 'mp'))
- tokens_grad: bfloat16 [6272, 768], P(('dp', 'mp'))
- ln1_gain_grad: float32 [768], replicated
- ln1_bias_grad: float32 [768], replicated
- qkv_weight_grad: float32 [768, 2304], P(('dp', 'mp'))
- qv_bias_grad: float32 [2, 768], replicated
- rel_pos_h_grad: float32 [27, 64], replicated
- rel_pos_w_grad: float32 [27, 64], replicated
- proj_weight_grad: float32 [768, 768], P(('dp', 'mp'))
- proj_bias_grad: float32 [768], replicated
- ln2_gain_grad: float32 [768], replicated
- ln2_bias_grad: float32 [768], replicated
- fc1_weight_grad: float32 [768, 3072], P('dp', 'mp')
- fc1_bias_grad: float32 [3072], P(('mp', 'dp'))
- fc2_weight_grad: float32 [3072, 768], P('mp', 'dp')
- fc2_bias_grad: float32 [768], replicated
Inputs may be any that keep to these rules, and one draw needn't show every extreme that they name: `keep_mask`: windows come nine to an image, in order, as its 3 x 3 grid of windows (the last image may hold fewer, its first windows in that order); a window's two flags equal those of the other windows of its image. `key_mask`: windows come nine to an image, in order, as its 3 x 3 grid; each window's mask is 1 exactly on a rectangle at its top-left corner, of all 14 rows (columns) in the first two rows (columns) of windows and of 1 to 4 in the last.
All inputs are finite; a program needn't handle non-finite values.
Results may differ from a plain program's by a relative error of at most 0.018.
Values may be sent and summed in bfloat16 or wider, within the bound.
No kernel may reach another device: no remote copies, remote signals or barrier semaphores. Data moves between devices by JAX's collectives and lax.ppermute only.
A program may use at most 128 MiB of HBM per device.

v0:
```python
from functools import partial

import jax
import jax.numpy as jnp
from jax import lax
from jax.sharding import PartitionSpec as P

D = 768
HEADS = 12
HEAD = 64
WIN = 14


def norm_parts(rows_in, gain, shift):
    center = rows_in - jnp.mean(rows_in, axis=-1, keepdims=True)
    factor = lax.rsqrt(jnp.mean(center * center, axis=-1, keepdims=True) + 1e-06)
    unit = center * factor
    return (unit * gain + shift, unit, factor)


def norm_back(grad, unit, factor, gain):
    inner = grad * gain
    return factor * (
        inner
        - jnp.mean(inner, axis=-1, keepdims=True)
        - unit * jnp.mean(inner * unit, axis=-1, keepdims=True)
    )


def shift_table(width):
    first = jnp.arange(width)[:, None, None]
    second = jnp.arange(width)[None, :, None]
    offset = jnp.arange(2 * width - 1)[None, None, :]
    return (first - second + width - 1 == offset).astype(jnp.float32)


def attn_scores(queries, key_part, tab_h, tab_w, mask):
    windows_here = queries.shape[0]
    scores = jnp.einsum(
        "nabhc,nxyhc->nhabxy", queries, key_part, preferred_element_type=jnp.float32
    ) * HEAD ** (-0.5)
    part_h = jnp.einsum("nabhc,axc->nhabx", queries, tab_h, preferred_element_type=jnp.float32)
    part_w = jnp.einsum("nabhc,byc->nhaby", queries, tab_w, preferred_element_type=jnp.float32)
    scores = scores + part_h[..., :, None] + part_w[..., None, :]
    scores = scores.reshape(windows_here, HEADS, WIN * WIN, WIN * WIN)
    return jnp.where(mask[:, None, None, :] > 0, scores, -1000000000.0)


def per_device(
    tokens,
    ln1_gain,
    ln1_bias,
    qkv_weight,
    qv_bias,
    rel_pos_h,
    rel_pos_w,
    proj_weight,
    proj_bias,
    ln2_gain,
    ln2_bias,
    fc1_weight,
    fc1_bias,
    fc2_weight,
    fc2_bias,
    keep_mask,
    key_mask,
    out_grad,
):
    f32 = jnp.float32
    bf16 = jnp.bfloat16
    highest = lax.Precision.HIGHEST
    windows_here = key_mask.shape[0]
    window_area = WIN * WIN
    local_rows = tokens.shape[0]
    qkv_full, proj_full = (
        lax.all_gather(qkv_weight, ("dp", "mp"), axis=0, tiled=True),
        lax.all_gather(proj_weight, ("dp", "mp"), axis=0, tiled=True),
    )
    gain_one = ln1_gain.astype(f32)
    gain_two = ln2_gain.astype(f32)
    residual = tokens.astype(f32)
    normed_in, unit_one, factor_one = norm_parts(residual, gain_one, ln1_bias.astype(f32))
    normed_one = normed_in.astype(bf16)
    qv_wide = qv_bias.astype(f32)
    bias_full = jnp.concatenate([qv_wide[0], jnp.zeros((D,), f32), qv_wide[1]])
    qkv = (jnp.dot(normed_one, qkv_full, preferred_element_type=f32) + bias_full).astype(bf16)
    blocks = qkv.reshape(windows_here, WIN, WIN, 3, HEADS, HEAD)
    queries, key_part, values = (blocks[:, :, :, 0], blocks[:, :, :, 1], blocks[:, :, :, 2])
    onehot = shift_table(WIN)
    tab_h = jnp.einsum("axr,rc->axc", onehot, rel_pos_h.astype(f32), precision=highest)
    tab_w = jnp.einsum("axr,rc->axc", onehot, rel_pos_w.astype(f32), precision=highest)
    scores = attn_scores(queries, key_part, tab_h.astype(bf16), tab_w.astype(bf16), key_mask)
    row_top = jnp.max(scores, axis=-1, keepdims=True)
    expo = jnp.exp(scores - row_top)
    row_total = jnp.sum(expo, axis=-1, keepdims=True)
    log_total = row_top + jnp.log(row_total)
    attn_probs = expo / row_total
    flat_values = values.reshape(windows_here, window_area, HEADS, HEAD)
    attended = jnp.einsum(
        "nhqk,nkhc->nqhc", attn_probs.astype(bf16), flat_values, preferred_element_type=f32
    )
    attended = attended.reshape(local_rows, D).astype(bf16)
    branch = jnp.dot(attended, proj_full, preferred_element_type=f32) + proj_bias.astype(f32)
    keep_rows = jnp.repeat(keep_mask.astype(f32), window_area, axis=0) / 0.9
    middle = residual + keep_rows[:, 0:1] * branch
    normed_mid, unit_two, factor_two = norm_parts(middle, gain_two, ln2_bias.astype(f32))
    normed_two = normed_mid.astype(bf16)
    activate = partial(jax.nn.gelu, approximate=False)
    gathered = lax.all_gather(normed_two, "mp", axis=0, tiled=True)
    hidden = jnp.dot(gathered, fc1_weight, preferred_element_type=f32) + fc1_bias.astype(f32)
    activated_f, gelu_pull = jax.vjp(activate, hidden)
    activated = activated_f.astype(bf16)
    feed_out = lax.psum_scatter(
        jnp.dot(
            lax.slice_in_dim(activated, 0, local_rows * lax.axis_size("mp"), axis=0),
            fc2_weight,
            preferred_element_type=f32,
        ).astype(jnp.bfloat16),
        "mp",
        scatter_dimension=0,
        tiled=True,
    ).astype(jnp.float32)
    feed_out = feed_out + fc2_bias.astype(f32)
    result = (middle + keep_rows[:, 1:2] * feed_out).astype(bf16)
    grad_out = out_grad.astype(f32)
    grad_feed = (keep_rows[:, 1:2] * grad_out).astype(bf16)
    down_bias_grad = jnp.sum(grad_feed, axis=0, dtype=f32)
    grad_gathered = lax.all_gather(grad_feed, "mp", axis=0, tiled=True)
    grad_act = jnp.dot(grad_gathered, fc2_weight.T, preferred_element_type=f32)
    grad_hidden = gelu_pull(grad_act)[0].astype(bf16)
    down_grad = jnp.dot(activated.T, grad_gathered, preferred_element_type=f32)
    up_grad = jnp.dot(gathered.T, grad_hidden, preferred_element_type=f32)
    up_bias_grad = jnp.sum(grad_hidden, axis=0, dtype=f32)
    grad_second = lax.psum_scatter(
        jnp.dot(grad_hidden, fc1_weight.T, preferred_element_type=f32).astype(jnp.bfloat16),
        "mp",
        scatter_dimension=0,
        tiled=True,
    ).astype(jnp.float32)
    up_grad, down_grad, up_bias_grad = (
        lax.psum_scatter(
            up_grad.astype(jnp.bfloat16), "dp", scatter_dimension=0, tiled=True
        ).astype(jnp.float32),
        lax.psum_scatter(
            down_grad.astype(jnp.bfloat16), "dp", scatter_dimension=1, tiled=True
        ).astype(jnp.float32),
        lax.psum_scatter(
            up_bias_grad.astype(jnp.bfloat16), "dp", scatter_dimension=0, tiled=True
        ).astype(jnp.float32),
    )
    gain_two_grad = jnp.sum(grad_second * unit_two, axis=0)
    shift_two_grad = jnp.sum(grad_second, axis=0)
    grad_middle = grad_out + norm_back(grad_second, unit_two, factor_two, gain_two)
    grad_branch = (keep_rows[:, 0:1] * grad_middle).astype(bf16)
    proj_bias_grad = jnp.sum(grad_branch, axis=0, dtype=f32)
    proj_grad = jnp.dot(attended.T, grad_branch, preferred_element_type=f32)
    grad_att = jnp.dot(grad_branch, proj_full.T, preferred_element_type=f32).astype(bf16)
    grad_att = grad_att.reshape(windows_here, window_area, HEADS, HEAD)
    scores = attn_scores(queries, key_part, tab_h.astype(bf16), tab_w.astype(bf16), key_mask)
    attn_probs = jnp.exp(scores - log_total)
    values_grad = jnp.einsum(
        "nhqk,nqhc->nkhc", attn_probs.astype(bf16), grad_att, preferred_element_type=f32
    )
    probs_grad = jnp.einsum("nqhc,nkhc->nhqk", grad_att, flat_values, preferred_element_type=f32)
    score_grad = attn_probs * (
        probs_grad - jnp.sum(attn_probs * probs_grad, axis=-1, keepdims=True)
    )
    grid_grad = score_grad.astype(bf16).reshape(windows_here, HEADS, WIN, WIN, WIN, WIN)
    row_grad = jnp.sum(grid_grad, axis=5, dtype=f32)
    col_grad = jnp.sum(grid_grad, axis=4, dtype=f32)
    queries_grad = jnp.einsum(
        "nhabxy,nxyhc->nabhc", grid_grad, key_part, preferred_element_type=f32
    ) * HEAD ** (-0.5)
    queries_grad = queries_grad + jnp.einsum("nhabx,axc->nabhc", row_grad, tab_h, precision=highest)
    queries_grad = queries_grad + jnp.einsum("nhaby,byc->nabhc", col_grad, tab_w, precision=highest)
    keys_grad = jnp.einsum(
        "nhabxy,nabhc->nxyhc", grid_grad, queries, preferred_element_type=f32
    ) * HEAD ** (-0.5)
    query_wide = queries.astype(f32)
    tabh_grad = jnp.einsum("nhabx,nabhc->axc", row_grad, query_wide, precision=highest)
    tabw_grad = jnp.einsum("nhaby,nabhc->byc", col_grad, query_wide, precision=highest)
    relh_grad = jnp.einsum("axr,axc->rc", onehot, tabh_grad, precision=highest)
    relw_grad = jnp.einsum("axr,axc->rc", onehot, tabw_grad, precision=highest)
    values_grad = values_grad.reshape(windows_here, WIN, WIN, HEADS, HEAD)
    qkv_grad = (
        jnp.stack([queries_grad, keys_grad, values_grad], axis=3)
        .astype(bf16)
        .reshape(local_rows, 3 * D)
    )
    qv_grad = jnp.stack(
        [
            jnp.sum(qkv_grad[:, :D], axis=0, dtype=f32),
            jnp.sum(qkv_grad[:, 2 * D :], axis=0, dtype=f32),
        ]
    )
    qkv_w_grad = jnp.dot(normed_one.T, qkv_grad, preferred_element_type=f32)
    grad_first = jnp.dot(qkv_grad, qkv_full.T, preferred_element_type=f32)
    gain_one_grad = jnp.sum(grad_first * unit_one, axis=0)
    shift_one_grad = jnp.sum(grad_first, axis=0)
    grad_input = grad_middle + norm_back(grad_first, unit_one, factor_one, gain_one)
    qkv_w_grad, proj_grad = (
        lax.psum_scatter(qkv_w_grad, ("dp", "mp"), scatter_dimension=0, tiled=True),
        lax.psum_scatter(proj_grad, ("dp", "mp"), scatter_dimension=0, tiled=True),
    )
    (
        gain_one_grad,
        shift_one_grad,
        qv_grad,
        relh_grad,
        relw_grad,
        proj_bias_grad,
        gain_two_grad,
        shift_two_grad,
        down_bias_grad,
    ) = lax.psum(
        (
            gain_one_grad,
            shift_one_grad,
            qv_grad,
            relh_grad,
            relw_grad,
            proj_bias_grad,
            gain_two_grad,
            shift_two_grad,
            down_bias_grad,
        ),
        ("dp", "mp"),
    )
    return (
        result,
        grad_input.astype(bf16),
        gain_one_grad,
        shift_one_grad,
        qkv_w_grad,
        qv_grad,
        relh_grad,
        relw_grad,
        proj_grad,
        proj_bias_grad,
        gain_two_grad,
        shift_two_grad,
        up_grad,
        up_bias_grad,
        down_grad,
        down_bias_grad,
    )


def solution(mesh):
    in_specs = (
        P(("dp", "mp"), None),
        P(),
        P(),
        P(("dp", "mp"), None),
        P(),
        P(),
        P(),
        P(("dp", "mp"), None),
        P(),
        P(),
        P(),
        P(None, "mp"),
        P("mp"),
        P("mp", None),
        P(),
        P(("dp", "mp"), None),
        P(("dp", "mp"), None),
        P(("dp", "mp"), None),
    )
    out_specs = (
        P(("dp", "mp"), None),
        P(("dp", "mp"), None),
        P(),
        P(),
        P(("dp", "mp"), None),
        P(),
        P(),
        P(),
        P(("dp", "mp"), None),
        P(),
        P(),
        P(),
        P("dp", "mp"),
        P(("mp", "dp")),
        P("mp", "dp"),
        P(),
    )
    return jax.shard_map(
        per_device, mesh=mesh, in_specs=in_specs, out_specs=out_specs, check_vma=False
    )
```

profile of v0, /device:TPU:0, one launch (start us, length us, event | category | flops | bytes accessed | tf_op | source)
XLA Modules:
  0.0 547.3 jit_solution(16702787436069990206)
XLA Ops:
  22.7 10.9 %all-gather.1 = bf16[2,196,768]{2,1,0:T(8,128)(2,1)S(1)} all-gather(bf16[1,196,768]{2,1,0:T(8,128)(2,1)S(1)} %fusion.91), channel_id=1, replica_groups=mesh['dp'=16,'mp'=2] {'mp'}, dimensions={0}, use_global_device_ids=true | all-gather | bytes 903168 | tf_op jit(solution)/shard_map/all_gather | solution.py:128
  34.5 39.3 %all-gather.5.cloned.1.call-done = bf16[768,2304]{1,0:T(8,128)(2,1)} async-done(((bf16[24,2304]{1,0:T(8,128)(2,1)}), bf16[768,2304]{1,0:T(8,128)(2,1)}) %all-gather.5.cloned.1.call-update) | async-done | bytes 3538960 | tf_op jit(solution)/shard_map/all_gather | solution.py:76
  73.9 3.9 fusion.7
  77.8 4.0 reshape.314
  81.8 3.4 fusion.117
  85.2 2.8 convolution_bitcast_fusion.1
  88.0 3.9 copy.77
  91.9 2.6 convolution_bitcast_fusion.2
  94.5 10.9 %select_reduce_fusion = (f32[12,14,14]{2,1,0:T(8,128)S(1)}, f32[12,14,14,14,14]{2,4,3,1,0:T(8,128)}) fusion(pred[14,14]{1,0:T(8,128)(4,1)S(1)} %gt.18, f32[12,14,14,14]{2,3,1,0:T(8,128)} %copy.77, bf16[1,14,14,1,12,64]{5,4,3,2,1,0:T(8,128)(2,1)} %get-tuple-element.52, bf16[1,14,14,1,12,64]{5,4,3,2,1,0:T(8,128)(2,1)} %get-tuple-element.51, ...), kind=kOutput, calls=%fused_computation.3 | convolution fusion | flops 61309584 | bytes 2719108 | tf_op jit(solution)/shard_map/nabhc,nxyhc->nhabxy/dot_general | solution.py:39
  105.5 19.4 %copy.118 = f32[12,14,14,14,14]{2,1,4,3,0:T(8,128)} copy(f32[12,14,14,14,14]{2,4,3,1,0:T(8,128)} %get-tuple-element.58) | data formatting | bytes 3687936 | tf_op jit(solution)/shard_map/reshape | solution.py:45
  124.9 11.5 %exponential_reduce_fusion = f32[12,14,14]{2,1,0:T(8,128)S(1)} fusion(f32[12,14,14,14,14]{2,4,3,1,0:T(8,128)} %get-tuple-element.58, f32[12,14,14]{2,1,0:T(8,128)S(1)} %get-tuple-element.57, pred[14,14]{1,0:T(8,128)(4,1)S(1)} %gt.18), kind=kLoop, calls=%fused_computation.1 | loop fusion | flops 1380624 | bytes 1862980 | tf_op jit(solution)/shard_map/reduce_sum | solution.py:95
  136.6 12.7 %reshape.340 = f32[12,196,196]{1,2,0:T(8,128)} reshape(f32[12,14,14,14,14]{2,1,4,3,0:T(8,128)} %copy.118) | data formatting | bytes 3687936 | tf_op jit(solution)/shard_map/reshape | solution.py:45
  149.3 3.2 convolution_convert_fusion.5
  152.5 2.6 fusion.119
  155.6 10.2 %all-gather = bf16[2,196,768]{2,1,0:T(8,128)(2,1)} all-gather(bf16[1,196,768]{2,1,0:T(8,128)(2,1)S(1)} %fusion.90), channel_id=1, replica_groups=mesh['dp'=16,'mp'=2] {'mp'}, dimensions={0}, use_global_device_ids=true | all-gather | bytes 903168 | tf_op jit(solution)/shard_map/all_gather | solution.py:109
  167.8 3.0 convolution_add_fusion.1
  170.9 8.2 %fusion.115 = (bf16[1536]{0:T(1024)(128)(2,1)S(1)}, bf16[392,1536]{1,0:T(8,128)(2,1)S(1)}, f32[392,1536]{1,0:T(8,128)}) fusion(f32[392,1536]{1,0:T(8,128)S(1)} %convolution_add_fusion.1, bf16[392,768]{1,0:T(8,128)(2,1)S(1)} %copy-done.21, bf16[1536,768]{1,0:T(8,128)(2,1)S(1)} %copy-done), kind=kOutput, calls=%fused_computation.164 | convolution fusion | flops 968796672 | bytes 8985600 | tf_op jit(solution)/shard_map/dot_general | solution.py:129
  180.1 2.9 convolution_convert_fusion.1
  183.1 3.0 multiply_convert_fusion.1
  187.1 2.9 convolution_convert_fusion
  191.4 3.4 convolution_convert_fusion.3
  196.8 18.6 %fusion.114 = (bf16[200,768]{1,0:T(8,128)(2,1)}, bf16[200,768]{1,0:T(8,128)(2,1)}) fusion(bf16[392,768]{1,0:T(8,128)(2,1)} %convolution_convert_fusion.3, bf16[392,768]{1,0:T(8,128)(2,1)} %convolution_convert_fusion.2), kind=kCustom, calls=%all-reduce-scatter.2 | all-reduce-scatter fusion | flops 614401 | bytes 1819136
  216.1 3.3 collective-permute-start
  221.4 3.3 concatenate.7
  224.7 3.3 concatenate.8
  229.5 3.9 convert_reduce_fusion.3
  236.8 2.4 multiply_convert_fusion
  239.2 2.8 copy.85
  242.0 12.7 %reshape.321 = f32[1,12,14,14,14,14]{5,4,3,2,1,0:T(8,128)} reshape(f32[12,196,196]{2,1,0:T(8,128)} %copy.85) | data formatting | bytes 3687936 | tf_op jit(solution)/shard_map/convert_element_type | solution.py:169
  254.7 2.9 fusion.120
  257.8 11.2 %fusion.113 = (f32[12,14,14,14]{3,2,1,0:T(8,128)}, f32[12,14,14,14]{3,2,1,0:T(8,128)}) fusion(f32[1,12,14,14,14,14]{5,4,3,2,1,0:T(8,128)} %reshape.321), kind=kLoop, calls=%fused_computation.163 | loop fusion | flops 856128 | bytes 2107392 | tf_op jit(solution)/shard_map/reduce_sum | solution.py:169
  269.1 12.9 %reshape.320 = bf16[12,14,14,14,14]{2,1,4,3,0:T(8,128)(2,1)} reshape(bf16[12,196,196]{1,2,0:T(8,128)(2,1)} %multiply_convert_fusion) | data formatting | bytes 1843968 | tf_op jit(solution)/shard_map/reshape.50
  282.0 3.6 copy.96
  285.5 3.1 fusion.52
  288.7 2.1 copy.92
  290.8 2.1 stack.22
  293.0 3.9 fusion.92
  296.9 6.7 %fusion.32 = f32[1,14,14,12,64]{4,2,1,3,0:T(8,128)S(1)} fusion(bf16[12,14,14,14,14]{2,1,4,3,0:T(8,128)(2,1)} %reshape.320, bf16[1,14,14,1,12,64]{5,4,3,2,1,0:T(8,128)(2,1)S(1)} %copy-done.11), kind=kOutput, calls=%fused_computation.46 | convolution fusion | flops 59157504 | bytes 1825152 | tf_op jit(solution)/shard_map/nhabxy,nxyhc->nabhc/dot_general | solution.py:171
  305.6 3.4 fusion.39
  309.7 2.2 copy.93
  311.9 4.4 convert_element_type.201
  316.3 5.4 fusion.110
  323.5 29.7 %all-reduce.2 = bf16[1536]{0:T(1024)(128)(2,1)S(1)} all-reduce(bf16[1536]{0:T(1024)(128)(2,1)S(1)} %get-tuple-element.43), channel_id=7, replica_groups=mesh['dp'=16,'mp'=2] {'dp'}, use_global_device_ids=true, to_apply=%region_34.35.clone | all-reduce | flops 1536 | bytes 6144
  355.1 2.9 convolution_bitcast_fusion.3
  360.0 4.2 fusion.75
  364.2 39.1 %all-reduce.5 = (f32[768]{0:T(1024)}, f32[768]{0:T(1024)}, f32[2,768]{1,0:T(2,128)}, f32[27,64]{1,0:T(8,128)}, f32[27,64]{1,0:T(8,128)}, /*index=5*/f32[768]{0:T...) all-reduce(f32[768]{0:T(1024)S(1)} %get-tuple-element.20, ...), channel_id=1, replica_groups=mesh['dp'=16,'mp'=2] {'dp','mp'}, use_global_device_ids=true, to_apply=%region_16.17 | all-reduce | flops 9600 | bytes 76800 | tf_op jit(solution)/shard_map/psum | solution.py:215
  408.6 6.5 %reduce-scatter.11.cloned.1.call-done = f32[24,768]{1,0:T(8,128)} async-done(((f32[768,768]{1,0:T(8,128)}), f32[24,768]{1,0:T(8,128)}) %reduce-scatter.11.cloned.1.call-update) | async-done | bytes 73744 | tf_op jit(solution)/shard_map/reduce_scatter | solution.py:203
  415.2 124.9 %reduce-scatter.9.cloned.1.call-done = f32[24,2304]{1,0:T(8,128)} async-done(((f32[768,2304]{1,0:T(8,128)}), f32[24,2304]{1,0:T(8,128)}) %reduce-scatter.9.cloned.1.call-update) | async-done | bytes 221200 | tf_op jit(solution)/shard_map/reduce_scatter | solution.py:202
  (142 shorter events, 44.5 us)
Async XLA Ops:
  7.2 163.6 %copy-start = (bf16[1536,768]{1,0:T(8,128)(2,1)S(1)}, bf16[1536,768]{1,0:T(8,128)(2,1)}, u32[]{:S(2)}) copy-start(bf16[1536,768]{1,0:T(8,128)(2,1)} %param.31) | copy-start | bytes 7077892
  7.2 66.7 %copy-start.6 = (bf16[196,768]{1,0:T(8,128)(2,1)S(1)}, bf16[196,768]{1,0:T(8,128)(2,1)}, u32[]{:S(2)}) copy-start(bf16[196,768]{1,0:T(8,128)(2,1)} %param.18) | copy-start | bytes 903172
  7.2 66.7 %all-gather.5.cloned.1.call-start = ((), (), s32[]{:S(2)}) async-start(), calls=%async_computation.4 | async-start | bytes 3649536 | tf_op jit(solution)/shard_map/all_gather | solution.py:76
  7.9 144.6 %all-gather.7.cloned.1.call-start = ((), (), s32[]{:S(2)}) async-start(), calls=%async_computation.5 | async-start | bytes 1216512 | tf_op jit(solution)/shard_map/all_gather | solution.py:77
  8.7 396.6 %reduce-scatter.13.cloned.1.call-start = ((), (), s32[]{:S(2)}) async-start(), calls=%async_computation.8 | async-start | bytes 2506752 | tf_op jit(solution)/shard_map/reduce_scatter | solution.py:141
  81.8 3.4 copy-start.20
  85.2 6.7 %copy-start.3 = (bf16[14,14,12,64]{3,2,1,0:T(8,128)(2,1)}, bf16[14,14,12,64]{3,2,1,0:T(8,128)(2,1)S(1)}, u32[]{:S(2)}) copy-start(bf16[14,14,12,64]{3,2,1,0:T(8,128)(2,1)S(1)} %get-tuple-element.50) | copy-start | bytes 903172
  136.6 12.8 %copy-start.15 = (bf16[1,14,14,1,12,64]{5,4,3,2,1,0:T(8,128)(2,1)S(1)}, bf16[1,14,14,1,12,64]{5,4,3,2,1,0:T(8,128)(2,1)}, u32[]{:S(2)}) copy-start(bf16[1,14,14,1,12,64]{5,4,3,2,1,0:T(8,128)(2,1)} %get-tuple-element.49) | copy-start | bytes 903172
  167.8 3.0 copy-start.21
  170.8 8.3 %copy-start.17 = (f32[392,1536]{1,0:T(8,128)}, f32[392,1536]{1,0:T(8,128)S(1)}, u32[]{:S(2)}) copy-start(f32[392,1536]{1,0:T(8,128)S(1)} %convolution_add_fusion.1) | copy-start | bytes 7225348
  170.8 9.3 %copy-start.23 = (bf16[392,768]{1,0:T(8,128)(2,1)S(1)}, bf16[392,768]{1,0:T(8,128)(2,1)}, u32[]{:S(2)}) copy-start(bf16[392,768]{1,0:T(8,128)(2,1)} %reshape.323) | copy-start | bytes 1806340
  179.1 1.0 copy-start.28
  183.0 224.0 %reduce-scatter.15.cloned.1.call-start = ((), (), s32[]{:S(2)}) async-start(), calls=%async_computation.9 | async-start | bytes 2506752 | tf_op jit(solution)/shard_map/reduce_scatter | solution.py:144
  183.1 4.0 copy-start.22
  186.1 1.0 copy-start.18
  187.1 3.0 copy-start.25
  187.1 4.3 copy-start.24
  190.1 225.1 %reduce-scatter.11.cloned.1.call-start = ((), (), s32[]{:S(2)}) async-start(), calls=%async_computation.7 | async-start | bytes 2433024 | tf_op jit(solution)/shard_map/reduce_scatter | solution.py:203
  191.4 3.4 copy-start.26
  191.4 3.4 copy-start.29
  216.1 5.3 collective-permute-start
  220.1 4.6 collective-permute-start.1
  228.0 6.1 %copy-start.8 = (bf16[768,768]{1,0:T(8,128)(2,1)S(1)}, bf16[768,768]{1,0:T(8,128)(2,1)}, u32[]{:S(2)}) copy-start(bf16[768,768]{1,0:T(8,128)(2,1)} %all-gather.7.cloned.1.call-done) | copy-start | bytes 3538948
  233.4 0.7 copy-start.12
  234.8 1.9 copy-start.5
  242.0 12.7 %copy-start.13 = (bf16[196,768]{1,0:T(8,128)(2,1)S(1)}, bf16[196,768]{1,0:T(8,128)(2,1)}, u32[]{:S(2)}) copy-start(bf16[196,768]{1,0:T(8,128)(2,1)} %copy-done.12) | copy-start | bytes 903172
  257.6 282.4 %reduce-scatter.9.cloned.1.call-start = ((), (), s32[]{:S(2)}) async-start(), calls=%async_computation.6 | async-start | bytes 7299072 | tf_op jit(solution)/shard_map/reduce_scatter | solution.py:202
  288.7 8.2 %copy-start.11 = (bf16[1,14,14,1,12,64]{5,4,3,2,1,0:T(8,128)(2,1)S(1)}, bf16[1,14,14,1,12,64]{5,4,3,2,1,0:T(8,128)(2,1)}, u32[]{:S(2)}) copy-start(bf16[1,14,14,1,12,64]{5,4,3,2,1,0:T(8,128)(2,1)} %get-tuple-element.52) | copy-start | bytes 903172
  293.0 12.6 %slice-start = ((s8[9633792]{0:T(1024)(128)(4,1)}), s8[4194304]{0:T(1024)(128)(4,1)S(1)}, s32[]{:S(2)}) async-start(s8[9633792]{0:T(1024)(128)(4,1)} %bitcast.181), calls=%async_computation.10 | async-start | bytes 8388608
  296.8 6.8 %copy-start.1 = (f32[12,14,14,14]{3,2,1,0:T(8,128)S(1)}, f32[12,14,14,14]{3,2,1,0:T(8,128)}, u32[]{:S(2)}) copy-start(f32[12,14,14,14]{3,2,1,0:T(8,128)} %get-tuple-element.16) | copy-start | bytes 395140
  296.9 6.8 %copy-start.19 = (f32[14,14,64]{2,1,0:T(8,128)S(1)}, f32[14,14,64]{2,1,0:T(8,128)}, u32[]{:S(2)}) copy-start(f32[14,14,64]{2,1,0:T(8,128)} %fusion.96) | copy-start | bytes 150532
  296.9 8.7 %slice-start.1 = ((s8[9633792]{0:T(1024)(128)(4,1)}), s8[4194304]{0:T(1024)(128)(4,1)S(1)}, s32[]{:S(2)}) async-start(s8[9633792]{0:T(1024)(128)(4,1)} %bitcast.181), calls=%async_computation.11 | async-start | bytes 8388608
  296.9 8.7 %slice-start.2 = ((s8[9633792]{0:T(1024)(128)(4,1)}), s8[1245184]{0:T(1024)(128)(4,1)S(1)}, s32[]{:S(2)}) async-start(s8[9633792]{0:T(1024)(128)(4,1)} %bitcast.181), calls=%async_computation.12 | async-start | bytes 2490368
  303.6 2.0 copy-start.9
  305.6 3.4 copy-start.14
  321.6 0.7 copy-start.27
  321.7 33.5 %copy-start.4 = (bf16[14,14,12,64]{3,2,1,0:T(8,128)(2,1)S(1)}, bf16[14,14,12,64]{3,2,1,0:T(8,128)(2,1)}, u32[]{:S(2)}) copy-start(bf16[14,14,12,64]{3,2,1,0:T(8,128)(2,1)} %copy-done.3) | copy-start | bytes 903172
  353.2 5.1 copy-start.2
  353.2 5.2 copy-start.10
  355.1 4.9 copy-start.7
  360.0 43.3 %copy-start.16 = (f32[196,768]{1,0:T(8,128)S(1)}, f32[196,768]{1,0:T(8,128)}, u32[]{:S(2)}) copy-start(f32[196,768]{1,0:T(8,128)} %get-tuple-element.48) | copy-start | bytes 1806340
Sparse Core Ops, SparseCore 0:
  11.0 62.8 all-gather.4
  76.8 52.9 all-gather.6
  183.1 61.7 reduce-scatter.12
  249.0 61.9 reduce-scatter.14
  316.8 98.3 reduce-scatter.10
  422.2 117.7 reduce-scatter.8
where the time goes:
time: 558 us; the launch traced here: 547 us
  waiting for transfers between devices  172 us (31%)
  blocking collectives  108 us (19%)
  local copies, waits for them, and re-layouts  103 us (18%)
  matrix products  90.3 us (16%)
  other arithmetic  51.9 us (9%)
  between operations  16.3 us (3%)
    reduce_scatter x1, waiting for transfers between devices, per_device(): lax.psum_scatter(qkv_w_grad, ('dp', 'mp'), scatter_dimension=0, tiled=True)  125 us
    unnamed x2, blocking collectives  48.3 us
    all_gather x1, waiting for transfers between devices, per_device(): lax.all_gather(qkv_weight, ('dp', 'mp'), axis=0, tiled=True)  39.3 us
    psum x1, blocking collectives, per_device(): lax.psum((gain_one_grad, shift_one_grad, qv_grad, relh_grad, relw_grad, p...  39.1 us
    reshape x2, local copies, waits for them, and re-layouts, attn_scores(): scores = scores.reshape(windows_here, HEADS, WIN * WIN, WIN * WIN)  32.1 us
    unnamed x74, local copies, waits for them, and re-layouts  15.8 us
    convert_element_type x2, local copies, waits for them, and re-layouts, per_device(): row_grad = jnp.sum(grid_grad, axis=5, dtype=f32)  15.5 us
    another operation x1, local copies, waits for them, and re-layouts  12.9 us
  transfers between devices with their start and end apart: 8, of which 3 were waited for; matrix products, arithmetic and copies ran while one was open for 44% of the time, Pallas kernels for 0%

commit v1 on v0

--- a/solution.py
+++ b/solution.py
@@ -9,6 +9,134 @@
 HEADS = 12
 HEAD = 64
 WIN = 14
+
+
+def dp_pairs(count, dz=0, dy=0, dc=0):
+    depth = count // 4
+    pairs = []
+    for place in range(count):
+        z, y, c = place // 4, place // 2 % 2, place % 2
+        pairs.append((place, (z + dz) % depth * 4 + (y + dy) % 2 * 2 + (c + dc) % 2))
+    return pairs
+
+
+def move_z(value, step):
+    count = lax.axis_size("dp")
+    return lax.ppermute(value, "dp", dp_pairs(count, dz=step))
+
+
+def move_y(value, step=1):
+    return lax.ppermute(value, "dp", dp_pairs(lax.axis_size("dp"), dy=step))
+
+
+def move_c(value, step=1):
+    return lax.ppermute(value, "dp", dp_pairs(lax.axis_size("dp"), dc=step))
+
+
+def move_x(value, step=1):
+    count = lax.axis_size("mp")
+    return lax.ppermute(value, "mp", [(i, (i + step) % count) for i in range(count)])
+
+
+def pick(value, index, axis):
+    return lax.dynamic_index_in_dim(value, index, axis, keepdims=False)
+
+
+def in_order(blocks, index):
+    count = len(blocks)
+    if count == 2:
+        first, second = blocks
+        swap = index == 1
+        return jnp.stack([jnp.where(swap, second, first), jnp.where(swap, first, second)])
+    twice = jnp.stack([blocks[-j % count] for j in range(count)] * 2)
+    return lax.dynamic_slice_in_dim(twice, count - index, count, axis=0)
+
+
+def places():
+    dp = lax.axis_index("dp")
+    return dp // 4, dp // 2 % 2, dp % 2, lax.axis_index("mp")
+
+
+def gather_rows(shard, chunks):
+    z, y, c, x = places()
+    depth, wide = lax.axis_size("dp") // 4, lax.axis_size("mp")
+    rows, columns = shard.shape
+    width = columns // chunks
+    lines = []
+    for k in range(chunks):
+        part = shard[:, k * width : (k + 1) * width]
+        lines.append(in_order([part] + [move_z(part, s) for s in range(1, depth)], z))
+    outs = []
+    for line in lines:
+        half = width // 2
+        along_x = [line] + [move_x(line, s) for s in range(1, wide)]
+        along_y = move_y(line)
+        left = [move_y(b[..., :half]) for b in along_x[1:]]
+        right = [move_x(along_y[..., half:], s) for s in range(1, wide)]
+        far = [along_y] + [jnp.concatenate([p, q], -1) for p, q in zip(left, right)]
+        both = in_order([in_order(along_x, x), in_order(far, x)], y)
+        both = in_order([both, move_c(both)], c)
+        outs.append(both.transpose(3, 1, 0, 2, 4, 5).reshape(-1, width))
+    return jnp.concatenate(outs, -1)
+
+
+def scatter_axis(value, axis, size, index, move):
+    total = pick(value, index, axis).astype(jnp.float32)
+    for step in range(1, size):
+        block = pick(value, (index + step) % size, axis).astype(jnp.bfloat16)
+        total = total + move(block, step).astype(jnp.float32)
+    return total
+
+
+def scatter_rows(grad):
+    z, y, c, x = places()
+    depth, wide = lax.axis_size("dp") // 4, lax.axis_size("mp")
+    columns = grad.shape[1]
+    blocks = grad.reshape(depth, 2, 2, wide, -1, columns)
+    blocks = scatter_axis(blocks, 2, 2, c, move_c)
+    half = columns // 2
+    first, second = blocks[..., :half], blocks[..., half:]
+    first = scatter_axis(first, 2, wide, x, move_x)
+    second = scatter_axis(second, 1, 2, y, move_y)
+    first = scatter_axis(first, 1, 2, y, move_y)
+    second = scatter_axis(second, 1, wide, x, move_x)
+    first = scatter_axis(first, 0, depth, z, move_z)
+    second = scatter_axis(second, 0, depth, z, move_z)
+    return jnp.concatenate([first, second], -1)
+
+
+def scatter_dp(grad):
+    z, y, c, x = places()
+    depth = lax.axis_size("dp") // 4
+    blocks = grad.reshape(depth, 2, 2, -1, grad.shape[1])
+    blocks = scatter_axis(blocks, 2, 2, c, move_c)
+    blocks = scatter_axis(blocks, 1, 2, y, move_y)
+    return scatter_axis(blocks, 0, depth, z, move_z)
+
+
+def sum_all(parts):
+    depth, wide = lax.axis_size("dp") // 4, lax.axis_size("mp")
+    flat = jnp.concatenate([p.reshape(-1) for p in parts])
+    size = flat.shape[0]
+    flat = jnp.pad(flat, (0, -size % 1024)).reshape(-1, 128)
+    flat = flat + move_c(flat)
+    flat = sum([move_x(flat, s) for s in range(1, wide)], flat)
+    flat = flat + move_y(flat)
+    flat = sum([move_z(flat, s) for s in range(1, depth)], flat)
+    flat = flat.reshape(-1)
+    outs, at = [], 0
+    for p in parts:
+        outs.append(flat[at : at + p.size].reshape(p.shape))
+        at += p.size
+    return outs
+
+
+def sum_back(partial_rows, wide):
+    blocks = partial_rows.reshape(wide, -1, partial_rows.shape[-1])
+    total = blocks[0]
+    for step in range(1, wide):
+        total = total + move_x(blocks[step].astype(jnp.bfloat16), -step).astype(jnp.float32)
+    return total
 
 
 def norm_parts(rows_in, gain, shift):
@@ -72,10 +200,9 @@
     windows_here = key_mask.shape[0]
     window_area = WIN * WIN
     local_rows = tokens.shape[0]
-    qkv_full, proj_full = (
-        lax.all_gather(qkv_weight, ("dp", "mp"), axis=0, tiled=True),
-        lax.all_gather(proj_weight, ("dp", "mp"), axis=0, tiled=True),
-    )
+    wide = lax.axis_size("mp")
+    weights = gather_rows(jnp.concatenate([qkv_weight, proj_weight], -1), 2)
+    qkv_full, proj_full = weights[:, : 3 * D], weights[:, 3 * D :]
     gain_one = ln1_gain.astype(f32)
     gain_two = ln2_gain.astype(f32)
     residual = tokens.astype(f32)
@@ -106,47 +233,27 @@
     normed_mid, unit_two, factor_two = norm_parts(middle, gain_two, ln2_bias.astype(f32))
     normed_two = normed_mid.astype(bf16)
     activate = partial(jax.nn.gelu, approximate=False)
-    gathered = lax.all_gather(normed_two, "mp", axis=0, tiled=True)
+    gathered = jnp.concatenate([normed_two] + [move_x(normed_two, s) for s in range(1, wide)])
     hidden = jnp.dot(gathered, fc1_weight, preferred_element_type=f32) + fc1_bias.astype(f32)
     activated_f, gelu_pull = jax.vjp(activate, hidden)
     activated = activated_f.astype(bf16)
-    feed_out = lax.psum_scatter(
-        jnp.dot(
-            lax.slice_in_dim(activated, 0, local_rows * lax.axis_size("mp"), axis=0),
-            fc2_weight,
-            preferred_element_type=f32,
-        ).astype(jnp.bfloat16),
-        "mp",
-        scatter_dimension=0,
-        tiled=True,
-    ).astype(jnp.float32)
+    feed_out = sum_back(jnp.dot(activated, fc2_weight, preferred_element_type=f32), wide)
     feed_out = feed_out + fc2_bias.astype(f32)
     result = (middle + keep_rows[:, 1:2] * feed_out).astype(bf16)
     grad_out = out_grad.astype(f32)
     grad_feed = (keep_rows[:, 1:2] * grad_out).astype(bf16)
     down_bias_grad = jnp.sum(grad_feed, axis=0, dtype=f32)
-    grad_gathered = lax.all_gather(grad_feed, "mp", axis=0, tiled=True)
+    grad_gathered = jnp.concatenate([grad_feed] + [move_x(grad_feed, s) for s in range(1, wide)])
     grad_act = jnp.dot(grad_gathered, fc2_weight.T, preferred_element_type=f32)
     grad_hidden = gelu_pull(grad_act)[0].astype(bf16)
-    down_grad = jnp.dot(activated.T, grad_gathered, preferred_element_type=f32)
+    down_grad = jnp.dot(grad_gathered.T, activated, preferred_element_type=f32)
     up_grad = jnp.dot(gathered.T, grad_hidden, preferred_element_type=f32)
     up_bias_grad = jnp.sum(grad_hidden, axis=0, dtype=f32)
-    grad_second = lax.psum_scatter(
-        jnp.dot(grad_hidden, fc1_weight.T, preferred_element_type=f32).astype(jnp.bfloat16),
-        "mp",
-        scatter_dimension=0,
-        tiled=True,
-    ).astype(jnp.float32)
-    up_grad, down_grad, up_bias_grad = (
-        lax.psum_scatter(
-            up_grad.astype(jnp.bfloat16), "dp", scatter_dimension=0, tiled=True
-        ).astype(jnp.float32),
-        lax.psum_scatter(
-            down_grad.astype(jnp.bfloat16), "dp", scatter_dimension=1, tiled=True
-        ).astype(jnp.float32),
-        lax.psum_scatter(
-            up_bias_grad.astype(jnp.bfloat16), "dp", scatter_dimension=0, tiled=True
-        ).astype(jnp.float32),
+    grad_second = sum_back(jnp.dot(grad_hidden, fc1_weight.T, preferred_element_type=f32), wide)
+    up_grad = scatter_dp(up_grad)
+    down_grad = scatter_dp(down_grad).T
+    up_bias_all = lax.dynamic_update_slice(
+        jnp.zeros((wide, up_bias_grad.shape[0]), f32), up_bias_grad[None], (lax.axis_index("mp"), 0)
     )
     gain_two_grad = jnp.sum(grad_second * unit_two, axis=0)
     shift_two_grad = jnp.sum(grad_second, axis=0)
@@ -198,10 +305,8 @@
     gain_one_grad = jnp.sum(grad_first * unit_one, axis=0)
     shift_one_grad = jnp.sum(grad_first, axis=0)
     grad_input = grad_middle + norm_back(grad_first, unit_one, factor_one, gain_one)
-    qkv_w_grad, proj_grad = (
-        lax.psum_scatter(qkv_w_grad, ("dp", "mp"), scatter_dimension=0, tiled=True),
-        lax.psum_scatter(proj_grad, ("dp", "mp"), scatter_dimension=0, tiled=True),
-    )
+    both_grad = scatter_rows(jnp.concatenate([qkv_w_grad, proj_grad], -1))
+    qkv_w_grad, proj_grad = both_grad[:, : 3 * D], both_grad[:, 3 * D :]
     (
         gain_one_grad,
         shift_one_grad,
@@ -212,7 +317,8 @@
         gain_two_grad,
         shift_two_grad,
         down_bias_grad,
-    ) = lax.psum(
+        up_bias_all,
+    ) = sum_all(
         (
             gain_one_grad,
             shift_one_grad,
@@ -223,8 +329,13 @@
             gain_two_grad,
             shift_two_grad,
             down_bias_grad,
-        ),
-        ("dp", "mp"),
+            up_bias_all,
+        )
+    )
+    up_bias_grad = pick(
+        pick(up_bias_all, lax.axis_index("mp"), 0).reshape(lax.axis_size("dp"), -1),
+        lax.axis_index("dp"),
+        0,
     )
     return (
         result,

time: 558 us -> 393 us (0.70)
  blocking collectives: 108 us -> 0 us
  waiting for transfers between devices: 172 us -> 80.3 us
  starting transfers between devices: 4.98 us -> 59.3 us
  matrix products: 90.3 us -> 76.2 us
  between operations: 16.3 us -> 2.53 us
  other arithmetic: 51.9 us -> 62.7 us
    reduce_scatter x4 -> x0, waiting for transfers between devices: 131 us -> none  [the longest x1 125 us: per_device(): lax.psum_scatter(qkv_w_grad, ('dp', 'mp'), scatter_dimension=0, tiled=True)]
    ppermute x0 -> x47, waiting for transfers between devices: none -> 80.3 us  [the longest x11 32.8 us: move_x(): lax.ppermute(value, 'mp', [(i, (i + step) % count) for i in range(count)])]
    ppermute x0 -> x47, starting transfers between devices: none -> 59.3 us  [the longest x21 33.1 us: move_z(): return lax.ppermute(value, 'dp', dp_pairs(count, dz=step))]
    unnamed x2 -> x0, blocking collectives: 48.3 us -> none
    all_gather x2 -> x0, waiting for transfers between devices: 39.3 us -> none  [the longest x1 39.3 us: per_device(): lax.all_gather(qkv_weight, ('dp', 'mp'), axis=0, tiled=True)]
    psum x1 -> x0, blocking collectives: 39.1 us -> none  [per_device(): lax.psum((gain_one_grad, shift_one_grad, qv_grad, relh_grad, relw_grad, p...]
    all_gather x2 -> x0, blocking collectives: 21.1 us -> none  [the longest x1 10.9 us: per_device(): grad_gathered = lax.all_gather(grad_feed, 'mp', axis=0, tiled=True)]
    add x0 -> x16, other arithmetic: none -> 9.05 us  [the longest x12 8.99 us: scatter_axis(): total = total + move(block, step).astype(jnp.float32)]
  transfers between devices with their start and end apart: 8 -> 47, of which waited for: 3 -> 22; matrix products, arithmetic and copies ran while one was open for 44% -> 39% of each run, Pallas kernels for 0% -> 0%
where the time goes in v1:
time: 393 us; the launch traced here: 388 us
  local copies, waits for them, and re-layouts  107 us (27%)
  waiting for transfers between devices  80.3 us (20%)
  matrix products  76.2 us (19%)
  other arithmetic  62.7 us (16%)
  starting transfers between devices  59.3 us (15%)
    ppermute x21, starting transfers between devices, move_z(): return lax.ppermute(value, 'dp', dp_pairs(count, dz=step))  33.1 us
    ppermute x11, waiting for transfers between devices, move_x(): lax.ppermute(value, 'mp', [(i, (i + step) % count) for i in range(count)])  32.8 us
    reshape x2, local copies, waits for them, and re-layouts, attn_scores(): scores = scores.reshape(windows_here, HEADS, WIN * WIN, WIN * WIN)  32.4 us
    ppermute x9, waiting for transfers between devices, move_y(): return lax.ppermute(value, 'dp', dp_pairs(lax.axis_size('dp'), dy=step))  30.1 us
    ppermute x21, waiting for transfers between devices, move_z(): return lax.ppermute(value, 'dp', dp_pairs(count, dz=step))  16.4 us
    convert_element_type x2, local copies, waits for them, and re-layouts, per_device(): row_grad = jnp.sum(grid_grad, axis=5, dtype=f32)  14.6 us
    ppermute x11, starting transfers between devices, move_x(): lax.ppermute(value, 'mp', [(i, (i + step) % count) for i in range(count)])  13.8 us
    reduce_sum x1, other arithmetic, per_device(): row_total = jnp.sum(expo, axis=-1, keepdims=True)  12.1 us
  transfers between devices with their start and end apart: 47, of which 22 were waited for; matrix products, arithmetic and copies ran while one was open for 39% of the time, Pallas kernels for 0%

profile of v1, /device:TPU:0, one launch (start us, length us, event | category | flops | bytes accessed | tf_op | source)
XLA Modules:
  0.0 387.7 jit_solution(3738575431386646577)
XLA Ops:
  1.7 5.0 %collective-permute-start = (bf16[24,1536]{1,0:T(8,128)(2,1)S(1)}, bf16[24,1536]{1,0:T(8,128)(2,1)S(1)}, u32[]{:S(2)}, u32[]{:S(2)}) collective-permute-start(bf16[24,1536]{1,0:T(8,128)(2,1)S(1)} %slice.147), channel_id=1, source_target_pairs={{0,24},{2,26},{4,28},{6,30},{8,0},{10,2},{12,4},{14,6},{16,8},{18,... | collective-permute-start | bytes 221192 | tf_op jit(solution)/shard_map/ppermute | solution.py:25
  19.3 2.9 collective-permute-start.8
  26.4 4.6 %collective-permute-done.9 = bf16[24,1536]{1,0:T(8,128)(2,1)S(1)} collective-permute-done((bf16[24,1536]{1,0:T(8,128)(2,1)S(1)}, bf16[24,1536]{1,0:T(8,128)(2,1)S(1)}, u32[]{:S(2)}, u32[]{:S(2)}) %collective-permute-start.9) | collective-permute-done | bytes 73760 | tf_op jit(solution)/shard_map/ppermute | solution.py:25
  37.0 5.1 %collective-permute-done.11 = bf16[4,24,1536]{2,1,0:T(8,128)(2,1)S(1)} collective-permute-done((bf16[4,24,1536]{2,1,0:T(8,128)(2,1)S(1)}, bf16[4,24,1536]{2,1,0:T(8,128)(2,1)S(1)}, u32[]{:S(2)}, u32[]{:S(2)}) %collective-permute-start.11) | collective-permute-done | bytes 294944 | tf_op jit(solution)/shard_map/ppermute | solution.py:38
  44.4 2.9 collective-permute-done.12
  54.9 4.2 %reshape.640 = bf16[1,14,14,3,12,64]{5,4,3,2,1,0:T(8,128)(2,1)} reshape(bf16[196,2304]{1,0:T(8,128)(2,1)} %fusion.5) | data formatting | bytes 1806336 | tf_op jit(solution)/shard_map/reshape | solution.py:214
  59.2 3.3 fusion.156
  62.5 2.8 convolution_bitcast_fusion.1
  65.3 3.8 copy.109
  69.2 2.6 convolution_bitcast_fusion.2
  71.8 11.5 %select_reduce_fusion = (f32[12,14,14]{2,1,0:T(8,128)}, f32[12,14,14,14,14]{2,4,3,1,0:T(8,128)}) fusion(pred[14,14]{1,0:T(8,128)(4,1)S(1)} %gt.18, f32[12,14,14,14]{2,3,1,0:T(8,128)} %copy.109, bf16[1,14,14,1,12,64]{5,4,3,2,1,0:T(8,128)(2,1)} %get-tuple-element.44, bf16[1,14,14,1,12,64]{5,4,3,2,1,0:T(8,128)(2,1)} %get-tuple-element.43, ...), kind=kOutput, calls=%fused_computation.3 | convolution fusion | flops 61309584 | bytes 2719108 | tf_op jit(solution)/shard_map/nabhc,nxyhc->nhabxy/dot_general | solution.py:167
  83.3 19.3 %copy.158 = f32[12,14,14,14,14]{2,1,4,3,0:T(8,128)} copy(f32[12,14,14,14,14]{2,4,3,1,0:T(8,128)} %get-tuple-element.86) | data formatting | bytes 3687936 | tf_op jit(solution)/shard_map/reshape | solution.py:173
  102.6 12.1 %exponential_reduce_fusion = f32[12,14,14]{2,1,0:T(8,128)} fusion(f32[12,14,14,14,14]{2,4,3,1,0:T(8,128)} %get-tuple-element.86, f32[12,14,14]{2,1,0:T(8,128)} %get-tuple-element.85, pred[14,14]{1,0:T(8,128)(4,1)S(1)} %gt.18), kind=kLoop, calls=%fused_computation.1 | loop fusion | flops 1380624 | bytes 1862980 | tf_op jit(solution)/shard_map/reduce_sum | solution.py:222
  116.7 13.1 %reshape.673 = f32[12,196,196]{1,2,0:T(8,128)} reshape(f32[12,14,14,14,14]{2,1,4,3,0:T(8,128)} %copy.158) | data formatting | bytes 3687936 | tf_op jit(solution)/shard_map/reshape | solution.py:173
  129.8 2.9 convolution_convert_fusion.1
  139.4 6.1 %collective-permute-done.16 = bf16[196,768]{1,0:T(8,128)(2,1)} collective-permute-done((bf16[196,768]{1,0:T(8,128)(2,1)S(1)}, bf16[196,768]{1,0:T(8,128)(2,1)}, u32[]{:S(2)}, u32[]{:S(2)}) %collective-permute-start.16) | collective-permute-done | bytes 301088 | tf_op jit(solution)/shard_map/ppermute | solution.py:38
  145.5 6.8 %multiply_convert_fusion.1 = (bf16[392,1536]{1,0:T(8,128)(2,1)S(1)}, f32[392,1536]{1,0:T(8,128)S(1)}, f32[392,1536]{1,0:T(8,128)S(1)}) fusion(f32[1536]{0:T(1024)S(1)} %convert_element_type.357, bf16[768,1536]{1,0:T(8,128)(2,1)S(1)} %copy-done, bf16[196,768]{1,0:T(8,128)(2,1)} %collective-permute-done.16, bf16[196,768]{1,0:T(8,128)(2,1)S(1)} %add_convert_fusion.1), kind=kOutput, calls=%fused_computation.24 | convolution fusion | flops 965787648 | bytes 8988672 | tf_op jit(solution)/shard_map/dot_general | solution.py:237
  152.3 2.6 fusion.95
  158.3 2.8 convert_reduce_fusion
  162.2 2.8 fusion.97
  172.6 5.3 %collective-permute-done.19 = bf16[196,768]{1,0:T(8,128)(2,1)S(1)} collective-permute-done((bf16[196,768]{1,0:T(8,128)(2,1)}, bf16[196,768]{1,0:T(8,128)(2,1)S(1)}, u32[]{:S(2)}, u32[]{:S(2)}) %collective-permute-start.19) | collective-permute-done | bytes 301088 | tf_op jit(solution)/shard_map/ppermute | solution.py:38
  178.9 5.4 %collective-permute-done.17 = bf16[196,768]{1,0:T(8,128)(2,1)} collective-permute-done((bf16[196,768]{1,0:T(8,128)(2,1)}, bf16[196,768]{1,0:T(8,128)(2,1)}, u32[]{:S(2)}, u32[]{:S(2)}) %collective-permute-start.17) | collective-permute-done | bytes 301088 | tf_op jit(solution)/shard_map/ppermute | solution.py:38
  184.2 4.5 %convert_reduce_fusion.3 = (f32[768]{0:T(1024)}, bf16[196,768]{1,0:T(8,128)(2,1)S(1)}, f32[196,768]{1,0:T(8,128)}, bf16[196,768]{1,0:T(8,128)(2,1)}) fusion(f32[]{:T(128)} %bitcast, f32[196]{0:T(256)S(1)} %get-tuple-element.93, f32[196,768]{1,0:T(8,128)S(1)} %copy-done.5, f32[196]{0:T(256)S(1)} %broadcast_multiply_fusion.4, f32[196]{0:T(256)S(1)} %get-tuple-element.94, ...), kind=kLoop, calls=%fused_computation.132 | loop fusion | flops 3160320 | bytes 3926088 | tf_op jit(solution)/shard_map/reduce_sum | solution.py:262
  193.2 11.9 %reshape.646 = bf16[12,14,14,14,14]{2,1,4,3,0:T(8,128)(2,1)} reshape(bf16[12,196,196]{1,2,0:T(8,128)(2,1)S(1)} %multiply_convert_fusion) | data formatting | bytes 1843968 | tf_op jit(solution)/shard_map/reshape.60
  206.9 7.9 %fusion.32 = f32[1,14,14,12,64]{4,2,1,3,0:T(8,128)} fusion(bf16[12,14,14,14,14]{2,1,4,3,0:T(8,128)(2,1)} %reshape.646, bf16[1,14,14,1,12,64]{5,4,3,2,1,0:T(8,128)(2,1)} %get-tuple-element.44), kind=kOutput, calls=%fused_computation.57 | convolution fusion | flops 59157504 | bytes 1825152 | tf_op jit(solution)/shard_map/nhabxy,nxyhc->nabhc/dot_general | solution.py:278
  214.8 4.4 %fusion.39 = bf16[1,14,14,1,12,64]{5,2,1,4,3,0:T(8,128)(2,1)} fusion(bf16[12,14,14,14,14]{2,1,4,3,0:T(8,128)(2,1)S(1)} %copy-done.2, bf16[1,14,14,1,12,64]{5,4,3,2,1,0:T(8,128)(2,1)S(1)} %copy-done.13), kind=kOutput, calls=%fused_computation.60 | convolution fusion | flops 59308032 | bytes 1524096 | tf_op jit(solution)/shard_map/nhabxy,nabhc->nxyhc/dot_general | solution.py:283
  222.1 12.8 %reshape.658 = f32[1,12,14,14,14,14]{5,4,3,2,1,0:T(8,128)} reshape(f32[12,196,196]{2,1,0:T(8,128)} %copy.117) | data formatting | bytes 3687936 | tf_op jit(solution)/shard_map/convert_element_type | solution.py:276
  234.9 11.0 %fusion.152 = (f32[12,14,14,14]{3,2,1,0:T(8,128)}, f32[12,14,14,14]{3,2,1,0:T(8,128)}) fusion(f32[1,12,14,14,14,14]{5,4,3,2,1,0:T(8,128)} %reshape.658), kind=kLoop, calls=%fused_computation.305 | loop fusion | flops 856128 | bytes 2107392 | tf_op jit(solution)/shard_map/reduce_sum | solution.py:276
  246.0 2.5 copy.128
  248.5 3.4 fusion.115
  257.7 3.7 fusion.42
  264.3 3.8 convert_element_type.372
  268.1 4.2 %fusion.148 = f32[768,2304]{1,0:T(8,128)} fusion(bf16[196,2304]{1,0:T(8,128)(2,1)S(1)} %convert_element_type.372, bf16[196,768]{1,0:T(8,128)(2,1)S(1)} %copy-done.10, f32[768]{0:T(1024)S(1)} %copy-done.45, f32[768]{0:T(1024)S(1)} %copy-done.43, f32[196]{0:T(256)S(1)} %copy-done.52, f32[196]{0:T(256)S(1)} %copy-done.50), kind=kOutput, calls=%fused_computation.303 | convolution fusion | flops 694536192 | bytes 8289824 | tf_op jit(solution)/shard_map/dot_general | solution.py:303
  275.8 8.1 %pad_maximum_fusion = f32[768,3072]{1,0:T(8,128)} fusion(f32[768,768]{1,0:T(8,128)S(1)} %copy-done.8, f32[768,2304]{1,0:T(8,128)} %fusion.148), kind=kLoop, calls=%fused_computation.8 | loop fusion | flops 2359296 | bytes 18874368 | tf_op jit(solution)/shard_map/concatenate | solution.py:308
  283.9 4.2 %fusion.13 = bf16[4,2,2,24,3072]{4,3,0,1,2:T(8,128)(2,1)} fusion(f32[4,2,2,2,24,3072]{5,4,3,2,1,0:T(8,128)} %bitcast.335, s32[]{:T(128)S(6)} %select_n.313), kind=kLoop, calls=%fused_computation.38 | loop fusion | bytes 4718596 | tf_op jit(solution)/shard_map/convert_element_type | solution.py:86
  289.6 2.7 collective-permute-done.21
  297.6 2.9 collective-permute-start.25
  306.1 2.5 bitcast_add_fusion.1
  310.5 2.4 bitcast_add_fusion.2
  313.5 11.5 %collective-permute-done.43 = bf16[4,48,1536]{2,1,0:T(8,128)(2,1)S(1)} collective-permute-done((bf16[4,48,1536]{2,1,0:T(8,128)(2,1)S(1)}, bf16[4,48,1536]{2,1,0:T(8,128)(2,1)S(1)}, u32[]{:S(2)}, u32[]{:S(2)}) %collective-permute-start.43) | collective-permute-done | bytes 589856 | tf_op jit(solution)/shard_map/ppermute | solution.py:29
  329.4 7.1 %collective-permute-done.38 = bf16[4,48,1536]{2,1,0:T(8,128)(2,1)S(1)} collective-permute-done((bf16[4,48,1536]{2,1,0:T(8,128)(2,1)S(1)}, bf16[4,48,1536]{2,1,0:T(8,128)(2,1)S(1)}, u32[]{:S(2)}, u32[]{:S(2)}) %collective-permute-start.38) | collective-permute-done | bytes 589856 | tf_op jit(solution)/shard_map/ppermute | solution.py:29
  338.0 2.8 collective-permute-start.41
  341.6 2.6 bitcast_add_fusion
  346.6 3.1 collective-permute-done.40
  352.0 6.2 %collective-permute-done.32 = bf16[4,2,24,1536]{3,2,0,1:T(8,128)(2,1)S(1)} collective-permute-done((bf16[4,2,24,1536]{3,2,0,1:T(8,128)(2,1)S(1)}, bf16[4,2,24,1536]{3,2,0,1:T(8,128)(2,1)S(1)}, u32[]{:S(2)}, u32[]{:S(2)}) %collective-permute-start.32) | collective-permute-done | bytes 589856 | tf_op jit(solution)/shard_map/ppermute | solution.py:29
  359.8 6.7 %collective-permute-done.27 = bf16[4,2,24,1536]{3,2,0,1:T(8,128)(2,1)S(1)} collective-permute-done((bf16[4,2,24,1536]{3,2,0,1:T(8,128)(2,1)S(1)}, bf16[4,2,24,1536]{3,2,0,1:T(8,128)(2,1)S(1)}, u32[]{:S(2)}, u32[]{:S(2)}) %collective-permute-start.27) | collective-permute-done | bytes 589856 | tf_op jit(solution)/shard_map/ppermute | solution.py:38
  369.8 4.5 %collective-permute-start.34 = (bf16[24,1536]{1,0:T(8,128)(2,1)S(1)}, bf16[24,1536]{1,0:T(8,128)(2,1)S(1)}, u32[]{:S(2)}, u32[]{:S(2)}) collective-permute-start(bf16[24,1536]{1,0:T(8,128)(2,1)S(1)} %get-tuple-element.63), channel_id=1, source_target_pairs={{0,8},{2,10},{4,12},{6,14},{8,16},{10,18},{12,20},{14,22},{16,24},... | collective-permute-start | bytes 221192 | tf_op jit(solution)/shard_map/ppermute | solution.py:25
  380.7 3.2 collective-permute-done.35
  (357 shorter events, 116.5 us)
Async XLA Ops:
  1.7 16.5 %collective-permute-start = (bf16[24,1536]{1,0:T(8,128)(2,1)S(1)}, bf16[24,1536]{1,0:T(8,128)(2,1)S(1)}, u32[]{:S(2)}, u32[]{:S(2)}) collective-permute-start(bf16[24,1536]{1,0:T(8,128)(2,1)S(1)} %slice.147), channel_id=1, source_target_pairs={{0,24},{2,26},{4,28},{6,30},{8,0},{10,2},{12,4},{14,6},{16,8},{18,... | collective-permute-start | bytes 221192 | tf_op jit(solution)/shard_map/ppermute | solution.py:25
  6.8 11.5 %collective-permute-start.1 = (bf16[24,1536]{1,0:T(8,128)(2,1)S(1)}, bf16[24,1536]{1,0:T(8,128)(2,1)S(1)}, u32[]{:S(2)}, u32[]{:S(2)}) collective-permute-start(bf16[24,1536]{1,0:T(8,128)(2,1)S(1)} %slice.147), channel_id=1, source_target_pairs={{0,16},{2,18},{4,20},{6,22},{8,24},{10,26},{12,28},{14,30},{16,0},... | collective-permute-start | bytes 221192 | tf_op jit(solution)/shard_map/ppermute | solution.py:25
  6.8 11.5 %collective-permute-start.2 = (bf16[24,1536]{1,0:T(8,128)(2,1)S(1)}, bf16[24,1536]{1,0:T(8,128)(2,1)S(1)}, u32[]{:S(2)}, u32[]{:S(2)}) collective-permute-start(bf16[24,1536]{1,0:T(8,128)(2,1)S(1)} %slice.147), channel_id=1, source_target_pairs={{0,8},{2,10},{4,12},{6,14},{8,16},{10,18},{12,20},{14,22},{16,24},... | collective-permute-start | bytes 221192 | tf_op jit(solution)/shard_map/ppermute | solution.py:25
  13.8 176.8 %copy-start.60 = (pred[196]{0:T(512)(128)(4,1)}, pred[196]{0:T(512)(128)(4,1)S(1)}, u32[]{:S(2)}) copy-start(pred[196]{0:T(512)(128)(4,1)S(1)} %compare_reduce_fusion) | copy-start | bytes 592
  19.3 7.1 %collective-permute-start.8 = (bf16[24,1536]{1,0:T(8,128)(2,1)S(1)}, bf16[24,1536]{1,0:T(8,128)(2,1)S(1)}, u32[]{:S(2)}, u32[]{:S(2)}) collective-permute-start(bf16[24,1536]{1,0:T(8,128)(2,1)S(1)} %get-tuple-element.38), channel_id=1, source_target_pairs={{0,24},{2,26},{4,28},{6,30},{8,0},{10,2},{12,4},{14,6},{16,8},{18,... | collective-permute-start | bytes 221192 | tf_op jit(solution)/shard_map/ppermute | solution.py:25
  22.2 11.6 %collective-permute-start.3 = (bf16[4,24,1536]{2,1,0:T(8,128)(2,1)S(1)}, bf16[4,24,1536]{2,1,0:T(8,128)(2,1)S(1)}, u32[]{:S(2)}, u32[]{:S(2)}) collective-permute-start(bf16[4,24,1536]{2,1,0:T(8,128)(2,1)S(1)} %constant_dynamic-slice_fusion.9), channel_id=1, source_target_pairs={{0,1},{1,0},{2,3},{3,2},{4,5},{5,4},{6,7},{7,6},{8,9},{9,8},{10,11... | collective-permute-start | bytes 884744 | tf_op jit(solution)/shard_map/ppermute | solution.py:38
  23.8 11.6 %collective-permute-start.5 = (bf16[4,24,1536]{2,1,0:T(8,128)(2,1)S(1)}, bf16[4,24,1536]{2,1,0:T(8,128)(2,1)S(1)}, u32[]{:S(2)}, u32[]{:S(2)}) collective-permute-start(bf16[4,24,1536]{2,1,0:T(8,128)(2,1)S(1)} %constant_dynamic-slice_fusion.9), channel_id=1, source_target_pairs={{0,4},{2,6},{4,0},{6,2},{8,12},{10,14},{12,8},{14,10},{16,20},{18,... | collective-permute-start | bytes 884744 | tf_op jit(solution)/shard_map/ppermute | solution.py:29
  25.3 5.8 %collective-permute-start.9 = (bf16[24,1536]{1,0:T(8,128)(2,1)S(1)}, bf16[24,1536]{1,0:T(8,128)(2,1)S(1)}, u32[]{:S(2)}, u32[]{:S(2)}) collective-permute-start(bf16[24,1536]{1,0:T(8,128)(2,1)S(1)} %get-tuple-element.38), channel_id=1, source_target_pairs={{0,16},{2,18},{4,20},{6,22},{8,24},{10,26},{12,28},{14,30},{16,0},... | collective-permute-start | bytes 221192 | tf_op jit(solution)/shard_map/ppermute | solution.py:25
  26.4 6.2 %collective-permute-start.10 = (bf16[24,1536]{1,0:T(8,128)(2,1)S(1)}, bf16[24,1536]{1,0:T(8,128)(2,1)S(1)}, u32[]{:S(2)}, u32[]{:S(2)}) collective-permute-start(bf16[24,1536]{1,0:T(8,128)(2,1)S(1)} %get-tuple-element.38), channel_id=1, source_target_pairs={{0,8},{2,10},{4,12},{6,14},{8,16},{10,18},{12,20},{14,22},{16,24},... | collective-permute-start | bytes 221192 | tf_op jit(solution)/shard_map/ppermute | solution.py:25
  32.6 9.5 %collective-permute-start.11 = (bf16[4,24,1536]{2,1,0:T(8,128)(2,1)S(1)}, bf16[4,24,1536]{2,1,0:T(8,128)(2,1)S(1)}, u32[]{:S(2)}, u32[]{:S(2)}) collective-permute-start(bf16[4,24,1536]{2,1,0:T(8,128)(2,1)S(1)} %constant_dynamic-slice_fusion.8), channel_id=1, source_target_pairs={{0,1},{1,0},{2,3},{3,2},{4,5},{5,4},{6,7},{7,6},{8,9},{9,8},{10,11... | collective-permute-start | bytes 884744 | tf_op jit(solution)/shard_map/ppermute | solution.py:38
  33.2 9.1 %collective-permute-start.13 = (bf16[4,24,1536]{2,1,0:T(8,128)(2,1)S(1)}, bf16[4,24,1536]{2,1,0:T(8,128)(2,1)S(1)}, u32[]{:S(2)}, u32[]{:S(2)}) collective-permute-start(bf16[4,24,1536]{2,1,0:T(8,128)(2,1)S(1)} %constant_dynamic-slice_fusion.8), channel_id=1, source_target_pairs={{0,4},{2,6},{4,0},{6,2},{8,12},{10,14},{12,8},{14,10},{16,20},{18,... | collective-permute-start | bytes 884744 | tf_op jit(solution)/shard_map/ppermute | solution.py:29
  33.8 10.2 %collective-permute-start.4 = (bf16[4,24,768]{2,1,0:T(8,128)(2,1)S(1)}, bf16[4,24,768]{2,1,0:T(8,128)(2,1)S(1)}, u32[]{:S(2)}, u32[]{:S(2)}) collective-permute-start(bf16[4,24,768]{2,1,0:T(8,128)(2,1)S(1)} %slice.189), channel_id=1, source_target_pairs={{0,4},{2,6},{4,0},{6,2},{8,12},{10,14},{12,8},{14,10},{16,20},{18,... | collective-permute-start | bytes 442376 | tf_op jit(solution)/shard_map/ppermute | solution.py:29
  35.4 8.7 %collective-permute-start.6 = (bf16[4,24,768]{2,1,0:T(8,128)(2,1)S(1)}, bf16[4,24,768]{2,1,0:T(8,128)(2,1)S(1)}, u32[]{:S(2)}, u32[]{:S(2)}) collective-permute-start(bf16[4,24,768]{2,1,0:T(8,128)(2,1)S(1)} %slice.190), channel_id=1, source_target_pairs={{0,1},{1,0},{2,3},{3,2},{4,5},{5,4},{6,7},{7,6},{8,9},{9,8},{10,11... | collective-permute-start | bytes 442376 | tf_op jit(solution)/shard_map/ppermute | solution.py:38
  42.1 5.2 %collective-permute-start.12 = (bf16[4,24,768]{2,1,0:T(8,128)(2,1)S(1)}, bf16[4,24,768]{2,1,0:T(8,128)(2,1)S(1)}, u32[]{:S(2)}, u32[]{:S(2)}) collective-permute-start(bf16[4,24,768]{2,1,0:T(8,128)(2,1)S(1)} %slice.191), channel_id=1, source_target_pairs={{0,4},{2,6},{4,0},{6,2},{8,12},{10,14},{12,8},{14,10},{16,20},{18,... | collective-permute-start | bytes 442376 | tf_op jit(solution)/shard_map/ppermute | solution.py:29
  42.4 5.2 %collective-permute-start.14 = (bf16[4,24,768]{2,1,0:T(8,128)(2,1)S(1)}, bf16[4,24,768]{2,1,0:T(8,128)(2,1)S(1)}, u32[]{:S(2)}, u32[]{:S(2)}) collective-permute-start(bf16[4,24,768]{2,1,0:T(8,128)(2,1)S(1)} %slice.192), channel_id=1, source_target_pairs={{0,1},{1,0},{2,3},{3,2},{4,5},{5,4},{6,7},{7,6},{8,9},{9,8},{10,11... | collective-permute-start | bytes 442376 | tf_op jit(solution)/shard_map/ppermute | solution.py:38
  44.3 5.1 %collective-permute-start.7 = (bf16[2,2,4,24,1536]{4,3,1,0,2:T(8,128)(2,1)S(1)}, bf16[2,2,4,24,1536]{4,3,1,0,2:T(8,128)(2,1)S(1)}, u32[]{:S(2)}, u32[]{:S(2)}) collective-permute-start(bf16[2,2,4,24,1536]{4,3,1,0,2:T(8,128)(2,1)S(1)} %pad_maximum_fusion.6), channel_id=1, source_target_pairs={{0,2},{2,0},{4,6},{6,4},{8,10},{10,8},{12,14},{14,12},{16,18},{18,... | collective-permute-start | bytes 3538952 | tf_op jit(solution)/shard_map/ppermute | solution.py:33
  47.9 2.9 collective-permute-start.15
  135.2 10.3 %collective-permute-start.16 = (bf16[196,768]{1,0:T(8,128)(2,1)S(1)}, bf16[196,768]{1,0:T(8,128)(2,1)}, u32[]{:S(2)}, u32[]{:S(2)}) collective-permute-start(bf16[196,768]{1,0:T(8,128)(2,1)S(1)} %add_convert_fusion.1), channel_id=1, source_target_pairs={{0,1},{1,0},{2,3},{3,2},{4,5},{5,4},{6,7},{7,6},{8,9},{9,8},{10,11... | collective-permute-start | bytes 903176 | tf_op jit(solution)/shard_map/ppermute | solution.py:38
  138.8 13.5 %collective-permute-start.18 = (bf16[196,768]{1,0:T(8,128)(2,1)}, bf16[196,768]{1,0:T(8,128)(2,1)}, u32[]{:S(2)}, u32[]{:S(2)}) collective-permute-start(bf16[196,768]{1,0:T(8,128)(2,1)} %get-tuple-element.31), channel_id=1, source_target_pairs={{0,1},{1,0},{2,3},{3,2},{4,5},{5,4},{6,7},{7,6},{8,9},{9,8},{10,11... | collective-permute-start | bytes 903176 | tf_op jit(solution)/shard_map/ppermute | solution.py:38
  158.3 147.8 %collective-permute-start.42 = (bf16[4,2,48,1536]{3,2,0,1:T(8,128)(2,1)}, bf16[4,2,48,1536]{3,2,0,1:T(8,128)(2,1)}, u32[]{:S(2)}, u32[]{:S(2)}) collective-permute-start(bf16[4,2,48,1536]{3,2,0,1:T(8,128)(2,1)} %fusion.56), channel_id=1, source_target_pairs={{0,2},{2,0},{4,6},{6,4},{8,10},{10,8},{12,14},{14,12},{16,18},{18,... | collective-permute-start | bytes 3538952 | tf_op jit(solution)/shard_map/ppermute | solution.py:33
  166.4 144.1 %collective-permute-start.37 = (bf16[4,2,48,1536]{3,2,0,1:T(8,128)(2,1)}, bf16[4,2,48,1536]{3,2,0,1:T(8,128)(2,1)}, u32[]{:S(2)}, u32[]{:S(2)}) collective-permute-start(bf16[4,2,48,1536]{3,2,0,1:T(8,128)(2,1)} %fusion.55), channel_id=1, source_target_pairs={{0,2},{2,0},{4,6},{6,4},{8,10},{10,8},{12,14},{14,12},{16,18},{18,... | collective-permute-start | bytes 3538952 | tf_op jit(solution)/shard_map/ppermute | solution.py:33
  167.7 10.3 %collective-permute-start.19 = (bf16[196,768]{1,0:T(8,128)(2,1)}, bf16[196,768]{1,0:T(8,128)(2,1)S(1)}, u32[]{:S(2)}, u32[]{:S(2)}) collective-permute-start(bf16[196,768]{1,0:T(8,128)(2,1)} %slice.257), channel_id=1, source_target_pairs={{0,1},{1,0},{2,3},{3,2},{4,5},{5,4},{6,7},{7,6},{8,9},{9,8},{10,11... | collective-permute-start | bytes 903176 | tf_op jit(solution)/shard_map/ppermute | solution.py:38
  171.4 12.9 %collective-permute-start.17 = (bf16[196,768]{1,0:T(8,128)(2,1)}, bf16[196,768]{1,0:T(8,128)(2,1)}, u32[]{:S(2)}, u32[]{:S(2)}) collective-permute-start(bf16[196,768]{1,0:T(8,128)(2,1)} %slice.258), channel_id=1, source_target_pairs={{0,1},{1,0},{2,3},{3,2},{4,5},{5,4},{6,7},{7,6},{8,9},{9,8},{10,11... | collective-permute-start | bytes 903176 | tf_op jit(solution)/shard_map/ppermute | solution.py:38
  275.7 12.4 %collective-permute-start.20 = (f32[104,128]{1,0:T(8,128)S(1)}, f32[104,128]{1,0:T(8,128)S(1)}, u32[]{:S(2)}, u32[]{:S(2)}) collective-permute-start(f32[104,128]{1,0:T(8,128)S(1)} %pad_bitcast_fusion), channel_id=1, source_target_pairs={{0,2},{2,0},{4,6},{6,4},{8,10},{10,8},{12,14},{14,12},{16,18},{18,... | collective-permute-start | bytes 159752 | tf_op jit(solution)/shard_map/ppermute | solution.py:33
  288.1 4.3 %collective-permute-start.21 = (f32[104,128]{1,0:T(8,128)S(1)}, f32[104,128]{1,0:T(8,128)S(1)}, u32[]{:S(2)}, u32[]{:S(2)}) collective-permute-start(f32[104,128]{1,0:T(8,128)S(1)} %fusion.147), channel_id=1, source_target_pairs={{0,1},{1,0},{2,3},{3,2},{4,5},{5,4},{6,7},{7,6},{8,9},{9,8},{10,11... | collective-permute-start | bytes 159752 | tf_op jit(solution)/shard_map/ppermute | solution.py:38
  292.4 4.2 %collective-permute-start.22 = (f32[104,128]{1,0:T(8,128)S(1)}, f32[104,128]{1,0:T(8,128)S(1)}, u32[]{:S(2)}, u32[]{:S(2)}) collective-permute-start(f32[104,128]{1,0:T(8,128)S(1)} %fusion.185), channel_id=1, source_target_pairs={{0,4},{2,6},{4,0},{6,2},{8,12},{10,14},{12,8},{14,10},{16,20},{18,... | collective-permute-start | bytes 159752 | tf_op jit(solution)/shard_map/ppermute | solution.py:29
  296.6 6.1 %collective-permute-start.23 = (f32[104,128]{1,0:T(8,128)S(1)}, f32[104,128]{1,0:T(8,128)S(1)}, u32[]{:S(2)}, u32[]{:S(2)}) collective-permute-start(f32[104,128]{1,0:T(8,128)S(1)} %add.411), channel_id=1, source_target_pairs={{0,8},{2,10},{4,12},{6,14},{8,16},{10,18},{12,20},{14,22},{16,24},... | collective-permute-start | bytes 159752 | tf_op jit(solution)/shard_map/ppermute | solution.py:25
  296.7 6.8 %collective-permute-start.24 = (f32[104,128]{1,0:T(8,128)S(1)}, f32[104,128]{1,0:T(8,128)S(1)}, u32[]{:S(2)}, u32[]{:S(2)}) collective-permute-start(f32[104,128]{1,0:T(8,128)S(1)} %add.411), channel_id=1, source_target_pairs={{0,16},{2,18},{4,20},{6,22},{8,24},{10,26},{12,28},{14,30},{16,0},... | collective-permute-start | bytes 159752 | tf_op jit(solution)/shard_map/ppermute | solution.py:25
  297.6 5.9 %collective-permute-start.25 = (f32[104,128]{1,0:T(8,128)S(1)}, f32[104,128]{1,0:T(8,128)S(1)}, u32[]{:S(2)}, u32[]{:S(2)}) collective-permute-start(f32[104,128]{1,0:T(8,128)S(1)} %add.411), channel_id=1, source_target_pairs={{0,24},{2,26},{4,28},{6,30},{8,0},{10,2},{12,4},{14,6},{16,8},{18,... | collective-permute-start | bytes 159752 | tf_op jit(solution)/shard_map/ppermute | solution.py:25
  302.7 38.9 %collective-permute-start.26 = (bf16[4,2,2,24,3072]{4,3,0,1,2:T(8,128)(2,1)}, bf16[4,2,2,24,3072]{4,3,0,1,2:T(8,128)(2,1)}, u32[]{:S(2)}, u32[]{:S(2)}) collective-permute-start(bf16[4,2,2,24,3072]{4,3,0,1,2:T(8,128)(2,1)} %fusion.13), channel_id=1, source_target_pairs={{0,2},{2,0},{4,6},{6,4},{8,10},{10,8},{12,14},{14,12},{16,18},{18,... | collective-permute-start | bytes 7077896 | tf_op jit(solution)/shard_map/ppermute | solution.py:33
  308.6 16.3 %collective-permute-start.43 = (bf16[4,48,1536]{2,1,0:T(8,128)(2,1)S(1)}, bf16[4,48,1536]{2,1,0:T(8,128)(2,1)S(1)}, u32[]{:S(2)}, u32[]{:S(2)}) collective-permute-start(bf16[4,48,1536]{2,1,0:T(8,128)(2,1)S(1)} %fusion.86), channel_id=1, source_target_pairs={{0,4},{2,6},{4,0},{6,2},{8,12},{10,14},{12,8},{14,10},{16,20},{18,... | collective-permute-start | bytes 1769480 | tf_op jit(solution)/shard_map/ppermute | solution.py:29
  313.0 23.5 %collective-permute-start.38 = (bf16[4,48,1536]{2,1,0:T(8,128)(2,1)S(1)}, bf16[4,48,1536]{2,1,0:T(8,128)(2,1)S(1)}, u32[]{:S(2)}, u32[]{:S(2)}) collective-permute-start(bf16[4,48,1536]{2,1,0:T(8,128)(2,1)S(1)} %fusion.85), channel_id=1, source_target_pairs={{0,4},{2,6},{4,0},{6,2},{8,12},{10,14},{12,8},{14,10},{16,20},{18,... | collective-permute-start | bytes 1769480 | tf_op jit(solution)/shard_map/ppermute | solution.py:29
  325.1 12.1 %collective-permute-start.44 = (bf16[48,1536]{1,0:T(8,128)(2,1)S(1)}, bf16[48,1536]{1,0:T(8,128)(2,1)S(1)}, u32[]{:S(2)}, u32[]{:S(2)}) collective-permute-start(bf16[48,1536]{1,0:T(8,128)(2,1)S(1)} %get-tuple-element.49), channel_id=1, source_target_pairs={{0,8},{2,10},{4,12},{6,14},{8,16},{10,18},{12,20},{14,22},{16,24},... | collective-permute-start | bytes 442376 | tf_op jit(solution)/shard_map/ppermute | solution.py:25
  326.9 11.0 %collective-permute-start.45 = (bf16[48,1536]{1,0:T(8,128)(2,1)S(1)}, bf16[48,1536]{1,0:T(8,128)(2,1)S(1)}, u32[]{:S(2)}, u32[]{:S(2)}) collective-permute-start(bf16[48,1536]{1,0:T(8,128)(2,1)S(1)} %get-tuple-element.51), channel_id=1, source_target_pairs={{0,16},{2,18},{4,20},{6,22},{8,24},{10,26},{12,28},{14,30},{16,0},... | collective-permute-start | bytes 442376 | tf_op jit(solution)/shard_map/ppermute | solution.py:25
  328.7 12.1 %collective-permute-start.46 = (bf16[48,1536]{1,0:T(8,128)(2,1)S(1)}, bf16[48,1536]{1,0:T(8,128)(2,1)S(1)}, u32[]{:S(2)}, u32[]{:S(2)}) collective-permute-start(bf16[48,1536]{1,0:T(8,128)(2,1)S(1)} %get-tuple-element.50), channel_id=1, source_target_pairs={{0,24},{2,26},{4,28},{6,30},{8,0},{10,2},{12,4},{14,6},{16,8},{18,... | collective-permute-start | bytes 442376 | tf_op jit(solution)/shard_map/ppermute | solution.py:25
  336.7 9.9 %collective-permute-start.39 = (bf16[48,1536]{1,0:T(8,128)(2,1)S(1)}, bf16[48,1536]{1,0:T(8,128)(2,1)S(1)}, u32[]{:S(2)}, u32[]{:S(2)}) collective-permute-start(bf16[48,1536]{1,0:T(8,128)(2,1)S(1)} %get-tuple-element.52), channel_id=1, source_target_pairs={{0,8},{2,10},{4,12},{6,14},{8,16},{10,18},{12,20},{14,22},{16,24},... | collective-permute-start | bytes 442376 | tf_op jit(solution)/shard_map/ppermute | solution.py:25
  337.3 12.5 %collective-permute-start.40 = (bf16[48,1536]{1,0:T(8,128)(2,1)S(1)}, bf16[48,1536]{1,0:T(8,128)(2,1)S(1)}, u32[]{:S(2)}, u32[]{:S(2)}) collective-permute-start(bf16[48,1536]{1,0:T(8,128)(2,1)S(1)} %get-tuple-element.54), channel_id=1, source_target_pairs={{0,16},{2,18},{4,20},{6,22},{8,24},{10,26},{12,28},{14,30},{16,0},... | collective-permute-start | bytes 442376 | tf_op jit(solution)/shard_map/ppermute | solution.py:25
  338.0 11.7 %collective-permute-start.41 = (bf16[48,1536]{1,0:T(8,128)(2,1)S(1)}, bf16[48,1536]{1,0:T(8,128)(2,1)S(1)}, u32[]{:S(2)}, u32[]{:S(2)}) collective-permute-start(bf16[48,1536]{1,0:T(8,128)(2,1)S(1)} %get-tuple-element.53), channel_id=1, source_target_pairs={{0,24},{2,26},{4,28},{6,30},{8,0},{10,2},{12,4},{14,6},{16,8},{18,... | collective-permute-start | bytes 442376 | tf_op jit(solution)/shard_map/ppermute | solution.py:25
  344.7 13.5 %collective-permute-start.32 = (bf16[4,2,24,1536]{3,2,0,1:T(8,128)(2,1)S(1)}, bf16[4,2,24,1536]{3,2,0,1:T(8,128)(2,1)S(1)}, u32[]{:S(2)}, u32[]{:S(2)}) collective-permute-start(bf16[4,2,24,1536]{3,2,0,1:T(8,128)(2,1)S(1)} %fusion.84), channel_id=1, source_target_pairs={{0,4},{2,6},{4,0},{6,2},{8,12},{10,14},{12,8},{14,10},{16,20},{18,... | collective-permute-start | bytes 1769480 | tf_op jit(solution)/shard_map/ppermute | solution.py:29
  350.6 15.9 %collective-permute-start.27 = (bf16[4,2,24,1536]{3,2,0,1:T(8,128)(2,1)S(1)}, bf16[4,2,24,1536]{3,2,0,1:T(8,128)(2,1)S(1)}, u32[]{:S(2)}, u32[]{:S(2)}) collective-permute-start(bf16[4,2,24,1536]{3,2,0,1:T(8,128)(2,1)S(1)} %fusion.83), channel_id=1, source_target_pairs={{0,1},{1,0},{2,3},{3,2},{4,5},{5,4},{6,7},{7,6},{8,9},{9,8},{10,11... | collective-permute-start | bytes 1769480 | tf_op jit(solution)/shard_map/ppermute | solution.py:38
  358.4 11.3 %collective-permute-start.33 = (bf16[4,24,1536]{2,1,0:T(8,128)(2,1)S(1)}, bf16[4,24,1536]{2,1,0:T(8,128)(2,1)S(1)}, u32[]{:S(2)}, u32[]{:S(2)}) collective-permute-start(bf16[4,24,1536]{2,1,0:T(8,128)(2,1)S(1)} %fusion.99), channel_id=1, source_target_pairs={{0,1},{1,0},{2,3},{3,2},{4,5},{5,4},{6,7},{7,6},{8,9},{9,8},{10,11... | collective-permute-start | bytes 884744 | tf_op jit(solution)/shard_map/ppermute | solution.py:38
  366.7 10.0 %collective-permute-start.28 = (bf16[4,24,1536]{2,1,0:T(8,128)(2,1)S(1)}, bf16[4,24,1536]{2,1,0:T(8,128)(2,1)S(1)}, u32[]{:S(2)}, u32[]{:S(2)}) collective-permute-start(bf16[4,24,1536]{2,1,0:T(8,128)(2,1)S(1)} %fusion.98), channel_id=1, source_target_pairs={{0,4},{2,6},{4,0},{6,2},{8,12},{10,14},{12,8},{14,10},{16,20},{18,... | collective-permute-start | bytes 884744 | tf_op jit(solution)/shard_map/ppermute | solution.py:29
  369.8 9.6 %collective-permute-start.34 = (bf16[24,1536]{1,0:T(8,128)(2,1)S(1)}, bf16[24,1536]{1,0:T(8,128)(2,1)S(1)}, u32[]{:S(2)}, u32[]{:S(2)}) collective-permute-start(bf16[24,1536]{1,0:T(8,128)(2,1)S(1)} %get-tuple-element.63), channel_id=1, source_target_pairs={{0,8},{2,10},{4,12},{6,14},{8,16},{10,18},{12,20},{14,22},{16,24},... | collective-permute-start | bytes 221192 | tf_op jit(solution)/shard_map/ppermute | solution.py:25
  374.2 9.7 %collective-permute-start.35 = (bf16[24,1536]{1,0:T(8,128)(2,1)S(1)}, bf16[24,1536]{1,0:T(8,128)(2,1)S(1)}, u32[]{:S(2)}, u32[]{:S(2)}) collective-permute-start(bf16[24,1536]{1,0:T(8,128)(2,1)S(1)} %get-tuple-element.65), channel_id=1, source_target_pairs={{0,16},{2,18},{4,20},{6,22},{8,24},{10,26},{12,28},{14,30},{16,0},... | collective-permute-start | bytes 221192 | tf_op jit(solution)/shard_map/ppermute | solution.py:25
  374.8 9.1 %collective-permute-start.36 = (bf16[24,1536]{1,0:T(8,128)(2,1)S(1)}, bf16[24,1536]{1,0:T(8,128)(2,1)S(1)}, u32[]{:S(2)}, u32[]{:S(2)}) collective-permute-start(bf16[24,1536]{1,0:T(8,128)(2,1)S(1)} %get-tuple-element.64), channel_id=1, source_target_pairs={{0,24},{2,26},{4,28},{6,30},{8,0},{10,2},{12,4},{14,6},{16,8},{18,... | collective-permute-start | bytes 221192 | tf_op jit(solution)/shard_map/ppermute | solution.py:25
  376.8 7.8 %collective-permute-start.29 = (bf16[24,1536]{1,0:T(8,128)(2,1)S(1)}, bf16[24,1536]{1,0:T(8,128)(2,1)S(1)}, u32[]{:S(2)}, u32[]{:S(2)}) collective-permute-start(bf16[24,1536]{1,0:T(8,128)(2,1)S(1)} %get-tuple-element.60), channel_id=1, source_target_pairs={{0,8},{2,10},{4,12},{6,14},{8,16},{10,18},{12,20},{14,22},{16,24},... | collective-permute-start | bytes 221192 | tf_op jit(solution)/shard_map/ppermute | solution.py:25
  377.0 9.5 %collective-permute-start.30 = (bf16[24,1536]{1,0:T(8,128)(2,1)S(1)}, bf16[24,1536]{1,0:T(8,128)(2,1)S(1)}, u32[]{:S(2)}, u32[]{:S(2)}) collective-permute-start(bf16[24,1536]{1,0:T(8,128)(2,1)S(1)} %get-tuple-element.62), channel_id=1, source_target_pairs={{0,16},{2,18},{4,20},{6,22},{8,24},{10,26},{12,28},{14,30},{16,0},... | collective-permute-start | bytes 221192 | tf_op jit(solution)/shard_map/ppermute | solution.py:25
  379.4 7.2 %collective-permute-start.31 = (bf16[24,1536]{1,0:T(8,128)(2,1)S(1)}, bf16[24,1536]{1,0:T(8,128)(2,1)S(1)}, u32[]{:S(2)}, u32[]{:S(2)}) collective-permute-start(bf16[24,1536]{1,0:T(8,128)(2,1)S(1)} %get-tuple-element.61), channel_id=1, source_target_pairs={{0,24},{2,26},{4,28},{6,30},{8,0},{10,2},{12,4},{14,6},{16,8},{18,... | collective-permute-start | bytes 221192 | tf_op jit(solution)/shard_map/ppermute | solution.py:25
  (65 other events, 774.6 us)

commit v2 on v1

v2 whole, which is shorter than its diff:
```python
from functools import partial

import jax
import jax.numpy as jnp
from jax import lax
from jax.experimental import pallas as pl
from jax.experimental.pallas import tpu as pltpu
from jax.sharding import PartitionSpec as P

D = 768
HEADS = 12
HEAD = 64
WIN = 14
ROW = 16
R = WIN * ROW
PAIRS = HEADS // 2
LANES = 128
F32 = jnp.float32
BF16 = jnp.bfloat16
VMEM = pl.BlockSpec(memory_space=pltpu.VMEM)
SMEM = pl.BlockSpec(memory_space=pltpu.SMEM)
LIMIT = 56 * 2**20


def dp_pairs(count, dz=0, dy=0, dc=0):
    depth = count // 4
    pairs = []
    for place in range(count):
        z, y, c = place // 4, place // 2 % 2, place % 2
        pairs.append((place, (z + dz) % depth * 4 + (y + dy) % 2 * 2 + (c + dc) % 2))
    return pairs


def move_z(value, step):
    count = lax.axis_size("dp")
    return lax.ppermute(value, "dp", dp_pairs(count, dz=step))


def move_y(value, step=1):
    return lax.ppermute(value, "dp", dp_pairs(lax.axis_size("dp"), dy=step))


def move_c(value, step=1):
    return lax.ppermute(value, "dp", dp_pairs(lax.axis_size("dp"), dc=step))


def move_x(value, step=1):
    count = lax.axis_size("mp")
    return lax.ppermute(value, "mp", [(i, (i + step) % count) for i in range(count)])


def pick(value, index, axis):
    return lax.dynamic_index_in_dim(value, index, axis, keepdims=False)


def in_order(blocks, index):
    count = len(blocks)
    if count == 2:
        first, second = blocks
        swap = index == 1
        return jnp.stack([jnp.where(swap, second, first), jnp.where(swap, first, second)])
    twice = jnp.stack([blocks[-j % count] for j in range(count)] * 2)
    return lax.dynamic_slice_in_dim(twice, count - index, count, axis=0)


def places():
    dp = lax.axis_index("dp")
    return dp // 4, dp // 2 % 2, dp % 2, lax.axis_index("mp")


def gather_rows(shard, chunks):
    z, y, c, x = places()
    depth, wide = lax.axis_size("dp") // 4, lax.axis_size("mp")
    rows, columns = shard.shape
    width = columns // chunks
    lines = []
    for k in range(chunks):
        part = shard[:, k * width : (k + 1) * width]
        lines.append(in_order([part] + [move_z(part, s) for s in range(1, depth)], z))
    outs = []
    for line in lines:
        half = width // 2
        along_x = [line] + [move_x(line, s) for s in range(1, wide)]
        along_y = move_y(line)
        left = [move_y(b[..., :half]) for b in along_x[1:]]
        right = [move_x(along_y[..., half:], s) for s in range(1, wide)]
        far = [along_y] + [jnp.concatenate([p, q], -1) for p, q in zip(left, right)]
        both = in_order([in_order(along_x, x), in_order(far, x)], y)
        both = in_order([both, move_c(both)], c)
        outs.append(both.transpose(3, 1, 0, 2, 4, 5).reshape(-1, width))
    return jnp.concatenate(outs, -1)


def scatter_axis(value, axis, size, index, move):
    total = pick(value, index, axis).astype(F32)
    for step in range(1, size):
        block = pick(value, (index + step) % size, axis).astype(BF16)
        total = total + move(block, step).astype(F32)
    return total


def scatter_all(keep, send):
    z, y, _, x = places()
    depth, wide = lax.axis_size("dp") // 4, lax.axis_size("mp")
    columns = keep.shape[1]
    blocks = keep.astype(F32) + move_c(send).astype(F32)
    blocks = blocks.reshape(depth, 2, wide, -1, columns)
    half = columns // 2
    first, second = blocks[..., :half], blocks[..., half:]
    first = scatter_axis(first, 2, wide, x, move_x)
    second = scatter_axis(second, 1, 2, y, move_y)
    first = scatter_axis(first, 1, 2, y, move_y)
    second = scatter_axis(second, 1, wide, x, move_x)
    first = scatter_axis(first, 0, depth, z, move_z)
    second = scatter_axis(second, 0, depth, z, move_z)
    return jnp.concatenate([first, second], -1)


def scatter_dp(keep, send):
    z, y, _, _ = places()
    depth = lax.axis_size("dp") // 4
    blocks = keep.astype(F32) + move_c(send).astype(F32)
    blocks = blocks.reshape(depth, 2, -1, keep.shape[1])
    blocks = scatter_axis(blocks, 1, 2, y, move_y)
    return scatter_axis(blocks, 0, depth, z, move_z)


def sum_all(parts):
    depth, wide = lax.axis_size("dp") // 4, lax.axis_size("mp")
    flat = jnp.concatenate([p.reshape(-1) for p in parts])
    size = flat.shape[0]
    flat = jnp.pad(flat, (0, -size % 1024)).reshape(-1, 128)
    flat = flat + move_c(flat)
    flat = sum([move_x(flat, s) for s in range(1, wide)], flat)
    flat = flat + move_y(flat)
    flat = sum([move_z(flat, s) for s in range(1, depth)], flat)
    flat = flat.reshape(-1)
    outs, at = [], 0
    for p in parts:
        outs.append(flat[at : at + p.size].reshape(p.shape))
        at += p.size
    return outs


def dot_nn(a, b):
    return lax.dot_general(a, b, (((1,), (0,)), ((), ())), preferred_element_type=F32)


def dot_nt(a, b):
    return lax.dot_general(a, b, (((1,), (1,)), ((), ())), preferred_element_type=F32)


def dot_tn(a, b):
    return lax.dot_general(a, b, (((0,), (0,)), ((), ())), preferred_element_type=F32)


def norm_parts(rows_in):
    center = rows_in - jnp.mean(rows_in, axis=-1, keepdims=True)
    factor = lax.rsqrt(jnp.mean(center * center, axis=-1, keepdims=True) + 1e-06)
    return center * factor, factor


def norm_back(grad, unit, factor, gain):
    inner = grad * gain
    return factor * (
        inner
        - jnp.mean(inner, axis=-1, keepdims=True)
        - unit * jnp.mean(inner * unit, axis=-1, keepdims=True)
    )


def lane_ids():
    return lax.broadcasted_iota(jnp.int32, (R, LANES), 1)


def row_masks():
    lane = lane_ids() % HEAD
    key = lax.broadcasted_iota(jnp.int32, (R, LANES), 0)
    spot = lane % ROW
    part = lane // ROW % 2
    here = jnp.where(part == 0, key // ROW, key % ROW)
    return (spot == here).astype(F32)


def query_offsets(table, base):
    lane = lax.broadcasted_iota(jnp.int32, (ROW, LANES), 1)
    in_h = (lane >= base) & (lane < base + ROW)
    in_w = (lane >= base + ROW) & (lane < base + 2 * ROW)
    outs = []
    for a in range(WIN):
        group = table[a * ROW : (a + 1) * ROW]
        at_h = pltpu.roll(group, (base - 13 + a) % LANES, 1)
        at_w = pltpu.roll(group, (base + ROW - HEAD - 13) % LANES, 1, stride=1, stride_axis=0)
        both = jnp.where(in_h, at_h, jnp.where(in_w, at_w, 0.0))
        high = both.astype(BF16).astype(F32)
        outs.append(high + pltpu.roll(both - high, 2 * ROW, 1))
    return jnp.concatenate(outs, axis=0)


def offset_grads(grad, base):
    lane = lax.broadcasted_iota(jnp.int32, (ROW, LANES), 1)
    in_h = (lane >= base) & (lane < base + ROW)
    in_w = (lane >= base + ROW) & (lane < base + 2 * ROW)
    outs = []
    for a in range(WIN):
        group = grad[a * ROW : (a + 1) * ROW]
        from_h = pltpu.roll(jnp.where(in_h, group, 0.0), (13 - a - base) % LANES, 1)
        flipped = jnp.where(in_w, group, 0.0)
        from_w = jnp.concatenate(
            [
                pltpu.roll(flipped[b : b + 1], (HEAD + 13 - b - base - ROW) % LANES, 1)
                for b in range(ROW)
            ],
            axis=0,
        )
        outs.append(from_h + from_w)
    return jnp.concatenate(outs, axis=0)


def augmented(q2, k2, tables, ones):
    lane = lane_ids()
    left = lane < HEAD
    q2 = q2.astype(F32)
    k2 = k2.astype(F32)
    products = dot_nn(q2.astype(BF16), tables)
    heads = []
    for side in range(2):
        offsets = query_offsets(products[:, side * LANES : (side + 1) * LANES], HEAD * (1 - side))
        mine = left if side == 0 else ~left
        heads.append(
            (
                jnp.where(mine, q2 * HEAD**-0.5, offsets).astype(BF16),
                jnp.where(mine, k2, ones).astype(BF16),
            )
        )
    return heads


def attend_kernel(
    x_ref, w_ref, gain1_ref, bias1_ref, qkvb_ref, table_ref, projb_ref, gain2_ref, bias2_ref, fill_ref, keep_ref,
    a1_ref, qkv_ref, p_ref, o_ref, mid_ref, a2_ref,
):
    x = x_ref[...].astype(F32)
    unit, _ = norm_parts(x)
    a1 = (unit * gain1_ref[...] + bias1_ref[...]).astype(BF16)
    a1_ref[...] = a1
    qkv_ref[...] = (dot_nn(a1, w_ref[:, : 3 * D]) + qkvb_ref[...]).astype(BF16)
    ones = row_masks()
    left = lane_ids() < HEAD
    fill = fill_ref[...]
    for pair in range(PAIRS):
        at = pair * LANES
        q2 = qkv_ref[:, at : at + LANES]
        k2 = qkv_ref[:, D + at : D + at + LANES]
        v2 = qkv_ref[:, 2 * D + at : 2 * D + at + LANES]
        outs = []
        for side, (q_aug, k_aug) in enumerate(augmented(q2, k2, table_ref[...], ones)):
            scores = dot_nt(q_aug, k_aug)
            scores = jnp.where(fill < 0.0, fill, scores)
            expo = jnp.exp(scores - jnp.max(scores, axis=-1, keepdims=True))
            probs = (expo / jnp.sum(expo, axis=-1, keepdims=True)).astype(BF16)
            p_ref[2 * pair + side] = probs
            outs.append(dot_nn(probs, v2))
        o_ref[:, at : at + LANES] = jnp.where(left, outs[0], outs[1]).astype(BF16)
    branch = dot_nn(o_ref[...], w_ref[:, 3 * D :]) + projb_ref[...]
    middle = x + keep_ref[0] * branch
    mid_ref[...] = middle
    unit, _ = norm_parts(middle)
    a2_ref[...] = (unit * gain2_ref[...] + bias2_ref[...]).astype(BF16)


def attend(*args):
    shape = jax.ShapeDtypeStruct
    return pl.pallas_call(
        attend_kernel,
        in_specs=[VMEM] * 10 + [SMEM],
        out_specs=[VMEM] * 6,
        out_shape=[
            shape((R, D), BF16),
            shape((R, 3 * D), BF16),
            shape((HEADS, R, R), BF16),
            shape((R, D), BF16),
            shape((R, D), F32),
            shape((R, D), BF16),
        ],
        compiler_params=pltpu.CompilerParams(vmem_limit_bytes=LIMIT),
        cost_estimate=pl.CostEstimate(flops=2 * R * D * 4 * D, bytes_accessed=12 * 2**20, transcendentals=HEADS * R * R),
    )(*args)


def attend_back_kernel(
    own_ref, got_ref, mid_ref, grad_ref, x_ref, w_ref, qkv_ref, p_ref, table_ref, gain1_ref, gain2_ref, keep_ref,
    dy_ref, dqkv_ref, dx_ref, gain1_out, bias1_out, qkvb_out, table_out, projb_out, gain2_out, bias2_out,
    do_ref,
):
    da2 = own_ref[...] + got_ref[...]
    unit, factor = norm_parts(mid_ref[...])
    gain2_out[...] = jnp.sum(da2 * unit, axis=0, keepdims=True)
    bias2_out[...] = jnp.sum(da2, axis=0, keepdims=True)
    dmid = grad_ref[...].astype(F32) + norm_back(da2, unit, factor, gain2_ref[...])
    dy = (keep_ref[0] * dmid).astype(BF16)
    dy_ref[...] = dy
    projb_out[...] = jnp.sum(dy.astype(F32), axis=0, keepdims=True)
    do_ref[...] = dot_nt(dy, w_ref[:, 3 * D :]).astype(BF16)
    ones = row_masks()
    left = lane_ids() < HEAD
    tables = table_ref[...]
    table_grad = jnp.zeros((LANES, 2 * LANES), F32)
    for pair in range(PAIRS):
        at = pair * LANES
        q2 = qkv_ref[:, at : at + LANES].astype(F32)
        k2 = qkv_ref[:, D + at : D + at + LANES].astype(F32)
        v2 = qkv_ref[:, 2 * D + at : 2 * D + at + LANES]
        do2 = do_ref[:, at : at + LANES].astype(F32)
        dq2 = jnp.zeros((R, LANES), F32)
        dk2 = jnp.zeros((R, LANES), F32)
        dv2 = jnp.zeros((R, LANES), F32)
        offsets = []
        for side in range(2):
            mine = left if side == 0 else ~left
            probs = p_ref[2 * pair + side]
            do_mine = jnp.where(mine, do2, 0.0).astype(BF16)
            dv2 = dv2 + dot_tn(probs, do_mine)
            dp = dot_nt(do_mine, v2)
            wide = probs.astype(F32)
            ds = (wide * (dp - jnp.sum(wide * dp, axis=-1, keepdims=True))).astype(BF16)
            k_aug = jnp.where(mine, k2, ones).astype(BF16)
            dq_aug = dot_nn(ds, k_aug)
            dq2 = jnp.where(mine, dq_aug, dq2)
            offsets.append(offset_grads(dq_aug, HEAD * (1 - side)))
            dk2 = dk2 + dot_tn(ds, jnp.where(mine, q2, 0.0).astype(BF16))
        spread = jnp.concatenate(offsets, axis=1).astype(BF16)
        dq2 = dq2 * HEAD**-0.5 + dot_nt(spread, tables)
        table_grad = table_grad + dot_tn(q2.astype(BF16), spread)
        dqkv_ref[:, at : at + LANES] = dq2.astype(BF16)
        dqkv_ref[:, D + at : D + at + LANES] = (dk2 * HEAD**-0.5).astype(BF16)
        dqkv_ref[:, 2 * D + at : 2 * D + at + LANES] = dv2.astype(BF16)
    table_out[...] = table_grad
    qkvb_out[...] = jnp.sum(dqkv_ref[...].astype(F32), axis=0, keepdims=True)
    da1 = dot_nt(dqkv_ref[...], w_ref[:, : 3 * D])
    unit, factor = norm_parts(x_ref[...].astype(F32))
    gain1_out[...] = jnp.sum(da1 * unit, axis=0, keepdims=True)
    bias1_out[...] = jnp.sum(da1, axis=0, keepdims=True)
    dx_ref[...] = (dmid + norm_back(da1, unit, factor, gain1_ref[...])).astype(BF16)


def attend_back(*args):
    shape = jax.ShapeDtypeStruct
    return pl.pallas_call(
        attend_back_kernel,
        in_specs=[VMEM] * 11 + [SMEM],
        out_specs=[VMEM] * 10,
        out_shape=[
            shape((R, D), BF16),
            shape((R, 3 * D), BF16),
            shape((R, D), BF16),
            shape((1, D), F32),
            shape((1, D), F32),
            shape((1, 3 * D), F32),
            shape((LANES, 2 * LANES), F32),
            shape((1, D), F32),
            shape((1, D), F32),
            shape((1, D), F32),
        ],
        scratch_shapes=[pltpu.VMEM((R, D), BF16)],
        compiler_params=pltpu.CompilerParams(vmem_limit_bytes=LIMIT),
        cost_estimate=pl.CostEstimate(flops=2 * R * D * 6 * D, bytes_accessed=14 * 2**20, transcendentals=0),
    )(*args)


def feed_kernel(a2_ref, up_ref, upb_ref, gact_ref, g_ref, dh_ref, da2_ref, acc_ref):
    step = pl.program_id(0)
    hidden = dot_nn(a2_ref[...], up_ref[...]) + upb_ref[...]
    phi = 0.5 + 0.5 * lax.erf(hidden * 0.5**0.5)
    g_ref[...] = (hidden * phi).astype(BF16)
    slope = phi + hidden * (jnp.exp(-0.5 * hidden * hidden) * 0.3989422804014327)
    dh = (gact_ref[...] * slope).astype(BF16)
    dh_ref[...] = dh
    part = dot_nt(dh, up_ref[...])

    @pl.when(step == 0)
    def _():
        acc_ref[...] = part

    @pl.when(step > 0)
    def _():
        acc_ref[...] += part

    @pl.when(step == pl.num_programs(0) - 1)
    def _():
        da2_ref[...] = acc_ref[...].astype(da2_ref.dtype)


def feed(a2, up, upb, gact, kind):
    hidden = up.shape[1]
    width = 384
    shape = jax.ShapeDtypeStruct
    return pl.pallas_call(
        feed_kernel,
        grid=(hidden // width,),
        in_specs=[
            pl.BlockSpec((R, D), lambda i: (0, 0)),
            pl.BlockSpec((D, width), lambda i: (0, i)),
            pl.BlockSpec((1, width), lambda i: (0, i)),
            pl.BlockSpec((R, width), lambda i: (0, i)),
        ],
        out_specs=[
            pl.BlockSpec((R, width), lambda i: (0, i)),
            pl.BlockSpec((R, width), lambda i: (0, i)),
            pl.BlockSpec((R, D), lambda i: (0, 0)),
        ],
        out_shape=[shape((R, hidden), BF16), shape((R, hidden), BF16), shape((R, D), kind)],
        scratch_shapes=[pltpu.VMEM((R, D), F32)],
        compiler_params=pltpu.CompilerParams(vmem_limit_bytes=LIMIT),
        cost_estimate=pl.CostEstimate(flops=4 * R * D * hidden, bytes_accessed=6 * 2**20, transcendentals=2 * R * hidden),
    )(a2, up, upb, gact)


def weights_kernel(count, core_ref, *refs):
    lefts, rights = refs[:count], refs[count : 2 * count]
    keep_ref, send_ref = refs[2 * count : 2 * count + 2]
    sides = refs[2 * count + 2 :]
    core = core_ref[0]
    rows = keep_ref.shape[0]
    block = rows // (D // 96)

    @pl.when(pl.program_id(0) == 0)
    def _():
        for j in range(count):
            turned = lefts[j][...].astype(F32).T.astype(BF16)
            sides[2 * count][...] = turned
            for k in range(D // 96):
                for s in range(2):
                    which = core if s == 0 else 1 - core
                    start = pl.multiple_of(k * 96 + which * 48, 48)
                    sides[2 * j + s][k * block : (k + 1) * block, :] = sides[2 * count][pl.ds(start, 48), :]

    for s, out in enumerate((keep_ref, send_ref)):
        total = dot_nn(sides[s][...], rights[0][...])
        for j in range(1, count):
            total = total + dot_nn(sides[2 * j + s][...], rights[j][...])
        out[...] = total.astype(BF16)


def weight_grads(core, lefts, rights, width):
    count = len(lefts)
    columns = rights[0].shape[1]
    shape = jax.ShapeDtypeStruct
    half = D // 2
    return pl.pallas_call(
        partial(weights_kernel, count),
        grid=(columns // width,),
        in_specs=[SMEM]
        + [pl.BlockSpec((R, D), lambda i: (0, 0))] * count
        + [pl.BlockSpec((R, width), lambda i: (0, i))] * count,
        out_specs=[pl.BlockSpec((half, width), lambda i: (0, i))] * 2,
        out_shape=[shape((half, columns), BF16)] * 2,
        scratch_shapes=[pltpu.VMEM((half, R), BF16)] * (2 * count) + [pltpu.VMEM((D, R), BF16)],
        compiler_params=pltpu.CompilerParams(vmem_limit_bytes=LIMIT),
        cost_estimate=pl.CostEstimate(
            flops=2 * count * R * D * columns, bytes_accessed=6 * 2**20, transcendentals=0
        ),
    )(core, *lefts, *rights)


def pad_rows(rows):
    rows = rows.reshape(WIN, WIN, rows.shape[-1])
    return jnp.pad(rows, ((0, 0), (0, ROW - WIN), (0, 0))).reshape(R, -1)


def cut_rows(rows):
    return rows.reshape(WIN, ROW, -1)[:, :WIN].reshape(WIN * WIN, -1)


def per_device(
    tokens, ln1_gain, ln1_bias, qkv_weight, qv_bias, rel_pos_h, rel_pos_w, proj_weight, proj_bias,
    ln2_gain, ln2_bias, fc1_weight, fc1_bias, fc2_weight, fc2_bias, keep_mask, key_mask, out_grad,
):
    wide = lax.axis_size("mp")
    z, y, c, x = places()
    core = c.astype(jnp.int32).reshape(1)
    keep = keep_mask.astype(F32).reshape(2) / 0.9
    keep_att, keep_feed = keep[0:1], keep[1]

    def line(v):
        return v.astype(F32).reshape(1, -1)

    rows_in = pad_rows(tokens)
    grad_out = pad_rows(out_grad)
    grad_feed = (keep_feed * grad_out.astype(F32)).astype(BF16)
    dms = [grad_feed] + [move_x(grad_feed, s) for s in range(1, wide)]
    weights = gather_rows(jnp.concatenate([qkv_weight, proj_weight], -1), 2)
    gacts = [jnp.dot(dm, fc2_weight.T, preferred_element_type=F32) for dm in dms]

    reverse_h, reverse_w = rel_pos_h[::-1].T, rel_pos_w[::-1].T
    one = jnp.concatenate(
        [jnp.pad(reverse_h, ((0, 0), (0, HEAD - 27))), jnp.pad(reverse_w, ((0, 0), (0, HEAD - 27)))], axis=1
    )
    blank = jnp.zeros_like(one)
    tables = jnp.concatenate(
        [jnp.concatenate([one, blank], axis=1), jnp.concatenate([blank, one], axis=1)], axis=0
    )
    qv_wide = qv_bias.astype(F32)
    qkv_bias = jnp.concatenate([qv_wide[0], jnp.zeros((D,), F32), qv_wide[1]]).reshape(1, -1)
    mask = jnp.where(key_mask > 0, 0.0, -1e9).astype(F32).reshape(WIN, WIN)
    fill = jnp.pad(mask, ((0, 0), (0, ROW - WIN)), constant_values=-3e38).reshape(1, R)
    gain_one, gain_two = line(ln1_gain), line(ln2_gain)
    a1, qkv, probs, attended, middle, a2 = attend(
        rows_in, weights, gain_one, line(ln1_bias), qkv_bias, tables, line(proj_bias), gain_two, line(ln2_bias),
        fill, keep_att,
    )
    a2s = [a2] + [move_x(a2, s) for s in range(1, wide)]
    upb = line(fc1_bias)
    fed = [feed(a2s[j], fc1_weight, upb, gacts[j], F32 if j == 0 else BF16) for j in range(wide)]
    da2 = fed[0][2]
    got = move_x(fed[1][2], -1).astype(F32)
    for step in range(2, wide):
        got = got + move_x(fed[step][2], -step).astype(F32)
    feeds = [jnp.dot(f[0], fc2_weight, preferred_element_type=F32) for f in fed]
    feed_out = feeds[0]
    for step in range(1, wide):
        feed_out = feed_out + move_x(feeds[step].astype(BF16), -step).astype(F32)
    result = (middle + keep_feed * (feed_out + fc2_bias.astype(F32))).astype(BF16)

    down_keep, down_send = weight_grads(core, dms, [f[0] for f in fed], 768)
    up_keep, up_send = weight_grads(core, a2s, [f[1] for f in fed], 768)
    down_grad = scatter_dp(down_keep, down_send)
    up_grad = scatter_dp(up_keep, up_send)
    up_bias_grad = sum(jnp.sum(f[1].astype(F32), axis=0) for f in fed)
    down_bias_grad = jnp.sum(grad_feed.astype(F32), axis=0)

    (
        grad_branch, grad_qkv, grad_in, gain_one_grad, shift_one_grad, qkv_bias_grad, table_grad,
        proj_bias_grad, gain_two_grad, shift_two_grad,
    ) = attend_back(
        da2, got, middle, grad_out, rows_in, weights, qkv, probs, tables, gain_one, gain_two, keep_att
    )
    qkv_keep, qkv_send = weight_grads(core, [a1], [grad_qkv], 768)
    proj_keep, proj_send = weight_grads(core, [attended], [grad_branch], 768)
    qkv_w_grad = scatter_all(qkv_keep, qkv_send)
    proj_grad = scatter_all(proj_keep, proj_send)
    table_one = table_grad[:HEAD, :LANES] + table_grad[HEAD:, LANES:]
    relh_grad = table_one[:, :27].T[::-1]
    relw_grad = table_one[:, HEAD : HEAD + 27].T[::-1]
    qv_grad = jnp.concatenate([qkv_bias_grad[:, :D], qkv_bias_grad[:, 2 * D :]], axis=0)
    up_bias_all = lax.dynamic_update_slice(
        jnp.zeros((wide, up_bias_grad.shape[0]), F32), up_bias_grad[None], (lax.axis_index("mp"), 0)
    )
    (
        gain_one_grad, shift_one_grad, qv_grad, relh_grad, relw_grad, proj_bias_grad, gain_two_grad,
        shift_two_grad, down_bias_grad, up_bias_all,
    ) = sum_all(
        (
            gain_one_grad.reshape(D), shift_one_grad.reshape(D), qv_grad, relh_grad, relw_grad,
            proj_bias_grad.reshape(D), gain_two_grad.reshape(D), shift_two_grad.reshape(D), down_bias_grad,
            up_bias_all,
        )
    )
    up_bias_grad = pick(
        pick(up_bias_all, lax.axis_index("mp"), 0).reshape(lax.axis_size("dp"), -1), lax.axis_index("dp"), 0
    )
    return (
        cut_rows(result), cut_rows(grad_in), gain_one_grad, shift_one_grad, qkv_w_grad, qv_grad, relh_grad,
        relw_grad, proj_grad, proj_bias_grad, gain_two_grad, shift_two_grad, up_grad, up_bias_grad,
        down_grad.T, down_bias_grad,
    )


def solution(mesh):
    in_specs = (
        P(("dp", "mp"), None),
        P(),
        P(),
        P(("dp", "mp"), None),
        P(),
        P(),
        P(),
        P(("dp", "mp"), None),
        P(),
        P(),
        P(),
        P(None, "mp"),
        P("mp"),
        P("mp", None),
        P(),
        P(("dp", "mp"), None),
        P(("dp", "mp"), None),
        P(("dp", "mp"), None),
    )
    out_specs = (
        P(("dp", "mp"), None),
        P(("dp", "mp"), None),
        P(),
        P(),
        P(("dp", "mp"), None),
        P(),
        P(),
        P(),
        P(("dp", "mp"), None),
        P(),
        P(),
        P(),
        P("dp", "mp"),
        P(("mp", "dp")),
        P("mp", "dp"),
        P(),
    )
    return jax.shard_map(
        per_device, mesh=mesh, in_specs=in_specs, out_specs=out_specs, check_vma=False
    )
```

time: 393 us -> 271 us (0.69)
  local copies, waits for them, and re-layouts: 107 us -> 34.6 us
  matrix products: 76.2 us -> 10.4 us
  Pallas kernels: 0 us -> 52.9 us
  other arithmetic: 62.7 us -> 29.6 us
  starting transfers between devices: 59.3 us -> 69.1 us
  waiting for transfers between devices: 80.3 us -> 70.9 us
    dot_general x28 -> x4, matrix products: 76.2 us -> 10.4 us  [the longest x2 5.95 us: per_device(): jnp.dot(dm, fc2_weight.T, preferred_element_type=F32)]
    pallas_call x0 -> x8, Pallas kernels: none -> 52.9 us  [the longest x4 15.6 us: weight_grads(): pl.pallas_call(partial(weights_kernel, count), grid=(columns // width,),...]
    reduce_sum x9 -> x3, other arithmetic: 33.1 us -> 3.64 us  [the longest x1 2.31 us: per_device(): down_bias_grad = jnp.sum(grad_feed.astype(F32), axis=0)]
    convert_element_type x17 -> x16, local copies, waits for them, and re-layouts: 25.7 us -> 0.62 us  [scatter_axis(): block = pick(value, (index + step) % size, axis).astype(BF16)]
    reshape x3 -> x13, local copies, waits for them, and re-layouts: 36.7 us -> 12.7 us  [the longest x6 6.91 us: line(): return v.astype(F32).reshape(1, -1)]
    another operation x5 -> x0, local copies, waits for them, and re-layouts: 15.5 us -> none
    ppermute x11 -> x13, waiting for transfers between devices: 32.8 us -> 21.9 us  [move_x(): lax.ppermute(value, 'mp', [(i, (i + step) % count) for i in range(count)])]
    ppermute x21 -> x27, starting transfers between devices: 33.1 us -> 40.4 us  [move_z(): return lax.ppermute(value, 'dp', dp_pairs(count, dz=step))]
  transfers between devices with their start and end apart: 47 -> 58, of which waited for: 22 -> 25; matrix products, arithmetic and copies ran while one was open for 39% -> 25% of each run, Pallas kernels for 0% -> 13%
where the time goes in v2:
time: 271 us; the launch traced here: 269 us
  waiting for transfers between devices  70.9 us (26%)
  starting transfers between devices  69.1 us (25%)
  Pallas kernels  52.9 us (20%)
  local copies, waits for them, and re-layouts  34.6 us (13%)
  other arithmetic  29.6 us (11%)
  matrix products  10.4 us (4%)
    ppermute x27, starting transfers between devices, move_z(): return lax.ppermute(value, 'dp', dp_pairs(count, dz=step))  40.4 us
    ppermute x11, waiting for transfers between devices, move_y(): return lax.ppermute(value, 'dp', dp_pairs(lax.axis_size('dp'), dy=step))  27.2 us
    ppermute x13, waiting for transfers between devices, move_x(): lax.ppermute(value, 'mp', [(i, (i + step) % count) for i in range(count)])  21.9 us
    ppermute x27, waiting for transfers between devices, move_z(): return lax.ppermute(value, 'dp', dp_pairs(count, dz=step))  21.7 us
    pallas_call x4, Pallas kernels, weight_grads(): pl.pallas_call(partial(weights_kernel, count), grid=(columns // width,),...  15.6 us
    ppermute x11, starting transfers between devices, move_y(): return lax.ppermute(value, 'dp', dp_pairs(lax.axis_size('dp'), dy=step))  15.5 us
    pallas_call x1, Pallas kernels, attend_back(): pl.pallas_call(attend_back_kernel, in_specs=[VMEM] * 11 + [SMEM], out_spe...  14.3 us
    ppermute x13, starting transfers between devices, move_x(): lax.ppermute(value, 'mp', [(i, (i + step) % count) for i in range(count)])  12.2 us
  transfers between devices with their start and end apart: 58, of which 25 were waited for; matrix products, arithmetic and copies ran while one was open for 25% of the time, Pallas kernels for 13%

profile of v2, /device:TPU:0, one launch (start us, length us, event | category | flops | bytes accessed | tf_op | source)
XLA Modules:
  0.0 269.2 jit_solution(3469766842843990503)
XLA Ops:
  0.7 1.7 slice.124
  2.4 4.0 %collective-permute-start.1 = (bf16[24,1536]{1,0:T(8,128)(2,1)}, bf16[24,1536]{1,0:T(8,128)(2,1)S(1)}, u32[]{:S(2)}, u32[]{:S(2)}) collective-permute-start(bf16[24,1536]{1,0:T(8,128)(2,1)} %slice.124), channel_id=1, source_target_pairs={{0,16},{2,18},{4,20},{6,22},{8,24},{10,26},{12,28},{14,30},{16,0},... | collective-permute-start | bytes 221192 | tf_op jit(solution)/shard_map/ppermute | solution.py:36
  13.0 1.5 collective-permute-start.17
  18.8 2.9 %collective-permute-start.8 = (bf16[24,1536]{1,0:T(8,128)(2,1)S(1)}, bf16[24,1536]{1,0:T(8,128)(2,1)S(1)}, u32[]{:S(2)}, u32[]{:S(2)}) collective-permute-start(bf16[24,1536]{1,0:T(8,128)(2,1)S(1)} %get-tuple-element.79), channel_id=1, source_target_pairs={{0,24},{2,26},{4,28},{6,30},{8,0},{10,2},{12,4},{14,6},{16,8},{18,... | collective-permute-start | bytes 221192 | tf_op jit(solution)/shard_map/ppermute | solution.py:36
  22.7 1.6 collective-permute-start.5
  24.8 3.0 %collective-permute-done.10 = bf16[24,1536]{1,0:T(8,128)(2,1)S(1)} collective-permute-done((bf16[24,1536]{1,0:T(8,128)(2,1)S(1)}, bf16[24,1536]{1,0:T(8,128)(2,1)S(1)}, u32[]{:S(2)}, u32[]{:S(2)}) %collective-permute-start.10) | collective-permute-done | bytes 73760 | tf_op jit(solution)/shard_map/ppermute | solution.py:36
  27.9 1.6 collective-permute-start.13
  32.6 2.1 collective-permute-start.4
  34.7 3.0 %collective-permute-done.13 = bf16[4,24,1536]{2,1,0:T(8,128)(2,1)S(1)} collective-permute-done((bf16[4,24,1536]{2,1,0:T(8,128)(2,1)S(1)}, bf16[4,24,1536]{2,1,0:T(8,128)(2,1)S(1)}, u32[]{:S(2)}, u32[]{:S(2)}) %collective-permute-start.13) | collective-permute-done | bytes 294944 | tf_op jit(solution)/shard_map/ppermute | solution.py:40
  42.2 2.5 collective-permute-done.12
  63.7 1.8 reshape.456
  65.5 1.7 pad.22
  67.2 2.3 convert_reduce_fusion.2
  69.5 3.0 %fusion.54.gact_ref = f32[224,1536]{1,0:T(8,128)} fusion(bf16[224,768]{1,0:T(8,128)(2,1)} %multiply_convert_fusion.1.refs_0_, bf16[1536,768]{1,0:T(8,128)(2,1)S(1)} %copy-done), kind=kOutput, calls=%fused_computation.187 | convolution fusion | flops 528482304 | bytes 4079616 | tf_op jit(solution)/shard_map/dot_general | solution.py:493
  74.0 3.0 %fusion.56.gact_ref = f32[224,1536]{1,0:T(8,128)} fusion(bf16[224,768]{1,0:T(8,128)(2,1)} %collective-permute-done.17.refs_1_, bf16[1536,768]{1,0:T(8,128)(2,1)S(1)} %copy-done), kind=kOutput, calls=%fused_computation.189 | convolution fusion | flops 528482304 | bytes 4079616 | tf_op jit(solution)/shard_map/dot_general | solution.py:493
  79.6 2.8 %pad_maximum_fusion.w_ref = bf16[768,3072]{1,0:T(8,128)(2,1)} fusion(bf16[768,1536]{1,0:T(8,128)(2,1)S(1)} %bitcast.236, bf16[768,1536]{1,0:T(8,128)(2,1)S(1)} %bitcast.235), kind=kLoop, calls=%fused_computation | loop fusion | flops 9437184 | bytes 9437184 | tf_op jit(solution)/shard_map/concatenate | solution.py:91
  82.4 10.9 %shard_map.297 = (bf16[224,768]{1,0:T(8,128)(2,1)}, bf16[224,2304]{1,0:T(8,128)(2,1)}, bf16[12,224,224]{2,1,0:T(8,128)(2,1)}, bf16[224,768]{1,0:T(8,128)(2,1)}, ...) custom-call(bf16[224,768]{1,0:T(8,128)(2,1)} %bitcast.243, bf16[768,3072]{1,0:T(8,128)(2,1)} %pad_maximum_fusion.w_ref, ...), custom_call_target="tpu_custom_call" | custom-call | flops 1056964608 | bytes 12582912 | tf_op jit(solution)/shard_map/pallas_call | solution.py:274
  93.8 6.2 %shard_map.298 = (bf16[224,1536]{1,0:T(8,128)(2,1)}, bf16[224,1536]{1,0:T(8,128)(2,1)}, f32[224,768]{1,0:T(8,128)}) custom-call(bf16[224,768]{1,0:T(8,128)(2,1)} %get-tuple-element.47.a2_ref.refs_0_, bf16[768,1536]{1,0:T(8,128)(2,1)} %up_ref.3, f32[1,1536]{1,0:T(1,128)} %reshape.510.upb_ref, f32[224,1536]{1,0:T(8,128)} %fusion.54.gact_ref), custom_call_target="tpu_custom_call" | custom-call | flops 1056964608 | bytes 6291456 | tf_op jit(solution)/shard_map/pallas_call | solution.py:398
  101.2 1.8 fusion.55
  104.3 6.0 %shard_map.299 = (bf16[224,1536]{1,0:T(8,128)(2,1)}, bf16[224,1536]{1,0:T(8,128)(2,1)}, bf16[224,768]{1,0:T(8,128)(2,1)}) custom-call(bf16[224,768]{1,0:T(8,128)(2,1)} %copy-done.17, bf16[768,1536]{1,0:T(8,128)(2,1)} %up_ref.3, f32[1,1536]{1,0:T(1,128)} %reshape.510.upb_ref, f32[224,1536]{1,0:T(8,128)} %fusion.56.gact_ref), custom_call_target="tpu_custom_call" | custom-call | flops 1056964608 | bytes 6291456 | tf_op jit(solution)/shard_map/pallas_call | solution.py:398
  111.3 2.6 convolution_convert_fusion
  115.2 6.3 %collective-permute-done.19 = bf16[224,768]{1,0:T(8,128)(2,1)S(1)} collective-permute-done((bf16[224,768]{1,0:T(8,128)(2,1)}, bf16[224,768]{1,0:T(8,128)(2,1)S(1)}, u32[]{:S(2)}, u32[]{:S(2)}) %collective-permute-start.19) | collective-permute-done | bytes 344096 | tf_op jit(solution)/shard_map/ppermute | solution.py:49
  122.5 14.3 %shard_map.300 = (bf16[224,768]{1,0:T(8,128)(2,1)}, bf16[224,2304]{1,0:T(8,128)(2,1)}, bf16[224,768]{1,0:T(8,128)(2,1)}, f32[1,768]{1,0:T(1,128)}, f32[1,768]{1,...) custom-call(f32[224,768]{1,0:T(8,128)} %get-tuple-element.50.own_ref, ...), custom_call_target="tpu_custom_call" | custom-call | flops 1585446912 | bytes 14680064 | tf_op jit(solution)/shard_map/pallas_call | solution.py:349
  142.5 4.4 %shard_map.304 = (bf16[384,1536]{1,0:T(8,128)(2,1)}, bf16[384,1536]{1,0:T(8,128)(2,1)}) custom-call(s32[1]{0:T(128)} %bitcast.37.core_ref, bf16[224,768]{1,0:T(8,128)(2,1)} %multiply_convert_fusion.1.refs_0_, bf16[224,768]{1,0:T(8,128)(2,1)} %collective-permute-done.17.refs_1_, bf16[224,1536]{1,0:T(8,128)(2,1)} %get-tuple-element.48.refs_2_, ...), custom_call_target="tpu_custom_call" | custom-call | flops 1056964608 | bytes 6291456 | tf_op jit(solution)/shard_map/pallas_call | solution.py:450
  148.2 4.0 %shard_map.303 = (bf16[384,1536]{1,0:T(8,128)(2,1)}, bf16[384,1536]{1,0:T(8,128)(2,1)}) custom-call(s32[1]{0:T(128)} %bitcast.37.core_ref, bf16[224,768]{1,0:T(8,128)(2,1)} %get-tuple-element.47.a2_ref.refs_0_, bf16[224,768]{1,0:T(8,128)(2,1)} %copy-done.17, bf16[224,1536]{1,0:T(8,128)(2,1)} %get-tuple-element.62.refs_2_, ...), custom_call_target="tpu_custom_call" | custom-call | flops 1056964608 | bytes 6291456 | tf_op jit(solution)/shard_map/pallas_call | solution.py:450
  152.2 1.5 collective-permute-start.22
  156.1 2.6 shard_map.302
  158.8 4.7 %collective-permute-start.25 = (f32[104,128]{1,0:T(8,128)S(1)}, f32[104,128]{1,0:T(8,128)S(1)}, u32[]{:S(2)}, u32[]{:S(2)}) collective-permute-start(f32[104,128]{1,0:T(8,128)S(1)} %add.341), channel_id=1, source_target_pairs={{0,24},{2,26},{4,28},{6,30},{8,0},{10,2},{12,4},{14,6},{16,8},{18,... | collective-permute-start | bytes 159752 | tf_op jit(solution)/shard_map/ppermute | solution.py:36
  164.1 4.5 %shard_map.301 = (bf16[384,2304]{1,0:T(8,128)(2,1)}, bf16[384,2304]{1,0:T(8,128)(2,1)}) custom-call(s32[1]{0:T(128)} %bitcast.37.core_ref, bf16[224,768]{1,0:T(8,128)(2,1)} %get-tuple-element.64.refs_0_, bf16[224,2304]{1,0:T(8,128)(2,1)} %get-tuple-element.65.refs_1_), custom_call_target="tpu_custom_call" | custom-call | flops 792723456 | bytes 6291456 | tf_op jit(solution)/shard_map/pallas_call | solution.py:450
  175.0 2.0 collective-permute-done.43
  179.6 1.9 collective-permute-start.39
  181.6 2.9 %collective-permute-start.45 = (bf16[24,384]{1,0:T(8,128)(2,1)S(1)}, bf16[24,384]{1,0:T(8,128)(2,1)S(1)}, u32[]{:S(2)}, u32[]{:S(2)}) collective-permute-start(bf16[24,384]{1,0:T(8,128)(2,1)S(1)} %get-tuple-element.115), channel_id=1, source_target_pairs={{0,8},{2,10},{4,12},{6,14},{8,16},{10,18},{12,20},{14,22},{16,24},... | collective-permute-start | bytes 55304 | tf_op jit(solution)/shard_map/ppermute | solution.py:36
  188.3 2.7 %collective-permute-start.42 = (bf16[24,384]{1,0:T(8,128)(2,1)S(1)}, bf16[24,384]{1,0:T(8,128)(2,1)S(1)}, u32[]{:S(2)}, u32[]{:S(2)}) collective-permute-start(bf16[24,384]{1,0:T(8,128)(2,1)S(1)} %get-tuple-element.113), channel_id=1, source_target_pairs={{0,24},{2,26},{4,28},{6,30},{8,0},{10,2},{12,4},{14,6},{16,8},{18,... | collective-permute-start | bytes 55304 | tf_op jit(solution)/shard_map/ppermute | solution.py:36
  191.1 1.7 collective-permute-done.40
  192.8 2.9 %collective-permute-done.41 = bf16[24,384]{1,0:T(8,128)(2,1)S(1)} collective-permute-done((bf16[24,384]{1,0:T(8,128)(2,1)S(1)}, bf16[24,384]{1,0:T(8,128)(2,1)S(1)}, u32[]{:S(2)}, u32[]{:S(2)}) %collective-permute-start.41) | collective-permute-done | bytes 18464 | tf_op jit(solution)/shard_map/ppermute | solution.py:36
  196.4 1.6 convert_add_fusion.1
  199.2 1.6 convert_add_fusion.2
  202.1 12.3 %collective-permute-done.54 = bf16[4,48,1536]{2,1,0:T(8,128)(2,1)S(1)} collective-permute-done((bf16[4,48,1536]{2,1,0:T(8,128)(2,1)S(1)}, bf16[4,48,1536]{2,1,0:T(8,128)(2,1)S(1)}, u32[]{:S(2)}, u32[]{:S(2)}) %collective-permute-start.54) | collective-permute-done | bytes 589856 | tf_op jit(solution)/shard_map/ppermute | solution.py:40
  215.0 3.5 %collective-permute-start.57 = (bf16[48,1536]{1,0:T(8,128)(2,1)S(1)}, bf16[48,1536]{1,0:T(8,128)(2,1)S(1)}, u32[]{:S(2)}, u32[]{:S(2)}) collective-permute-start(bf16[48,1536]{1,0:T(8,128)(2,1)S(1)} %get-tuple-element.87), channel_id=1, source_target_pairs={{0,24},{2,26},{4,28},{6,30},{8,0},{10,2},{12,4},{14,6},{16,8},{18,... | collective-permute-start | bytes 442376 | tf_op jit(solution)/shard_map/ppermute | solution.py:36
  218.5 5.1 %collective-permute-done.49 = bf16[4,48,1536]{2,1,0:T(8,128)(2,1)S(1)} collective-permute-done((bf16[4,48,1536]{2,1,0:T(8,128)(2,1)S(1)}, bf16[4,48,1536]{2,1,0:T(8,128)(2,1)S(1)}, u32[]{:S(2)}, u32[]{:S(2)}) %collective-permute-start.49) | collective-permute-done | bytes 589856 | tf_op jit(solution)/shard_map/ppermute | solution.py:40
  224.2 3.5 %collective-permute-start.52 = (bf16[48,1536]{1,0:T(8,128)(2,1)S(1)}, bf16[48,1536]{1,0:T(8,128)(2,1)S(1)}, u32[]{:S(2)}, u32[]{:S(2)}) collective-permute-start(bf16[48,1536]{1,0:T(8,128)(2,1)S(1)} %get-tuple-element.90), channel_id=1, source_target_pairs={{0,24},{2,26},{4,28},{6,30},{8,0},{10,2},{12,4},{14,6},{16,8},{18,... | collective-permute-start | bytes 442376 | tf_op jit(solution)/shard_map/ppermute | solution.py:36
  227.7 4.3 %collective-permute-done.56 = bf16[48,1536]{1,0:T(8,128)(2,1)S(1)} collective-permute-done((bf16[48,1536]{1,0:T(8,128)(2,1)S(1)}, bf16[48,1536]{1,0:T(8,128)(2,1)S(1)}, u32[]{:S(2)}, u32[]{:S(2)}) %collective-permute-start.56) | collective-permute-done | bytes 147488 | tf_op jit(solution)/shard_map/ppermute | solution.py:36
  234.7 4.1 %collective-permute-done.51 = bf16[48,1536]{1,0:T(8,128)(2,1)S(1)} collective-permute-done((bf16[48,1536]{1,0:T(8,128)(2,1)S(1)}, bf16[48,1536]{1,0:T(8,128)(2,1)S(1)}, u32[]{:S(2)}, u32[]{:S(2)}) %collective-permute-start.51) | collective-permute-done | bytes 147488 | tf_op jit(solution)/shard_map/ppermute | solution.py:36
  243.2 9.6 %collective-permute-done.27 = bf16[4,2,24,1152]{3,2,0,1:T(8,128)(2,1)S(1)} collective-permute-done((bf16[4,2,24,1152]{3,2,0,1:T(8,128)(2,1)S(1)}, bf16[4,2,24,1152]{3,2,0,1:T(8,128)(2,1)S(1)}, u32[]{:S(2)}, u32[]{:S(2)}) %collective-permute-start.27) | collective-permute-done | bytes 442400 | tf_op jit(solution)/shard_map/ppermute | solution.py:49
  255.6 3.8 %collective-permute-start.36 = (bf16[24,1152]{1,0:T(8,128)(2,1)S(1)}, bf16[24,1152]{1,0:T(8,128)(2,1)S(1)}, u32[]{:S(2)}, u32[]{:S(2)}) collective-permute-start(bf16[24,1152]{1,0:T(8,128)(2,1)S(1)} %get-tuple-element.110), channel_id=1, source_target_pairs={{0,24},{2,26},{4,28},{6,30},{8,0},{10,2},{12,4},{14,6},{16,8},{18,... | collective-permute-start | bytes 165896 | tf_op jit(solution)/shard_map/ppermute | solution.py:36
  260.2 3.3 %collective-permute-start.31 = (bf16[24,1152]{1,0:T(8,128)(2,1)S(1)}, bf16[24,1152]{1,0:T(8,128)(2,1)S(1)}, u32[]{:S(2)}, u32[]{:S(2)}) collective-permute-start(bf16[24,1152]{1,0:T(8,128)(2,1)S(1)} %get-tuple-element.107), channel_id=1, source_target_pairs={{0,24},{2,26},{4,28},{6,30},{8,0},{10,2},{12,4},{14,6},{16,8},{18,... | collective-permute-start | bytes 165896 | tf_op jit(solution)/shard_map/ppermute | solution.py:36
  264.5 1.9 collective-permute-done.35
  266.9 1.6 collective-permute-done.30
  (285 shorter events, 89.0 us)
Async XLA Ops:
  2.4 14.5 %collective-permute-start.1 = (bf16[24,1536]{1,0:T(8,128)(2,1)}, bf16[24,1536]{1,0:T(8,128)(2,1)S(1)}, u32[]{:S(2)}, u32[]{:S(2)}) collective-permute-start(bf16[24,1536]{1,0:T(8,128)(2,1)} %slice.124), channel_id=1, source_target_pairs={{0,16},{2,18},{4,20},{6,22},{8,24},{10,26},{12,28},{14,30},{16,0},... | collective-permute-start | bytes 221192 | tf_op jit(solution)/shard_map/ppermute | solution.py:36
  6.4 9.6 %collective-permute-start = (bf16[24,1536]{1,0:T(8,128)(2,1)}, bf16[24,1536]{1,0:T(8,128)(2,1)}, u32[]{:S(2)}, u32[]{:S(2)}) collective-permute-start(bf16[24,1536]{1,0:T(8,128)(2,1)} %slice.124), channel_id=1, source_target_pairs={{0,24},{2,26},{4,28},{6,30},{8,0},{10,2},{12,4},{14,6},{16,8},{18,... | collective-permute-start | bytes 221192 | tf_op jit(solution)/shard_map/ppermute | solution.py:36
  7.7 9.1 %collective-permute-start.2 = (bf16[24,1536]{1,0:T(8,128)(2,1)}, bf16[24,1536]{1,0:T(8,128)(2,1)S(1)}, u32[]{:S(2)}, u32[]{:S(2)}) collective-permute-start(bf16[24,1536]{1,0:T(8,128)(2,1)} %slice.124), channel_id=1, source_target_pairs={{0,8},{2,10},{4,12},{6,14},{8,16},{10,18},{12,20},{14,22},{16,24},... | collective-permute-start | bytes 221192 | tf_op jit(solution)/shard_map/ppermute | solution.py:36
  13.0 60.9 %collective-permute-start.17 = (bf16[224,768]{1,0:T(8,128)(2,1)}, bf16[224,768]{1,0:T(8,128)(2,1)}, u32[]{:S(2)}, u32[]{:S(2)}) collective-permute-start(bf16[224,768]{1,0:T(8,128)(2,1)} %multiply_convert_fusion.1.refs_0_), channel_id=1, source_target_pairs={{0,1},{1,0},{2,3},{3,2},{4,5},{5,4},{6,7},{7,6},{8,9},{9,8},{10,11... | collective-permute-start | bytes 1032200 | tf_op jit(solution)/shard_map/ppermute | solution.py:49
  17.7 7.1 %collective-permute-start.9 = (bf16[24,1536]{1,0:T(8,128)(2,1)S(1)}, bf16[24,1536]{1,0:T(8,128)(2,1)S(1)}, u32[]{:S(2)}, u32[]{:S(2)}) collective-permute-start(bf16[24,1536]{1,0:T(8,128)(2,1)S(1)} %get-tuple-element.79), channel_id=1, source_target_pairs={{0,16},{2,18},{4,20},{6,22},{8,24},{10,26},{12,28},{14,30},{16,0},... | collective-permute-start | bytes 221192 | tf_op jit(solution)/shard_map/ppermute | solution.py:36
  21.7 6.2 %collective-permute-start.10 = (bf16[24,1536]{1,0:T(8,128)(2,1)S(1)}, bf16[24,1536]{1,0:T(8,128)(2,1)S(1)}, u32[]{:S(2)}, u32[]{:S(2)}) collective-permute-start(bf16[24,1536]{1,0:T(8,128)(2,1)S(1)} %get-tuple-element.79), channel_id=1, source_target_pairs={{0,8},{2,10},{4,12},{6,14},{8,16},{10,18},{12,20},{14,22},{16,24},... | collective-permute-start | bytes 221192 | tf_op jit(solution)/shard_map/ppermute | solution.py:36
  22.7 8.7 %collective-permute-start.5 = (bf16[4,24,1536]{2,1,0:T(8,128)(2,1)S(1)}, bf16[4,24,1536]{2,1,0:T(8,128)(2,1)S(1)}, u32[]{:S(2)}, u32[]{:S(2)}) collective-permute-start(bf16[4,24,1536]{2,1,0:T(8,128)(2,1)S(1)} %constant_dynamic-slice_fusion.11), channel_id=1, source_target_pairs={{0,4},{2,6},{4,0},{6,2},{8,12},{10,14},{12,8},{14,10},{16,20},{18,... | collective-permute-start | bytes 884744 | tf_op jit(solution)/shard_map/ppermute | solution.py:40
  24.3 8.3 %collective-permute-start.3 = (bf16[4,24,1536]{2,1,0:T(8,128)(2,1)S(1)}, bf16[4,24,1536]{2,1,0:T(8,128)(2,1)S(1)}, u32[]{:S(2)}, u32[]{:S(2)}) collective-permute-start(bf16[4,24,1536]{2,1,0:T(8,128)(2,1)S(1)} %constant_dynamic-slice_fusion.11), channel_id=1, source_target_pairs={{0,1},{1,0},{2,3},{3,2},{4,5},{5,4},{6,7},{7,6},{8,9},{9,8},{10,11... | collective-permute-start | bytes 884744 | tf_op jit(solution)/shard_map/ppermute | solution.py:49
  27.9 9.7 %collective-permute-start.13 = (bf16[4,24,1536]{2,1,0:T(8,128)(2,1)S(1)}, bf16[4,24,1536]{2,1,0:T(8,128)(2,1)S(1)}, u32[]{:S(2)}, u32[]{:S(2)}) collective-permute-start(bf16[4,24,1536]{2,1,0:T(8,128)(2,1)S(1)} %constant_dynamic-slice_fusion.10), channel_id=1, source_target_pairs={{0,4},{2,6},{4,0},{6,2},{8,12},{10,14},{12,8},{14,10},{16,20},{18,... | collective-permute-start | bytes 884744 | tf_op jit(solution)/shard_map/ppermute | solution.py:40
  29.5 9.9 %collective-permute-start.11 = (bf16[4,24,1536]{2,1,0:T(8,128)(2,1)S(1)}, bf16[4,24,1536]{2,1,0:T(8,128)(2,1)S(1)}, u32[]{:S(2)}, u32[]{:S(2)}) collective-permute-start(bf16[4,24,1536]{2,1,0:T(8,128)(2,1)S(1)} %constant_dynamic-slice_fusion.10), channel_id=1, source_target_pairs={{0,1},{1,0},{2,3},{3,2},{4,5},{5,4},{6,7},{7,6},{8,9},{9,8},{10,11... | collective-permute-start | bytes 884744 | tf_op jit(solution)/shard_map/ppermute | solution.py:49
  31.3 10.8 %collective-permute-start.6 = (bf16[4,24,768]{2,1,0:T(8,128)(2,1)S(1)}, bf16[4,24,768]{2,1,0:T(8,128)(2,1)S(1)}, u32[]{:S(2)}, u32[]{:S(2)}) collective-permute-start(bf16[4,24,768]{2,1,0:T(8,128)(2,1)S(1)} %slice.165), channel_id=1, source_target_pairs={{0,1},{1,0},{2,3},{3,2},{4,5},{5,4},{6,7},{7,6},{8,9},{9,8},{10,11... | collective-permute-start | bytes 442376 | tf_op jit(solution)/shard_map/ppermute | solution.py:49
  32.6 8.5 %collective-permute-start.4 = (bf16[4,24,768]{2,1,0:T(8,128)(2,1)S(1)}, bf16[4,24,768]{2,1,0:T(8,128)(2,1)S(1)}, u32[]{:S(2)}, u32[]{:S(2)}) collective-permute-start(bf16[4,24,768]{2,1,0:T(8,128)(2,1)S(1)} %slice.164), channel_id=1, source_target_pairs={{0,4},{2,6},{4,0},{6,2},{8,12},{10,14},{12,8},{14,10},{16,20},{18,... | collective-permute-start | bytes 442376 | tf_op jit(solution)/shard_map/ppermute | solution.py:40
  37.7 7.0 %collective-permute-start.14 = (bf16[4,24,768]{2,1,0:T(8,128)(2,1)S(1)}, bf16[4,24,768]{2,1,0:T(8,128)(2,1)S(1)}, u32[]{:S(2)}, u32[]{:S(2)}) collective-permute-start(bf16[4,24,768]{2,1,0:T(8,128)(2,1)S(1)} %slice.167), channel_id=1, source_target_pairs={{0,1},{1,0},{2,3},{3,2},{4,5},{5,4},{6,7},{7,6},{8,9},{9,8},{10,11... | collective-permute-start | bytes 442376 | tf_op jit(solution)/shard_map/ppermute | solution.py:49
  47.0 29.9 %collective-permute-start.7 = (bf16[2,2,4,24,1536]{4,3,2,1,0:T(8,128)(2,1)}, bf16[2,2,4,24,1536]{4,3,2,1,0:T(8,128)(2,1)}, u32[]{:S(2)}, u32[]{:S(2)}) collective-permute-start(bf16[2,2,4,24,1536]{4,3,2,1,0:T(8,128)(2,1)} %pad_maximum_fusion.1), channel_id=1, source_target_pairs={{0,2},{2,0},{4,6},{6,4},{8,10},{10,8},{12,14},{14,12},{16,18},{18,... | collective-permute-start | bytes 3538952 | tf_op jit(solution)/shard_map/ppermute | solution.py:44
  73.4 5.5 %collective-permute-start.15 = (bf16[2,2,4,24,1536]{4,3,2,1,0:T(8,128)(2,1)S(1)}, bf16[2,2,4,24,1536]{4,3,2,1,0:T(8,128)(2,1)S(1)}, u32[]{:S(2)}, u32[]{:S(2)}) collective-permute-start(bf16[2,2,4,24,1536]{4,3,2,1,0:T(8,128)(2,1)S(1)} %pad_maximum_fusion.2), channel_id=1, source_target_pairs={{0,2},{2,0},{4,6},{6,4},{8,10},{10,8},{12,14},{14,12},{16,18},{18,... | collective-permute-start | bytes 3538952 | tf_op jit(solution)/shard_map/ppermute | solution.py:44
  93.3 10.3 %collective-permute-start.16 = (bf16[224,768]{1,0:T(8,128)(2,1)}, bf16[224,768]{1,0:T(8,128)(2,1)S(1)}, u32[]{:S(2)}, u32[]{:S(2)}) collective-permute-start(bf16[224,768]{1,0:T(8,128)(2,1)} %get-tuple-element.47.a2_ref.refs_0_), channel_id=1, source_target_pairs={{0,1},{1,0},{2,3},{3,2},{4,5},{5,4},{6,7},{7,6},{8,9},{9,8},{10,11... | collective-permute-start | bytes 1032200 | tf_op jit(solution)/shard_map/ppermute | solution.py:49
  110.3 11.3 %collective-permute-start.19 = (bf16[224,768]{1,0:T(8,128)(2,1)}, bf16[224,768]{1,0:T(8,128)(2,1)S(1)}, u32[]{:S(2)}, u32[]{:S(2)}) collective-permute-start(bf16[224,768]{1,0:T(8,128)(2,1)} %get-tuple-element.51), channel_id=1, source_target_pairs={{0,1},{1,0},{2,3},{3,2},{4,5},{5,4},{6,7},{7,6},{8,9},{9,8},{10,11... | collective-permute-start | bytes 1032200 | tf_op jit(solution)/shard_map/ppermute | solution.py:49
  113.9 39.8 %collective-permute-start.18 = (bf16[224,768]{1,0:T(8,128)(2,1)}, bf16[224,768]{1,0:T(8,128)(2,1)S(1)}, u32[]{:S(2)}, u32[]{:S(2)}) collective-permute-start(bf16[224,768]{1,0:T(8,128)(2,1)} %convolution_convert_fusion), channel_id=1, source_target_pairs={{0,1},{1,0},{2,3},{3,2},{4,5},{5,4},{6,7},{7,6},{8,9},{9,8},{10,11... | collective-permute-start | bytes 1032200 | tf_op jit(solution)/shard_map/ppermute | solution.py:49
  146.9 49.5 %collective-permute-start.53 = (bf16[384,1536]{1,0:T(8,128)(2,1)}, bf16[384,1536]{1,0:T(8,128)(2,1)}, u32[]{:S(2)}, u32[]{:S(2)}) collective-permute-start(bf16[384,1536]{1,0:T(8,128)(2,1)} %get-tuple-element.75), channel_id=1, source_target_pairs={{0,2},{2,0},{4,6},{6,4},{8,10},{10,8},{12,14},{14,12},{16,18},{18,... | collective-permute-start | bytes 3538952 | tf_op jit(solution)/shard_map/ppermute | solution.py:44
  152.2 47.0 %collective-permute-start.48 = (bf16[384,1536]{1,0:T(8,128)(2,1)}, bf16[384,1536]{1,0:T(8,128)(2,1)}, u32[]{:S(2)}, u32[]{:S(2)}) collective-permute-start(bf16[384,1536]{1,0:T(8,128)(2,1)} %get-tuple-element.73), channel_id=1, source_target_pairs={{0,2},{2,0},{4,6},{6,4},{8,10},{10,8},{12,14},{14,12},{16,18},{18,... | collective-permute-start | bytes 3538952 | tf_op jit(solution)/shard_map/ppermute | solution.py:44
  152.2 6.6 %collective-permute-start.22 = (f32[104,128]{1,0:T(8,128)S(1)}, f32[104,128]{1,0:T(8,128)S(1)}, u32[]{:S(2)}, u32[]{:S(2)}) collective-permute-start(f32[104,128]{1,0:T(8,128)S(1)} %fusion.65), channel_id=1, source_target_pairs={{0,4},{2,6},{4,0},{6,2},{8,12},{10,14},{12,8},{14,10},{16,20},{18,... | collective-permute-start | bytes 159752 | tf_op jit(solution)/shard_map/ppermute | solution.py:40
  158.8 9.9 %collective-permute-start.25 = (f32[104,128]{1,0:T(8,128)S(1)}, f32[104,128]{1,0:T(8,128)S(1)}, u32[]{:S(2)}, u32[]{:S(2)}) collective-permute-start(f32[104,128]{1,0:T(8,128)S(1)} %add.341), channel_id=1, source_target_pairs={{0,24},{2,26},{4,28},{6,30},{8,0},{10,2},{12,4},{14,6},{16,8},{18,... | collective-permute-start | bytes 159752 | tf_op jit(solution)/shard_map/ppermute | solution.py:36
  163.5 6.0 %collective-permute-start.24 = (f32[104,128]{1,0:T(8,128)S(1)}, f32[104,128]{1,0:T(8,128)S(1)}, u32[]{:S(2)}, u32[]{:S(2)}) collective-permute-start(f32[104,128]{1,0:T(8,128)S(1)} %add.341), channel_id=1, source_target_pairs={{0,16},{2,18},{4,20},{6,22},{8,24},{10,26},{12,28},{14,30},{16,0},... | collective-permute-start | bytes 159752 | tf_op jit(solution)/shard_map/ppermute | solution.py:36
  163.5 6.0 %collective-permute-start.23 = (f32[104,128]{1,0:T(8,128)S(1)}, f32[104,128]{1,0:T(8,128)S(1)}, u32[]{:S(2)}, u32[]{:S(2)}) collective-permute-start(f32[104,128]{1,0:T(8,128)S(1)} %add.341), channel_id=1, source_target_pairs={{0,8},{2,10},{4,12},{6,14},{8,16},{10,18},{12,20},{14,22},{16,24},... | collective-permute-start | bytes 159752 | tf_op jit(solution)/shard_map/ppermute | solution.py:36
  171.3 5.7 %collective-permute-start.43 = (bf16[4,2,24,384]{3,2,0,1:T(8,128)(2,1)S(1)}, bf16[4,2,24,384]{3,2,0,1:T(8,128)(2,1)S(1)}, u32[]{:S(2)}, u32[]{:S(2)}) collective-permute-start(bf16[4,2,24,384]{3,2,0,1:T(8,128)(2,1)S(1)} %fusion.22), channel_id=1, source_target_pairs={{0,4},{2,6},{4,0},{6,2},{8,12},{10,14},{12,8},{14,10},{16,20},{18,... | collective-permute-start | bytes 442376 | tf_op jit(solution)/shard_map/ppermute | solution.py:40
  173.8 5.8 %collective-permute-start.38 = (bf16[4,2,24,384]{3,2,0,1:T(8,128)(2,1)S(1)}, bf16[4,2,24,384]{3,2,0,1:T(8,128)(2,1)S(1)}, u32[]{:S(2)}, u32[]{:S(2)}) collective-permute-start(bf16[4,2,24,384]{3,2,0,1:T(8,128)(2,1)S(1)} %fusion.21), channel_id=1, source_target_pairs={{0,1},{1,0},{2,3},{3,2},{4,5},{5,4},{6,7},{7,6},{8,9},{9,8},{10,11... | collective-permute-start | bytes 442376 | tf_op jit(solution)/shard_map/ppermute | solution.py:49
  179.6 5.8 %collective-permute-start.39 = (bf16[4,24,384]{2,1,0:T(8,128)(2,1)S(1)}, bf16[4,24,384]{2,1,0:T(8,128)(2,1)S(1)}, u32[]{:S(2)}, u32[]{:S(2)}) collective-permute-start(bf16[4,24,384]{2,1,0:T(8,128)(2,1)S(1)} %fusion.27), channel_id=1, source_target_pairs={{0,4},{2,6},{4,0},{6,2},{8,12},{10,14},{12,8},{14,10},{16,20},{18,... | collective-permute-start | bytes 221192 | tf_op jit(solution)/shard_map/ppermute | solution.py:40
  181.6 5.6 %collective-permute-start.45 = (bf16[24,384]{1,0:T(8,128)(2,1)S(1)}, bf16[24,384]{1,0:T(8,128)(2,1)S(1)}, u32[]{:S(2)}, u32[]{:S(2)}) collective-permute-start(bf16[24,384]{1,0:T(8,128)(2,1)S(1)} %get-tuple-element.115), channel_id=1, source_target_pairs={{0,8},{2,10},{4,12},{6,14},{8,16},{10,18},{12,20},{14,22},{16,24},... | collective-permute-start | bytes 55304 | tf_op jit(solution)/shard_map/ppermute | solution.py:36
  185.5 5.6 %collective-permute-start.46 = (bf16[24,384]{1,0:T(8,128)(2,1)S(1)}, bf16[24,384]{1,0:T(8,128)(2,1)S(1)}, u32[]{:S(2)}, u32[]{:S(2)}) collective-permute-start(bf16[24,384]{1,0:T(8,128)(2,1)S(1)} %get-tuple-element.117), channel_id=1, source_target_pairs={{0,16},{2,18},{4,20},{6,22},{8,24},{10,26},{12,28},{14,30},{16,0},... | collective-permute-start | bytes 55304 | tf_op jit(solution)/shard_map/ppermute | solution.py:36
  187.2 5.6 %collective-permute-start.40 = (bf16[24,384]{1,0:T(8,128)(2,1)S(1)}, bf16[24,384]{1,0:T(8,128)(2,1)S(1)}, u32[]{:S(2)}, u32[]{:S(2)}) collective-permute-start(bf16[24,384]{1,0:T(8,128)(2,1)S(1)} %get-tuple-element.112), channel_id=1, source_target_pairs={{0,8},{2,10},{4,12},{6,14},{8,16},{10,18},{12,20},{14,22},{16,24},... | collective-permute-start | bytes 55304 | tf_op jit(solution)/shard_map/ppermute | solution.py:36
  192.8 40.0 %collective-permute-start.26 = (bf16[384,2304]{1,0:T(8,128)(2,1)S(1)}, bf16[384,2304]{1,0:T(8,128)(2,1)S(1)}, u32[]{:S(2)}, u32[]{:S(2)}) collective-permute-start(bf16[384,2304]{1,0:T(8,128)(2,1)S(1)} %copy-done.23), channel_id=1, source_target_pairs={{0,2},{2,0},{4,6},{6,4},{8,10},{10,8},{12,14},{14,12},{16,18},{18,... | collective-permute-start | bytes 5308424 | tf_op jit(solution)/shard_map/ppermute | solution.py:44
  198.1 16.3 %collective-permute-start.54 = (bf16[4,48,1536]{2,1,0:T(8,128)(2,1)S(1)}, bf16[4,48,1536]{2,1,0:T(8,128)(2,1)S(1)}, u32[]{:S(2)}, u32[]{:S(2)}) collective-permute-start(bf16[4,48,1536]{2,1,0:T(8,128)(2,1)S(1)} %fusion.3), channel_id=1, source_target_pairs={{0,4},{2,6},{4,0},{6,2},{8,12},{10,14},{12,8},{14,10},{16,20},{18,... | collective-permute-start | bytes 1769480 | tf_op jit(solution)/shard_map/ppermute | solution.py:40
  200.9 22.7 %collective-permute-start.49 = (bf16[4,48,1536]{2,1,0:T(8,128)(2,1)S(1)}, bf16[4,48,1536]{2,1,0:T(8,128)(2,1)S(1)}, u32[]{:S(2)}, u32[]{:S(2)}) collective-permute-start(bf16[4,48,1536]{2,1,0:T(8,128)(2,1)S(1)} %fusion.2), channel_id=1, source_target_pairs={{0,4},{2,6},{4,0},{6,2},{8,12},{10,14},{12,8},{14,10},{16,20},{18,... | collective-permute-start | bytes 1769480 | tf_op jit(solution)/shard_map/ppermute | solution.py:40
  214.6 9.6 %collective-permute-start.55 = (bf16[48,1536]{1,0:T(8,128)(2,1)S(1)}, bf16[48,1536]{1,0:T(8,128)(2,1)S(1)}, u32[]{:S(2)}, u32[]{:S(2)}) collective-permute-start(bf16[48,1536]{1,0:T(8,128)(2,1)S(1)} %get-tuple-element.86), channel_id=1, source_target_pairs={{0,8},{2,10},{4,12},{6,14},{8,16},{10,18},{12,20},{14,22},{16,24},... | collective-permute-start | bytes 442376 | tf_op jit(solution)/shard_map/ppermute | solution.py:36
  215.0 12.7 %collective-permute-start.57 = (bf16[48,1536]{1,0:T(8,128)(2,1)S(1)}, bf16[48,1536]{1,0:T(8,128)(2,1)S(1)}, u32[]{:S(2)}, u32[]{:S(2)}) collective-permute-start(bf16[48,1536]{1,0:T(8,128)(2,1)S(1)} %get-tuple-element.87), channel_id=1, source_target_pairs={{0,24},{2,26},{4,28},{6,30},{8,0},{10,2},{12,4},{14,6},{16,8},{18,... | collective-permute-start | bytes 442376 | tf_op jit(solution)/shard_map/ppermute | solution.py:36
  218.5 13.5 %collective-permute-start.56 = (bf16[48,1536]{1,0:T(8,128)(2,1)S(1)}, bf16[48,1536]{1,0:T(8,128)(2,1)S(1)}, u32[]{:S(2)}, u32[]{:S(2)}) collective-permute-start(bf16[48,1536]{1,0:T(8,128)(2,1)S(1)} %get-tuple-element.88), channel_id=1, source_target_pairs={{0,16},{2,18},{4,20},{6,22},{8,24},{10,26},{12,28},{14,30},{16,0},... | collective-permute-start | bytes 442376 | tf_op jit(solution)/shard_map/ppermute | solution.py:36
  223.8 10.9 %collective-permute-start.50 = (bf16[48,1536]{1,0:T(8,128)(2,1)S(1)}, bf16[48,1536]{1,0:T(8,128)(2,1)S(1)}, u32[]{:S(2)}, u32[]{:S(2)}) collective-permute-start(bf16[48,1536]{1,0:T(8,128)(2,1)S(1)} %get-tuple-element.89), channel_id=1, source_target_pairs={{0,8},{2,10},{4,12},{6,14},{8,16},{10,18},{12,20},{14,22},{16,24},... | collective-permute-start | bytes 442376 | tf_op jit(solution)/shard_map/ppermute | solution.py:36
  224.2 10.6 %collective-permute-start.52 = (bf16[48,1536]{1,0:T(8,128)(2,1)S(1)}, bf16[48,1536]{1,0:T(8,128)(2,1)S(1)}, u32[]{:S(2)}, u32[]{:S(2)}) collective-permute-start(bf16[48,1536]{1,0:T(8,128)(2,1)S(1)} %get-tuple-element.90), channel_id=1, source_target_pairs={{0,24},{2,26},{4,28},{6,30},{8,0},{10,2},{12,4},{14,6},{16,8},{18,... | collective-permute-start | bytes 442376 | tf_op jit(solution)/shard_map/ppermute | solution.py:36
  227.7 11.1 %collective-permute-start.51 = (bf16[48,1536]{1,0:T(8,128)(2,1)S(1)}, bf16[48,1536]{1,0:T(8,128)(2,1)S(1)}, u32[]{:S(2)}, u32[]{:S(2)}) collective-permute-start(bf16[48,1536]{1,0:T(8,128)(2,1)S(1)} %get-tuple-element.91), channel_id=1, source_target_pairs={{0,16},{2,18},{4,20},{6,22},{8,24},{10,26},{12,28},{14,30},{16,0},... | collective-permute-start | bytes 442376 | tf_op jit(solution)/shard_map/ppermute | solution.py:36
  233.5 8.4 %collective-permute-start.32 = (bf16[4,2,24,1152]{3,2,0,1:T(8,128)(2,1)S(1)}, bf16[4,2,24,1152]{3,2,0,1:T(8,128)(2,1)S(1)}, u32[]{:S(2)}, u32[]{:S(2)}) collective-permute-start(bf16[4,2,24,1152]{3,2,0,1:T(8,128)(2,1)S(1)} %fusion.5), channel_id=1, source_target_pairs={{0,4},{2,6},{4,0},{6,2},{8,12},{10,14},{12,8},{14,10},{16,20},{18,... | collective-permute-start | bytes 1327112 | tf_op jit(solution)/shard_map/ppermute | solution.py:40
  239.6 13.2 %collective-permute-start.27 = (bf16[4,2,24,1152]{3,2,0,1:T(8,128)(2,1)S(1)}, bf16[4,2,24,1152]{3,2,0,1:T(8,128)(2,1)S(1)}, u32[]{:S(2)}, u32[]{:S(2)}) collective-permute-start(bf16[4,2,24,1152]{3,2,0,1:T(8,128)(2,1)S(1)} %fusion.4), channel_id=1, source_target_pairs={{0,1},{1,0},{2,3},{3,2},{4,5},{5,4},{6,7},{7,6},{8,9},{9,8},{10,11... | collective-permute-start | bytes 1327112 | tf_op jit(solution)/shard_map/ppermute | solution.py:49
  242.0 13.4 %collective-permute-start.33 = (bf16[4,24,1152]{2,1,0:T(8,128)(2,1)S(1)}, bf16[4,24,1152]{2,1,0:T(8,128)(2,1)S(1)}, u32[]{:S(2)}, u32[]{:S(2)}) collective-permute-start(bf16[4,24,1152]{2,1,0:T(8,128)(2,1)S(1)} %fusion.14), channel_id=1, source_target_pairs={{0,1},{1,0},{2,3},{3,2},{4,5},{5,4},{6,7},{7,6},{8,9},{9,8},{10,11... | collective-permute-start | bytes 663560 | tf_op jit(solution)/shard_map/ppermute | solution.py:49
  252.9 6.5 %collective-permute-start.28 = (bf16[4,24,1152]{2,1,0:T(8,128)(2,1)S(1)}, bf16[4,24,1152]{2,1,0:T(8,128)(2,1)S(1)}, u32[]{:S(2)}, u32[]{:S(2)}) collective-permute-start(bf16[4,24,1152]{2,1,0:T(8,128)(2,1)S(1)} %fusion.13), channel_id=1, source_target_pairs={{0,4},{2,6},{4,0},{6,2},{8,12},{10,14},{12,8},{14,10},{16,20},{18,... | collective-permute-start | bytes 663560 | tf_op jit(solution)/shard_map/ppermute | solution.py:40
  255.6 7.9 %collective-permute-start.34 = (bf16[24,1152]{1,0:T(8,128)(2,1)S(1)}, bf16[24,1152]{1,0:T(8,128)(2,1)S(1)}, u32[]{:S(2)}, u32[]{:S(2)}) collective-permute-start(bf16[24,1152]{1,0:T(8,128)(2,1)S(1)} %get-tuple-element.109), channel_id=1, source_target_pairs={{0,8},{2,10},{4,12},{6,14},{8,16},{10,18},{12,20},{14,22},{16,24},... | collective-permute-start | bytes 165896 | tf_op jit(solution)/shard_map/ppermute | solution.py:36
  255.6 8.9 %collective-permute-start.36 = (bf16[24,1152]{1,0:T(8,128)(2,1)S(1)}, bf16[24,1152]{1,0:T(8,128)(2,1)S(1)}, u32[]{:S(2)}, u32[]{:S(2)}) collective-permute-start(bf16[24,1152]{1,0:T(8,128)(2,1)S(1)} %get-tuple-element.110), channel_id=1, source_target_pairs={{0,24},{2,26},{4,28},{6,30},{8,0},{10,2},{12,4},{14,6},{16,8},{18,... | collective-permute-start | bytes 165896 | tf_op jit(solution)/shard_map/ppermute | solution.py:36
  259.4 7.0 %collective-permute-start.35 = (bf16[24,1152]{1,0:T(8,128)(2,1)S(1)}, bf16[24,1152]{1,0:T(8,128)(2,1)S(1)}, u32[]{:S(2)}, u32[]{:S(2)}) collective-permute-start(bf16[24,1152]{1,0:T(8,128)(2,1)S(1)} %get-tuple-element.111), channel_id=1, source_target_pairs={{0,16},{2,18},{4,20},{6,22},{8,24},{10,26},{12,28},{14,30},{16,0},... | collective-permute-start | bytes 165896 | tf_op jit(solution)/shard_map/ppermute | solution.py:36
  259.5 6.9 %collective-permute-start.29 = (bf16[24,1152]{1,0:T(8,128)(2,1)S(1)}, bf16[24,1152]{1,0:T(8,128)(2,1)S(1)}, u32[]{:S(2)}, u32[]{:S(2)}) collective-permute-start(bf16[24,1152]{1,0:T(8,128)(2,1)S(1)} %get-tuple-element.106), channel_id=1, source_target_pairs={{0,8},{2,10},{4,12},{6,14},{8,16},{10,18},{12,20},{14,22},{16,24},... | collective-permute-start | bytes 165896 | tf_op jit(solution)/shard_map/ppermute | solution.py:36
  260.2 6.8 %collective-permute-start.31 = (bf16[24,1152]{1,0:T(8,128)(2,1)S(1)}, bf16[24,1152]{1,0:T(8,128)(2,1)S(1)}, u32[]{:S(2)}, u32[]{:S(2)}) collective-permute-start(bf16[24,1152]{1,0:T(8,128)(2,1)S(1)} %get-tuple-element.107), channel_id=1, source_target_pairs={{0,24},{2,26},{4,28},{6,30},{8,0},{10,2},{12,4},{14,6},{16,8},{18,... | collective-permute-start | bytes 165896 | tf_op jit(solution)/shard_map/ppermute | solution.py:36
  (35 other events, 308.7 us)

commit v3 on v0

v3 whole, which is shorter than its diff:
```python
from functools import partial

import jax
import jax.numpy as jnp
import numpy as np
from jax import lax
from jax.experimental import pallas as pl
from jax.experimental.pallas import tpu as pltpu
from jax.sharding import PartitionSpec as P

D = 768
HEADS = 12
HEAD = 64
WIN = 14
AREA = WIN * WIN
ROW = 16
R = WIN * ROW
PAIRS = HEADS // 2
LANES = 128
TABLE = 2 * WIN - 1
HALF = D // 2
STEP = 384
TIER = 3 * HALF
F32 = jnp.float32
BF16 = jnp.bfloat16
VMEM = pl.BlockSpec(memory_space=pltpu.VMEM)
SMEM = pl.BlockSpec(memory_space=pltpu.SMEM)
LIMIT = 20 * 2**20
CHEAP = pl.CostEstimate(flops=1, bytes_accessed=1, transcendentals=0)
SMALL = {"gain1": 0, "shift1": 6, "qbias": 12, "vbias": 18, "projb": 24, "gain2": 30, "shift2": 36, "downb": 42}
SMALL_TABLE = 48
SMALL_UP = SMALL_TABLE + HEAD


def shape_of(shape, kind):
    return jax.ShapeDtypeStruct(shape, kind)


def kernel_call(name, body, n_in, outs, *, smem=0, scratch=(), far=()):
    call = pl.pallas_call(
        body,
        name=name,
        in_specs=[SMEM] * smem + [VMEM] * (n_in - smem),
        out_specs=[VMEM] * len(outs),
        out_shape=[pltpu.VMEM(o.shape, o.dtype) for o in outs],
        scratch_shapes=list(scratch),
        compiler_params=pltpu.CompilerParams(vmem_limit_bytes=LIMIT),
        cost_estimate=CHEAP,
    )

    def run(*args):
        spaces = [pltpu.HBM if i in far else pltpu.VMEM for i in range(smem, n_in)]
        return call(*args[:smem], *map(pltpu.with_memory_space_constraint, args[smem:], spaces))

    return run


def after(value, *others):
    return lax.optimization_barrier((value,) + others)[0]


def dp_pairs(count, dz=0, dy=0, dc=0):
    depth = count // 4
    pairs = []
    for place in range(count):
        z, y, c = place // 4, place // 2 % 2, place % 2
        pairs.append((place, (z + dz) % depth * 4 + (y + dy) % 2 * 2 + (c + dc) % 2))
    return pairs


def move_z(value, step):
    return lax.ppermute(value, "dp", dp_pairs(lax.axis_size("dp"), dz=step))


def move_y(value):
    return lax.ppermute(value, "dp", dp_pairs(lax.axis_size("dp"), dy=1))


def move_c(value):
    return lax.ppermute(value, "dp", dp_pairs(lax.axis_size("dp"), dc=1))


def move_x(value, step=1):
    count = lax.axis_size("mp")
    return lax.ppermute(value, "mp", [(i, (i + step) % count) for i in range(count)])


def places():
    dp = lax.axis_index("dp")
    return dp // 4, dp // 2 % 2, dp % 2, lax.axis_index("mp")


def row_maps(count, wide):
    depth = count // 4
    place = np.arange(D)
    rows = D // (count * wide)
    block = place // rows
    att = [block % depth, block // depth % 2, block // (2 * depth) % wide, block // (2 * depth * wide), place % rows]
    rows = D // count
    block = place // rows
    feed = [block % depth, block // depth % 2, 0 * block, block // (2 * depth), place % rows]
    return np.stack(att + feed, axis=1).astype(np.int32)


def rows_from(maps_ref, start, rows, wide):
    depth = lax.axis_size("dp") // 4
    dp = lax.axis_index("dp")

    def turned(i, here, size):
        there = maps_ref[:, start + i : start + i + 1] + here
        return jnp.where(there >= size, there - size, there)

    block = (turned(0, dp // 4, depth) * 2 + turned(1, dp // 2 % 2, 2)) * 2 + turned(3, dp % 2, 2)
    if wide > 1:
        block = block * wide + turned(2, lax.axis_index("mp"), wide)
    return block * rows + maps_ref[:, start + 4 : start + 5]


def gather_z(part):
    depth = lax.axis_size("dp") // 4
    return jnp.concatenate([part] + [move_z(part, -s) for s in range(1, depth)])


def gather_near(line):
    wide = lax.axis_size("mp")
    return [move_x(line, -s) for s in range(1, wide)], move_y(line)


def gather_far(near):
    along_x, along_y = near
    half = along_y.shape[1] // 2
    left = [move_y(b[:, :half]) for b in along_x]
    right = [move_x(along_y[:, half:], -s) for s in range(1, lax.axis_size("mp"))]
    return left, right


def gather_join(line, near, far):
    blocks = [line, near[1]]
    for along_x, first, second in zip(near[0], *far):
        blocks += [along_x, jnp.concatenate([first, second], axis=1)]
    return jnp.concatenate(blocks)


def add_up(first, *others):
    total = first.astype(F32)
    for other in others:
        total = total + other.astype(F32)
    return total


def scatter_x(rows):
    wide = lax.axis_size("mp")
    size = rows.shape[0] // wide
    return add_up(rows[:size], *[move_x(rows[s * size : (s + 1) * size].astype(BF16), s) for s in range(1, wide)])


def scatter_y(rows, *others):
    size = rows.shape[0] // 2
    return add_up(rows[:size], after(move_y(rows[size:].astype(BF16)), *others))


def scatter_z(rows):
    depth = lax.axis_size("dp") // 4
    size = rows.shape[0] // depth
    return add_up(rows[:size], *[move_z(rows[s * size : (s + 1) * size].astype(BF16), s) for s in range(1, depth)])


def sum_small(flat):
    depth, wide = lax.axis_size("dp") // 4, lax.axis_size("mp")
    flat = flat + move_c(flat)
    flat = sum([move_x(flat, s) for s in range(1, wide)], flat)
    flat = flat + move_y(flat)
    return sum([move_z(flat, s) for s in range(1, depth)], flat)


def dot_nn(a, b):
    return lax.dot_general(a, b, (((1,), (0,)), ((), ())), preferred_element_type=F32)


def dot_nt(a, b):
    return lax.dot_general(a, b, (((1,), (1,)), ((), ())), preferred_element_type=F32)


def dot_tn(a, b):
    return lax.dot_general(a, b, (((0,), (0,)), ((), ())), preferred_element_type=F32)


def iota(shape, axis):
    return lax.broadcasted_iota(jnp.int32, shape, axis)


def norm_parts(rows_in):
    center = rows_in - jnp.mean(rows_in, axis=-1, keepdims=True)
    factor = lax.rsqrt(jnp.mean(center * center, axis=-1, keepdims=True) + 1e-06)
    return center * factor, factor


def norm_back(grad, unit, factor, gain):
    inner = grad * gain
    return factor * (
        inner
        - jnp.mean(inner, axis=-1, keepdims=True)
        - unit * jnp.mean(inner * unit, axis=-1, keepdims=True)
    )


def spread_rows():
    row, patch = iota((R, AREA), 0), iota((R, AREA), 1)
    return ((row % ROW < WIN) & (patch == row // ROW * WIN + row % ROW)).astype(F32).astype(BF16)


def row_masks():
    lane = iota((R, LANES), 1) % HEAD
    key = iota((R, LANES), 0)
    here = jnp.where(lane // ROW % 2 == 0, key // ROW, key % ROW)
    return (lane % ROW == here).astype(F32)


def offset_lanes(rows, base):
    lane = iota((rows, LANES), 1)
    in_h = (lane >= base) & (lane < base + ROW)
    in_w = (lane >= base + ROW) & (lane < base + 2 * ROW)
    return in_h, in_w


def query_offsets(table, base):
    in_h, in_w = offset_lanes(ROW, base)
    outs = []
    for a in range(WIN):
        group = table[a * ROW : (a + 1) * ROW]
        at_h = pltpu.roll(group, (HEAD - 13 + a) % LANES, 1)
        at_w = pltpu.roll(group, LANES - ROW + 1, 1, stride=1, stride_axis=0)
        both = jnp.where(in_h, at_h, jnp.where(in_w, at_w, 0.0))
        high = both.astype(BF16).astype(F32)
        outs.append(high + pltpu.roll(both - high, 2 * ROW, 1))
    return jnp.concatenate(outs, axis=0)


def offset_grads(grad, base):
    in_h, in_w = offset_lanes(R, base)
    column = iota((R, LANES), 0) % ROW
    from_w = jnp.where(in_w, grad, 0.0)
    for bit in (1, 2, 4, 8):
        from_w = jnp.where((ROW - 1 - column) & bit > 0, pltpu.roll(from_w, bit, 1), from_w)
    only_h = jnp.where(in_h, grad, 0.0)
    from_h = [pltpu.roll(only_h[a * ROW : (a + 1) * ROW], (HEAD + 13 - a) % LANES, 1) for a in range(WIN)]
    return jnp.concatenate(from_h, axis=0) + from_w


def table_places(kind):
    row, lane = iota((TABLE, LANES), 0), iota((TABLE, LANES), 1)
    start = 0 if kind == "h" else HEAD + ROW + 2
    return (lane - start == TABLE - 1 - row).astype(F32)


def pack_kernel(qkv_ref, proj_ref, gain1_ref, shift1_ref, projb_ref, gain2_ref, shift2_ref, downb_ref, qvb_ref, first_ref, second_ref, params_ref):
    for tier, out in enumerate((first_ref, second_ref)):
        for i in range(3):
            out[:, i * HALF : (i + 1) * HALF] = qkv_ref[:, i * D + tier * HALF : i * D + (tier + 1) * HALF]
    second_ref[:, TIER:] = proj_ref[...]
    for i, ref in enumerate((gain1_ref, shift1_ref, projb_ref, gain2_ref, shift2_ref, downb_ref)):
        params_ref[i : i + 1] = ref[...].astype(F32).reshape(1, D)
    params_ref[6:8] = qvb_ref[...].astype(F32)


def pack(qkv_weight, *args):
    rows = qkv_weight.shape[0]
    return kernel_call(
        "pack",
        pack_kernel, 9, [shape_of((rows, TIER), BF16), shape_of((rows, TIER + D), BF16), shape_of((8, D), F32)], far=range(9)
    )(qkv_weight, *args)


def prepare_kernel(
    count, wide, keep_ref, tokens_ref, grad_ref, maps_ref, params_ref, relh_ref, relw_ref, mask_ref, upb_ref,
    x_ref, a1_ref, turned_ref, g_ref, dm_ref, att_ref, feed_ref, table_ref, fill_ref, downb_ref, wideb_ref,
):
    wideb_ref[...] = upb_ref[...].astype(F32).reshape(wideb_ref.shape)
    spread = spread_rows()
    x = dot_nn(spread, tokens_ref[...])
    x_ref[...] = x.astype(BF16)
    grad = dot_nn(spread, grad_ref[...])
    g_ref[...] = grad.astype(BF16)
    dm = (jnp.where(keep_ref[0, 1] > 0, 1.0 / 0.9, 0.0).astype(F32) * grad).astype(BF16)
    dm_ref[...] = dm
    downb_ref[...] = jnp.sum(dm.astype(F32), axis=0, keepdims=True)
    source = iota((D, D), 1)
    att = (rows_from(maps_ref, 0, D // (count * wide), wide) == source).astype(F32).astype(BF16)
    att_ref[...] = att
    feed_ref[...] = (rows_from(maps_ref, 5, D // count, 1) == source).astype(F32).astype(BF16)
    unit, _ = norm_parts(x)
    a1 = (unit * params_ref[0:1] + params_ref[1:2]).astype(BF16)
    a1_ref[...] = dot_nt(a1, att).astype(BF16)
    turned_ref[...] = dot_nt(att, a1).astype(BF16)
    one = dot_tn(relh_ref[...], table_places("h").astype(BF16)) + dot_tn(relw_ref[...], table_places("w").astype(BF16))
    blank = jnp.zeros((HEAD, LANES), F32)
    table_ref[:HEAD, :] = jnp.concatenate([one, blank], axis=1).astype(BF16)
    table_ref[HEAD:, :] = jnp.concatenate([blank, pltpu.roll(one, HEAD, 1)], axis=1).astype(BF16)
    seen = dot_nt((mask_ref[...] > 0).astype(F32).astype(BF16), spread)
    key = iota((1, R), 1)
    fill_ref[...] = jnp.where(key % ROW >= WIN, -3e38, jnp.where(seen > 0.5, 0.0, -1e9))


def prepare(keep, tokens, grad, params, rel_h, rel_w, mask, upb):
    count, wide = lax.axis_size("dp"), lax.axis_size("mp")
    return kernel_call(
        "prepare",
        partial(prepare_kernel, count, wide),
        9,
        [
            shape_of((R, D), BF16), shape_of((R, D), BF16), shape_of((D, R), BF16), shape_of((R, D), BF16),
            shape_of((R, D), BF16), shape_of((D, D), BF16), shape_of((D, D), BF16),
            shape_of((LANES, 2 * LANES), BF16), shape_of((1, R), F32), shape_of((1, D), F32),
            shape_of((1, upb.shape[0]), F32),
        ],
        smem=1, far=(1, 2, 3, 5, 6, 7, 8),
    )(keep, tokens, grad, row_maps(count, wide), params, rel_h, rel_w, mask, upb)


def act_kernel(dm_ref, down_ref, out_ref):
    out_ref[...] = dot_nt(dm_ref[...], down_ref[...])


def act_grad(dm, down):
    return kernel_call("act", act_kernel, 2, [shape_of((R, down.shape[0]), F32)])(dm, down)[0]


def heads_forward(qkv_ref, tables, fill, p_ref, out):
    ones = row_masks()
    left = iota((R, LANES), 1) < HEAD
    for pair in range(PAIRS // 2):
        at = pair * LANES
        q2 = qkv_ref[:, at : at + LANES]
        k2 = qkv_ref[:, HALF + at : HALF + at + LANES].astype(F32)
        v2 = qkv_ref[:, 2 * HALF + at : 2 * HALF + at + LANES]
        products = dot_nn(q2, tables)
        q2 = q2.astype(F32) * HEAD**-0.5
        outs = []
        for side in range(2):
            mine = left if side == 0 else ~left
            offsets = query_offsets(products[:, side * LANES : (side + 1) * LANES], HEAD * (1 - side))
            q_aug = jnp.where(mine, q2, offsets).astype(BF16)
            k_aug = jnp.where(mine, k2, ones).astype(BF16)
            scores = dot_nt(q_aug, k_aug)
            scores = jnp.where(fill < 0.0, fill, scores)
            expo = jnp.exp(scores - jnp.max(scores, axis=-1, keepdims=True))
            probs = (expo / jnp.sum(expo, axis=-1, keepdims=True)).astype(BF16)
            p_ref[2 * pair + side] = probs
            outs.append(dot_nn(probs, v2))
        out(at, jnp.where(left, outs[0], outs[1]).astype(BF16))


def project(a1_ref, own_ref, other_ref, bias, qkv_ref):
    total = dot_nn(a1_ref[:, :HALF], own_ref[:, :TIER]) + dot_nn(a1_ref[:, HALF:], other_ref[:, :TIER])
    qkv_ref[...] = (total + bias).astype(BF16)


def tier_bias(params_ref, tier):
    at = tier * HALF
    return jnp.concatenate(
        [
            params_ref[6:7, at : at + HALF],
            jnp.zeros((1, HALF), F32),
            params_ref[7:8, at : at + HALF],
        ],
        axis=1,
    )


def attend_first_kernel(a1_ref, own_ref, other_ref, params_ref, table_ref, fill_ref, qkv_ref, p_ref, o_ref):
    project(a1_ref, own_ref, other_ref, tier_bias(params_ref, 0), qkv_ref)

    def out(at, value):
        o_ref[:, at : at + LANES] = value

    heads_forward(qkv_ref, table_ref[...], fill_ref[...], p_ref, out)


def attend_first(*args):
    return kernel_call(
        "attend1",
        attend_first_kernel,
        6,
        [shape_of((R, TIER), BF16), shape_of((HEADS // 2, R, R), BF16), shape_of((R, HALF), BF16)],
    )(*args)


def attend_second_kernel(
    keep_ref, a1_ref, own_ref, other_ref, params_ref, table_ref, fill_ref, first_ref, x_ref, att_ref,
    qkv_ref, p_ref, turned_ref, mid_ref, a2_ref,
    o_ref,
):
    project(a1_ref, own_ref, other_ref, tier_bias(params_ref, 1), qkv_ref)
    o_ref[:, :HALF] = first_ref[...]

    def out(at, value):
        o_ref[:, HALF + at : HALF + at + LANES] = value

    heads_forward(qkv_ref, table_ref[...], fill_ref[...], p_ref, out)
    moved = dot_nt(o_ref[...], att_ref[...]).astype(BF16)
    branch = dot_nn(moved[:, :HALF], own_ref[:, TIER:]) + dot_nn(moved[:, HALF:], other_ref[:, TIER:])
    turned_ref[...] = dot_nt(att_ref[...], o_ref[...]).astype(BF16)
    rate = jnp.where(keep_ref[0, 0] > 0, 1.0 / 0.9, 0.0).astype(F32)
    middle = x_ref[...].astype(F32) + rate * (branch + params_ref[2:3])
    mid_ref[...] = middle
    unit, _ = norm_parts(middle)
    a2_ref[...] = (unit * params_ref[3:4] + params_ref[4:5]).astype(BF16)


def attend_second(*args):
    return kernel_call(
        "attend2",
        attend_second_kernel,
        10,
        [
            shape_of((R, TIER), BF16), shape_of((HEADS // 2, R, R), BF16), shape_of((D, R), BF16),
            shape_of((R, D), F32), shape_of((R, D), BF16),
        ],
        smem=1, scratch=[pltpu.VMEM((R, D), BF16)],
    )(*args)


def feed_kernel(a2_ref, up_ref, upb_ref, gact_ref, g_ref, dh_ref, da2_ref):
    total = None
    for at in range(0, up_ref.shape[1], STEP):
        here = slice(at, at + STEP)
        hidden = dot_nn(a2_ref[...], up_ref[:, here]) + upb_ref[:, here]
        phi = 0.5 + 0.5 * lax.erf(hidden * 0.5**0.5)
        g_ref[:, here] = (hidden * phi).astype(BF16)
        slope = phi + hidden * (jnp.exp(-0.5 * hidden * hidden) * 0.3989422804014327)
        dh = (gact_ref[:, here] * slope).astype(BF16)
        dh_ref[:, here] = dh
        part = dot_nt(dh, up_ref[:, here])
        total = part if total is None else total + part
    da2_ref[...] = total.astype(da2_ref.dtype)


def feed(a2, up, upb, gact, kind):
    hidden = up.shape[1]
    return kernel_call(
        "feed",
        feed_kernel,
        4,
        [shape_of((R, hidden), BF16), shape_of((R, hidden), BF16), shape_of((R, D), kind)],
    )(a2, up, upb, gact)


def feed_weights_kernel(count, map_ref, down_ref, *refs):
    dms, acts, a2s, dhs = (refs[i * count : (i + 1) * count] for i in range(4))
    downk_ref, downs_ref, upk_ref, ups_ref, sum_ref, *outs = refs[4 * count :]
    for lefts, rights, keep_ref, send_ref in ((dms, acts, downk_ref, downs_ref), (a2s, dhs, upk_ref, ups_ref)):
        turned = [dot_nt(map_ref[...], left[...]).astype(BF16) for left in lefts]
        for at in range(0, keep_ref.shape[1], STEP):
            here = slice(at, at + STEP)
            total = dot_nn(turned[0], rights[0][:, here])
            for j in range(1, count):
                total = total + dot_nn(turned[j], rights[j][:, here])
            keep_ref[:, here] = total[:HALF].astype(BF16)
            send_ref[:, here] = total[HALF:].astype(BF16)
    for j in range(count):
        outs[j][...] = dot_nn(acts[j][...], down_ref[...]).astype(outs[j].dtype)
    sums = jnp.sum(dhs[0][...].astype(F32), axis=0, keepdims=True)
    for j in range(1, count):
        sums = sums + jnp.sum(dhs[j][...].astype(F32), axis=0, keepdims=True)
    sum_ref[...] = sums


def feed_weights(row_map, down, dms, acts, a2s, dhs):
    count = len(dms)
    columns = acts[0].shape[1]
    return kernel_call(
        "feedw",
        partial(feed_weights_kernel, count),
        2 + 4 * count,
        [shape_of((HALF, columns), BF16)] * 4
        + [shape_of((1, columns), F32)]
        + [shape_of((R, D), F32 if j == 0 else BF16) for j in range(count)],
    )(row_map, down, *dms, *acts, *a2s, *dhs)


def heads_back(qkv_ref, p_ref, do_at, tables, dqkv_ref):
    ones = row_masks()
    left = iota((R, LANES), 1) < HEAD
    table_grad = jnp.zeros((LANES, 2 * LANES), F32)
    for pair in range(PAIRS // 2):
        at = pair * LANES
        q2 = qkv_ref[:, at : at + LANES]
        q_wide = q2.astype(F32)
        k2 = qkv_ref[:, HALF + at : HALF + at + LANES].astype(F32)
        v2 = qkv_ref[:, 2 * HALF + at : 2 * HALF + at + LANES]
        do2 = do_at(at).astype(F32)
        dq2 = dk2 = dv2 = None
        offsets = []
        for side in range(2):
            mine = left if side == 0 else ~left
            probs = p_ref[2 * pair + side]
            do_mine = jnp.where(mine, do2, 0.0).astype(BF16)
            dv = dot_tn(probs, do_mine)
            dp = dot_nt(do_mine, v2)
            wide = probs.astype(F32)
            ds = (wide * (dp - jnp.sum(wide * dp, axis=-1, keepdims=True))).astype(BF16)
            k_aug = jnp.where(mine, k2, ones).astype(BF16)
            dq_aug = dot_nn(ds, k_aug)
            offsets.append(offset_grads(dq_aug, HEAD * (1 - side)))
            dk = dot_tn(ds, jnp.where(mine, q_wide, 0.0).astype(BF16))
            if side == 0:
                dq2, dk2, dv2 = dq_aug, dk, dv
            else:
                dq2, dk2, dv2 = jnp.where(mine, dq_aug, dq2), dk2 + dk, dv2 + dv
        spread = jnp.concatenate(offsets, axis=1).astype(BF16)
        dq2 = dq2 * HEAD**-0.5 + dot_nt(spread, tables)
        table_grad = table_grad + dot_tn(q2, spread)
        dqkv_ref[:, at : at + LANES] = dq2.astype(BF16)
        dqkv_ref[:, HALF + at : HALF + at + LANES] = (dk2 * HEAD**-0.5).astype(BF16)
        dqkv_ref[:, 2 * HALF + at : 2 * HALF + at + LANES] = dv2.astype(BF16)
    return table_grad[:HEAD, :LANES] + pltpu.roll(table_grad[HEAD:, LANES:], HEAD, 1)


def back_norm_kernel(
    keep_ref, da2_ref, got_ref, mid_ref, g_ref, params_ref, own_ref, other_ref, att_ref, dmid_ref, dy_ref, do_ref, sums_ref
):
    da2 = da2_ref[...] + got_ref[...].astype(F32)
    unit, factor = norm_parts(mid_ref[...])
    dmid = g_ref[...].astype(F32) + norm_back(da2, unit, factor, params_ref[3:4])
    dmid_ref[...] = dmid
    rate = jnp.where(keep_ref[0, 0] > 0, 1.0 / 0.9, 0.0).astype(F32)
    dy = (rate * dmid).astype(BF16)
    dy_ref[...] = dy
    moved = jnp.concatenate(
        [dot_nt(dy, own_ref[:, TIER:]).astype(BF16), dot_nt(dy, other_ref[:, TIER:]).astype(BF16)], axis=1
    )
    do_ref[...] = dot_nn(moved, att_ref[...]).astype(BF16)
    sums_ref[0:1] = jnp.sum(dy.astype(F32), axis=0, keepdims=True)
    sums_ref[1:2] = jnp.sum(da2 * unit, axis=0, keepdims=True)
    sums_ref[2:3] = jnp.sum(da2, axis=0, keepdims=True)


def back_norm(*args):
    return kernel_call(
        "backnorm",
        back_norm_kernel,
        9,
        [shape_of((R, D), F32), shape_of((R, D), BF16), shape_of((R, D), BF16), shape_of((3, D), F32)],
        smem=1,
    )(*args)


def back_first_kernel(
    dy_ref, do_ref, turned_ref, o_ref, qkv_ref, p_ref, table_ref,
    dqkv_ref, weights_ref, send_ref, sums_ref, tablegrad_ref,
):
    tablegrad_ref[...] = heads_back(qkv_ref, p_ref, lambda at: do_ref[:, at : at + LANES], table_ref[...], dqkv_ref)
    for s, out in enumerate((weights_ref, send_ref)):
        rows = slice(s * HALF, (s + 1) * HALF)
        out[:, :TIER] = dot_nn(turned_ref[rows], dqkv_ref[...]).astype(BF16)
        out[:, TIER:] = dot_nn(o_ref[rows], dy_ref[...]).astype(BF16)
    sums_ref[:, :HALF] = jnp.sum(dqkv_ref[:, :HALF].astype(F32), axis=0, keepdims=True)
    sums_ref[:, HALF:] = jnp.sum(dqkv_ref[:, 2 * HALF :].astype(F32), axis=0, keepdims=True)


def back_first(*args):
    return kernel_call(
        "back1",
        back_first_kernel,
        7,
        [
            shape_of((R, TIER), BF16), shape_of((HALF, TIER + D), BF16), shape_of((HALF, TIER + D), BF16),
            shape_of((1, D), F32), shape_of((HEAD, LANES), F32),
        ],
    )(*args)


def back_second_kernel(
    do_ref, turned_ref, qkv_ref, p_ref, table_ref, dqkv_ref, keep_ref, send_ref, sums_ref, tablegrad_ref
):
    tablegrad_ref[...] = heads_back(qkv_ref, p_ref, lambda at: do_ref[:, HALF + at : HALF + at + LANES], table_ref[...], dqkv_ref)
    for s, out in enumerate((keep_ref, send_ref)):
        out[...] = dot_nn(turned_ref[s * HALF : (s + 1) * HALF], dqkv_ref[...]).astype(BF16)
    sums_ref[:, :HALF] = jnp.sum(dqkv_ref[:, :HALF].astype(F32), axis=0, keepdims=True)
    sums_ref[:, HALF:] = jnp.sum(dqkv_ref[:, 2 * HALF :].astype(F32), axis=0, keepdims=True)


def back_second(*args):
    return kernel_call(
        "back2",
        back_second_kernel,
        5,
        [
            shape_of((R, TIER), BF16), shape_of((HALF, TIER), BF16), shape_of((HALF, TIER), BF16),
            shape_of((1, D), F32), shape_of((HEAD, LANES), F32),
        ],
    )(*args)


def finish_kernel(
    wide, keep_ref, dq1_ref, dq2_ref, own1_ref, other1_ref, own2_ref, other2_ref, att_ref, x_ref, dmid_ref,
    params_ref, mid_ref, m_ref, mgot_ref, downb_ref, upb_ref, sums0_ref, sums1_ref, sums2_ref, tab1_ref, tab2_ref,
    dx_ref, result_ref, small_ref,
):
    halves = []
    for first, second in ((own1_ref, own2_ref), (other1_ref, other2_ref)):
        halves.append(dot_nt(dq1_ref[...], first[...]) + dot_nt(dq2_ref[...], second[:, :TIER]))
    moved = jnp.concatenate(halves, axis=1)
    high = moved.astype(BF16)
    low = (moved - high.astype(F32)).astype(BF16)
    da1 = dot_nn(high, att_ref[...]) + dot_nn(low, att_ref[...])
    unit, factor = norm_parts(x_ref[...].astype(F32))
    dx = (dmid_ref[...] + norm_back(da1, unit, factor, params_ref[0:1])).astype(BF16)
    rate = jnp.where(keep_ref[0, 1] > 0, 1.0 / 0.9, 0.0).astype(F32)
    total = m_ref[...] + mgot_ref[...].astype(F32) + params_ref[5:6]
    result = (mid_ref[...] + rate * total).astype(BF16)
    spread = spread_rows()
    dx_ref[...] = dot_tn(spread, dx).astype(BF16)
    result_ref[...] = dot_tn(spread, result).astype(BF16)

    def put(name, value):
        for i in range(D // LANES):
            small_ref[SMALL[name] + i : SMALL[name] + i + 1] = value[:, i * LANES : (i + 1) * LANES]

    put("gain1", jnp.sum(da1 * unit, axis=0, keepdims=True))
    put("shift1", jnp.sum(da1, axis=0, keepdims=True))
    put("projb", sums0_ref[0:1])
    put("gain2", sums0_ref[1:2])
    put("shift2", sums0_ref[2:3])
    put("qbias", jnp.concatenate([sums1_ref[:, :HALF], sums2_ref[:, :HALF]], axis=1))
    put("vbias", jnp.concatenate([sums1_ref[:, HALF:], sums2_ref[:, HALF:]], axis=1))
    put("downb", downb_ref[...])
    small_ref[SMALL_TABLE : SMALL_TABLE + HEAD] = tab1_ref[...] + tab2_ref[...]
    rows = upb_ref.shape[1] // LANES
    for m in range(wide):
        for i in range(rows):
            value = upb_ref[:, i * LANES : (i + 1) * LANES]
            at = SMALL_UP + m * rows + i
            small_ref[at : at + 1] = jnp.where(lax.axis_index("mp") == m, value, 0.0)


def finish(wide, rows, *args):
    return kernel_call(
        "finish",
        partial(finish_kernel, wide),
        21,
        [shape_of((AREA, D), BF16), shape_of((AREA, D), BF16), shape_of((rows, LANES), F32)],
        smem=1,
    )(*args)


def per_device(
    tokens, ln1_gain, ln1_bias, qkv_weight, qv_bias, rel_pos_h, rel_pos_w, proj_weight, proj_bias,
    ln2_gain, ln2_bias, fc1_weight, fc1_bias, fc2_weight, fc2_bias, keep_mask, key_mask, out_grad,
):
    wide = lax.axis_size("mp")
    hidden = fc1_weight.shape[1]
    first, second, params = pack(
        qkv_weight, proj_weight, ln1_gain, ln1_bias, proj_bias, ln2_gain, ln2_bias, fc2_bias, qv_bias
    )
    line1 = gather_z(first)
    line2 = gather_z(second)
    rows_in, a1, a1_turned, grad_out, dm, att_map, feed_map, tables, fill, downb, upb = prepare(
        keep_mask, tokens, out_grad, params, rel_pos_h, rel_pos_w, key_mask, fc1_bias
    )
    dms = [dm] + [move_x(dm, -s) for s in range(1, wide)]
    line1 = after(line1, a1)
    near1 = gather_near(line1)
    gacts = [act_grad(dm, fc2_weight)]
    near1, line2, dms, gacts = lax.optimization_barrier((near1, line2, dms, gacts))
    far1 = gather_far(near1)
    near2 = gather_near(line2)
    for v in dms[1:]:
        gacts.append(act_grad(after(v, gacts[-1]), fc2_weight))
    far1, near2, gacts = lax.optimization_barrier((far1, near2, gacts))
    own1 = gather_join(line1, near1, far1)
    other1 = move_c(own1)
    far2 = gather_far(near2)
    qkv1, probs1, att1 = attend_first(a1, own1, other1, params, tables, fill)
    far2, att1 = lax.optimization_barrier((far2, att1))
    own2 = gather_join(line2, near2, far2)
    other2 = move_c(own2)
    qkv2, probs2, att_turned, middle, a2 = attend_second(
        keep_mask, a1, own2, other2, params, tables, fill, att1, rows_in, att_map
    )

    a2s = [a2] + [move_x(a2, -s) for s in range(1, wide)]
    fed = [feed(a2, fc1_weight, upb, gacts[0], F32)]
    for j in range(1, wide):
        fed.append(feed(after(a2s[j], fed[-1][2]), fc1_weight, upb, gacts[j], BF16))
    da2 = fed[0][2]
    got = [move_x(fed[s][2], s) for s in range(1, wide)]
    down_keep, down_send, up_keep, up_send, upb_sum, *outs = feed_weights(
        after(feed_map, fed[-1][2]), fc2_weight, dms, [f[0] for f in fed], a2s, [f[1] for f in fed]
    )
    got, down_send, up_send, outs = lax.optimization_barrier((got, down_send, up_send, outs))
    got = got[0] if wide == 2 else add_up(*got)
    down_rows = add_up(down_keep, move_c(down_send))
    up_rows = add_up(up_keep, move_c(up_send))
    dmid, dy, do, sums0 = back_norm(keep_mask, da2, got, middle, grad_out, params, own2, other2, att_map)
    down_rows, up_rows, do = lax.optimization_barrier((down_rows, up_rows, do))
    out_got = [move_x(outs[s], s) for s in range(1, wide)]
    dqkv1, keep1, send1, sums1, tab1 = back_first(dy, do, a1_turned, att_turned, qkv1, probs1, tables)
    rows1 = add_up(keep1, move_c(send1))
    rows1, do = lax.optimization_barrier((rows1, do))
    down_rows = scatter_y(down_rows)
    out_got = out_got[0] if wide == 2 else add_up(*out_got)
    rows1 = scatter_x(rows1)
    down_grad = scatter_z(down_rows)
    dqkv2, keep2, send2, sums2, tab2 = back_second(do, a1_turned, qkv2, probs2, tables)
    up_rows = scatter_y(up_rows, send2)
    rows2 = add_up(keep2, move_c(send2))
    rows1, rows2, dqkv2 = lax.optimization_barrier((rows1, rows2, dqkv2))
    rows1 = scatter_y(rows1)
    rows2 = scatter_x(rows2)
    up_grad = scatter_z(up_rows)
    small_rows = SMALL_UP + wide * hidden // LANES
    small_rows += -small_rows % 8
    grad_in, result, small = finish(
        wide, small_rows, keep_mask, dqkv1, dqkv2, own1, other1, own2, other2, att_map, rows_in, dmid, params,
        middle, outs[0], out_got, downb, upb_sum, sums0, sums1, sums2, tab1, tab2,
    )
    rows1, rows2, small = lax.optimization_barrier((rows1, rows2, small))
    rows1 = scatter_z(rows1)
    rows2 = scatter_z(scatter_y(rows2))
    small = sum_small(small)

    pieces = [
        piece
        for i in range(3)
        for piece in (rows1[:, i * HALF : (i + 1) * HALF], rows2[:, i * HALF : (i + 1) * HALF])
    ]
    qkv_grad = jnp.concatenate(pieces, axis=1)
    proj_grad = rows1[:, TIER:]

    def vector(name):
        return small[SMALL[name] : SMALL[name] + D // LANES].reshape(D)

    table = small[SMALL_TABLE : SMALL_TABLE + HEAD]
    relh_grad = table[:, :TABLE].T[::-1]
    relw_grad = table[:, HEAD + ROW + 2 : HEAD + ROW + 2 + TABLE].T[::-1]
    up_all = small[SMALL_UP : SMALL_UP + wide * hidden // LANES].reshape(-1)
    size = hidden // lax.axis_size("dp")
    up_bias_grad = lax.dynamic_slice(up_all, (lax.axis_index("mp") * hidden + lax.axis_index("dp") * size,), (size,))
    qv_grad = jnp.stack([vector("qbias"), vector("vbias")])
    return (
        result, grad_in, vector("gain1"), vector("shift1"), qkv_grad, qv_grad, relh_grad, relw_grad, proj_grad,
        vector("projb"), vector("gain2"), vector("shift2"), up_grad, up_bias_grad, down_grad.T, vector("downb"),
    )


def solution(mesh):
    in_specs = (
        P(("dp", "mp"), None),
        P(),
        P(),
        P(("dp", "mp"), None),
        P(),
        P(),
        P(),
        P(("dp", "mp"), None),
        P(),
        P(),
        P(),
        P(None, "mp"),
        P("mp"),
        P("mp", None),
        P(),
        P(("dp", "mp"), None),
        P(("dp", "mp"), None),
        P(("dp", "mp"), None),
    )
    out_specs = (
        P(("dp", "mp"), None),
        P(("dp", "mp"), None),
        P(),
        P(),
        P(("dp", "mp"), None),
        P(),
        P(),
        P(),
        P(("dp", "mp"), None),
        P(),
        P(),
        P(),
        P("dp", "mp"),
        P(("mp", "dp")),
        P("mp", "dp"),
        P(),
    )
    return jax.shard_map(
        per_device, mesh=mesh, in_specs=in_specs, out_specs=out_specs, check_vma=False
    )
```

time: 558 us -> 180 us (0.32); the launches traced: 547 us -> 180 us
  waiting for transfers between devices: 172 us -> 59.5 us
  blocking collectives: 108 us -> 0 us
  matrix products: 90.3 us -> 0 us
  local copies, waits for them, and re-layouts: 103 us -> 14.8 us
  starting transfers between devices: 4.98 us -> 53.6 us
  other arithmetic: 51.9 us -> 10.2 us
  Pallas kernels: 0 us -> 40.2 us
  between operations: 16.3 us -> 1.33 us
    reduce_scatter x4 -> x0, waiting for transfers between devices: 131 us -> none  [the longest x1 125 us: per_device(): lax.psum_scatter(qkv_w_grad, ('dp', 'mp'), scatter_dimension=0, tiled=True)]
    dot_general x28 -> x0, matrix products: 90.3 us -> none  [the longest x1 10.9 us: attn_scores(): jnp.einsum('nabhc,nxyhc->nhabxy', queries, key_part, preferred_element_ty...]
    ppermute x0 -> x48, waiting for transfers between devices: none -> 59.5 us  [the longest x11 33.6 us: move_x(): lax.ppermute(value, 'mp', [(i, (i + step) % count) for i in range(count)])]
    ppermute x0 -> x48, starting transfers between devices: none -> 53.6 us  [the longest x21 34.2 us: move_z(): return lax.ppermute(value, 'dp', dp_pairs(lax.axis_size('dp'), dz=step))]
    unnamed x2 -> x0, blocking collectives: 48.3 us -> none
    pallas_call x0 -> x13, Pallas kernels: none -> 40.2 us  [run(): call(*args[:smem], *map(pltpu.with_memory_space_constraint, args[smem:],...]
    all_gather x2 -> x0, waiting for transfers between devices: 39.3 us -> none  [the longest x1 39.3 us: per_device(): lax.all_gather(qkv_weight, ('dp', 'mp'), axis=0, tiled=True)]
    psum x1 -> x0, blocking collectives: 39.1 us -> none  [per_device(): lax.psum((gain_one_grad, shift_one_grad, qv_grad, relh_grad, relw_grad, p...]
  transfers between devices with their start and end apart: 8 -> 48, of which waited for: 3 -> 21; matrix products, arithmetic and copies ran while one was open for 44% -> 6% of each run, Pallas kernels for 0% -> 18%
where the time goes in v3:
time: 180 us
  waiting for transfers between devices  59.5 us (33%)
  starting transfers between devices  53.6 us (30%)
  Pallas kernels  40.2 us (22%)
  local copies, waits for them, and re-layouts  14.8 us (8%)
  other arithmetic  10.2 us (6%)
    pallas_call x13, Pallas kernels, run(): call(*args[:smem], *map(pltpu.with_memory_space_constraint, args[smem:],...  40.2 us
    ppermute x21, starting transfers between devices, move_z(): return lax.ppermute(value, 'dp', dp_pairs(lax.axis_size('dp'), dz=step))  34.2 us
    ppermute x11, waiting for transfers between devices, move_x(): lax.ppermute(value, 'mp', [(i, (i + step) % count) for i in range(count)])  33.6 us
    ppermute x21, waiting for transfers between devices, move_z(): return lax.ppermute(value, 'dp', dp_pairs(lax.axis_size('dp'), dz=step))  13.7 us
    ppermute x9, starting transfers between devices, move_y(): return lax.ppermute(value, 'dp', dp_pairs(lax.axis_size('dp'), dy=1))  10.1 us
    unnamed x73, local copies, waits for them, and re-layouts  8.66 us
    ppermute x11, starting transfers between devices, move_x(): lax.ppermute(value, 'mp', [(i, (i + step) % count) for i in range(count)])  8.48 us
    ppermute x9, waiting for transfers between devices, move_y(): return lax.ppermute(value, 'dp', dp_pairs(lax.axis_size('dp'), dy=1))  8.45 us
  transfers between devices with their start and end apart: 48, of which 21 were waited for; matrix products, arithmetic and copies ran while one was open for 6% of the time, Pallas kernels for 18%

profile of v3, /device:TPU:0, one launch (start us, length us, event | category | flops | bytes accessed | tf_op | source)
XLA Modules:
  0.0 179.6 jit_solution(5557517079305382384)
XLA Ops:
  1.7 5.1 %collective-permute-start = (bf16[24,1152]{1,0:T(8,128)(2,1)S(1)}, bf16[24,1152]{1,0:T(8,128)(2,1)S(1)}, u32[]{:S(2)}, u32[]{:S(2)}) collective-permute-start(bf16[24,1152]{1,0:T(8,128)(2,1)S(1)} %get-tuple-element.106), channel_id=1, source_target_pairs={{0,24},{2,26},{4,28},{6,30},{8,0},{10,2},{12,4},{14,6},{16,8},{18,... | collective-permute-start | bytes 165896 | tf_op jit(solution)/shard_map/ppermute | solution.py:72
  7.8 2.8 %collective-permute-start.5 = (bf16[24,1920]{1,0:T(8,128)(2,1)S(1)}, bf16[24,1920]{1,0:T(8,128)(2,1)S(1)}, u32[]{:S(2)}, u32[]{:S(2)}) collective-permute-start(bf16[24,1920]{1,0:T(8,128)(2,1)S(1)} %get-tuple-element.108), channel_id=1, source_target_pairs={{0,24},{2,26},{4,28},{6,30},{8,0},{10,2},{12,4},{14,6},{16,8},{18,... | collective-permute-start | bytes 276488 | tf_op jit(solution)/shard_map/ppermute | solution.py:72
  12.4 3.5 %prepare.1 = (bf16[224,768]{1,0:T(8,128)(2,1)S(1)}, bf16[224,768]{1,0:T(8,128)(2,1)S(1)}, bf16[768,224]{1,0:T(8,128)(2,1)S(1)}, bf16[224,768]{1,0:T(8,128)(2,1)S...) custom-call(s32[1,2]{1,0:T(1,128)S(1)} %copy-done.27, ...), custom_call_target="tpu_custom_call" | custom-call | flops 1 | bytes 1 | tf_op jit(solution)/shard_map/prepare/pallas_call | solution.py:53
  15.9 2.2 %copy-done = bf16[1536,768]{1,0:T(8,128)(2,1)S(1)} copy-done((bf16[1536,768]{1,0:T(8,128)(2,1)S(1)}, bf16[1536,768]{1,0:T(8,128)(2,1)}, u32[]{:S(2)}) %copy-start) | copy-done | bytes 2359320
  19.2 1.6 collective-permute-start.8
  21.4 1.5 collective-permute-start.4
  22.9 2.6 %collective-permute-done.7 = bf16[24,1920]{1,0:T(8,128)(2,1)S(1)} collective-permute-done((bf16[24,1920]{1,0:T(8,128)(2,1)S(1)}, bf16[24,1920]{1,0:T(8,128)(2,1)S(1)}, u32[]{:S(2)}, u32[]{:S(2)}) %collective-permute-start.7) | collective-permute-done | bytes 92192 | tf_op jit(solution)/shard_map/ppermute | solution.py:72
  25.6 6.8 %collective-permute-done.3 = bf16[96,1152]{1,0:T(8,128)(2,1)S(1)} collective-permute-done((bf16[96,1152]{1,0:T(8,128)(2,1)S(1)}, bf16[96,1152]{1,0:T(8,128)(2,1)S(1)}, u32[]{:S(2)}, u32[]{:S(2)}) %collective-permute-start.3) | collective-permute-done | bytes 221216 | tf_op jit(solution)/shard_map/ppermute | solution.py:85
  32.4 1.5 collective-permute-start.11
  33.9 1.5 collective-permute-start.12
  37.6 5.5 %collective-permute-done.10 = bf16[96,576]{1,0:T(8,128)(2,1)S(1)} collective-permute-done((bf16[96,576]{1,0:T(8,128)(2,1)S(1)}, bf16[96,576]{1,0:T(8,128)(2,1)S(1)}, u32[]{:S(2)}, u32[]{:S(2)}) %collective-permute-start.10) | collective-permute-done | bytes 110624 | tf_op jit(solution)/shard_map/ppermute | solution.py:85
  44.5 1.6 collective-permute-start.13
  46.9 3.3 %attend1.1 = (bf16[224,1152]{1,0:T(8,128)(2,1)S(1)}, bf16[6,224,224]{2,1,0:T(8,128)(2,1)S(1)}, bf16[224,384]{1,0:T(8,128)(2,1)S(1)}) custom-call(bf16[224,768]{1,0:T(8,128)(2,1)S(1)} %get-tuple-element.105.a1_ref, bf16[384,1152]{1,0:T(8,128)(2,1)S(1)} %fusion.1.own_ref.own1_ref, bf16[384,1152]{1,0:T(8,128)(2,1)S(1)} %collective-permute-done.15.other_ref.other1_ref, ...), custom_call_target="tpu_custom_call" | custom-call | flops 1 | bytes 1 | tf_op jit(solution)/shard_map/attend1/pallas_call | solution.py:53
  50.2 1.6 collective-permute-done.13
  53.6 3.3 %collective-permute-done.16.other_ref.other2_ref = bf16[384,1920]{1,0:T(8,128)(2,1)S(1)} collective-permute-done((bf16[384,1920]{1,0:T(8,128)(2,1)S(1)}, bf16[384,1920]{1,0:T(8,128)(2,1)S(1)}, u32[]{:S(2)}, u32[]{:S(2)}) %collective-permute-start.16) | collective-permute-done | bytes 1474592 | tf_op jit(solution)/shard_map/ppermute | solution.py:80
  56.8 5.1 %attend2.1 = (bf16[224,1152]{1,0:T(8,128)(2,1)S(1)}, bf16[6,224,224]{2,1,0:T(8,128)(2,1)S(1)}, bf16[768,224]{1,0:T(8,128)(2,1)S(1)}, f32[224,768]{1,0:T(8,128)S(1)}, bf16[224,768]{1,0:T(8,128)(2,1)S(1)}) custom-call(s32[1,2]{1,0:T(1,128)S(1)} %copy-done.28, bf16[224,768]{1,0:T(8,128)(2,1)S(1)} %get-tuple-element.105.a1_ref, ...), custom_call_target="tpu_custom_call" | custom-call | flops 1 | bytes 1 | tf_op jit(solution)/shard_map/attend2/pallas_call | solution.py:53
  62.6 2.1 %feed.2 = (bf16[224,1536]{1,0:T(8,128)(2,1)S(1)}, bf16[224,1536]{1,0:T(8,128)(2,1)S(1)}, f32[224,768]{1,0:T(8,128)S(1)}) custom-call(bf16[224,768]{1,0:T(8,128)(2,1)S(1)} %get-tuple-element.128.a2_ref.refs_4_, bf16[768,1536]{1,0:T(8,128)(2,1)S(1)} %copy-done.4, f32[1,1536]{1,0:T(1,128)S(1)} %get-tuple-element.129.upb_ref, f32[224,1536]{1,0:T(8,128)S(1)} %act.2.gact_ref), custom_call_target="tpu_custom_call" | custom-call | flops 1 | bytes 1 | tf_op jit(solution)/shard_map/feed/pallas_call | solution.py:53
  64.7 7.5 %collective-permute-done.17.a2_ref.refs_5_ = bf16[224,768]{1,0:T(8,128)(2,1)S(1)} collective-permute-done((bf16[224,768]{1,0:T(8,128)(2,1)S(1)}, bf16[224,768]{1,0:T(8,128)(2,1)S(1)}, u32[]{:S(2)}, u32[]{:S(2)}) %collective-permute-start.17) | collective-permute-done | bytes 344096 | tf_op jit(solution)/shard_map/ppermute | solution.py:85
  72.1 2.1 %feed.3 = (bf16[224,1536]{1,0:T(8,128)(2,1)S(1)}, bf16[224,1536]{1,0:T(8,128)(2,1)S(1)}, bf16[224,768]{1,0:T(8,128)(2,1)S(1)}) custom-call(bf16[224,768]{1,0:T(8,128)(2,1)S(1)} %collective-permute-done.17.a2_ref.refs_5_, bf16[768,1536]{1,0:T(8,128)(2,1)S(1)} %copy-done.4, f32[1,1536]{1,0:T(1,128)S(1)} %get-tuple-element.129.upb_ref, f32[224,1536]{1,0:T(8,128)S(1)} %act.3.gact_ref), custom_call_target="tpu_custom_call" | custom-call | flops 1 | bytes 1 | tf_op jit(solution)/shard_map/feed/pallas_call | solution.py:53
  74.8 6.1 %feedw.1 = (bf16[384,1536]{1,0:T(8,128)(2,1)S(1)}, bf16[384,1536]{1,0:T(8,128)(2,1)S(1)}, bf16[384,1536]{1,0:T(8,128)(2,1)S(1)}, bf16[384,1536]{1,0:T(8,128)(2,1...) custom-call(bf16[768,768]{1,0:T(8,128)(2,1)S(1)} %get-tuple-element.136.map_ref, ...), custom_call_target="tpu_custom_call" | custom-call | flops 1 | bytes 1 | tf_op jit(solution)/shard_map/feedw/pallas_call | solution.py:53
  81.8 1.7 collective-permute-done.18.got_ref
  84.0 1.9 %backnorm.1 = (f32[224,768]{1,0:T(8,128)S(1)}, bf16[224,768]{1,0:T(8,128)(2,1)S(1)}, bf16[224,768]{1,0:T(8,128)(2,1)S(1)}, f32[3,768]{1,0:T(4,128)S(1)}) custom-call(s32[1,2]{1,0:T(1,128)S(1)} %copy-done.28, f32[224,768]{1,0:T(8,128)S(1)} %get-tuple-element.131.da2_ref, bf16[224,768]{1,0:T(8,128)(2,1)S(1)} %collective-permute-done.18.got_ref, ...), custom_call_target="tpu_custom_call" | custom-call | flops 1 | bytes 1 | tf_op jit(solution)/shard_map/backnorm/pallas_call | solution.py:53
  86.4 1.7 convert_add_fusion.1
  88.1 1.7 convert_add_fusion.2
  89.8 2.2 %slice.308 = bf16[192,1536]{1,0:T(8,128)(2,1)} slice(f32[384,1536]{1,0:T(8,128)} %convert_add_fusion.2), slice={[192:384], [0:1536]} | slice | bytes 1179648 | tf_op jit(solution)/shard_map/slice | solution.py:159
  92.6 5.7 %back1.1 = (bf16[224,1152]{1,0:T(8,128)(2,1)S(1)}, bf16[384,1920]{1,0:T(8,128)(2,1)S(1)}, bf16[384,1920]{1,0:T(8,128)(2,1)}, f32[1,768]{1,0:T(1,128)S(1)}, f32[64,128]{1,0:T(8,128)S(1)}) custom-call(bf16[224,768]{1,0:T(8,128)(2,1)S(1)} %get-tuple-element.149.dy_ref, bf16[224,768]{1,0:T(8,128)(2,1)S(1)} %get-tuple-element.164.do_ref, ...), custom_call_target="tpu_custom_call" | custom-call | flops 1 | bytes 1 | tf_op jit(solution)/shard_map/back1/pallas_call | solution.py:53
  102.1 1.6 collective-permute-start.40
  103.7 4.8 %collective-permute-done.44 = bf16[192,1536]{1,0:T(8,128)(2,1)} collective-permute-done((bf16[192,1536]{1,0:T(8,128)(2,1)}, bf16[192,1536]{1,0:T(8,128)(2,1)}, u32[]{:S(2)}, u32[]{:S(2)}) %collective-permute-start.44) | collective-permute-done | bytes 589856 | tf_op jit(solution)/shard_map/ppermute | solution.py:76
  108.5 1.6 fusion.9
  110.2 2.4 %collective-permute-start.45 = (bf16[48,1536]{1,0:T(8,128)(2,1)S(1)}, bf16[48,1536]{1,0:T(8,128)(2,1)S(1)}, u32[]{:S(2)}, u32[]{:S(2)}) collective-permute-start(bf16[48,1536]{1,0:T(8,128)(2,1)S(1)} %get-tuple-element.214), channel_id=1, source_target_pairs={{0,8},{2,10},{4,12},{6,14},{8,16},{10,18},{12,20},{14,22},{16,24},... | collective-permute-start | bytes 442376 | tf_op jit(solution)/shard_map/ppermute | solution.py:72
  114.0 1.5 collective-permute-start.47
  115.5 1.7 convert_add_fusion
  117.3 1.6 collective-permute-done.45
  119.5 3.2 %collective-permute-done.46 = bf16[48,1536]{1,0:T(8,128)(2,1)S(1)} collective-permute-done((bf16[48,1536]{1,0:T(8,128)(2,1)S(1)}, bf16[48,1536]{1,0:T(8,128)(2,1)S(1)}, u32[]{:S(2)}, u32[]{:S(2)}) %collective-permute-start.46) | collective-permute-done | bytes 147488 | tf_op jit(solution)/shard_map/ppermute | solution.py:72
  123.5 4.3 %back2.1 = (bf16[224,1152]{1,0:T(8,128)(2,1)S(1)}, bf16[384,1152]{1,0:T(8,128)(2,1)S(1)}, bf16[384,1152]{1,0:T(8,128)(2,1)S(1)}, f32[1,768]{1,0:T(1,128)S(1)}, f32[64,128]{1,0:T(8,128)S(1)}) custom-call(bf16[224,768]{1,0:T(8,128)(2,1)S(1)} %copy-done.16, bf16[768,224]{1,0:T(8,128)(2,1)S(1)} %get-tuple-element.156.turned_ref, ...), custom_call_target="tpu_custom_call" | custom-call | flops 1 | bytes 1 | tf_op jit(solution)/shard_map/back2/pallas_call | solution.py:53
  128.0 5.4 %collective-permute-done.22 = bf16[192,1920]{1,0:T(8,128)(2,1)S(1)} collective-permute-done((bf16[192,1920]{1,0:T(8,128)(2,1)S(1)}, bf16[192,1920]{1,0:T(8,128)(2,1)S(1)}, u32[]{:S(2)}, u32[]{:S(2)}) %collective-permute-start.22) | collective-permute-done | bytes 737312 | tf_op jit(solution)/shard_map/ppermute | solution.py:85
  135.5 2.0 %collective-permute-start.42 = (bf16[48,1536]{1,0:T(8,128)(2,1)S(1)}, bf16[48,1536]{1,0:T(8,128)(2,1)S(1)}, u32[]{:S(2)}, u32[]{:S(2)}) collective-permute-start(bf16[48,1536]{1,0:T(8,128)(2,1)S(1)} %get-tuple-element.219), channel_id=1, source_target_pairs={{0,16},{2,18},{4,20},{6,22},{8,24},{10,26},{12,28},{14,30},{16,0},... | collective-permute-start | bytes 442376 | tf_op jit(solution)/shard_map/ppermute | solution.py:72
  137.5 2.8 %collective-permute-start.43 = (bf16[48,1536]{1,0:T(8,128)(2,1)S(1)}, bf16[48,1536]{1,0:T(8,128)(2,1)S(1)}, u32[]{:S(2)}, u32[]{:S(2)}) collective-permute-start(bf16[48,1536]{1,0:T(8,128)(2,1)S(1)} %get-tuple-element.218), channel_id=1, source_target_pairs={{0,24},{2,26},{4,28},{6,30},{8,0},{10,2},{12,4},{14,6},{16,8},{18,... | collective-permute-start | bytes 442376 | tf_op jit(solution)/shard_map/ppermute | solution.py:72
  141.0 3.5 %finish.1 = (bf16[196,768]{1,0:T(8,128)(2,1)S(1)}, bf16[196,768]{1,0:T(8,128)(2,1)S(1)}, f32[136,128]{1,0:T(8,128)S(1)}) custom-call(s32[1,2]{1,0:T(1,128)S(1)} %copy-done.28, bf16[224,1152]{1,0:T(8,128)(2,1)S(1)} %copy-done.24, bf16[224,1152]{1,0:T(8,128)(2,1)S(1)} %get-tuple-element.170.dq2_ref, bf16[384,1152]{1,0:T(8,128)(2,1)S(1)} %copy-done.6, ...), custom_call_target="tpu_custom_call" | custom-call | flops 1 | bytes 1 | tf_op jit(solution)/shard_map/finish/pallas_call | solution.py:53
  144.6 4.2 %collective-permute-done.26 = bf16[192,1152]{1,0:T(8,128)(2,1)S(1)} collective-permute-done((bf16[192,1152]{1,0:T(8,128)(2,1)S(1)}, bf16[192,1152]{1,0:T(8,128)(2,1)S(1)}, u32[]{:S(2)}, u32[]{:S(2)}) %collective-permute-start.26) | collective-permute-done | bytes 442400 | tf_op jit(solution)/shard_map/ppermute | solution.py:85
  149.9 1.5 collective-permute-start.34
  151.3 1.6 collective-permute-start.35
  155.2 1.5 collective-permute-start.36
  157.5 2.4 %collective-permute-done.34 = bf16[24,1920]{1,0:T(8,128)(2,1)S(1)} collective-permute-done((bf16[24,1920]{1,0:T(8,128)(2,1)S(1)}, bf16[24,1920]{1,0:T(8,128)(2,1)S(1)}, u32[]{:S(2)}, u32[]{:S(2)}) %collective-permute-start.34) | collective-permute-done | bytes 92192 | tf_op jit(solution)/shard_map/ppermute | solution.py:72
  164.7 2.6 %collective-permute-start.39 = (bf16[24,1152]{1,0:T(8,128)(2,1)S(1)}, bf16[24,1152]{1,0:T(8,128)(2,1)S(1)}, u32[]{:S(2)}, u32[]{:S(2)}) collective-permute-start(bf16[24,1152]{1,0:T(8,128)(2,1)S(1)} %get-tuple-element.224), channel_id=1, source_target_pairs={{0,24},{2,26},{4,28},{6,30},{8,0},{10,2},{12,4},{14,6},{16,8},{18,... | collective-permute-start | bytes 165896 | tf_op jit(solution)/shard_map/ppermute | solution.py:72
  169.5 2.7 %collective-permute-start.32 = (f32[136,128]{1,0:T(8,128)S(1)}, f32[136,128]{1,0:T(8,128)S(1)}, u32[]{:S(2)}, u32[]{:S(2)}) collective-permute-start(f32[136,128]{1,0:T(8,128)S(1)} %add.99), channel_id=1, source_target_pairs={{0,24},{2,26},{4,28},{6,30},{8,0},{10,2},{12,4},{14,6},{16,8},{18,... | collective-permute-start | bytes 208904 | tf_op jit(solution)/shard_map/ppermute | solution.py:72
  172.3 2.0 %collective-permute-done.30 = f32[136,128]{1,0:T(8,128)S(1)} collective-permute-done((f32[136,128]{1,0:T(8,128)S(1)}, f32[136,128]{1,0:T(8,128)S(1)}, u32[]{:S(2)}, u32[]{:S(2)}) %collective-permute-start.30) | collective-permute-done | bytes 69664 | tf_op jit(solution)/shard_map/ppermute | solution.py:72
  174.3 1.9 %collective-permute-done.31 = f32[136,128]{1,0:T(8,128)S(1)} collective-permute-done((f32[136,128]{1,0:T(8,128)S(1)}, f32[136,128]{1,0:T(8,128)S(1)}, u32[]{:S(2)}, u32[]{:S(2)}) %collective-permute-start.31) | collective-permute-done | bytes 69664 | tf_op jit(solution)/shard_map/ppermute | solution.py:72
  (181 shorter events, 39.3 us)
Async XLA Ops:
  1.7 17.3 %collective-permute-start = (bf16[24,1152]{1,0:T(8,128)(2,1)S(1)}, bf16[24,1152]{1,0:T(8,128)(2,1)S(1)}, u32[]{:S(2)}, u32[]{:S(2)}) collective-permute-start(bf16[24,1152]{1,0:T(8,128)(2,1)S(1)} %get-tuple-element.106), channel_id=1, source_target_pairs={{0,24},{2,26},{4,28},{6,30},{8,0},{10,2},{12,4},{14,6},{16,8},{18,... | collective-permute-start | bytes 165896 | tf_op jit(solution)/shard_map/ppermute | solution.py:72
  6.8 12.4 %collective-permute-start.1 = (bf16[24,1152]{1,0:T(8,128)(2,1)S(1)}, bf16[24,1152]{1,0:T(8,128)(2,1)S(1)}, u32[]{:S(2)}, u32[]{:S(2)}) collective-permute-start(bf16[24,1152]{1,0:T(8,128)(2,1)S(1)} %get-tuple-element.106), channel_id=1, source_target_pairs={{0,16},{2,18},{4,20},{6,22},{8,24},{10,26},{12,28},{14,30},{16,0},... | collective-permute-start | bytes 165896 | tf_op jit(solution)/shard_map/ppermute | solution.py:72
  6.8 14.0 %collective-permute-start.2 = (bf16[24,1152]{1,0:T(8,128)(2,1)S(1)}, bf16[24,1152]{1,0:T(8,128)(2,1)S(1)}, u32[]{:S(2)}, u32[]{:S(2)}) collective-permute-start(bf16[24,1152]{1,0:T(8,128)(2,1)S(1)} %get-tuple-element.106), channel_id=1, source_target_pairs={{0,8},{2,10},{4,12},{6,14},{8,16},{10,18},{12,20},{14,22},{16,24},... | collective-permute-start | bytes 165896 | tf_op jit(solution)/shard_map/ppermute | solution.py:72
  7.8 13.6 %collective-permute-start.5 = (bf16[24,1920]{1,0:T(8,128)(2,1)S(1)}, bf16[24,1920]{1,0:T(8,128)(2,1)S(1)}, u32[]{:S(2)}, u32[]{:S(2)}) collective-permute-start(bf16[24,1920]{1,0:T(8,128)(2,1)S(1)} %get-tuple-element.108), channel_id=1, source_target_pairs={{0,24},{2,26},{4,28},{6,30},{8,0},{10,2},{12,4},{14,6},{16,8},{18,... | collective-permute-start | bytes 276488 | tf_op jit(solution)/shard_map/ppermute | solution.py:72
  10.6 12.3 %collective-permute-start.6 = (bf16[24,1920]{1,0:T(8,128)(2,1)S(1)}, bf16[24,1920]{1,0:T(8,128)(2,1)S(1)}, u32[]{:S(2)}, u32[]{:S(2)}) collective-permute-start(bf16[24,1920]{1,0:T(8,128)(2,1)S(1)} %get-tuple-element.108), channel_id=1, source_target_pairs={{0,16},{2,18},{4,20},{6,22},{8,24},{10,26},{12,28},{14,30},{16,0},... | collective-permute-start | bytes 276488 | tf_op jit(solution)/shard_map/ppermute | solution.py:72
  19.0 6.6 %collective-permute-start.7 = (bf16[24,1920]{1,0:T(8,128)(2,1)S(1)}, bf16[24,1920]{1,0:T(8,128)(2,1)S(1)}, u32[]{:S(2)}, u32[]{:S(2)}) collective-permute-start(bf16[24,1920]{1,0:T(8,128)(2,1)S(1)} %get-tuple-element.108), channel_id=1, source_target_pairs={{0,8},{2,10},{4,12},{6,14},{8,16},{10,18},{12,20},{14,22},{16,24},... | collective-permute-start | bytes 276488 | tf_op jit(solution)/shard_map/ppermute | solution.py:72
  19.2 13.2 %collective-permute-start.8 = (bf16[224,768]{1,0:T(8,128)(2,1)S(1)}, bf16[224,768]{1,0:T(8,128)(2,1)S(1)}, u32[]{:S(2)}, u32[]{:S(2)}) collective-permute-start(bf16[224,768]{1,0:T(8,128)(2,1)S(1)} %get-tuple-element.137.dm_ref.refs_0_), channel_id=1, source_target_pairs={{0,1},{1,0},{2,3},{3,2},{4,5},{5,4},{6,7},{7,6},{8,9},{9,8},{10,11... | collective-permute-start | bytes 1032200 | tf_op jit(solution)/shard_map/ppermute | solution.py:85
  20.8 11.6 %collective-permute-start.3 = (bf16[96,1152]{1,0:T(8,128)(2,1)S(1)}, bf16[96,1152]{1,0:T(8,128)(2,1)S(1)}, u32[]{:S(2)}, u32[]{:S(2)}) collective-permute-start(bf16[96,1152]{1,0:T(8,128)(2,1)S(1)} %pad_maximum_fusion.3), channel_id=1, source_target_pairs={{0,1},{1,0},{2,3},{3,2},{4,5},{5,4},{6,7},{7,6},{8,9},{9,8},{10,11... | collective-permute-start | bytes 663560 | tf_op jit(solution)/shard_map/ppermute | solution.py:85
  21.4 11.0 %collective-permute-start.4 = (bf16[96,1152]{1,0:T(8,128)(2,1)S(1)}, bf16[96,1152]{1,0:T(8,128)(2,1)S(1)}, u32[]{:S(2)}, u32[]{:S(2)}) collective-permute-start(bf16[96,1152]{1,0:T(8,128)(2,1)S(1)} %pad_maximum_fusion.3), channel_id=1, source_target_pairs={{0,4},{2,6},{4,0},{6,2},{8,12},{10,14},{12,8},{14,10},{16,20},{18,... | collective-permute-start | bytes 663560 | tf_op jit(solution)/shard_map/ppermute | solution.py:76
  32.4 11.9 %collective-permute-start.11 = (bf16[96,1920]{1,0:T(8,128)(2,1)S(1)}, bf16[96,1920]{1,0:T(8,128)(2,1)S(1)}, u32[]{:S(2)}, u32[]{:S(2)}) collective-permute-start(bf16[96,1920]{1,0:T(8,128)(2,1)S(1)} %pad_maximum_fusion.2), channel_id=1, source_target_pairs={{0,1},{1,0},{2,3},{3,2},{4,5},{5,4},{6,7},{7,6},{8,9},{9,8},{10,11... | collective-permute-start | bytes 1105928 | tf_op jit(solution)/shard_map/ppermute | solution.py:85
  33.9 10.4 %collective-permute-start.12 = (bf16[96,1920]{1,0:T(8,128)(2,1)S(1)}, bf16[96,1920]{1,0:T(8,128)(2,1)S(1)}, u32[]{:S(2)}, u32[]{:S(2)}) collective-permute-start(bf16[96,1920]{1,0:T(8,128)(2,1)S(1)} %pad_maximum_fusion.2), channel_id=1, source_target_pairs={{0,4},{2,6},{4,0},{6,2},{8,12},{10,14},{12,8},{14,10},{16,20},{18,... | collective-permute-start | bytes 1105928 | tf_op jit(solution)/shard_map/ppermute | solution.py:76
  35.5 7.5 %collective-permute-start.10 = (bf16[96,576]{1,0:T(8,128)(2,1)S(1)}, bf16[96,576]{1,0:T(8,128)(2,1)S(1)}, u32[]{:S(2)}, u32[]{:S(2)}) collective-permute-start(bf16[96,576]{1,0:T(8,128)(2,1)S(1)} %slice.172), channel_id=1, source_target_pairs={{0,1},{1,0},{2,3},{3,2},{4,5},{5,4},{6,7},{7,6},{8,9},{9,8},{10,11... | collective-permute-start | bytes 331784 | tf_op jit(solution)/shard_map/ppermute | solution.py:85
  36.2 8.1 %collective-permute-start.9 = (bf16[96,576]{1,0:T(8,128)(2,1)S(1)}, bf16[96,576]{1,0:T(8,128)(2,1)S(1)}, u32[]{:S(2)}, u32[]{:S(2)}) collective-permute-start(bf16[96,576]{1,0:T(8,128)(2,1)S(1)} %slice.171), channel_id=1, source_target_pairs={{0,4},{2,6},{4,0},{6,2},{8,12},{10,14},{12,8},{14,10},{16,20},{18,... | collective-permute-start | bytes 331784 | tf_op jit(solution)/shard_map/ppermute | solution.py:76
  44.4 2.5 %collective-permute-start.15 = (bf16[384,1152]{1,0:T(8,128)(2,1)S(1)}, bf16[384,1152]{1,0:T(8,128)(2,1)S(1)}, u32[]{:S(2)}, u32[]{:S(2)}) collective-permute-start(bf16[384,1152]{1,0:T(8,128)(2,1)S(1)} %fusion.1.own_ref.own1_ref), channel_id=1, source_target_pairs={{0,2},{2,0},{4,6},{6,4},{8,10},{10,8},{12,14},{14,12},{16,18},{18,... | collective-permute-start | bytes 2654216 | tf_op jit(solution)/shard_map/ppermute | solution.py:80
  44.5 7.4 %collective-permute-start.13 = (bf16[96,960]{1,0:T(8,128)(2,1)S(1)}, bf16[96,960]{1,0:T(8,128)(2,1)S(1)}, u32[]{:S(2)}, u32[]{:S(2)}) collective-permute-start(bf16[96,960]{1,0:T(8,128)(2,1)S(1)} %slice.173), channel_id=1, source_target_pairs={{0,4},{2,6},{4,0},{6,2},{8,12},{10,14},{12,8},{14,10},{16,20},{18,... | collective-permute-start | bytes 552968 | tf_op jit(solution)/shard_map/ppermute | solution.py:76
  46.2 7.1 %collective-permute-start.14 = (bf16[96,960]{1,0:T(8,128)(2,1)S(1)}, bf16[96,960]{1,0:T(8,128)(2,1)S(1)}, u32[]{:S(2)}, u32[]{:S(2)}) collective-permute-start(bf16[96,960]{1,0:T(8,128)(2,1)S(1)} %slice.174), channel_id=1, source_target_pairs={{0,1},{1,0},{2,3},{3,2},{4,5},{5,4},{6,7},{7,6},{8,9},{9,8},{10,11... | collective-permute-start | bytes 552968 | tf_op jit(solution)/shard_map/ppermute | solution.py:85
  53.5 3.3 %collective-permute-start.16 = (bf16[384,1920]{1,0:T(8,128)(2,1)S(1)}, bf16[384,1920]{1,0:T(8,128)(2,1)S(1)}, u32[]{:S(2)}, u32[]{:S(2)}) collective-permute-start(bf16[384,1920]{1,0:T(8,128)(2,1)S(1)} %fusion.own_ref.own2_ref), channel_id=1, source_target_pairs={{0,2},{2,0},{4,6},{6,4},{8,10},{10,8},{12,14},{14,12},{16,18},{18,... | collective-permute-start | bytes 4423688 | tf_op jit(solution)/shard_map/ppermute | solution.py:80
  62.0 10.2 %collective-permute-start.17 = (bf16[224,768]{1,0:T(8,128)(2,1)S(1)}, bf16[224,768]{1,0:T(8,128)(2,1)S(1)}, u32[]{:S(2)}, u32[]{:S(2)}) collective-permute-start(bf16[224,768]{1,0:T(8,128)(2,1)S(1)} %get-tuple-element.128.a2_ref.refs_4_), channel_id=1, source_target_pairs={{0,1},{1,0},{2,3},{3,2},{4,5},{5,4},{6,7},{7,6},{8,9},{9,8},{10,11... | collective-permute-start | bytes 1032200 | tf_op jit(solution)/shard_map/ppermute | solution.py:85
  74.2 9.3 %collective-permute-start.18 = (bf16[224,768]{1,0:T(8,128)(2,1)S(1)}, bf16[224,768]{1,0:T(8,128)(2,1)S(1)}, u32[]{:S(2)}, u32[]{:S(2)}) collective-permute-start(bf16[224,768]{1,0:T(8,128)(2,1)S(1)} %get-tuple-element.134), channel_id=1, source_target_pairs={{0,1},{1,0},{2,3},{3,2},{4,5},{5,4},{6,7},{7,6},{8,9},{9,8},{10,11... | collective-permute-start | bytes 1032200 | tf_op jit(solution)/shard_map/ppermute | solution.py:85
  83.5 2.8 %collective-permute-start.20 = (bf16[384,1536]{1,0:T(8,128)(2,1)S(1)}, bf16[384,1536]{1,0:T(8,128)(2,1)S(1)}, u32[]{:S(2)}, u32[]{:S(2)}) collective-permute-start(bf16[384,1536]{1,0:T(8,128)(2,1)S(1)} %get-tuple-element.153), channel_id=1, source_target_pairs={{0,2},{2,0},{4,6},{6,4},{8,10},{10,8},{12,14},{14,12},{16,18},{18,... | collective-permute-start | bytes 3538952 | tf_op jit(solution)/shard_map/ppermute | solution.py:80
  83.5 4.6 %collective-permute-start.19 = (bf16[384,1536]{1,0:T(8,128)(2,1)S(1)}, bf16[384,1536]{1,0:T(8,128)(2,1)S(1)}, u32[]{:S(2)}, u32[]{:S(2)}) collective-permute-start(bf16[384,1536]{1,0:T(8,128)(2,1)S(1)} %get-tuple-element.151), channel_id=1, source_target_pairs={{0,2},{2,0},{4,6},{6,4},{8,10},{10,8},{12,14},{14,12},{16,18},{18,... | collective-permute-start | bytes 3538952 | tf_op jit(solution)/shard_map/ppermute | solution.py:80
  92.0 16.5 %collective-permute-start.44 = (bf16[192,1536]{1,0:T(8,128)(2,1)}, bf16[192,1536]{1,0:T(8,128)(2,1)}, u32[]{:S(2)}, u32[]{:S(2)}) collective-permute-start(bf16[192,1536]{1,0:T(8,128)(2,1)} %slice.308), channel_id=1, source_target_pairs={{0,4},{2,6},{4,0},{6,2},{8,12},{10,14},{12,8},{14,10},{16,20},{18,... | collective-permute-start | bytes 1769480 | tf_op jit(solution)/shard_map/ppermute | solution.py:76
  100.2 13.8 %collective-permute-start.21 = (bf16[384,1920]{1,0:T(8,128)(2,1)}, bf16[384,1920]{1,0:T(8,128)(2,1)}, u32[]{:S(2)}, u32[]{:S(2)}) collective-permute-start(bf16[384,1920]{1,0:T(8,128)(2,1)} %get-tuple-element.162), channel_id=1, source_target_pairs={{0,2},{2,0},{4,6},{6,4},{8,10},{10,8},{12,14},{14,12},{16,18},{18,... | collective-permute-start | bytes 4423688 | tf_op jit(solution)/shard_map/ppermute | solution.py:80
  100.2 40.1 %collective-permute-start.24 = (bf16[224,768]{1,0:T(8,128)(2,1)}, bf16[224,768]{1,0:T(8,128)(2,1)S(1)}, u32[]{:S(2)}, u32[]{:S(2)}) collective-permute-start(bf16[224,768]{1,0:T(8,128)(2,1)} %copy-done.29), channel_id=1, source_target_pairs={{0,1},{1,0},{2,3},{3,2},{4,5},{5,4},{6,7},{7,6},{8,9},{9,8},{10,11... | collective-permute-start | bytes 1032200 | tf_op jit(solution)/shard_map/ppermute | solution.py:85
  102.1 25.8 %collective-permute-start.40 = (bf16[192,1536]{1,0:T(8,128)(2,1)S(1)}, bf16[192,1536]{1,0:T(8,128)(2,1)S(1)}, u32[]{:S(2)}, u32[]{:S(2)}) collective-permute-start(bf16[192,1536]{1,0:T(8,128)(2,1)S(1)} %slice.309), channel_id=1, source_target_pairs={{0,4},{2,6},{4,0},{6,2},{8,12},{10,14},{12,8},{14,10},{16,20},{18,... | collective-permute-start | bytes 1769480 | tf_op jit(solution)/shard_map/ppermute | solution.py:76
  110.2 8.8 %collective-permute-start.45 = (bf16[48,1536]{1,0:T(8,128)(2,1)S(1)}, bf16[48,1536]{1,0:T(8,128)(2,1)S(1)}, u32[]{:S(2)}, u32[]{:S(2)}) collective-permute-start(bf16[48,1536]{1,0:T(8,128)(2,1)S(1)} %get-tuple-element.214), channel_id=1, source_target_pairs={{0,8},{2,10},{4,12},{6,14},{8,16},{10,18},{12,20},{14,22},{16,24},... | collective-permute-start | bytes 442376 | tf_op jit(solution)/shard_map/ppermute | solution.py:72
  112.5 10.2 %collective-permute-start.46 = (bf16[48,1536]{1,0:T(8,128)(2,1)S(1)}, bf16[48,1536]{1,0:T(8,128)(2,1)S(1)}, u32[]{:S(2)}, u32[]{:S(2)}) collective-permute-start(bf16[48,1536]{1,0:T(8,128)(2,1)S(1)} %get-tuple-element.216), channel_id=1, source_target_pairs={{0,16},{2,18},{4,20},{6,22},{8,24},{10,26},{12,28},{14,30},{16,0},... | collective-permute-start | bytes 442376 | tf_op jit(solution)/shard_map/ppermute | solution.py:72
  114.0 8.7 %collective-permute-start.47 = (bf16[48,1536]{1,0:T(8,128)(2,1)S(1)}, bf16[48,1536]{1,0:T(8,128)(2,1)S(1)}, u32[]{:S(2)}, u32[]{:S(2)}) collective-permute-start(bf16[48,1536]{1,0:T(8,128)(2,1)S(1)} %get-tuple-element.215), channel_id=1, source_target_pairs={{0,24},{2,26},{4,28},{6,30},{8,0},{10,2},{12,4},{14,6},{16,8},{18,... | collective-permute-start | bytes 442376 | tf_op jit(solution)/shard_map/ppermute | solution.py:72
  118.9 14.5 %collective-permute-start.22 = (bf16[192,1920]{1,0:T(8,128)(2,1)S(1)}, bf16[192,1920]{1,0:T(8,128)(2,1)S(1)}, u32[]{:S(2)}, u32[]{:S(2)}) collective-permute-start(bf16[192,1920]{1,0:T(8,128)(2,1)S(1)} %slice.307), channel_id=1, source_target_pairs={{0,1},{1,0},{2,3},{3,2},{4,5},{5,4},{6,7},{7,6},{8,9},{9,8},{10,11... | collective-permute-start | bytes 2211848 | tf_op jit(solution)/shard_map/ppermute | solution.py:85
  127.7 5.9 %collective-permute-start.23 = (bf16[384,1152]{1,0:T(8,128)(2,1)S(1)}, bf16[384,1152]{1,0:T(8,128)(2,1)S(1)}, u32[]{:S(2)}, u32[]{:S(2)}) collective-permute-start(bf16[384,1152]{1,0:T(8,128)(2,1)S(1)} %get-tuple-element.168), channel_id=1, source_target_pairs={{0,2},{2,0},{4,6},{6,4},{8,10},{10,8},{12,14},{14,12},{16,18},{18,... | collective-permute-start | bytes 2654216 | tf_op jit(solution)/shard_map/ppermute | solution.py:80
  133.9 10.6 %collective-permute-start.25 = (bf16[96,1920]{1,0:T(8,128)(2,1)S(1)}, bf16[96,1920]{1,0:T(8,128)(2,1)S(1)}, u32[]{:S(2)}, u32[]{:S(2)}) collective-permute-start(bf16[96,1920]{1,0:T(8,128)(2,1)S(1)} %slice.311), channel_id=1, source_target_pairs={{0,4},{2,6},{4,0},{6,2},{8,12},{10,14},{12,8},{14,10},{16,20},{18,... | collective-permute-start | bytes 1105928 | tf_op jit(solution)/shard_map/ppermute | solution.py:76
  134.6 15.3 %collective-permute-start.41 = (bf16[48,1536]{1,0:T(8,128)(2,1)S(1)}, bf16[48,1536]{1,0:T(8,128)(2,1)S(1)}, u32[]{:S(2)}, u32[]{:S(2)}) collective-permute-start(bf16[48,1536]{1,0:T(8,128)(2,1)S(1)} %get-tuple-element.217), channel_id=1, source_target_pairs={{0,8},{2,10},{4,12},{6,14},{8,16},{10,18},{12,20},{14,22},{16,24},... | collective-permute-start | bytes 442376 | tf_op jit(solution)/shard_map/ppermute | solution.py:72
  135.5 15.9 %collective-permute-start.42 = (bf16[48,1536]{1,0:T(8,128)(2,1)S(1)}, bf16[48,1536]{1,0:T(8,128)(2,1)S(1)}, u32[]{:S(2)}, u32[]{:S(2)}) collective-permute-start(bf16[48,1536]{1,0:T(8,128)(2,1)S(1)} %get-tuple-element.219), channel_id=1, source_target_pairs={{0,16},{2,18},{4,20},{6,22},{8,24},{10,26},{12,28},{14,30},{16,0},... | collective-permute-start | bytes 442376 | tf_op jit(solution)/shard_map/ppermute | solution.py:72
  137.5 15.5 %collective-permute-start.43 = (bf16[48,1536]{1,0:T(8,128)(2,1)S(1)}, bf16[48,1536]{1,0:T(8,128)(2,1)S(1)}, u32[]{:S(2)}, u32[]{:S(2)}) collective-permute-start(bf16[48,1536]{1,0:T(8,128)(2,1)S(1)} %get-tuple-element.218), channel_id=1, source_target_pairs={{0,24},{2,26},{4,28},{6,30},{8,0},{10,2},{12,4},{14,6},{16,8},{18,... | collective-permute-start | bytes 442376 | tf_op jit(solution)/shard_map/ppermute | solution.py:72
  140.4 8.4 %collective-permute-start.26 = (bf16[192,1152]{1,0:T(8,128)(2,1)S(1)}, bf16[192,1152]{1,0:T(8,128)(2,1)S(1)}, u32[]{:S(2)}, u32[]{:S(2)}) collective-permute-start(bf16[192,1152]{1,0:T(8,128)(2,1)S(1)} %slice.310), channel_id=1, source_target_pairs={{0,1},{1,0},{2,3},{3,2},{4,5},{5,4},{6,7},{7,6},{8,9},{9,8},{10,11... | collective-permute-start | bytes 1327112 | tf_op jit(solution)/shard_map/ppermute | solution.py:85
  148.9 7.9 %collective-permute-start.27 = (f32[136,128]{1,0:T(8,128)S(1)}, f32[136,128]{1,0:T(8,128)S(1)}, u32[]{:S(2)}, u32[]{:S(2)}) collective-permute-start(f32[136,128]{1,0:T(8,128)S(1)} %get-tuple-element.186), channel_id=1, source_target_pairs={{0,2},{2,0},{4,6},{6,4},{8,10},{10,8},{12,14},{14,12},{16,18},{18,... | collective-permute-start | bytes 208904 | tf_op jit(solution)/shard_map/ppermute | solution.py:80
  149.0 8.5 %collective-permute-start.33 = (bf16[24,1920]{1,0:T(8,128)(2,1)S(1)}, bf16[24,1920]{1,0:T(8,128)(2,1)S(1)}, u32[]{:S(2)}, u32[]{:S(2)}) collective-permute-start(bf16[24,1920]{1,0:T(8,128)(2,1)S(1)} %get-tuple-element.220), channel_id=1, source_target_pairs={{0,8},{2,10},{4,12},{6,14},{8,16},{10,18},{12,20},{14,22},{16,24},... | collective-permute-start | bytes 276488 | tf_op jit(solution)/shard_map/ppermute | solution.py:72
  149.9 10.1 %collective-permute-start.34 = (bf16[24,1920]{1,0:T(8,128)(2,1)S(1)}, bf16[24,1920]{1,0:T(8,128)(2,1)S(1)}, u32[]{:S(2)}, u32[]{:S(2)}) collective-permute-start(bf16[24,1920]{1,0:T(8,128)(2,1)S(1)} %get-tuple-element.222), channel_id=1, source_target_pairs={{0,16},{2,18},{4,20},{6,22},{8,24},{10,26},{12,28},{14,30},{16,0},... | collective-permute-start | bytes 276488 | tf_op jit(solution)/shard_map/ppermute | solution.py:72
  151.3 8.6 %collective-permute-start.35 = (bf16[24,1920]{1,0:T(8,128)(2,1)S(1)}, bf16[24,1920]{1,0:T(8,128)(2,1)S(1)}, u32[]{:S(2)}, u32[]{:S(2)}) collective-permute-start(bf16[24,1920]{1,0:T(8,128)(2,1)S(1)} %get-tuple-element.221), channel_id=1, source_target_pairs={{0,24},{2,26},{4,28},{6,30},{8,0},{10,2},{12,4},{14,6},{16,8},{18,... | collective-permute-start | bytes 276488 | tf_op jit(solution)/shard_map/ppermute | solution.py:72
  155.2 7.3 %collective-permute-start.36 = (bf16[96,1152]{1,0:T(8,128)(2,1)S(1)}, bf16[96,1152]{1,0:T(8,128)(2,1)S(1)}, u32[]{:S(2)}, u32[]{:S(2)}) collective-permute-start(bf16[96,1152]{1,0:T(8,128)(2,1)S(1)} %slice.312), channel_id=1, source_target_pairs={{0,4},{2,6},{4,0},{6,2},{8,12},{10,14},{12,8},{14,10},{16,20},{18,... | collective-permute-start | bytes 663560 | tf_op jit(solution)/shard_map/ppermute | solution.py:76
  156.8 4.4 %collective-permute-start.28 = (f32[136,128]{1,0:T(8,128)S(1)}, f32[136,128]{1,0:T(8,128)S(1)}, u32[]{:S(2)}, u32[]{:S(2)}) collective-permute-start(f32[136,128]{1,0:T(8,128)S(1)} %add.97), channel_id=1, source_target_pairs={{0,1},{1,0},{2,3},{3,2},{4,5},{5,4},{6,7},{7,6},{8,9},{9,8},{10,11... | collective-permute-start | bytes 208904 | tf_op jit(solution)/shard_map/ppermute | solution.py:85
  161.2 6.8 %collective-permute-start.29 = (f32[136,128]{1,0:T(8,128)S(1)}, f32[136,128]{1,0:T(8,128)S(1)}, u32[]{:S(2)}, u32[]{:S(2)}) collective-permute-start(f32[136,128]{1,0:T(8,128)S(1)} %add.98), channel_id=1, source_target_pairs={{0,4},{2,6},{4,0},{6,2},{8,12},{10,14},{12,8},{14,10},{16,20},{18,... | collective-permute-start | bytes 208904 | tf_op jit(solution)/shard_map/ppermute | solution.py:76
  162.7 6.8 %collective-permute-start.37 = (bf16[24,1152]{1,0:T(8,128)(2,1)S(1)}, bf16[24,1152]{1,0:T(8,128)(2,1)S(1)}, u32[]{:S(2)}, u32[]{:S(2)}) collective-permute-start(bf16[24,1152]{1,0:T(8,128)(2,1)S(1)} %get-tuple-element.223), channel_id=1, source_target_pairs={{0,8},{2,10},{4,12},{6,14},{8,16},{10,18},{12,20},{14,22},{16,24},... | collective-permute-start | bytes 165896 | tf_op jit(solution)/shard_map/ppermute | solution.py:72
  163.8 8.4 %collective-permute-start.38 = (bf16[24,1152]{1,0:T(8,128)(2,1)S(1)}, bf16[24,1152]{1,0:T(8,128)(2,1)S(1)}, u32[]{:S(2)}, u32[]{:S(2)}) collective-permute-start(bf16[24,1152]{1,0:T(8,128)(2,1)S(1)} %get-tuple-element.225), channel_id=1, source_target_pairs={{0,16},{2,18},{4,20},{6,22},{8,24},{10,26},{12,28},{14,30},{16,0},... | collective-permute-start | bytes 165896 | tf_op jit(solution)/shard_map/ppermute | solution.py:72
  164.7 7.5 %collective-permute-start.39 = (bf16[24,1152]{1,0:T(8,128)(2,1)S(1)}, bf16[24,1152]{1,0:T(8,128)(2,1)S(1)}, u32[]{:S(2)}, u32[]{:S(2)}) collective-permute-start(bf16[24,1152]{1,0:T(8,128)(2,1)S(1)} %get-tuple-element.224), channel_id=1, source_target_pairs={{0,24},{2,26},{4,28},{6,30},{8,0},{10,2},{12,4},{14,6},{16,8},{18,... | collective-permute-start | bytes 165896 | tf_op jit(solution)/shard_map/ppermute | solution.py:72
  168.0 6.3 %collective-permute-start.30 = (f32[136,128]{1,0:T(8,128)S(1)}, f32[136,128]{1,0:T(8,128)S(1)}, u32[]{:S(2)}, u32[]{:S(2)}) collective-permute-start(f32[136,128]{1,0:T(8,128)S(1)} %add.99), channel_id=1, source_target_pairs={{0,8},{2,10},{4,12},{6,14},{8,16},{10,18},{12,20},{14,22},{16,24},... | collective-permute-start | bytes 208904 | tf_op jit(solution)/shard_map/ppermute | solution.py:72
  168.0 8.1 %collective-permute-start.31 = (f32[136,128]{1,0:T(8,128)S(1)}, f32[136,128]{1,0:T(8,128)S(1)}, u32[]{:S(2)}, u32[]{:S(2)}) collective-permute-start(f32[136,128]{1,0:T(8,128)S(1)} %add.99), channel_id=1, source_target_pairs={{0,16},{2,18},{4,20},{6,22},{8,24},{10,26},{12,28},{14,30},{16,0},... | collective-permute-start | bytes 208904 | tf_op jit(solution)/shard_map/ppermute | solution.py:72
  169.5 6.6 %collective-permute-start.32 = (f32[136,128]{1,0:T(8,128)S(1)}, f32[136,128]{1,0:T(8,128)S(1)}, u32[]{:S(2)}, u32[]{:S(2)}) collective-permute-start(f32[136,128]{1,0:T(8,128)S(1)} %add.99), channel_id=1, source_target_pairs={{0,24},{2,26},{4,28},{6,30},{8,0},{10,2},{12,4},{14,6},{16,8},{18,... | collective-permute-start | bytes 208904 | tf_op jit(solution)/shard_map/ppermute | solution.py:72
  (32 other events, 300.3 us)

commit v4 on v3

--- a/solution.py
+++ b/solution.py
@@ -18,6 +18,7 @@
 PAIRS = HEADS // 2
 LANES = 128
 TABLE = 2 * WIN - 1
+W_START = HEAD + ROW + 2
 HALF = D // 2
 STEP = 384
 TIER = 3 * HALF
@@ -26,23 +27,32 @@
 VMEM = pl.BlockSpec(memory_space=pltpu.VMEM)
 SMEM = pl.BlockSpec(memory_space=pltpu.SMEM)
 LIMIT = 20 * 2**20
+Z_FIRST = (False, False)
+FRONT = ('dm', 'z1', 'prep', 'act1', 'z2', 'n1', 'n2', 'act0', 'f2', 'f1', 'c1', 'attend1', 'c2')
+ORDER = ('dc', 'dy', 'm', 'norm', 'back2', 'bc', 'back1', 'finish', 'ac', 'sc', 'by', 'uc', 'bx', 'dz', 'bz', 'uy', 'ax', 'ay', 'uz', 'az')
+GATES = {'n1:s': ['prep', 'dm'], 'n2:s': ['z2'], 'f1:s': ['n1'], 'act1:s': ['dm'], 'attend1:s': ['dm', 'f1'], 'z1:s': ['dm'], 'back1:s': ['dc'], 'back2:s': ['m'], 'finish:s': ['bc'], 'ay:r': ['ac', 'back1', 'dz'], 'uc:s': ['dc'], 'bc:s': ['dy'], 'bx:r': ['uc', 'dy'], 'm:s': ['dc'], 'bz:r': ['bc'], 'dz:s': ['finish'], 'ac:r': ['bc'], 'bx:s': ['ac'], 'uy:r': ['finish'], 'uc:r': ['back1'], 'dz:r': ['uc']}
 CHEAP = pl.CostEstimate(flops=1, bytes_accessed=1, transcendentals=0)
 SMALL = {"gain1": 0, "shift1": 6, "qbias": 12, "vbias": 18, "projb": 24, "gain2": 30, "shift2": 36, "downb": 42}
 SMALL_TABLE = 48
-SMALL_UP = SMALL_TABLE + HEAD
+SMALL_UP = SMALL_TABLE + HEAD // 2
+PIECES = TIER // LANES
+
+
+def piece(place):
+    return slice(place // PIECES, place // PIECES + 1), slice(place % PIECES * LANES, (place % PIECES + 1) * LANES)
 
 
 def shape_of(shape, kind):
     return jax.ShapeDtypeStruct(shape, kind)
 
 
-def kernel_call(name, body, n_in, outs, *, smem=0, scratch=(), far=()):
+def kernel_call(name, body, n_in, outs, *, smem=0, scratch=(), far=(), out_far=()):
     call = pl.pallas_call(
         body,
         name=name,
         in_specs=[SMEM] * smem + [VMEM] * (n_in - smem),
         out_specs=[VMEM] * len(outs),
-        out_shape=[pltpu.VMEM(o.shape, o.dtype) for o in outs],
+        out_shape=[o if i in out_far else pltpu.VMEM(o.shape, o.dtype) for i, o in enumerate(outs)],
         scratch_shapes=list(scratch),
         compiler_params=pltpu.CompilerParams(vmem_limit_bytes=LIMIT),
         cost_estimate=CHEAP,
@@ -148,29 +158,17 @@
     return total
 
 
-def scatter_x(rows):
-    wide = lax.axis_size("mp")
-    size = rows.shape[0] // wide
-    return add_up(rows[:size], *[move_x(rows[s * size : (s + 1) * size].astype(BF16), s) for s in range(1, wide)])
-
-
-def scatter_y(rows, *others):
-    size = rows.shape[0] // 2
-    return add_up(rows[:size], after(move_y(rows[size:].astype(BF16)), *others))
-
-
-def scatter_z(rows):
-    depth = lax.axis_size("dp") // 4
-    size = rows.shape[0] // depth
-    return add_up(rows[:size], *[move_z(rows[s * size : (s + 1) * size].astype(BF16), s) for s in range(1, depth)])
-
-
-def sum_small(flat):
-    depth, wide = lax.axis_size("dp") // 4, lax.axis_size("mp")
-    flat = flat + move_c(flat)
-    flat = sum([move_x(flat, s) for s in range(1, wide)], flat)
-    flat = flat + move_y(flat)
-    return sum([move_z(flat, s) for s in range(1, depth)], flat)
+def blocks_of(rows, count):
+    size = rows.shape[0] // count
+    return [rows[i * size : (i + 1) * size] for i in range(count)]
+
+
+def split(parts, count):
+    return list(zip(*[blocks_of(v, count) for v in parts]))
+
+
+def turn_y(value, step):
+    return move_y(value)
 
 
 def dot_nn(a, b):
@@ -247,13 +245,19 @@
     return jnp.concatenate(from_h, axis=0) + from_w
 
 
-def table_places(kind):
+def table_places(start):
     row, lane = iota((TABLE, LANES), 0), iota((TABLE, LANES), 1)
-    start = 0 if kind == "h" else HEAD + ROW + 2
     return (lane - start == TABLE - 1 - row).astype(F32)
 
 
-def pack_kernel(qkv_ref, proj_ref, gain1_ref, shift1_ref, projb_ref, gain2_ref, shift2_ref, downb_ref, qvb_ref, first_ref, second_ref, params_ref):
+def rate_of(keep_ref, branch):
+    return jnp.where(keep_ref[0, branch] > 0, 1.0 / 0.9, 0.0).astype(F32)
+
+
+def pack_kernel(
+    keep_ref, qkv_ref, proj_ref, gain1_ref, shift1_ref, projb_ref, gain2_ref, shift2_ref, downb_ref, qvb_ref, grad_ref,
+    first_ref, second_ref, params_ref, dm_ref,
+):
     for tier, out in enumerate((first_ref, second_ref)):
         for i in range(3):
             out[:, i * HALF : (i + 1) * HALF] = qkv_ref[:, i * D + tier * HALF : i * D + (tier + 1) * HALF]
@@ -261,29 +265,30 @@
     for i, ref in enumerate((gain1_ref, shift1_ref, projb_ref, gain2_ref, shift2_ref, downb_ref)):
         params_ref[i : i + 1] = ref[...].astype(F32).reshape(1, D)
     params_ref[6:8] = qvb_ref[...].astype(F32)
-
-
-def pack(qkv_weight, *args):
+    dm_ref[...] = (rate_of(keep_ref, 1) * grad_ref[...].astype(F32)).astype(BF16)
+
+
+def pack(keep, qkv_weight, *args):
     rows = qkv_weight.shape[0]
     return kernel_call(
         "pack",
-        pack_kernel, 9, [shape_of((rows, TIER), BF16), shape_of((rows, TIER + D), BF16), shape_of((8, D), F32)], far=range(9)
-    )(qkv_weight, *args)
+        pack_kernel,
+        11,
+        [
+            shape_of((rows, TIER), BF16), shape_of((rows, TIER + D), BF16), shape_of((8, D), F32),
+            shape_of((AREA, D), BF16),
+        ],
+        smem=1, far=range(1, 11),
+    )(keep, qkv_weight, *args)
 
 
 def prepare_kernel(
-    count, wide, keep_ref, tokens_ref, grad_ref, maps_ref, params_ref, relh_ref, relw_ref, mask_ref, upb_ref,
-    x_ref, a1_ref, turned_ref, g_ref, dm_ref, att_ref, feed_ref, table_ref, fill_ref, downb_ref, wideb_ref,
+    count, wide, tokens_ref, maps_ref, params_ref, relh_ref, relw_ref, mask_ref, upb_ref,
+    a1_ref, turned_ref, att_ref, feed_ref, table_ref, fill_ref, wideb_ref,
 ):
     wideb_ref[...] = upb_ref[...].astype(F32).reshape(wideb_ref.shape)
     spread = spread_rows()
     x = dot_nn(spread, tokens_ref[...])
-    x_ref[...] = x.astype(BF16)
-    grad = dot_nn(spread, grad_ref[...])
-    g_ref[...] = grad.astype(BF16)
-    dm = (jnp.where(keep_ref[0, 1] > 0, 1.0 / 0.9, 0.0).astype(F32) * grad).astype(BF16)
-    dm_ref[...] = dm
-    downb_ref[...] = jnp.sum(dm.astype(F32), axis=0, keepdims=True)
     source = iota((D, D), 1)
     att = (rows_from(maps_ref, 0, D // (count * wide), wide) == source).astype(F32).astype(BF16)
     att_ref[...] = att
@@ -292,7 +297,7 @@
     a1 = (unit * params_ref[0:1] + params_ref[1:2]).astype(BF16)
     a1_ref[...] = dot_nt(a1, att).astype(BF16)
     turned_ref[...] = dot_nt(att, a1).astype(BF16)
-    one = dot_tn(relh_ref[...], table_places("h").astype(BF16)) + dot_tn(relw_ref[...], table_places("w").astype(BF16))
+    one = dot_tn(relh_ref[...], table_places(0).astype(BF16)) + dot_tn(relw_ref[...], table_places(W_START).astype(BF16))
     blank = jnp.zeros((HEAD, LANES), F32)
     table_ref[:HEAD, :] = jnp.concatenate([one, blank], axis=1).astype(BF16)
     table_ref[HEAD:, :] = jnp.concatenate([blank, pltpu.roll(one, HEAD, 1)], axis=1).astype(BF16)
@@ -301,28 +306,27 @@
     fill_ref[...] = jnp.where(key % ROW >= WIN, -3e38, jnp.where(seen > 0.5, 0.0, -1e9))
 
 
-def prepare(keep, tokens, grad, params, rel_h, rel_w, mask, upb):
+def prepare(tokens, params, rel_h, rel_w, mask, upb):
     count, wide = lax.axis_size("dp"), lax.axis_size("mp")
     return kernel_call(
         "prepare",
         partial(prepare_kernel, count, wide),
-        9,
+        7,
         [
-            shape_of((R, D), BF16), shape_of((R, D), BF16), shape_of((D, R), BF16), shape_of((R, D), BF16),
-            shape_of((R, D), BF16), shape_of((D, D), BF16), shape_of((D, D), BF16),
-            shape_of((LANES, 2 * LANES), BF16), shape_of((1, R), F32), shape_of((1, D), F32),
-            shape_of((1, upb.shape[0]), F32),
+            shape_of((R, D), BF16), shape_of((D, R), BF16), shape_of((D, D), BF16), shape_of((D, D), BF16),
+            shape_of((LANES, 2 * LANES), BF16), shape_of((1, R), F32), shape_of((1, upb.shape[0]), F32),
         ],
-        smem=1, far=(1, 2, 3, 5, 6, 7, 8),
-    )(keep, tokens, grad, row_maps(count, wide), params, rel_h, rel_w, mask, upb)
-
-
-def act_kernel(dm_ref, down_ref, out_ref):
+        far=(0, 1, 3, 4, 5, 6),
+    )(tokens, row_maps(count, wide), params, rel_h, rel_w, mask, upb)
+
+
+def act_kernel(dm_ref, down_ref, out_ref, sum_ref):
+    sum_ref[...] = jnp.sum(dm_ref[...].astype(F32), axis=0, keepdims=True)
     out_ref[...] = dot_nt(dm_ref[...], down_ref[...])
 
 
 def act_grad(dm, down):
-    return kernel_call("act", act_kernel, 2, [shape_of((R, down.shape[0]), F32)])(dm, down)[0]
+    return kernel_call("act", act_kernel, 2, [shape_of((AREA, down.shape[0]), F32), shape_of((1, D), F32)])(dm, down)
 
 
 def heads_forward(qkv_ref, tables, fill, p_ref, out):
@@ -397,10 +401,11 @@
         o_ref[:, HALF + at : HALF + at + LANES] = value
 
     heads_forward(qkv_ref, table_ref[...], fill_ref[...], p_ref, out)
-    moved = dot_nt(o_ref[...], att_ref[...]).astype(BF16)
+    rows = dot_tn(spread_rows(), o_ref[...]).astype(BF16)
+    moved = dot_nt(rows, att_ref[...]).astype(BF16)
     branch = dot_nn(moved[:, :HALF], own_ref[:, TIER:]) + dot_nn(moved[:, HALF:], other_ref[:, TIER:])
-    turned_ref[...] = dot_nt(att_ref[...], o_ref[...]).astype(BF16)
-    rate = jnp.where(keep_ref[0, 0] > 0, 1.0 / 0.9, 0.0).astype(F32)
+    turned_ref[...] = dot_nt(att_ref[...], rows).astype(BF16)
+    rate = rate_of(keep_ref, 0)
     middle = x_ref[...].astype(F32) + rate * (branch + params_ref[2:3])
     mid_ref[...] = middle
     unit, _ = norm_parts(middle)
@@ -413,8 +418,8 @@
         attend_second_kernel,
         10,
         [
-            shape_of((R, TIER), BF16), shape_of((HEADS // 2, R, R), BF16), shape_of((D, R), BF16),
-            shape_of((R, D), F32), shape_of((R, D), BF16),
+            shape_of((R, TIER), BF16), shape_of((HEADS // 2, R, R), BF16), shape_of((D, AREA), BF16),
+            shape_of((AREA, D), F32), shape_of((AREA, D), BF16),
         ],
         smem=1, scratch=[pltpu.VMEM((R, D), BF16)],
     )(*args)
@@ -441,22 +446,35 @@
         "feed",
         feed_kernel,
         4,
-        [shape_of((R, hidden), BF16), shape_of((R, hidden), BF16), shape_of((R, D), kind)],
+        [shape_of((AREA, hidden), BF16), shape_of((AREA, hidden), BF16), shape_of((AREA, D), kind)],
     )(a2, up, upb, gact)
 
 
 def feed_weights_kernel(count, map_ref, down_ref, *refs):
     dms, acts, a2s, dhs = (refs[i * count : (i + 1) * count] for i in range(4))
-    downk_ref, downs_ref, upk_ref, ups_ref, sum_ref, *outs = refs[4 * count :]
-    for lefts, rights, keep_ref, send_ref in ((dms, acts, downk_ref, downs_ref), (a2s, dhs, upk_ref, ups_ref)):
+    refs = refs[4 * count :]
+    depth = lax.axis_size("dp") // 4
+    rows = HALF // (2 * depth)
+    for lefts, rights, by_z in ((dms, acts, Z_FIRST[0]), (a2s, dhs, Z_FIRST[1])):
+        blocks = depth if by_z else 2
+        outs, refs = refs[: 2 * blocks], refs[2 * blocks :]
         turned = [dot_nt(map_ref[...], left[...]).astype(BF16) for left in lefts]
-        for at in range(0, keep_ref.shape[1], STEP):
+        for at in range(0, rights[0].shape[1], STEP):
             here = slice(at, at + STEP)
             total = dot_nn(turned[0], rights[0][:, here])
             for j in range(1, count):
                 total = total + dot_nn(turned[j], rights[j][:, here])
-            keep_ref[:, here] = total[:HALF].astype(BF16)
-            send_ref[:, here] = total[HALF:].astype(BF16)
+            total = total.astype(BF16)
+            for s in range(2):
+                for y in range(2):
+                    if not by_z:
+                        start = s * HALF + y * HALF // 2
+                        outs[2 * s + y][:, here] = total[start : start + HALF // 2]
+                        continue
+                    for z in range(depth):
+                        start = s * HALF + (y * depth + z) * rows
+                        outs[depth * s + z][y * rows : (y + 1) * rows, here] = total[start : start + rows]
+    sum_ref, *outs = refs
     for j in range(count):
         outs[j][...] = dot_nn(acts[j][...], down_ref[...]).astype(outs[j].dtype)
     sums = jnp.sum(dhs[0][...].astype(F32), axis=0, keepdims=True)
@@ -468,14 +486,20 @@
 def feed_weights(row_map, down, dms, acts, a2s, dhs):
     count = len(dms)
     columns = acts[0].shape[1]
-    return kernel_call(
+    blocks = [lax.axis_size("dp") // 4 if by_z else 2 for by_z in Z_FIRST]
+    made = kernel_call(
         "feedw",
         partial(feed_weights_kernel, count),
         2 + 4 * count,
-        [shape_of((HALF, columns), BF16)] * 4
+        [shape_of((HALF // n, columns), BF16) for n in blocks for _ in range(2 * n)]
         + [shape_of((1, columns), F32)]
-        + [shape_of((R, D), F32 if j == 0 else BF16) for j in range(count)],
+        + [shape_of((AREA, D), F32 if j == 0 else BF16) for j in range(count)],
     )(row_map, down, *dms, *acts, *a2s, *dhs)
+    grads = []
+    for n in blocks:
+        grads += [made[:n], made[n : 2 * n]]
+        made = made[2 * n :]
+    return *grads, *made
 
 
 def heads_back(qkv_ref, p_ref, do_at, tables, dqkv_ref):
@@ -517,19 +541,20 @@
 
 
 def back_norm_kernel(
-    keep_ref, da2_ref, got_ref, mid_ref, g_ref, params_ref, own_ref, other_ref, att_ref, dmid_ref, dy_ref, do_ref, sums_ref
+    keep_ref, da2_ref, got_ref, mid_ref, g_ref, params_ref, own_ref, other_ref, att_ref,
+    dmid_ref, do_ref, dy_ref, sums_ref,
 ):
     da2 = da2_ref[...] + got_ref[...].astype(F32)
     unit, factor = norm_parts(mid_ref[...])
     dmid = g_ref[...].astype(F32) + norm_back(da2, unit, factor, params_ref[3:4])
     dmid_ref[...] = dmid
-    rate = jnp.where(keep_ref[0, 0] > 0, 1.0 / 0.9, 0.0).astype(F32)
-    dy = (rate * dmid).astype(BF16)
+    dy = (rate_of(keep_ref, 0) * dmid).astype(BF16)
     dy_ref[...] = dy
     moved = jnp.concatenate(
         [dot_nt(dy, own_ref[:, TIER:]).astype(BF16), dot_nt(dy, other_ref[:, TIER:]).astype(BF16)], axis=1
     )
-    do_ref[...] = dot_nn(moved, att_ref[...]).astype(BF16)
+    rows = dot_nn(moved, att_ref[...]).astype(BF16)
+    do_ref[...] = dot_nn(spread_rows(), rows).astype(BF16)
     sums_ref[0:1] = jnp.sum(dy.astype(F32), axis=0, keepdims=True)
     sums_ref[1:2] = jnp.sum(da2 * unit, axis=0, keepdims=True)
     sums_ref[2:3] = jnp.sum(da2, axis=0, keepdims=True)
@@ -540,56 +565,49 @@
         "backnorm",
         back_norm_kernel,
         9,
-        [shape_of((R, D), F32), shape_of((R, D), BF16), shape_of((R, D), BF16), shape_of((3, D), F32)],
+        [shape_of((AREA, D), F32), shape_of((R, D), BF16), shape_of((AREA, D), BF16), shape_of((3, D), F32)],
         smem=1,
     )(*args)
 
 
-def back_first_kernel(
-    dy_ref, do_ref, turned_ref, o_ref, qkv_ref, p_ref, table_ref,
-    dqkv_ref, weights_ref, send_ref, sums_ref, tablegrad_ref,
-):
-    tablegrad_ref[...] = heads_back(qkv_ref, p_ref, lambda at: do_ref[:, at : at + LANES], table_ref[...], dqkv_ref)
-    for s, out in enumerate((weights_ref, send_ref)):
-        rows = slice(s * HALF, (s + 1) * HALF)
-        out[:, :TIER] = dot_nn(turned_ref[rows], dqkv_ref[...]).astype(BF16)
-        out[:, TIER:] = dot_nn(o_ref[rows], dy_ref[...]).astype(BF16)
+def back_kernel(tier, do_ref, turned_ref, qkv_ref, p_ref, table_ref, *refs):
+    if tier == 0:
+        o_ref, dy_ref, *refs = refs
+    dqkv_ref, *refs, sums_ref, tab_ref = refs
+    tab_ref[...] = heads_back(
+        qkv_ref, p_ref, lambda at: do_ref[:, tier * HALF + at : tier * HALF + at + LANES], table_ref[...], dqkv_ref
+    )
+    wide = lax.axis_size("mp")
+    blocks = (wide, 2)[tier]
+    rows = HALF // (2 * wide)
+    for s in range(2):
+        part = dot_nn(turned_ref[s * HALF : (s + 1) * HALF], dqkv_ref[...]).astype(BF16)
+        outs = refs[s * blocks : (s + 1) * blocks]
+        if tier == 0:
+            more = dot_nn(o_ref[s * HALF : (s + 1) * HALF], dy_ref[...]).astype(BF16)
+        for x in range(wide):
+            if tier == 0:
+                outs[x][:, :TIER] = part[2 * x * rows : 2 * (x + 1) * rows]
+                outs[x][:, TIER:] = more[2 * x * rows : 2 * (x + 1) * rows]
+                continue
+            for y in range(2):
+                at_row = (x * 2 + y) * rows
+                outs[y][x * rows : (x + 1) * rows] = part[at_row : at_row + rows]
     sums_ref[:, :HALF] = jnp.sum(dqkv_ref[:, :HALF].astype(F32), axis=0, keepdims=True)
     sums_ref[:, HALF:] = jnp.sum(dqkv_ref[:, 2 * HALF :].astype(F32), axis=0, keepdims=True)
 
 
-def back_first(*args):
-    return kernel_call(
-        "back1",
-        back_first_kernel,
-        7,
-        [
-            shape_of((R, TIER), BF16), shape_of((HALF, TIER + D), BF16), shape_of((HALF, TIER + D), BF16),
-            shape_of((1, D), F32), shape_of((HEAD, LANES), F32),
-        ],
+def back(tier, *args):
+    blocks = (lax.axis_size("mp"), 2)[tier]
+    dqkv, *grads, sums, table = kernel_call(
+        f"back{tier + 1}",
+        partial(back_kernel, tier),
+        len(args),
+        [shape_of((R, TIER), BF16)]
+        + [shape_of((HALF // blocks, TIER + D * (tier == 0)), BF16)] * (2 * blocks)
+        + [shape_of((1, D), F32), shape_of((HEAD, LANES), F32)],
     )(*args)
-
-
-def back_second_kernel(
-    do_ref, turned_ref, qkv_ref, p_ref, table_ref, dqkv_ref, keep_ref, send_ref, sums_ref, tablegrad_ref
-):
-    tablegrad_ref[...] = heads_back(qkv_ref, p_ref, lambda at: do_ref[:, HALF + at : HALF + at + LANES], table_ref[...], dqkv_ref)
-    for s, out in enumerate((keep_ref, send_ref)):
-        out[...] = dot_nn(turned_ref[s * HALF : (s + 1) * HALF], dqkv_ref[...]).astype(BF16)
-    sums_ref[:, :HALF] = jnp.sum(dqkv_ref[:, :HALF].astype(F32), axis=0, keepdims=True)
-    sums_ref[:, HALF:] = jnp.sum(dqkv_ref[:, 2 * HALF :].astype(F32), axis=0, keepdims=True)
-
-
-def back_second(*args):
-    return kernel_call(
-        "back2",
-        back_second_kernel,
-        5,
-        [
-            shape_of((R, TIER), BF16), shape_of((HALF, TIER), BF16), shape_of((HALF, TIER), BF16),
-            shape_of((1, D), F32), shape_of((HEAD, LANES), F32),
-        ],
-    )(*args)
+    return dqkv, grads[:blocks], grads[blocks:], sums, table
 
 
 def finish_kernel(
@@ -597,25 +615,26 @@
     params_ref, mid_ref, m_ref, mgot_ref, downb_ref, upb_ref, sums0_ref, sums1_ref, sums2_ref, tab1_ref, tab2_ref,
     dx_ref, result_ref, small_ref,
 ):
+    spread = spread_rows()
+    dq1, dq2 = dot_tn(spread, dq1_ref[...]).astype(BF16), dot_tn(spread, dq2_ref[...]).astype(BF16)
     halves = []
     for first, second in ((own1_ref, own2_ref), (other1_ref, other2_ref)):
-        halves.append(dot_nt(dq1_ref[...], first[...]) + dot_nt(dq2_ref[...], second[:, :TIER]))
+        halves.append(dot_nt(dq1, first[...]) + dot_nt(dq2, second[:, :TIER]))
     moved = jnp.concatenate(halves, axis=1)
     high = moved.astype(BF16)
     low = (moved - high.astype(F32)).astype(BF16)
     da1 = dot_nn(high, att_ref[...]) + dot_nn(low, att_ref[...])
     unit, factor = norm_parts(x_ref[...].astype(F32))
-    dx = (dmid_ref[...] + norm_back(da1, unit, factor, params_ref[0:1])).astype(BF16)
-    rate = jnp.where(keep_ref[0, 1] > 0, 1.0 / 0.9, 0.0).astype(F32)
+    dx_ref[...] = (dmid_ref[...] + norm_back(da1, unit, factor, params_ref[0:1])).astype(BF16)
+    rate = rate_of(keep_ref, 1)
     total = m_ref[...] + mgot_ref[...].astype(F32) + params_ref[5:6]
-    result = (mid_ref[...] + rate * total).astype(BF16)
-    spread = spread_rows()
-    dx_ref[...] = dot_tn(spread, dx).astype(BF16)
-    result_ref[...] = dot_tn(spread, result).astype(BF16)
+    result_ref[...] = (mid_ref[...] + rate * total).astype(BF16)
+
+    small_ref[...] = jnp.zeros(small_ref.shape, F32)
 
     def put(name, value):
         for i in range(D // LANES):
-            small_ref[SMALL[name] + i : SMALL[name] + i + 1] = value[:, i * LANES : (i + 1) * LANES]
+            small_ref[piece(SMALL[name] + i)] = value[:, i * LANES : (i + 1) * LANES]
 
     put("gain1", jnp.sum(da1 * unit, axis=0, keepdims=True))
     put("shift1", jnp.sum(da1, axis=0, keepdims=True))
@@ -625,13 +644,28 @@
     put("qbias", jnp.concatenate([sums1_ref[:, :HALF], sums2_ref[:, :HALF]], axis=1))
     put("vbias", jnp.concatenate([sums1_ref[:, HALF:], sums2_ref[:, HALF:]], axis=1))
     put("downb", downb_ref[...])
-    small_ref[SMALL_TABLE : SMALL_TABLE + HEAD] = tab1_ref[...] + tab2_ref[...]
-    rows = upb_ref.shape[1] // LANES
+    table = tab1_ref[...] + tab2_ref[...]
+    low, high = table[: HEAD // 2], table[HEAD // 2 :]
+    lane = iota(low.shape, 1)
+    packed = jnp.where(
+        lane < 32,
+        low,
+        jnp.where(
+            lane < 64,
+            pltpu.roll(low, (32 - W_START) % LANES, 1),
+            jnp.where(lane < 96, pltpu.roll(high, 64, 1), pltpu.roll(high, (96 - W_START) % LANES, 1)),
+        ),
+    )
+    for i in range(HEAD // 2):
+        small_ref[piece(SMALL_TABLE + i)] = packed[i : i + 1]
+    count = lax.axis_size("dp")
+    size = upb_ref.shape[1] // count
     for m in range(wide):
-        for i in range(rows):
-            value = upb_ref[:, i * LANES : (i + 1) * LANES]
-            at = SMALL_UP + m * rows + i
-            small_ref[at : at + 1] = jnp.where(lax.axis_index("mp") == m, value, 0.0)
+        for i in range(count):
+            rows, lanes = piece(SMALL_UP + m * count + i)
+            value = upb_ref[:, i * size : (i + 1) * size]
+            lanes = slice(lanes.start, lanes.start + size)
+            small_ref[rows, lanes] = jnp.where(lax.axis_index("mp") == m, value, 0.0)
 
 
 def finish(wide, rows, *args):
@@ -639,9 +673,60 @@
         "finish",
         partial(finish_kernel, wide),
         21,
-        [shape_of((AREA, D), BF16), shape_of((AREA, D), BF16), shape_of((rows, LANES), F32)],
-        smem=1,
+        [shape_of((AREA, D), BF16), shape_of((AREA, D), BF16), shape_of((rows, TIER), F32)],
+        smem=1, out_far=(0, 1),
     )(*args)
+
+
+def outputs_kernel(
+    n_parts, rows, *refs
+):
+    parts, refs = refs[:n_parts], refs[n_parts:]
+    gain1_ref, shift1_ref, qv_ref, relh_ref, relw_ref, projb_ref, gain2_ref, shift2_ref, upb_ref, downb_ref = refs[:10]
+    table_ref, up_ref = refs[10:]
+    total = parts[0][...]
+    for part in parts[1:]:
+        total = total + part[part.shape[0] - rows :].astype(F32)
+    flat = {
+        "gain1": gain1_ref, "shift1": shift1_ref, "projb": projb_ref, "gain2": gain2_ref, "shift2": shift2_ref,
+        "downb": downb_ref,
+    }
+
+    def at(place):
+        here, lanes = piece(place)
+        return total[here, lanes]
+
+    for i in range(D // LANES):
+        here = slice(i * LANES, (i + 1) * LANES)
+        for name, ref in flat.items():
+            ref[here] = at(SMALL[name] + i)[0]
+        qv_ref[0:1, here] = at(SMALL["qbias"] + i)
+        qv_ref[1:2, here] = at(SMALL["vbias"] + i)
+    for i in range(HEAD // 2):
+        table_ref[i : i + 1] = at(SMALL_TABLE + i)
+    for start, ref in ((0, relh_ref), (32, relw_ref)):
+        for half in range(2):
+            ref[:, half * 32 : half * 32 + 32] = lax.dot_general(
+                table_places(start + 64 * half), table_ref[...], (((1,), (1,)), ((), ())),
+                precision=lax.Precision.HIGHEST, preferred_element_type=F32,
+            )
+    for i in range(up_ref.shape[0]):
+        up_ref[i : i + 1] = at(SMALL_UP + i)
+    place = lax.axis_index("mp") * lax.axis_size("dp") + lax.axis_index("dp")
+    upb_ref[...] = up_ref[place, : upb_ref.shape[0]]
+
+
+def outputs(parts, size, ups):
+    row = shape_of((D,), F32)
+    table = shape_of((TABLE, HEAD), F32)
+    return kernel_call(
+        "outputs",
+        partial(outputs_kernel, len(parts), parts[0].shape[0]),
+        len(parts),
+        [row, row, shape_of((2, D), F32), table, table, row, row, row, shape_of((size,), F32), row],
+        scratch=[pltpu.VMEM((HEAD // 2, LANES), F32), pltpu.VMEM((ups, LANES), F32)],
+        out_far=range(10),
+    )(*parts)
 
 
 def per_device(
@@ -650,33 +735,51 @@
 ):
     wide = lax.axis_size("mp")
     hidden = fc1_weight.shape[1]
-    first, second, params = pack(
-        qkv_weight, proj_weight, ln1_gain, ln1_bias, proj_bias, ln2_gain, ln2_bias, fc2_bias, qv_bias
-    )
-    line1 = gather_z(first)
-    line2 = gather_z(second)
-    rows_in, a1, a1_turned, grad_out, dm, att_map, feed_map, tables, fill, downb, upb = prepare(
-        keep_mask, tokens, out_grad, params, rel_pos_h, rel_pos_w, key_mask, fc1_bias
-    )
-    dms = [dm] + [move_x(dm, -s) for s in range(1, wide)]
-    line1 = after(line1, a1)
-    near1 = gather_near(line1)
-    gacts = [act_grad(dm, fc2_weight)]
-    near1, line2, dms, gacts = lax.optimization_barrier((near1, line2, dms, gacts))
-    far1 = gather_far(near1)
-    near2 = gather_near(line2)
-    for v in dms[1:]:
-        gacts.append(act_grad(after(v, gacts[-1]), fc2_weight))
-    far1, near2, gacts = lax.optimization_barrier((far1, near2, gacts))
-    own1 = gather_join(line1, near1, far1)
-    other1 = move_c(own1)
-    far2 = gather_far(near2)
-    qkv1, probs1, att1 = attend_first(a1, own1, other1, params, tables, fill)
-    far2, att1 = lax.optimization_barrier((far2, att1))
-    own2 = gather_join(line2, near2, far2)
-    other2 = move_c(own2)
+    first, second, params, dm = pack(
+        keep_mask, qkv_weight, proj_weight, ln1_gain, ln1_bias, proj_bias, ln2_gain, ln2_bias, fc2_bias, qv_bias, out_grad
+    )
+    made, chains = {}, {}
+
+    def gated(value, task, kind):
+        others = [made[name] for name in GATES.get(f"{task}:{kind}", ())]
+        return after(value, *others) if others else value
+
+    def front(name):
+        if name == "dm":
+            sent = gated(dm, name, "s")
+            return gated([move_x(sent, -s) for s in range(1, wide)], name, "r")
+        if name == "prep":
+            return prepare(gated(tokens, name, "s"), params, rel_pos_h, rel_pos_w, key_mask, fc1_bias)
+        if name == "act0":
+            return act_grad(gated(dm, name, "s"), fc2_weight)
+        if name == "act1":
+            return [act_grad(v, fc2_weight) for v in gated(made["dm"], name, "s")]
+        if name == "attend1":
+            a1, _, _, _, tables, fill, _ = made["prep"]
+            return attend_first(gated(a1, name, "s"), chains["1"], made["c1"], params, tables, fill)
+        step, tier = name
+        if step == "z":
+            sent = gated((first, second)[int(tier) - 1], name, "s")
+            chains[tier] = gated(gather_z(sent), name, "r")
+            return chains[tier]
+        if step == "n":
+            return gated(gather_near(gated(chains[tier], name, "s")), name, "r")
+        if step == "f":
+            made["n" + tier] = gated(made["n" + tier], name, "s")
+            return gated(gather_far(made["n" + tier]), name, "r")
+        chains[tier] = gated(gather_join(chains[tier], made["n" + tier], made["f" + tier]), name, "s")
+        return gated(move_c(chains[tier]), name, "r")
+
+    for name in FRONT:
+        made[name] = front(name)
+    a1, a1_turned, att_map, feed_map, tables, fill, upb = made["prep"]
+    dms = [dm, *made["dm"]]
+    acts = [made["act0"], *made["act1"]]
+    gacts, downb = [v[0] for v in acts], acts[0][1]
+    own1, other1, own2, other2 = chains["1"], made["c1"], chains["2"], made["c2"]
+    qkv1, probs1, att1 = made["attend1"]
     qkv2, probs2, att_turned, middle, a2 = attend_second(
-        keep_mask, a1, own2, other2, params, tables, fill, att1, rows_in, att_map
+        keep_mask, a1, own2, other2, params, tables, fill, att1, tokens, att_map
     )
 
     a2s = [a2] + [move_x(a2, -s) for s in range(1, wide)]
@@ -690,35 +793,81 @@
     )
     got, down_send, up_send, outs = lax.optimization_barrier((got, down_send, up_send, outs))
     got = got[0] if wide == 2 else add_up(*got)
-    down_rows = add_up(down_keep, move_c(down_send))
-    up_rows = add_up(up_keep, move_c(up_send))
-    dmid, dy, do, sums0 = back_norm(keep_mask, da2, got, middle, grad_out, params, own2, other2, att_map)
-    down_rows, up_rows, do = lax.optimization_barrier((down_rows, up_rows, do))
-    out_got = [move_x(outs[s], s) for s in range(1, wide)]
-    dqkv1, keep1, send1, sums1, tab1 = back_first(dy, do, a1_turned, att_turned, qkv1, probs1, tables)
-    rows1 = add_up(keep1, move_c(send1))
-    rows1, do = lax.optimization_barrier((rows1, do))
-    down_rows = scatter_y(down_rows)
-    out_got = out_got[0] if wide == 2 else add_up(*out_got)
-    rows1 = scatter_x(rows1)
-    down_grad = scatter_z(down_rows)
-    dqkv2, keep2, send2, sums2, tab2 = back_second(do, a1_turned, qkv2, probs2, tables)
-    up_rows = scatter_y(up_rows, send2)
-    rows2 = add_up(keep2, move_c(send2))
-    rows1, rows2, dqkv2 = lax.optimization_barrier((rows1, rows2, dqkv2))
-    rows1 = scatter_y(rows1)
-    rows2 = scatter_x(rows2)
-    up_grad = scatter_z(up_rows)
-    small_rows = SMALL_UP + wide * hidden // LANES
-    small_rows += -small_rows % 8
-    grad_in, result, small = finish(
-        wide, small_rows, keep_mask, dqkv1, dqkv2, own1, other1, own2, other2, att_map, rows_in, dmid, params,
-        middle, outs[0], out_got, downb, upb_sum, sums0, sums1, sums2, tab1, tab2,
-    )
-    rows1, rows2, small = lax.optimization_barrier((rows1, rows2, small))
-    rows1 = scatter_z(rows1)
-    rows2 = scatter_z(scatter_y(rows2))
-    small = sum_small(small)
+    depth = lax.axis_size("dp") // 4
+    moves = {"x": (move_x, wide), "y": (turn_y, 2), "z": (move_z, depth)}
+    small_rows = -(-(SMALL_UP + wide * lax.axis_size("dp")) // PIECES)
+    small_rows += -small_rows % 16
+
+    def cores(name, keep, send, axes):
+        sent = gated(send, f"{name}c", "s")
+        got = gated([move_c(v) for v in sent], f"{name}c", "r")
+        chains[name] = (list(zip(keep, got)), axes)
+        return got
+
+    def along(name, axis):
+        sums, axes = chains[name]
+        move, _ = moves[axis]
+        sent = [add_up(*v).astype(BF16) for v in sums[1:]]
+        if name == "b":
+            extra = chains["s"].astype(BF16)
+            sent = [jnp.concatenate([v, extra]) for v in sent]
+        sent = gated(sent, f"{name}{axis}", "s")
+        got = gated([move(v, s + 1) for s, v in enumerate(sent)], f"{name}{axis}", "r")
+        rest = [*sums[0], *got]
+        if name == "b":
+            rows = sums[0][0].shape[0]
+            rest = [*sums[0], *[v[:rows] for v in got]]
+            if axis == "z":
+                chains["s"] = [chains["s"], *got]
+            else:
+                chains["s"] = add_up(chains["s"], *[v[rows:] for v in got])
+        axes = axes[axes.index(axis) + 1 :]
+        chains[name] = (split(rest, moves[axes[0]][1]), axes) if axes else (rest, axes)
+        return got
+
+    def small_cores():
+        flat = gated(made["finish"][2], "sc", "s")
+        got = gated(move_c(flat), "sc", "r")
+        chains["s"] = flat + got
+        return got
+
+    def task(name):
+        if name == "norm":
+            return back_norm(keep_mask, da2, got, middle, out_grad, params, own2, other2, att_map)
+        if name in ("back1", "back2"):
+            tier = int(name[-1]) - 1
+            do = gated(made["norm"][1], name, "s")
+            more = (att_turned, made["norm"][2]) if tier == 0 else ()
+            return back(tier, do, a1_turned, (qkv1, qkv2)[tier], (probs1, probs2)[tier], tables, *more)
+        if name == "m":
+            moved = [move_x(v, s + 1) for s, v in enumerate(gated(outs[1:], "m", "s"))]
+            moved = gated(moved, "m", "r")
+            return moved[0] if wide == 2 else add_up(*moved)
+        if name == "finish":
+            first, second = made["back1"], made["back2"]
+            mid = gated(middle, "finish", "s")
+            return finish(
+                wide, small_rows, keep_mask, first[0], second[0], own1, other1, own2, other2, att_map, tokens,
+                made["norm"][0], params, mid, outs[0], made["m"], downb, upb_sum, made["norm"][3], first[3], second[3],
+                first[4], second[4],
+            )
+        chain, axis = name
+        if chain == "s":
+            return small_cores()
+        if axis != "c":
+            return along(chain, axis)
+        if chain in "du":
+            keep, send = (down_keep, down_send) if chain == "d" else (up_keep, up_send)
+            return cores(chain, keep, send, "zy" if Z_FIRST["du".index(chain)] else "yz")
+        tier = "ab".index(chain)
+        return cores(chain, made[f"back{tier + 1}"][1], made[f"back{tier + 1}"][2], ("xyz", "yxz")[tier])
+
+    for name in ORDER:
+        made[name] = task(name)
+    grad_in, result, _ = made["finish"]
+    small = chains["s"]
+    down_grad, up_grad, rows1, rows2 = (add_up(*chains[name][0]) for name in "duab")
+    proj_grad = rows1[:, TIER:]
 
     pieces = [
         piece
@@ -726,21 +875,13 @@
         for piece in (rows1[:, i * HALF : (i + 1) * HALF], rows2[:, i * HALF : (i + 1) * HALF])
     ]
     qkv_grad = jnp.concatenate(pieces, axis=1)
-    proj_grad = rows1[:, TIER:]
-
-    def vector(name):
-        return small[SMALL[name] : SMALL[name] + D // LANES].reshape(D)
-
-    table = small[SMALL_TABLE : SMALL_TABLE + HEAD]
-    relh_grad = table[:, :TABLE].T[::-1]
-    relw_grad = table[:, HEAD + ROW + 2 : HEAD + ROW + 2 + TABLE].T[::-1]
-    up_all = small[SMALL_UP : SMALL_UP + wide * hidden // LANES].reshape(-1)
-    size = hidden // lax.axis_size("dp")
-    up_bias_grad = lax.dynamic_slice(up_all, (lax.axis_index("mp") * hidden + lax.axis_index("dp") * size,), (size,))
-    qv_grad = jnp.stack([vector("qbias"), vector("vbias")])
+
+    gain1, shift1, qv_grad, relh_grad, relw_grad, projb, gain2, shift2, up_bias_grad, downb = outputs(
+        small, hidden // lax.axis_size("dp"), wide * lax.axis_size("dp")
+    )
     return (
-        result, grad_in, vector("gain1"), vector("shift1"), qkv_grad, qv_grad, relh_grad, relw_grad, proj_grad,
-        vector("projb"), vector("gain2"), vector("shift2"), up_grad, up_bias_grad, down_grad.T, vector("downb"),
+        result, grad_in, gain1, shift1, qkv_grad, qv_grad, relh_grad, relw_grad, proj_grad, projb, gain2, shift2,
+        up_grad, up_bias_grad, down_grad.T, downb,
     )
 
 

time: 180 us -> 150 us (0.83)
  local copies, waits for them, and re-layouts: 14.8 us -> 2.73 us
  waiting for transfers between devices: 59.5 us -> 48.5 us
  other arithmetic: 10.2 us -> 3.59 us
  starting transfers between devices: 53.6 us -> 51.4 us
    ppermute x11 -> x10, waiting for transfers between devices: 33.6 us -> 13.8 us  [move_x(): lax.ppermute(value, 'mp', [(i, (i + step) % count) for i in range(count)])]
    ppermute x21 -> x18, waiting for transfers between devices: 13.7 us -> 24.1 us  [move_z(): return lax.ppermute(value, 'dp', dp_pairs(lax.axis_size('dp'), dz=step))]
    unnamed x73 -> x31, local copies, waits for them, and re-layouts: 8.66 us -> 1.83 us
    ppermute x21 -> x18, starting transfers between devices: 34.2 us -> 28.1 us  [move_z(): return lax.ppermute(value, 'dp', dp_pairs(lax.axis_size('dp'), dz=step))]
    add x10 -> x3, other arithmetic: 6.51 us -> 0.98 us  [add_up(): total = total + other.astype(F32)]
    ppermute x11 -> x10, starting transfers between devices: 8.48 us -> 12.6 us  [move_x(): lax.ppermute(value, 'mp', [(i, (i + step) % count) for i in range(count)])]
    slice x10 -> x0, local copies, waits for them, and re-layouts: 3.79 us -> none  [the longest x4 3.56 us: scatter_y(): return add_up(rows[:size], after(move_y(rows[size:].astype(BF16)), *others))]
    another operation x5 -> x0, other arithmetic: 2.51 us -> none
  transfers between devices with their start and end apart: 48 -> 47, of which waited for: 21 -> 24; matrix products, arithmetic and copies ran while one was open for 6% -> 3% of each run, Pallas kernels for 18% -> 22%
where the time goes in v4:
time: 150 us; the launch traced here: 149 us
  starting transfers between devices  51.4 us (34%)
  waiting for transfers between devices  48.5 us (32%)
  Pallas kernels  42 us (28%)
  other arithmetic  3.59 us (2%)
  local copies, waits for them, and re-layouts  2.73 us (2%)
    pallas_call x14, Pallas kernels, run(): call(*args[:smem], *map(pltpu.with_memory_space_constraint, args[smem:],...  42 us
    ppermute x18, starting transfers between devices, move_z(): return lax.ppermute(value, 'dp', dp_pairs(lax.axis_size('dp'), dz=step))  28.1 us
    ppermute x18, waiting for transfers between devices, move_z(): return lax.ppermute(value, 'dp', dp_pairs(lax.axis_size('dp'), dz=step))  24.1 us
    ppermute x10, waiting for transfers between devices, move_x(): lax.ppermute(value, 'mp', [(i, (i + step) % count) for i in range(count)])  13.8 us
    ppermute x10, starting transfers between devices, move_x(): lax.ppermute(value, 'mp', [(i, (i + step) % count) for i in range(count)])  12.6 us
    ppermute x8, starting transfers between devices, move_y(): return lax.ppermute(value, 'dp', dp_pairs(lax.axis_size('dp'), dy=1))  8.67 us
    ppermute x8, waiting for transfers between devices, move_y(): return lax.ppermute(value, 'dp', dp_pairs(lax.axis_size('dp'), dy=1))  6.05 us
    ppermute x11, waiting for transfers between devices, move_c(): return lax.ppermute(value, 'dp', dp_pairs(lax.axis_size('dp'), dc=1))  4.53 us
  transfers between devices with their start and end apart: 47, of which 24 were waited for; matrix products, arithmetic and copies ran while one was open for 3% of the time, Pallas kernels for 22%

profile of v4, /device:TPU:0, one launch (start us, length us, event | category | flops | bytes accessed | tf_op | source)
XLA Modules:
  0.0 149.3 jit_solution(11719085614800210512)
XLA Ops:
  1.3 1.2 pack.1
  2.5 3.1 %collective-permute-start.2 = (bf16[24,1920]{1,0:T(8,128)(2,1)S(1)}, bf16[24,1920]{1,0:T(8,128)(2,1)S(1)}, u32[]{:S(2)}, u32[]{:S(2)}) collective-permute-start(bf16[24,1920]{1,0:T(8,128)(2,1)S(1)} %get-tuple-element.128), channel_id=1, source_target_pairs={{0,8},{2,10},{4,12},{6,14},{8,16},{10,18},{12,20},{14,22},{16,24},... | collective-permute-start | bytes 276488 | tf_op jit(solution)/shard_map/ppermute | solution.py:82
  5.6 2.6 %collective-permute-start.1 = (bf16[24,1920]{1,0:T(8,128)(2,1)S(1)}, bf16[24,1920]{1,0:T(8,128)(2,1)S(1)}, u32[]{:S(2)}, u32[]{:S(2)}) collective-permute-start(bf16[24,1920]{1,0:T(8,128)(2,1)S(1)} %get-tuple-element.128), channel_id=1, source_target_pairs={{0,16},{2,18},{4,20},{6,22},{8,24},{10,26},{12,28},{14,30},{16,0},... | collective-permute-start | bytes 276488 | tf_op jit(solution)/shard_map/ppermute | solution.py:82
  8.2 1.3 collective-permute-start
  9.6 1.5 collective-permute-start.8
  11.1 3.5 %prepare.1 = (bf16[224,768]{1,0:T(8,128)(2,1)S(1)}, bf16[768,224]{1,0:T(8,128)(2,1)S(1)}, bf16[768,768]{1,0:T(8,128)(2,1)S(1)}, bf16[768,768]{1,0:T(8,128)(2,1)S...) custom-call(bf16[196,768]{1,0:T(8,128)(2,1)} %x_ref.3, ...), custom_call_target="tpu_custom_call" | custom-call | flops 1 | bytes 1 | tf_op jit(solution)/shard_map/prepare/pallas_call | solution.py:63
  14.6 1.6 %collective-permute-start.4 = (bf16[96,1920]{1,0:T(8,128)(2,1)S(1)}, bf16[96,1920]{1,0:T(8,128)(2,1)S(1)}, u32[]{:S(2)}, u32[]{:S(2)}) collective-permute-start(bf16[96,1920]{1,0:T(8,128)(2,1)S(1)} %pad_maximum_fusion.1), channel_id=1, source_target_pairs={{0,1},{1,0},{2,3},{3,2},{4,5},{5,4},{6,7},{7,6},{8,9},{9,8},{10,11... | collective-permute-start | bytes 1105928 | tf_op jit(solution)/shard_map/ppermute | solution.py:95
  16.2 1.5 %collective-permute-start.3 = (bf16[96,1920]{1,0:T(8,128)(2,1)S(1)}, bf16[96,1920]{1,0:T(8,128)(2,1)S(1)}, u32[]{:S(2)}, u32[]{:S(2)}) collective-permute-start(bf16[96,1920]{1,0:T(8,128)(2,1)S(1)} %pad_maximum_fusion.1), channel_id=1, source_target_pairs={{0,4},{2,6},{4,0},{6,2},{8,12},{10,14},{12,8},{14,10},{16,20},{18,... | collective-permute-start | bytes 1105928 | tf_op jit(solution)/shard_map/ppermute | solution.py:86
  18.4 1.7 %collective-permute-start.11 = (bf16[24,1152]{1,0:T(8,128)(2,1)S(1)}, bf16[24,1152]{1,0:T(8,128)(2,1)S(1)}, u32[]{:S(2)}, u32[]{:S(2)}) collective-permute-start(bf16[24,1152]{1,0:T(8,128)(2,1)S(1)} %get-tuple-element.133), channel_id=1, source_target_pairs={{0,8},{2,10},{4,12},{6,14},{8,16},{10,18},{12,20},{14,22},{16,24},... | collective-permute-start | bytes 165896 | tf_op jit(solution)/shard_map/ppermute | solution.py:82
  20.1 1.7 %collective-permute-start.10 = (bf16[24,1152]{1,0:T(8,128)(2,1)S(1)}, bf16[24,1152]{1,0:T(8,128)(2,1)S(1)}, u32[]{:S(2)}, u32[]{:S(2)}) collective-permute-start(bf16[24,1152]{1,0:T(8,128)(2,1)S(1)} %get-tuple-element.133), channel_id=1, source_target_pairs={{0,16},{2,18},{4,20},{6,22},{8,24},{10,26},{12,28},{14,30},{16,0},... | collective-permute-start | bytes 165896 | tf_op jit(solution)/shard_map/ppermute | solution.py:82
  22.5 2.2 %collective-permute-done.11 = bf16[24,1152]{1,0:T(8,128)(2,1)S(1)} collective-permute-done((bf16[24,1152]{1,0:T(8,128)(2,1)S(1)}, bf16[24,1152]{1,0:T(8,128)(2,1)S(1)}, u32[]{:S(2)}, u32[]{:S(2)}) %collective-permute-start.11) | collective-permute-done | bytes 55328 | tf_op jit(solution)/shard_map/ppermute | solution.py:82
  24.8 1.4 collective-permute-done.10
  29.2 1.6 %collective-permute-start.6 = (bf16[96,960]{1,0:T(8,128)(2,1)S(1)}, bf16[96,960]{1,0:T(8,128)(2,1)S(1)}, u32[]{:S(2)}, u32[]{:S(2)}) collective-permute-start(bf16[96,960]{1,0:T(8,128)(2,1)S(1)} %slice.351), channel_id=1, source_target_pairs={{0,1},{1,0},{2,3},{3,2},{4,5},{5,4},{6,7},{7,6},{8,9},{9,8},{10,11... | collective-permute-start | bytes 552968 | tf_op jit(solution)/shard_map/ppermute | solution.py:95
  30.9 3.4 %collective-permute-done.13 = bf16[96,1152]{1,0:T(8,128)(2,1)S(1)} collective-permute-done((bf16[96,1152]{1,0:T(8,128)(2,1)S(1)}, bf16[96,1152]{1,0:T(8,128)(2,1)S(1)}, u32[]{:S(2)}, u32[]{:S(2)}) %collective-permute-start.13) | collective-permute-done | bytes 221216 | tf_op jit(solution)/shard_map/ppermute | solution.py:86
  34.8 1.6 %collective-permute-start.14 = (bf16[96,576]{1,0:T(8,128)(2,1)S(1)}, bf16[96,576]{1,0:T(8,128)(2,1)S(1)}, u32[]{:S(2)}, u32[]{:S(2)}) collective-permute-start(bf16[96,576]{1,0:T(8,128)(2,1)S(1)} %slice.274), channel_id=1, source_target_pairs={{0,4},{2,6},{4,0},{6,2},{8,12},{10,14},{12,8},{14,10},{16,20},{18,... | collective-permute-start | bytes 331784 | tf_op jit(solution)/shard_map/ppermute | solution.py:86
  37.5 2.2 %collective-permute-done.14 = bf16[96,576]{1,0:T(8,128)(2,1)S(1)} collective-permute-done((bf16[96,576]{1,0:T(8,128)(2,1)S(1)}, bf16[96,576]{1,0:T(8,128)(2,1)S(1)}, u32[]{:S(2)}, u32[]{:S(2)}) %collective-permute-start.14) | collective-permute-done | bytes 110624 | tf_op jit(solution)/shard_map/ppermute | solution.py:86
  39.7 1.5 %collective-permute-done.15 = bf16[96,576]{1,0:T(8,128)(2,1)S(1)} collective-permute-done((bf16[96,576]{1,0:T(8,128)(2,1)S(1)}, bf16[96,576]{1,0:T(8,128)(2,1)S(1)}, u32[]{:S(2)}, u32[]{:S(2)}) %collective-permute-start.15) | collective-permute-done | bytes 110624 | tf_op jit(solution)/shard_map/ppermute | solution.py:95
  41.4 2.4 %collective-permute-done.16.other_ref.other1_ref = bf16[384,1152]{1,0:T(8,128)(2,1)S(1)} collective-permute-done((bf16[384,1152]{1,0:T(8,128)(2,1)S(1)}, bf16[384,1152]{1,0:T(8,128)(2,1)S(1)}, u32[]{:S(2)}, u32[]{:S(2)}) %collective-permute-start.16) | collective-permute-done | bytes 884768 | tf_op jit(solution)/shard_map/ppermute | solution.py:90
  43.8 3.3 %attend1.1 = (bf16[224,1152]{1,0:T(8,128)(2,1)S(1)}, bf16[6,224,224]{2,1,0:T(8,128)(2,1)S(1)}, bf16[224,384]{1,0:T(8,128)(2,1)S(1)}) custom-call(bf16[224,768]{1,0:T(8,128)(2,1)S(1)} %get-tuple-element.141.a1_ref, bf16[384,1152]{1,0:T(8,128)(2,1)S(1)} %maximum_dynamic-update-slice_fusion.1.own_ref.own1_ref, ...), custom_call_target="tpu_custom_call" | custom-call | flops 1 | bytes 1 | tf_op jit(solution)/shard_map/attend1/pallas_call | solution.py:63
  47.2 5.2 %attend2.1 = (bf16[224,1152]{1,0:T(8,128)(2,1)S(1)}, bf16[6,224,224]{2,1,0:T(8,128)(2,1)S(1)}, bf16[768,196]{1,0:T(8,128)(2,1)S(1)}, f32[196,768]{1,0:T(8,128)S(1)}, bf16[196,768]{1,0:T(8,128)(2,1)S(1)}) custom-call(s32[1,2]{1,0:T(1,128)S(1)} %copy-done.5, bf16[224,768]{1,0:T(8,128)(2,1)S(1)} %get-tuple-element.141.a1_ref, ...), custom_call_target="tpu_custom_call" | custom-call | flops 1 | bytes 1 | tf_op jit(solution)/shard_map/attend2/pallas_call | solution.py:63
  54.3 1.4 act.3
  55.9 2.0 %feed.2 = (bf16[196,1536]{1,0:T(8,128)(2,1)S(1)}, bf16[196,1536]{1,0:T(8,128)(2,1)S(1)}, f32[196,768]{1,0:T(8,128)S(1)}) custom-call(bf16[196,768]{1,0:T(8,128)(2,1)S(1)} %get-tuple-element.143.a2_ref.refs_4_, bf16[768,1536]{1,0:T(8,128)(2,1)S(1)} %copy-done.1, f32[1,1536]{1,0:T(1,128)S(1)} %get-tuple-element.137.upb_ref, ...), custom_call_target="tpu_custom_call" | custom-call | flops 1 | bytes 1 | tf_op jit(solution)/shard_map/feed/pallas_call | solution.py:63
  58.0 3.9 %collective-permute-done.17.a2_ref.refs_5_ = bf16[196,768]{1,0:T(8,128)(2,1)S(1)} collective-permute-done((bf16[196,768]{1,0:T(8,128)(2,1)S(1)}, bf16[196,768]{1,0:T(8,128)(2,1)S(1)}, u32[]{:S(2)}, u32[]{:S(2)}) %collective-permute-start.17) | collective-permute-done | bytes 301088 | tf_op jit(solution)/shard_map/ppermute | solution.py:95
  61.8 2.0 %feed.3 = (bf16[196,1536]{1,0:T(8,128)(2,1)S(1)}, bf16[196,1536]{1,0:T(8,128)(2,1)S(1)}, bf16[196,768]{1,0:T(8,128)(2,1)S(1)}) custom-call(bf16[196,768]{1,0:T(8,128)(2,1)S(1)} %collective-permute-done.17.a2_ref.refs_5_, bf16[768,1536]{1,0:T(8,128)(2,1)S(1)} %copy-done.1, f32[1,1536]{1,0:T(1,128)S(1)} %get-tuple-element.137.upb_ref, ...), custom_call_target="tpu_custom_call" | custom-call | flops 1 | bytes 1 | tf_op jit(solution)/shard_map/feed/pallas_call | solution.py:63
  64.8 6.1 %feedw.1 = (bf16[192,1536]{1,0:T(8,128)(2,1)S(1)}, bf16[192,1536]{1,0:T(8,128)(2,1)S(1)}, bf16[192,1536]{1,0:T(8,128)(2,1)S(1)}, bf16[192,1536]{1,0:T(8,128)(2,1...) custom-call(bf16[768,768]{1,0:T(8,128)(2,1)S(1)} %get-tuple-element., ...), custom_call_target="tpu_custom_call" | custom-call | flops 1 | bytes 1 | tf_op jit(solution)/shard_map/feedw/pallas_call | solution.py:63
  70.8 1.5 %collective-permute-done.18.got_ref = bf16[196,768]{1,0:T(8,128)(2,1)S(1)} collective-permute-done((bf16[196,768]{1,0:T(8,128)(2,1)S(1)}, bf16[196,768]{1,0:T(8,128)(2,1)S(1)}, u32[]{:S(2)}, u32[]{:S(2)}) %collective-permute-start.18) | collective-permute-done | bytes 301088 | tf_op jit(solution)/shard_map/ppermute | solution.py:95
  72.9 1.5 %collective-permute-done.20 = bf16[192,1536]{1,0:T(8,128)(2,1)S(1)} collective-permute-done((bf16[192,1536]{1,0:T(8,128)(2,1)S(1)}, bf16[192,1536]{1,0:T(8,128)(2,1)S(1)}, u32[]{:S(2)}, u32[]{:S(2)}) %collective-permute-start.20) | collective-permute-done | bytes 589856 | tf_op jit(solution)/shard_map/ppermute | solution.py:90
  75.8 1.6 %collective-permute-start.21 = (bf16[196,768]{1,0:T(8,128)(2,1)S(1)}, bf16[196,768]{1,0:T(8,128)(2,1)S(1)}, u32[]{:S(2)}, u32[]{:S(2)}) collective-permute-start(bf16[196,768]{1,0:T(8,128)(2,1)S(1)} %get-tuple-element.173), channel_id=1, source_target_pairs={{0,1},{1,0},{2,3},{3,2},{4,5},{5,4},{6,7},{7,6},{8,9},{9,8},{10,11... | collective-permute-start | bytes 903176 | tf_op jit(solution)/shard_map/ppermute | solution.py:95
  77.3 2.1 %backnorm.1 = (f32[196,768]{1,0:T(8,128)S(1)}, bf16[224,768]{1,0:T(8,128)(2,1)S(1)}, bf16[196,768]{1,0:T(8,128)(2,1)S(1)}, f32[3,768]{1,0:T(4,128)S(1)}) custom-call(s32[1,2]{1,0:T(1,128)S(1)} %copy-done.5, f32[196,768]{1,0:T(8,128)S(1)} %get-tuple-element.145.da2_ref, bf16[196,768]{1,0:T(8,128)(2,1)S(1)} %collective-permute-done.18.got_ref, ...), custom_call_target="tpu_custom_call" | custom-call | flops 1 | bytes 1 | tf_op jit(solution)/shard_map/backnorm/pallas_call | solution.py:63
  79.4 4.6 %back1.1 = (bf16[224,1152]{1,0:T(8,128)(2,1)S(1)}, bf16[192,1920]{1,0:T(8,128)(2,1)S(1)}, bf16[192,1920]{1,0:T(8,128)(2,1)S(1)}, bf16[192,1920]{1,0:T(8,128)(2,1...) custom-call(bf16[224,768]{1,0:T(8,128)(2,1)S(1)} %get-tuple-element.174.do_ref, ...), custom_call_target="tpu_custom_call" | custom-call | flops 1 | bytes 1 | tf_op jit(solution)/shard_map/back1/pallas_call | solution.py:63
  85.1 4.5 %back2.1 = (bf16[224,1152]{1,0:T(8,128)(2,1)S(1)}, bf16[192,1152]{1,0:T(8,128)(2,1)S(1)}, bf16[192,1152]{1,0:T(8,128)(2,1)S(1)}, bf16[192,1152]{1,0:T(8,128)(2,1...) custom-call(bf16[224,768]{1,0:T(8,128)(2,1)S(1)} %get-tuple-element.174.do_ref, ...), custom_call_target="tpu_custom_call" | custom-call | flops 1 | bytes 1 | tf_op jit(solution)/shard_map/back2/pallas_call | solution.py:63
  92.4 4.3 %finish.1 = (bf16[196,768]{1,0:T(8,128)(2,1)}, bf16[196,768]{1,0:T(8,128)(2,1)}, f32[16,1152]{1,0:T(8,128)S(1)}) custom-call(s32[1,2]{1,0:T(1,128)S(1)} %copy-done.5, bf16[224,1152]{1,0:T(8,128)(2,1)S(1)} %get-tuple-element.171.dq1_ref, bf16[224,1152]{1,0:T(8,128)(2,1)S(1)} %get-tuple-element.177.dq2_ref, ...), custom_call_target="tpu_custom_call" | custom-call | flops 1 | bytes 1 | tf_op jit(solution)/shard_map/finish/pallas_call | solution.py:63
  96.9 1.6 %collective-permute-start.37 = (bf16[48,1536]{1,0:T(8,128)(2,1)S(1)}, bf16[48,1536]{1,0:T(8,128)(2,1)S(1)}, u32[]{:S(2)}, u32[]{:S(2)}) collective-permute-start(bf16[48,1536]{1,0:T(8,128)(2,1)S(1)} %get-tuple-element.218), channel_id=1, source_target_pairs={{0,8},{2,10},{4,12},{6,14},{8,16},{10,18},{12,20},{14,22},{16,24},... | collective-permute-start | bytes 442376 | tf_op jit(solution)/shard_map/ppermute | solution.py:82
  98.5 1.8 %collective-permute-start.38 = (bf16[48,1536]{1,0:T(8,128)(2,1)S(1)}, bf16[48,1536]{1,0:T(8,128)(2,1)S(1)}, u32[]{:S(2)}, u32[]{:S(2)}) collective-permute-start(bf16[48,1536]{1,0:T(8,128)(2,1)S(1)} %get-tuple-element.219), channel_id=1, source_target_pairs={{0,16},{2,18},{4,20},{6,22},{8,24},{10,26},{12,28},{14,30},{16,0},... | collective-permute-start | bytes 442376 | tf_op jit(solution)/shard_map/ppermute | solution.py:82
  101.6 1.1 collective-permute-start.35
  102.8 2.6 %collective-permute-done.37 = bf16[48,1536]{1,0:T(8,128)(2,1)S(1)} collective-permute-done((bf16[48,1536]{1,0:T(8,128)(2,1)S(1)}, bf16[48,1536]{1,0:T(8,128)(2,1)S(1)}, u32[]{:S(2)}, u32[]{:S(2)}) %collective-permute-start.37) | collective-permute-done | bytes 147488 | tf_op jit(solution)/shard_map/ppermute | solution.py:82
  105.5 1.3 collective-permute-start.26
  106.7 4.4 %collective-permute-done.38 = bf16[48,1536]{1,0:T(8,128)(2,1)S(1)} collective-permute-done((bf16[48,1536]{1,0:T(8,128)(2,1)S(1)}, bf16[48,1536]{1,0:T(8,128)(2,1)S(1)}, u32[]{:S(2)}, u32[]{:S(2)}) %collective-permute-start.38) | collective-permute-done | bytes 147488 | tf_op jit(solution)/shard_map/ppermute | solution.py:82
  111.3 3.7 %collective-permute-start.44 = (bf16[48,1536]{1,0:T(8,128)(2,1)S(1)}, bf16[48,1536]{1,0:T(8,128)(2,1)S(1)}, u32[]{:S(2)}, u32[]{:S(2)}) collective-permute-start(bf16[48,1536]{1,0:T(8,128)(2,1)S(1)} %get-tuple-element.243), channel_id=1, source_target_pairs={{0,8},{2,10},{4,12},{6,14},{8,16},{10,18},{12,20},{14,22},{16,24},... | collective-permute-start | bytes 442376 | tf_op jit(solution)/shard_map/ppermute | solution.py:82
  115.2 1.3 collective-permute-start.45
  117.5 1.4 collective-permute-start.29
  119.7 1.2 collective-permute-start.36
  120.8 4.4 %collective-permute-done.29 = bf16[112,1152]{1,0:T(8,128)(2,1)S(1)} collective-permute-done((bf16[112,1152]{1,0:T(8,128)(2,1)S(1)}, bf16[112,1152]{1,0:T(8,128)(2,1)S(1)}, u32[]{:S(2)}, u32[]{:S(2)}) %collective-permute-start.29) | collective-permute-done | bytes 258080 | tf_op jit(solution)/shard_map/ppermute | solution.py:95
  125.3 2.6 %collective-permute-start.34 = (bf16[40,1152]{1,0:T(8,128)(2,1)S(1)}, bf16[40,1152]{1,0:T(8,128)(2,1)S(1)}, u32[]{:S(2)}, u32[]{:S(2)}) collective-permute-start(bf16[40,1152]{1,0:T(8,128)(2,1)S(1)} %get-tuple-element.252), channel_id=1, source_target_pairs={{0,24},{2,26},{4,28},{6,30},{8,0},{10,2},{12,4},{14,6},{16,8},{18,... | collective-permute-start | bytes 276488 | tf_op jit(solution)/shard_map/ppermute | solution.py:82
  130.3 6.0 %collective-permute-done.33.refs_2_ = bf16[40,1152]{1,0:T(8,128)(2,1)S(1)} collective-permute-done((bf16[40,1152]{1,0:T(8,128)(2,1)S(1)}, bf16[40,1152]{1,0:T(8,128)(2,1)S(1)}, u32[]{:S(2)}, u32[]{:S(2)}) %collective-permute-start.33) | collective-permute-done | bytes 92192 | tf_op jit(solution)/shard_map/ppermute | solution.py:82
  136.5 3.8 %collective-permute-start.42 = (bf16[24,1920]{1,0:T(8,128)(2,1)S(1)}, bf16[24,1920]{1,0:T(8,128)(2,1)S(1)}, u32[]{:S(2)}, u32[]{:S(2)}) collective-permute-start(bf16[24,1920]{1,0:T(8,128)(2,1)S(1)} %get-tuple-element.241), channel_id=1, source_target_pairs={{0,24},{2,26},{4,28},{6,30},{8,0},{10,2},{12,4},{14,6},{16,8},{18,... | collective-permute-start | bytes 276488 | tf_op jit(solution)/shard_map/ppermute | solution.py:82
  141.3 2.5 %collective-permute-done.40 = bf16[24,1920]{1,0:T(8,128)(2,1)S(1)} collective-permute-done((bf16[24,1920]{1,0:T(8,128)(2,1)S(1)}, bf16[24,1920]{1,0:T(8,128)(2,1)S(1)}, u32[]{:S(2)}, u32[]{:S(2)}) %collective-permute-start.40) | collective-permute-done | bytes 92192 | tf_op jit(solution)/shard_map/ppermute | solution.py:82
  143.9 4.0 %collective-permute-done.41 = bf16[24,1920]{1,0:T(8,128)(2,1)S(1)} collective-permute-done((bf16[24,1920]{1,0:T(8,128)(2,1)S(1)}, bf16[24,1920]{1,0:T(8,128)(2,1)S(1)}, u32[]{:S(2)}, u32[]{:S(2)}) %collective-permute-start.41) | collective-permute-done | bytes 92192 | tf_op jit(solution)/shard_map/ppermute | solution.py:82
  (121 shorter events, 24.4 us)
Async XLA Ops:
  2.5 12.0 %collective-permute-start.2 = (bf16[24,1920]{1,0:T(8,128)(2,1)S(1)}, bf16[24,1920]{1,0:T(8,128)(2,1)S(1)}, u32[]{:S(2)}, u32[]{:S(2)}) collective-permute-start(bf16[24,1920]{1,0:T(8,128)(2,1)S(1)} %get-tuple-element.128), channel_id=1, source_target_pairs={{0,8},{2,10},{4,12},{6,14},{8,16},{10,18},{12,20},{14,22},{16,24},... | collective-permute-start | bytes 276488 | tf_op jit(solution)/shard_map/ppermute | solution.py:82
  5.6 8.9 %collective-permute-start.1 = (bf16[24,1920]{1,0:T(8,128)(2,1)S(1)}, bf16[24,1920]{1,0:T(8,128)(2,1)S(1)}, u32[]{:S(2)}, u32[]{:S(2)}) collective-permute-start(bf16[24,1920]{1,0:T(8,128)(2,1)S(1)} %get-tuple-element.128), channel_id=1, source_target_pairs={{0,16},{2,18},{4,20},{6,22},{8,24},{10,26},{12,28},{14,30},{16,0},... | collective-permute-start | bytes 276488 | tf_op jit(solution)/shard_map/ppermute | solution.py:82
  8.2 6.4 %collective-permute-start = (bf16[24,1920]{1,0:T(8,128)(2,1)S(1)}, bf16[24,1920]{1,0:T(8,128)(2,1)S(1)}, u32[]{:S(2)}, u32[]{:S(2)}) collective-permute-start(bf16[24,1920]{1,0:T(8,128)(2,1)S(1)} %get-tuple-element.128), channel_id=1, source_target_pairs={{0,24},{2,26},{4,28},{6,30},{8,0},{10,2},{12,4},{14,6},{16,8},{18,... | collective-permute-start | bytes 276488 | tf_op jit(solution)/shard_map/ppermute | solution.py:82
  9.6 8.8 %collective-permute-start.8 = (bf16[196,768]{1,0:T(8,128)(2,1)S(1)}, bf16[196,768]{1,0:T(8,128)(2,1)S(1)}, u32[]{:S(2)}, u32[]{:S(2)}) collective-permute-start(bf16[196,768]{1,0:T(8,128)(2,1)S(1)} %get-tuple-element.131.dm_ref.refs_0_), channel_id=1, source_target_pairs={{0,1},{1,0},{2,3},{3,2},{4,5},{5,4},{6,7},{7,6},{8,9},{9,8},{10,11... | collective-permute-start | bytes 903176 | tf_op jit(solution)/shard_map/ppermute | solution.py:95
  14.6 13.5 %collective-permute-start.4 = (bf16[96,1920]{1,0:T(8,128)(2,1)S(1)}, bf16[96,1920]{1,0:T(8,128)(2,1)S(1)}, u32[]{:S(2)}, u32[]{:S(2)}) collective-permute-start(bf16[96,1920]{1,0:T(8,128)(2,1)S(1)} %pad_maximum_fusion.1), channel_id=1, source_target_pairs={{0,1},{1,0},{2,3},{3,2},{4,5},{5,4},{6,7},{7,6},{8,9},{9,8},{10,11... | collective-permute-start | bytes 1105928 | tf_op jit(solution)/shard_map/ppermute | solution.py:95
  16.2 12.9 %collective-permute-start.3 = (bf16[96,1920]{1,0:T(8,128)(2,1)S(1)}, bf16[96,1920]{1,0:T(8,128)(2,1)S(1)}, u32[]{:S(2)}, u32[]{:S(2)}) collective-permute-start(bf16[96,1920]{1,0:T(8,128)(2,1)S(1)} %pad_maximum_fusion.1), channel_id=1, source_target_pairs={{0,4},{2,6},{4,0},{6,2},{8,12},{10,14},{12,8},{14,10},{16,20},{18,... | collective-permute-start | bytes 1105928 | tf_op jit(solution)/shard_map/ppermute | solution.py:86
  18.4 6.4 %collective-permute-start.11 = (bf16[24,1152]{1,0:T(8,128)(2,1)S(1)}, bf16[24,1152]{1,0:T(8,128)(2,1)S(1)}, u32[]{:S(2)}, u32[]{:S(2)}) collective-permute-start(bf16[24,1152]{1,0:T(8,128)(2,1)S(1)} %get-tuple-element.133), channel_id=1, source_target_pairs={{0,8},{2,10},{4,12},{6,14},{8,16},{10,18},{12,20},{14,22},{16,24},... | collective-permute-start | bytes 165896 | tf_op jit(solution)/shard_map/ppermute | solution.py:82
  20.1 6.1 %collective-permute-start.10 = (bf16[24,1152]{1,0:T(8,128)(2,1)S(1)}, bf16[24,1152]{1,0:T(8,128)(2,1)S(1)}, u32[]{:S(2)}, u32[]{:S(2)}) collective-permute-start(bf16[24,1152]{1,0:T(8,128)(2,1)S(1)} %get-tuple-element.133), channel_id=1, source_target_pairs={{0,16},{2,18},{4,20},{6,22},{8,24},{10,26},{12,28},{14,30},{16,0},... | collective-permute-start | bytes 165896 | tf_op jit(solution)/shard_map/ppermute | solution.py:82
  21.8 4.6 %collective-permute-start.9 = (bf16[24,1152]{1,0:T(8,128)(2,1)S(1)}, bf16[24,1152]{1,0:T(8,128)(2,1)S(1)}, u32[]{:S(2)}, u32[]{:S(2)}) collective-permute-start(bf16[24,1152]{1,0:T(8,128)(2,1)S(1)} %get-tuple-element.133), channel_id=1, source_target_pairs={{0,24},{2,26},{4,28},{6,30},{8,0},{10,2},{12,4},{14,6},{16,8},{18,... | collective-permute-start | bytes 165896 | tf_op jit(solution)/shard_map/ppermute | solution.py:82
  26.4 8.0 %collective-permute-start.13 = (bf16[96,1152]{1,0:T(8,128)(2,1)S(1)}, bf16[96,1152]{1,0:T(8,128)(2,1)S(1)}, u32[]{:S(2)}, u32[]{:S(2)}) collective-permute-start(bf16[96,1152]{1,0:T(8,128)(2,1)S(1)} %pad_maximum_fusion.3), channel_id=1, source_target_pairs={{0,4},{2,6},{4,0},{6,2},{8,12},{10,14},{12,8},{14,10},{16,20},{18,... | collective-permute-start | bytes 663560 | tf_op jit(solution)/shard_map/ppermute | solution.py:86
  26.9 7.7 %collective-permute-start.12 = (bf16[96,1152]{1,0:T(8,128)(2,1)S(1)}, bf16[96,1152]{1,0:T(8,128)(2,1)S(1)}, u32[]{:S(2)}, u32[]{:S(2)}) collective-permute-start(bf16[96,1152]{1,0:T(8,128)(2,1)S(1)} %pad_maximum_fusion.3), channel_id=1, source_target_pairs={{0,1},{1,0},{2,3},{3,2},{4,5},{5,4},{6,7},{7,6},{8,9},{9,8},{10,11... | collective-permute-start | bytes 663560 | tf_op jit(solution)/shard_map/ppermute | solution.py:95
  28.1 9.1 %collective-permute-start.5 = (bf16[96,960]{1,0:T(8,128)(2,1)S(1)}, bf16[96,960]{1,0:T(8,128)(2,1)S(1)}, u32[]{:S(2)}, u32[]{:S(2)}) collective-permute-start(bf16[96,960]{1,0:T(8,128)(2,1)S(1)} %slice.350), channel_id=1, source_target_pairs={{0,4},{2,6},{4,0},{6,2},{8,12},{10,14},{12,8},{14,10},{16,20},{18,... | collective-permute-start | bytes 552968 | tf_op jit(solution)/shard_map/ppermute | solution.py:86
  29.2 8.0 %collective-permute-start.6 = (bf16[96,960]{1,0:T(8,128)(2,1)S(1)}, bf16[96,960]{1,0:T(8,128)(2,1)S(1)}, u32[]{:S(2)}, u32[]{:S(2)}) collective-permute-start(bf16[96,960]{1,0:T(8,128)(2,1)S(1)} %slice.351), channel_id=1, source_target_pairs={{0,1},{1,0},{2,3},{3,2},{4,5},{5,4},{6,7},{7,6},{8,9},{9,8},{10,11... | collective-permute-start | bytes 552968 | tf_op jit(solution)/shard_map/ppermute | solution.py:95
  34.8 4.9 %collective-permute-start.14 = (bf16[96,576]{1,0:T(8,128)(2,1)S(1)}, bf16[96,576]{1,0:T(8,128)(2,1)S(1)}, u32[]{:S(2)}, u32[]{:S(2)}) collective-permute-start(bf16[96,576]{1,0:T(8,128)(2,1)S(1)} %slice.274), channel_id=1, source_target_pairs={{0,4},{2,6},{4,0},{6,2},{8,12},{10,14},{12,8},{14,10},{16,20},{18,... | collective-permute-start | bytes 331784 | tf_op jit(solution)/shard_map/ppermute | solution.py:86
  36.3 4.9 %collective-permute-start.15 = (bf16[96,576]{1,0:T(8,128)(2,1)S(1)}, bf16[96,576]{1,0:T(8,128)(2,1)S(1)}, u32[]{:S(2)}, u32[]{:S(2)}) collective-permute-start(bf16[96,576]{1,0:T(8,128)(2,1)S(1)} %slice.275), channel_id=1, source_target_pairs={{0,1},{1,0},{2,3},{3,2},{4,5},{5,4},{6,7},{7,6},{8,9},{9,8},{10,11... | collective-permute-start | bytes 331784 | tf_op jit(solution)/shard_map/ppermute | solution.py:95
  37.3 9.8 %collective-permute-start.7 = (bf16[384,1920]{1,0:T(8,128)(2,1)S(1)}, bf16[384,1920]{1,0:T(8,128)(2,1)S(1)}, u32[]{:S(2)}, u32[]{:S(2)}) collective-permute-start(bf16[384,1920]{1,0:T(8,128)(2,1)S(1)} %maximum_dynamic-update-slice_fusion.own_ref.own2_ref), channel_id=1, source_target_pairs={{0,2},{2,0},{4,6},{6,4},{8,10},{10,8},{12,14},{14,12},{16,18},{18,... | collective-permute-start | bytes 4423688 | tf_op jit(solution)/shard_map/ppermute | solution.py:90
  37.4 9.7 %copy-start.2 = (bf16[196,768]{1,0:T(8,128)(2,1)S(1)}, bf16[196,768]{1,0:T(8,128)(2,1)}, u32[]{:S(2)}) copy-start(bf16[196,768]{1,0:T(8,128)(2,1)} %x_ref.3) | copy-start | bytes 903172
  41.3 2.5 %collective-permute-start.16 = (bf16[384,1152]{1,0:T(8,128)(2,1)S(1)}, bf16[384,1152]{1,0:T(8,128)(2,1)S(1)}, u32[]{:S(2)}, u32[]{:S(2)}) collective-permute-start(bf16[384,1152]{1,0:T(8,128)(2,1)S(1)} %maximum_dynamic-update-slice_fusion.1.own_ref.own1_ref), channel_id=1, source_target_pairs={{0,2},{2,0},{4,6},{6,4},{8,10},{10,8},{12,14},{14,12},{16,18},{18,... | collective-permute-start | bytes 2654216 | tf_op jit(solution)/shard_map/ppermute | solution.py:90
  52.4 9.4 %collective-permute-start.17 = (bf16[196,768]{1,0:T(8,128)(2,1)S(1)}, bf16[196,768]{1,0:T(8,128)(2,1)S(1)}, u32[]{:S(2)}, u32[]{:S(2)}) collective-permute-start(bf16[196,768]{1,0:T(8,128)(2,1)S(1)} %get-tuple-element.143.a2_ref.refs_4_), channel_id=1, source_target_pairs={{0,1},{1,0},{2,3},{3,2},{4,5},{5,4},{6,7},{7,6},{8,9},{9,8},{10,11... | collective-permute-start | bytes 903176 | tf_op jit(solution)/shard_map/ppermute | solution.py:95
  63.8 8.5 %collective-permute-start.18 = (bf16[196,768]{1,0:T(8,128)(2,1)S(1)}, bf16[196,768]{1,0:T(8,128)(2,1)S(1)}, u32[]{:S(2)}, u32[]{:S(2)}) collective-permute-start(bf16[196,768]{1,0:T(8,128)(2,1)S(1)} %get-tuple-element.149), channel_id=1, source_target_pairs={{0,1},{1,0},{2,3},{3,2},{4,5},{5,4},{6,7},{7,6},{8,9},{9,8},{10,11... | collective-permute-start | bytes 903176 | tf_op jit(solution)/shard_map/ppermute | solution.py:95
  72.4 2.0 %collective-permute-start.20 = (bf16[192,1536]{1,0:T(8,128)(2,1)S(1)}, bf16[192,1536]{1,0:T(8,128)(2,1)S(1)}, u32[]{:S(2)}, u32[]{:S(2)}) collective-permute-start(bf16[192,1536]{1,0:T(8,128)(2,1)S(1)} %get-tuple-element.165), channel_id=1, source_target_pairs={{0,2},{2,0},{4,6},{6,4},{8,10},{10,8},{12,14},{14,12},{16,18},{18,... | collective-permute-start | bytes 1769480 | tf_op jit(solution)/shard_map/ppermute | solution.py:90
  72.4 2.8 %collective-permute-start.19 = (bf16[192,1536]{1,0:T(8,128)(2,1)S(1)}, bf16[192,1536]{1,0:T(8,128)(2,1)S(1)}, u32[]{:S(2)}, u32[]{:S(2)}) collective-permute-start(bf16[192,1536]{1,0:T(8,128)(2,1)S(1)} %get-tuple-element.164), channel_id=1, source_target_pairs={{0,2},{2,0},{4,6},{6,4},{8,10},{10,8},{12,14},{14,12},{16,18},{18,... | collective-permute-start | bytes 1769480 | tf_op jit(solution)/shard_map/ppermute | solution.py:90
  74.5 15.4 %collective-permute-start.22 = (bf16[192,1536]{1,0:T(8,128)(2,1)S(1)}, bf16[192,1536]{1,0:T(8,128)(2,1)S(1)}, u32[]{:S(2)}, u32[]{:S(2)}) collective-permute-start(bf16[192,1536]{1,0:T(8,128)(2,1)S(1)} %add_convert_fusion.2), channel_id=1, source_target_pairs={{0,4},{2,6},{4,0},{6,2},{8,12},{10,14},{12,8},{14,10},{16,20},{18,... | collective-permute-start | bytes 1769480 | tf_op jit(solution)/shard_map/ppermute | solution.py:86
  75.2 14.9 %collective-permute-start.30 = (bf16[192,1536]{1,0:T(8,128)(2,1)S(1)}, bf16[192,1536]{1,0:T(8,128)(2,1)S(1)}, u32[]{:S(2)}, u32[]{:S(2)}) collective-permute-start(bf16[192,1536]{1,0:T(8,128)(2,1)S(1)} %get-tuple-element.205), channel_id=1, source_target_pairs={{0,2},{2,0},{4,6},{6,4},{8,10},{10,8},{12,14},{14,12},{16,18},{18,... | collective-permute-start | bytes 1769480 | tf_op jit(solution)/shard_map/ppermute | solution.py:90
  75.4 15.1 %collective-permute-start.31 = (bf16[192,1536]{1,0:T(8,128)(2,1)S(1)}, bf16[192,1536]{1,0:T(8,128)(2,1)S(1)}, u32[]{:S(2)}, u32[]{:S(2)}) collective-permute-start(bf16[192,1536]{1,0:T(8,128)(2,1)S(1)} %get-tuple-element.206), channel_id=1, source_target_pairs={{0,2},{2,0},{4,6},{6,4},{8,10},{10,8},{12,14},{14,12},{16,18},{18,... | collective-permute-start | bytes 1769480 | tf_op jit(solution)/shard_map/ppermute | solution.py:90
  75.8 9.3 %collective-permute-start.21 = (bf16[196,768]{1,0:T(8,128)(2,1)S(1)}, bf16[196,768]{1,0:T(8,128)(2,1)S(1)}, u32[]{:S(2)}, u32[]{:S(2)}) collective-permute-start(bf16[196,768]{1,0:T(8,128)(2,1)S(1)} %get-tuple-element.173), channel_id=1, source_target_pairs={{0,1},{1,0},{2,3},{3,2},{4,5},{5,4},{6,7},{7,6},{8,9},{9,8},{10,11... | collective-permute-start | bytes 903176 | tf_op jit(solution)/shard_map/ppermute | solution.py:95
  84.0 14.5 %collective-permute-start.27 = (bf16[192,1920]{1,0:T(8,128)(2,1)S(1)}, bf16[192,1920]{1,0:T(8,128)(2,1)S(1)}, u32[]{:S(2)}, u32[]{:S(2)}) collective-permute-start(bf16[192,1920]{1,0:T(8,128)(2,1)S(1)} %get-tuple-element.198), channel_id=1, source_target_pairs={{0,2},{2,0},{4,6},{6,4},{8,10},{10,8},{12,14},{14,12},{16,18},{18,... | collective-permute-start | bytes 2211848 | tf_op jit(solution)/shard_map/ppermute | solution.py:90
  85.1 15.2 %collective-permute-start.28 = (bf16[192,1920]{1,0:T(8,128)(2,1)S(1)}, bf16[192,1920]{1,0:T(8,128)(2,1)S(1)}, u32[]{:S(2)}, u32[]{:S(2)}) collective-permute-start(bf16[192,1920]{1,0:T(8,128)(2,1)S(1)} %get-tuple-element.199), channel_id=1, source_target_pairs={{0,2},{2,0},{4,6},{6,4},{8,10},{10,8},{12,14},{14,12},{16,18},{18,... | collective-permute-start | bytes 2211848 | tf_op jit(solution)/shard_map/ppermute | solution.py:90
  90.0 1.9 %collective-permute-start.23 = (bf16[192,1152]{1,0:T(8,128)(2,1)S(1)}, bf16[192,1152]{1,0:T(8,128)(2,1)S(1)}, u32[]{:S(2)}, u32[]{:S(2)}) collective-permute-start(bf16[192,1152]{1,0:T(8,128)(2,1)S(1)} %get-tuple-element.182), channel_id=1, source_target_pairs={{0,2},{2,0},{4,6},{6,4},{8,10},{10,8},{12,14},{14,12},{16,18},{18,... | collective-permute-start | bytes 1327112 | tf_op jit(solution)/shard_map/ppermute | solution.py:90
  90.2 2.2 %collective-permute-start.24 = (bf16[192,1152]{1,0:T(8,128)(2,1)S(1)}, bf16[192,1152]{1,0:T(8,128)(2,1)S(1)}, u32[]{:S(2)}, u32[]{:S(2)}) collective-permute-start(bf16[192,1152]{1,0:T(8,128)(2,1)S(1)} %get-tuple-element.183), channel_id=1, source_target_pairs={{0,2},{2,0},{4,6},{6,4},{8,10},{10,8},{12,14},{14,12},{16,18},{18,... | collective-permute-start | bytes 1327112 | tf_op jit(solution)/shard_map/ppermute | solution.py:90
  90.6 20.5 %collective-permute-start.43 = (bf16[192,1536]{1,0:T(8,128)(2,1)S(1)}, bf16[192,1536]{1,0:T(8,128)(2,1)S(1)}, u32[]{:S(2)}, u32[]{:S(2)}) collective-permute-start(bf16[192,1536]{1,0:T(8,128)(2,1)S(1)} %add_convert_fusion.1), channel_id=1, source_target_pairs={{0,4},{2,6},{4,0},{6,2},{8,12},{10,14},{12,8},{14,10},{16,20},{18,... | collective-permute-start | bytes 1769480 | tf_op jit(solution)/shard_map/ppermute | solution.py:86
  96.7 4.9 %collective-permute-start.25 = (f32[16,1152]{1,0:T(8,128)S(1)}, f32[16,1152]{1,0:T(8,128)S(1)}, u32[]{:S(2)}, u32[]{:S(2)}) collective-permute-start(f32[16,1152]{1,0:T(8,128)S(1)} %get-tuple-element.195), channel_id=1, source_target_pairs={{0,2},{2,0},{4,6},{6,4},{8,10},{10,8},{12,14},{14,12},{16,18},{18,... | collective-permute-start | bytes 221192 | tf_op jit(solution)/shard_map/ppermute | solution.py:90
  96.9 8.6 %collective-permute-start.37 = (bf16[48,1536]{1,0:T(8,128)(2,1)S(1)}, bf16[48,1536]{1,0:T(8,128)(2,1)S(1)}, u32[]{:S(2)}, u32[]{:S(2)}) collective-permute-start(bf16[48,1536]{1,0:T(8,128)(2,1)S(1)} %get-tuple-element.218), channel_id=1, source_target_pairs={{0,8},{2,10},{4,12},{6,14},{8,16},{10,18},{12,20},{14,22},{16,24},... | collective-permute-start | bytes 442376 | tf_op jit(solution)/shard_map/ppermute | solution.py:82
  98.5 12.7 %collective-permute-start.38 = (bf16[48,1536]{1,0:T(8,128)(2,1)S(1)}, bf16[48,1536]{1,0:T(8,128)(2,1)S(1)}, u32[]{:S(2)}, u32[]{:S(2)}) collective-permute-start(bf16[48,1536]{1,0:T(8,128)(2,1)S(1)} %get-tuple-element.219), channel_id=1, source_target_pairs={{0,16},{2,18},{4,20},{6,22},{8,24},{10,26},{12,28},{14,30},{16,0},... | collective-permute-start | bytes 442376 | tf_op jit(solution)/shard_map/ppermute | solution.py:82
  100.2 10.9 %collective-permute-start.39 = (bf16[48,1536]{1,0:T(8,128)(2,1)S(1)}, bf16[48,1536]{1,0:T(8,128)(2,1)S(1)}, u32[]{:S(2)}, u32[]{:S(2)}) collective-permute-start(bf16[48,1536]{1,0:T(8,128)(2,1)S(1)} %get-tuple-element.220), channel_id=1, source_target_pairs={{0,24},{2,26},{4,28},{6,30},{8,0},{10,2},{12,4},{14,6},{16,8},{18,... | collective-permute-start | bytes 442376 | tf_op jit(solution)/shard_map/ppermute | solution.py:82
  101.6 17.9 %collective-permute-start.35 = (bf16[192,1920]{1,0:T(8,128)(2,1)S(1)}, bf16[192,1920]{1,0:T(8,128)(2,1)S(1)}, u32[]{:S(2)}, u32[]{:S(2)}) collective-permute-start(bf16[192,1920]{1,0:T(8,128)(2,1)S(1)} %add_convert_fusion), channel_id=1, source_target_pairs={{0,1},{1,0},{2,3},{3,2},{4,5},{5,4},{6,7},{7,6},{8,9},{9,8},{10,11... | collective-permute-start | bytes 2211848 | tf_op jit(solution)/shard_map/ppermute | solution.py:95
  105.5 11.9 %collective-permute-start.26 = (bf16[208,1152]{1,0:T(8,128)(2,1)S(1)}, bf16[208,1152]{1,0:T(8,128)(2,1)S(1)}, u32[]{:S(2)}, u32[]{:S(2)}) collective-permute-start(bf16[208,1152]{1,0:T(8,128)(2,1)S(1)} %pad_maximum_fusion), channel_id=1, source_target_pairs={{0,4},{2,6},{4,0},{6,2},{8,12},{10,14},{12,8},{14,10},{16,20},{18,... | collective-permute-start | bytes 1437704 | tf_op jit(solution)/shard_map/ppermute | solution.py:86
  111.3 16.6 %collective-permute-start.44 = (bf16[48,1536]{1,0:T(8,128)(2,1)S(1)}, bf16[48,1536]{1,0:T(8,128)(2,1)S(1)}, u32[]{:S(2)}, u32[]{:S(2)}) collective-permute-start(bf16[48,1536]{1,0:T(8,128)(2,1)S(1)} %get-tuple-element.243), channel_id=1, source_target_pairs={{0,8},{2,10},{4,12},{6,14},{8,16},{10,18},{12,20},{14,22},{16,24},... | collective-permute-start | bytes 442376 | tf_op jit(solution)/shard_map/ppermute | solution.py:82
  115.0 12.9 %collective-permute-start.46 = (bf16[48,1536]{1,0:T(8,128)(2,1)S(1)}, bf16[48,1536]{1,0:T(8,128)(2,1)S(1)}, u32[]{:S(2)}, u32[]{:S(2)}) collective-permute-start(bf16[48,1536]{1,0:T(8,128)(2,1)S(1)} %get-tuple-element.244), channel_id=1, source_target_pairs={{0,24},{2,26},{4,28},{6,30},{8,0},{10,2},{12,4},{14,6},{16,8},{18,... | collective-permute-start | bytes 442376 | tf_op jit(solution)/shard_map/ppermute | solution.py:82
  115.2 13.6 %collective-permute-start.45 = (bf16[48,1536]{1,0:T(8,128)(2,1)S(1)}, bf16[48,1536]{1,0:T(8,128)(2,1)S(1)}, u32[]{:S(2)}, u32[]{:S(2)}) collective-permute-start(bf16[48,1536]{1,0:T(8,128)(2,1)S(1)} %get-tuple-element.245), channel_id=1, source_target_pairs={{0,16},{2,18},{4,20},{6,22},{8,24},{10,26},{12,28},{14,30},{16,0},... | collective-permute-start | bytes 442376 | tf_op jit(solution)/shard_map/ppermute | solution.py:82
  117.5 7.7 %collective-permute-start.29 = (bf16[112,1152]{1,0:T(8,128)(2,1)S(1)}, bf16[112,1152]{1,0:T(8,128)(2,1)S(1)}, u32[]{:S(2)}, u32[]{:S(2)}) collective-permute-start(bf16[112,1152]{1,0:T(8,128)(2,1)S(1)} %pad_maximum_fusion.2), channel_id=1, source_target_pairs={{0,1},{1,0},{2,3},{3,2},{4,5},{5,4},{6,7},{7,6},{8,9},{9,8},{10,11... | collective-permute-start | bytes 774152 | tf_op jit(solution)/shard_map/ppermute | solution.py:95
  119.7 16.6 %collective-permute-start.36 = (bf16[96,1920]{1,0:T(8,128)(2,1)S(1)}, bf16[96,1920]{1,0:T(8,128)(2,1)S(1)}, u32[]{:S(2)}, u32[]{:S(2)}) collective-permute-start(bf16[96,1920]{1,0:T(8,128)(2,1)S(1)} %add_convert_fusion.4), channel_id=1, source_target_pairs={{0,4},{2,6},{4,0},{6,2},{8,12},{10,14},{12,8},{14,10},{16,20},{18,... | collective-permute-start | bytes 1105928 | tf_op jit(solution)/shard_map/ppermute | solution.py:86
  125.3 5.0 %collective-permute-start.34 = (bf16[40,1152]{1,0:T(8,128)(2,1)S(1)}, bf16[40,1152]{1,0:T(8,128)(2,1)S(1)}, u32[]{:S(2)}, u32[]{:S(2)}) collective-permute-start(bf16[40,1152]{1,0:T(8,128)(2,1)S(1)} %get-tuple-element.252), channel_id=1, source_target_pairs={{0,24},{2,26},{4,28},{6,30},{8,0},{10,2},{12,4},{14,6},{16,8},{18,... | collective-permute-start | bytes 276488 | tf_op jit(solution)/shard_map/ppermute | solution.py:82
  128.0 8.3 %collective-permute-start.33 = (bf16[40,1152]{1,0:T(8,128)(2,1)S(1)}, bf16[40,1152]{1,0:T(8,128)(2,1)S(1)}, u32[]{:S(2)}, u32[]{:S(2)}) collective-permute-start(bf16[40,1152]{1,0:T(8,128)(2,1)S(1)} %get-tuple-element.253), channel_id=1, source_target_pairs={{0,16},{2,18},{4,20},{6,22},{8,24},{10,26},{12,28},{14,30},{16,0},... | collective-permute-start | bytes 276488 | tf_op jit(solution)/shard_map/ppermute | solution.py:82
  128.0 8.3 %collective-permute-start.32 = (bf16[40,1152]{1,0:T(8,128)(2,1)S(1)}, bf16[40,1152]{1,0:T(8,128)(2,1)S(1)}, u32[]{:S(2)}, u32[]{:S(2)}) collective-permute-start(bf16[40,1152]{1,0:T(8,128)(2,1)S(1)} %get-tuple-element.254), channel_id=1, source_target_pairs={{0,8},{2,10},{4,12},{6,14},{8,16},{10,18},{12,20},{14,22},{16,24},... | collective-permute-start | bytes 276488 | tf_op jit(solution)/shard_map/ppermute | solution.py:82
  136.5 7.4 %collective-permute-start.40 = (bf16[24,1920]{1,0:T(8,128)(2,1)S(1)}, bf16[24,1920]{1,0:T(8,128)(2,1)S(1)}, u32[]{:S(2)}, u32[]{:S(2)}) collective-permute-start(bf16[24,1920]{1,0:T(8,128)(2,1)S(1)} %get-tuple-element.240), channel_id=1, source_target_pairs={{0,8},{2,10},{4,12},{6,14},{8,16},{10,18},{12,20},{14,22},{16,24},... | collective-permute-start | bytes 276488 | tf_op jit(solution)/shard_map/ppermute | solution.py:82
  136.5 7.4 %collective-permute-start.42 = (bf16[24,1920]{1,0:T(8,128)(2,1)S(1)}, bf16[24,1920]{1,0:T(8,128)(2,1)S(1)}, u32[]{:S(2)}, u32[]{:S(2)}) collective-permute-start(bf16[24,1920]{1,0:T(8,128)(2,1)S(1)} %get-tuple-element.241), channel_id=1, source_target_pairs={{0,24},{2,26},{4,28},{6,30},{8,0},{10,2},{12,4},{14,6},{16,8},{18,... | collective-permute-start | bytes 276488 | tf_op jit(solution)/shard_map/ppermute | solution.py:82
  140.3 7.5 %collective-permute-start.41 = (bf16[24,1920]{1,0:T(8,128)(2,1)S(1)}, bf16[24,1920]{1,0:T(8,128)(2,1)S(1)}, u32[]{:S(2)}, u32[]{:S(2)}) collective-permute-start(bf16[24,1920]{1,0:T(8,128)(2,1)S(1)} %get-tuple-element.242), channel_id=1, source_target_pairs={{0,16},{2,18},{4,20},{6,22},{8,24},{10,26},{12,28},{14,30},{16,0},... | collective-permute-start | bytes 276488 | tf_op jit(solution)/shard_map/ppermute | solution.py:82
  (6 other events, 25.4 us)

commit v5 on v4

--- a/solution.py
+++ b/solution.py
@@ -18,6 +18,7 @@
 PAIRS = HEADS // 2
 LANES = 128
 TABLE = 2 * WIN - 1
+TWICE = 59
 W_START = HEAD + ROW + 2
 HALF = D // 2
 STEP = 384
@@ -28,9 +29,11 @@
 SMEM = pl.BlockSpec(memory_space=pltpu.SMEM)
 LIMIT = 20 * 2**20
 Z_FIRST = (False, False)
+TREE = (True, True)
 FRONT = ('dm', 'z1', 'prep', 'act1', 'z2', 'n1', 'n2', 'act0', 'f2', 'f1', 'c1', 'attend1', 'c2')
-ORDER = ('dc', 'dy', 'm', 'norm', 'back2', 'bc', 'back1', 'finish', 'ac', 'sc', 'by', 'uc', 'bx', 'dz', 'bz', 'uy', 'ax', 'ay', 'uz', 'az')
-GATES = {'n1:s': ['prep', 'dm'], 'n2:s': ['z2'], 'f1:s': ['n1'], 'act1:s': ['dm'], 'attend1:s': ['dm', 'f1'], 'z1:s': ['dm'], 'back1:s': ['dc'], 'back2:s': ['m'], 'finish:s': ['bc'], 'ay:r': ['ac', 'back1', 'dz'], 'uc:s': ['dc'], 'bc:s': ['dy'], 'bx:r': ['uc', 'dy'], 'm:s': ['dc'], 'bz:r': ['bc'], 'dz:s': ['finish'], 'ac:r': ['bc'], 'bx:s': ['ac'], 'uy:r': ['finish'], 'uc:r': ['back1'], 'dz:r': ['uc']}
+ORDER = ('dc', 'dy', 'm', 'norm', 'back2', 'bc', 'back1', 'finish', 'ac', 'sc', 'by', 'bx', 'ax', 'd0', 'd1', 'bz', 'uc', 'uy', 'ay', 'u0', 'u1', 'az')
+GATES = {'n1:s': ['prep', 'dm'], 'n2:s': ['z2'], 'f1:s': ['n1'], 'act1:s': ['dm'], 'attend1:s': ['dm', 'f1'], 'z1:s': ['dm'], 'back1:s': ['dc'], 'back2:s': ['m', 'dc', 'norm'], 'finish:s': ['bc'], 'ay:r': ['ac', 'back1', 'd1'], 'uc:s': ['dc'], 'bc:s': ['dy'], 'bx:r': ['dy'], 'bz:r': ['bc'], 'd0:s': ['finish'], 'd1:r': ['dy'], 'az:r': ['bz'], 'u1:r': ['by', 'bx'], 'uc:r': ['back2'], 'sc:r': ['ac']}
+ROUTE = {"y": "b", "x": "b", "z": "b"}
 CHEAP = pl.CostEstimate(flops=1, bytes_accessed=1, transcendentals=0)
 SMALL = {"gain1": 0, "shift1": 6, "qbias": 12, "vbias": 18, "projb": 24, "gain2": 30, "shift2": 36, "downb": 42}
 SMALL_TABLE = 48
@@ -82,6 +85,11 @@
     return lax.ppermute(value, "dp", dp_pairs(lax.axis_size("dp"), dz=step))
 
 
+def swap_z(value, mask):
+    pairs = [(place, place ^ (mask * 4)) for place in range(lax.axis_size("dp"))]
+    return lax.ppermute(value, "dp", pairs)
+
+
 def move_y(value):
     return lax.ppermute(value, "dp", dp_pairs(lax.axis_size("dp"), dy=1))
 
@@ -112,7 +120,7 @@
     return np.stack(att + feed, axis=1).astype(np.int32)
 
 
-def rows_from(maps_ref, start, rows, wide):
+def rows_from(maps_ref, start, rows, wide, paired=False):
     depth = lax.axis_size("dp") // 4
     dp = lax.axis_index("dp")
 
@@ -120,7 +128,8 @@
         there = maps_ref[:, start + i : start + i + 1] + here
         return jnp.where(there >= size, there - size, there)
 
-    block = (turned(0, dp // 4, depth) * 2 + turned(1, dp // 2 % 2, 2)) * 2 + turned(3, dp % 2, 2)
+    across = maps_ref[:, start : start + 1] ^ (dp // 4) if paired else turned(0, dp // 4, depth)
+    block = (across * 2 + turned(1, dp // 2 % 2, 2)) * 2 + turned(3, dp % 2, 2)
     if wide > 1:
         block = block * wide + turned(2, lax.axis_index("mp"), wide)
     return block * rows + maps_ref[:, start + 4 : start + 5]
@@ -207,47 +216,45 @@
     return ((row % ROW < WIN) & (patch == row // ROW * WIN + row % ROW)).astype(F32).astype(BF16)
 
 
-def row_masks():
+def row_masks(down=False):
     lane = iota((R, LANES), 1) % HEAD
     key = iota((R, LANES), 0)
-    here = jnp.where(lane // ROW % 2 == 0, key // ROW, key % ROW)
+    column = ROW - 1 - key % ROW if down else key % ROW
+    here = jnp.where(lane // ROW % 2 == 0, key // ROW, column)
     return (lane % ROW == here).astype(F32)
 
 
-def offset_lanes(rows, base):
-    lane = iota((rows, LANES), 1)
-    in_h = (lane >= base) & (lane < base + ROW)
-    in_w = (lane >= base + ROW) & (lane < base + 2 * ROW)
-    return in_h, in_w
-
-
 def query_offsets(table, base):
-    in_h, in_w = offset_lanes(ROW, base)
+    lane = iota((ROW, LANES), 1)
+    inside = (lane >= base) & (lane < base + HEAD)
+    in_h = inside & (lane // ROW % 2 == 0)
+    rounded = lane // (2 * ROW) % 2 == 0
     outs = []
     for a in range(WIN):
         group = table[a * ROW : (a + 1) * ROW]
-        at_h = pltpu.roll(group, (HEAD - 13 + a) % LANES, 1)
-        at_w = pltpu.roll(group, LANES - ROW + 1, 1, stride=1, stride_axis=0)
-        both = jnp.where(in_h, at_h, jnp.where(in_w, at_w, 0.0))
+        at_h = pltpu.roll(group, (base - 13 + a) % LANES, 1)
+        at_w = pltpu.roll(group, (base + ROW - TWICE - 13) % LANES, 1, stride=1, stride_axis=0)
+        both = jnp.where(in_h, at_h, at_w)
         high = both.astype(BF16).astype(F32)
-        outs.append(high + pltpu.roll(both - high, 2 * ROW, 1))
+        outs.append(jnp.where(rounded, high, both - high))
     return jnp.concatenate(outs, axis=0)
 
 
 def offset_grads(grad, base):
-    in_h, in_w = offset_lanes(R, base)
-    column = iota((R, LANES), 0) % ROW
-    from_w = jnp.where(in_w, grad, 0.0)
-    for bit in (1, 2, 4, 8):
-        from_w = jnp.where((ROW - 1 - column) & bit > 0, pltpu.roll(from_w, bit, 1), from_w)
-    only_h = jnp.where(in_h, grad, 0.0)
-    from_h = [pltpu.roll(only_h[a * ROW : (a + 1) * ROW], (HEAD + 13 - a) % LANES, 1) for a in range(WIN)]
-    return jnp.concatenate(from_h, axis=0) + from_w
-
-
-def table_places(start):
+    lane = iota((ROW, LANES), 1)
+    in_h = (lane >= base) & (lane < base + ROW)
+    in_w = (lane >= base + ROW) & (lane < base + 2 * ROW)
+    outs = []
+    for a in range(WIN):
+        group = grad[a * ROW : (a + 1) * ROW]
+        from_h = pltpu.roll(jnp.where(in_h, group, 0.0), (HEAD + 13 - a) % LANES, 1)
+        outs.append(from_h + pltpu.roll(jnp.where(in_w, group, 0.0), 0, 1, stride=1, stride_axis=0))
+    return jnp.concatenate(outs, axis=0)
+
+
+def table_places(start, straight=False):
     row, lane = iota((TABLE, LANES), 0), iota((TABLE, LANES), 1)
-    return (lane - start == TABLE - 1 - row).astype(F32)
+    return (lane - start == (row if straight else TABLE - 1 - row)).astype(F32)
 
 
 def rate_of(keep_ref, branch):
@@ -284,7 +291,7 @@
 
 def prepare_kernel(
     count, wide, tokens_ref, maps_ref, params_ref, relh_ref, relw_ref, mask_ref, upb_ref,
-    a1_ref, turned_ref, att_ref, feed_ref, table_ref, fill_ref, wideb_ref,
+    a1_ref, turned_ref, att_ref, feed_ref, table_ref, twice_ref, fill_ref, wideb_ref,
 ):
     wideb_ref[...] = upb_ref[...].astype(F32).reshape(wideb_ref.shape)
     spread = spread_rows()
@@ -292,15 +299,24 @@
     source = iota((D, D), 1)
     att = (rows_from(maps_ref, 0, D // (count * wide), wide) == source).astype(F32).astype(BF16)
     att_ref[...] = att
-    feed_ref[...] = (rows_from(maps_ref, 5, D // count, 1) == source).astype(F32).astype(BF16)
+    feed_ref[...] = (rows_from(maps_ref, 5, D // count, 1, paired=True) == source).astype(F32).astype(BF16)
     unit, _ = norm_parts(x)
     a1 = (unit * params_ref[0:1] + params_ref[1:2]).astype(BF16)
     a1_ref[...] = dot_nt(a1, att).astype(BF16)
     turned_ref[...] = dot_nt(att, a1).astype(BF16)
-    one = dot_tn(relh_ref[...], table_places(0).astype(BF16)) + dot_tn(relw_ref[...], table_places(W_START).astype(BF16))
+    one = dot_tn(relh_ref[...], table_places(0).astype(BF16)) + dot_tn(
+        relw_ref[...], table_places(W_START, straight=True).astype(BF16)
+    )
     blank = jnp.zeros((HEAD, LANES), F32)
     table_ref[:HEAD, :] = jnp.concatenate([one, blank], axis=1).astype(BF16)
     table_ref[HEAD:, :] = jnp.concatenate([blank, pltpu.roll(one, HEAD, 1)], axis=1).astype(BF16)
+    twice = sum(
+        dot_tn(ref[...], table_places(start + more).astype(BF16))
+        for ref, start in ((relh_ref, 0), (relw_ref, TWICE))
+        for more in (0, 2 * ROW)
+    )
+    twice_ref[:HEAD, :] = jnp.concatenate([twice, blank], axis=1).astype(BF16)
+    twice_ref[HEAD:, :] = jnp.concatenate([blank, twice], axis=1).astype(BF16)
     seen = dot_nt((mask_ref[...] > 0).astype(F32).astype(BF16), spread)
     key = iota((1, R), 1)
     fill_ref[...] = jnp.where(key % ROW >= WIN, -3e38, jnp.where(seen > 0.5, 0.0, -1e9))
@@ -314,7 +330,8 @@
         7,
         [
             shape_of((R, D), BF16), shape_of((D, R), BF16), shape_of((D, D), BF16), shape_of((D, D), BF16),
-            shape_of((LANES, 2 * LANES), BF16), shape_of((1, R), F32), shape_of((1, upb.shape[0]), F32),
+            shape_of((LANES, 2 * LANES), BF16), shape_of((LANES, 2 * LANES), BF16), shape_of((1, R), F32),
+            shape_of((1, upb.shape[0]), F32),
         ],
         far=(0, 1, 3, 4, 5, 6),
     )(tokens, row_maps(count, wide), params, rel_h, rel_w, mask, upb)
@@ -331,12 +348,13 @@
 
 def heads_forward(qkv_ref, tables, fill, p_ref, out):
     ones = row_masks()
+    sums = jnp.ones((R, LANES), BF16)
     left = iota((R, LANES), 1) < HEAD
     for pair in range(PAIRS // 2):
         at = pair * LANES
         q2 = qkv_ref[:, at : at + LANES]
         k2 = qkv_ref[:, HALF + at : HALF + at + LANES].astype(F32)
-        v2 = qkv_ref[:, 2 * HALF + at : 2 * HALF + at + LANES]
+        v2 = jnp.concatenate([qkv_ref[:, 2 * HALF + at : 2 * HALF + at + LANES], sums], axis=1)
         products = dot_nn(q2, tables)
         q2 = q2.astype(F32) * HEAD**-0.5
         outs = []
@@ -348,9 +366,11 @@
             scores = dot_nt(q_aug, k_aug)
             scores = jnp.where(fill < 0.0, fill, scores)
             expo = jnp.exp(scores - jnp.max(scores, axis=-1, keepdims=True))
-            probs = (expo / jnp.sum(expo, axis=-1, keepdims=True)).astype(BF16)
-            p_ref[2 * pair + side] = probs
-            outs.append(dot_nn(probs, v2))
+            mixed = dot_nn(expo.astype(BF16), v2)
+            scale = 1.0 / mixed[:, LANES:]
+            scale = jnp.concatenate([scale, scale[:, : R - LANES]], axis=1)
+            p_ref[2 * pair + side] = (expo * scale).astype(BF16)
+            outs.append(mixed[:, :LANES] * scale[:, :LANES])
         out(at, jnp.where(left, outs[0], outs[1]).astype(BF16))
 
 
@@ -503,7 +523,7 @@
 
 
 def heads_back(qkv_ref, p_ref, do_at, tables, dqkv_ref):
-    ones = row_masks()
+    ones = row_masks(down=True)
     left = iota((R, LANES), 1) < HEAD
     table_grad = jnp.zeros((LANES, 2 * LANES), F32)
     for pair in range(PAIRS // 2):
@@ -707,7 +727,7 @@
     for start, ref in ((0, relh_ref), (32, relw_ref)):
         for half in range(2):
             ref[:, half * 32 : half * 32 + 32] = lax.dot_general(
-                table_places(start + 64 * half), table_ref[...], (((1,), (1,)), ((), ())),
+                table_places(start + 64 * half, straight=start > 0), table_ref[...], (((1,), (1,)), ((), ())),
                 precision=lax.Precision.HIGHEST, preferred_element_type=F32,
             )
     for i in range(up_ref.shape[0]):
@@ -755,8 +775,8 @@
         if name == "act1":
             return [act_grad(v, fc2_weight) for v in gated(made["dm"], name, "s")]
         if name == "attend1":
-            a1, _, _, _, tables, fill, _ = made["prep"]
-            return attend_first(gated(a1, name, "s"), chains["1"], made["c1"], params, tables, fill)
+            a1, _, _, _, _, twice, fill, _ = made["prep"]
+            return attend_first(gated(a1, name, "s"), chains["1"], made["c1"], params, twice, fill)
         step, tier = name
         if step == "z":
             sent = gated((first, second)[int(tier) - 1], name, "s")
@@ -772,14 +792,14 @@
 
     for name in FRONT:
         made[name] = front(name)
-    a1, a1_turned, att_map, feed_map, tables, fill, upb = made["prep"]
+    a1, a1_turned, att_map, feed_map, tables, twice, fill, upb = made["prep"]
     dms = [dm, *made["dm"]]
     acts = [made["act0"], *made["act1"]]
     gacts, downb = [v[0] for v in acts], acts[0][1]
     own1, other1, own2, other2 = chains["1"], made["c1"], chains["2"], made["c2"]
     qkv1, probs1, att1 = made["attend1"]
     qkv2, probs2, att_turned, middle, a2 = attend_second(
-        keep_mask, a1, own2, other2, params, tables, fill, att1, tokens, att_map
+        keep_mask, a1, own2, other2, params, twice, fill, att1, tokens, att_map
     )
 
     a2s = [a2] + [move_x(a2, -s) for s in range(1, wide)]
@@ -804,17 +824,37 @@
         chains[name] = (list(zip(keep, got)), axes)
         return got
 
+    def count_of(axis):
+        return depth if axis in "z0" else depth >> int(axis) if axis.isdigit() else moves[axis][1]
+
     def along(name, axis):
         sums, axes = chains[name]
-        move, _ = moves[axis]
+        carries = ROUTE.get(axis) == name
+        if axis.isdigit():
+            mask = 1 << int(axis)
+            sent = [jnp.concatenate([add_up(*v).astype(BF16) for v in sums[1::2]])]
+            sent = gated(sent, f"{name}{axis}", "s")
+            got = gated([swap_z(v, mask) for v in sent], f"{name}{axis}", "r")
+            size = sums[0][0].shape[0]
+            sums = [[*v, got[0][i * size : (i + 1) * size]] for i, v in enumerate(sums[::2])]
+            axes = axes[axes.index(axis) + 1 :]
+            if axes and axes[0].isdigit():
+                chains[name] = (sums, axes)
+            else:
+                chains[name] = (split(sums[0], count_of(axes[0])), axes) if axes else (sums[0], axes)
+            return got
+        if axis == "z" and name in "du":
+            move = swap_z
+        else:
+            move, _ = moves[axis]
         sent = [add_up(*v).astype(BF16) for v in sums[1:]]
-        if name == "b":
+        if carries:
             extra = chains["s"].astype(BF16)
             sent = [jnp.concatenate([v, extra]) for v in sent]
         sent = gated(sent, f"{name}{axis}", "s")
         got = gated([move(v, s + 1) for s, v in enumerate(sent)], f"{name}{axis}", "r")
         rest = [*sums[0], *got]
-        if name == "b":
+        if carries:
             rows = sums[0][0].shape[0]
             rest = [*sums[0], *[v[:rows] for v in got]]
             if axis == "z":
@@ -822,7 +862,7 @@
             else:
                 chains["s"] = add_up(chains["s"], *[v[rows:] for v in got])
         axes = axes[axes.index(axis) + 1 :]
-        chains[name] = (split(rest, moves[axes[0]][1]), axes) if axes else (rest, axes)
+        chains[name] = (split(rest, count_of(axes[0])), axes) if axes else (rest, axes)
         return got
 
     def small_cores():
@@ -858,12 +898,15 @@
             return along(chain, axis)
         if chain in "du":
             keep, send = (down_keep, down_send) if chain == "d" else (up_keep, up_send)
-            return cores(chain, keep, send, "zy" if Z_FIRST["du".index(chain)] else "yz")
+            bits = "".join(str(i) for i in range(depth.bit_length() - 1)) if TREE["du".index(chain)] else "z"
+            return cores(chain, keep, send, bits + "y" if Z_FIRST["du".index(chain)] else "y" + bits)
         tier = "ab".index(chain)
         return cores(chain, made[f"back{tier + 1}"][1], made[f"back{tier + 1}"][2], ("xyz", "yxz")[tier])
 
     for name in ORDER:
         made[name] = task(name)
+        while name[-1] == "1" and name[0] in "du" and chains[name[0]][1][:1].isdigit():
+            along(name[0], chains[name[0]][1][0])
     grad_in, result, _ = made["finish"]
     small = chains["s"]
     down_grad, up_grad, rows1, rows2 = (add_up(*chains[name][0]) for name in "duab")

time: 150 us -> 143 us (0.953)
  Pallas kernels: 42 us -> 36.7 us
  starting transfers between devices: 51.4 us -> 48.4 us
  waiting for transfers between devices: 48.5 us -> 50.1 us
    ppermute x18 -> x12, waiting for transfers between devices: 24.1 us -> 11.4 us  [move_z(): return lax.ppermute(value, 'dp', dp_pairs(lax.axis_size('dp'), dz=step))]
    ppermute x18 -> x12, starting transfers between devices: 28.1 us -> 19.7 us  [move_z(): return lax.ppermute(value, 'dp', dp_pairs(lax.axis_size('dp'), dz=step))]
    ppermute x8, waiting for transfers between devices: 6.05 us -> 13.2 us  [move_y(): return lax.ppermute(value, 'dp', dp_pairs(lax.axis_size('dp'), dy=1))]
    ppermute x0 -> x4, waiting for transfers between devices: none -> 6.96 us  [swap_z(): return lax.ppermute(value, 'dp', pairs)]
    ppermute x0 -> x4, starting transfers between devices: none -> 5.88 us  [swap_z(): return lax.ppermute(value, 'dp', pairs)]
    pallas_call x14, Pallas kernels: 42 us -> 36.7 us  [run(): call(*args[:smem], *map(pltpu.with_memory_space_constraint, args[smem:],...]
  transfers between devices with their start and end apart: 47 -> 45, of which waited for: 24 -> 21; matrix products, arithmetic and copies ran while one was open for 3% -> 3% of each run, Pallas kernels for 22% -> 21%
where the time goes in v5:
time: 143 us
  waiting for transfers between devices  50.1 us (35%)
  starting transfers between devices  48.4 us (34%)
  Pallas kernels  36.7 us (26%)
  other arithmetic  3.65 us (3%)
  local copies, waits for them, and re-layouts  2.73 us (2%)
    pallas_call x14, Pallas kernels, run(): call(*args[:smem], *map(pltpu.with_memory_space_constraint, args[smem:],...  36.7 us
    ppermute x12, starting transfers between devices, move_z(): return lax.ppermute(value, 'dp', dp_pairs(lax.axis_size('dp'), dz=step))  19.7 us
    ppermute x10, waiting for transfers between devices, move_x(): lax.ppermute(value, 'mp', [(i, (i + step) % count) for i in range(count)])  14.4 us
    ppermute x8, waiting for transfers between devices, move_y(): return lax.ppermute(value, 'dp', dp_pairs(lax.axis_size('dp'), dy=1))  13.2 us
    ppermute x10, starting transfers between devices, move_x(): lax.ppermute(value, 'mp', [(i, (i + step) % count) for i in range(count)])  12.6 us
    ppermute x12, waiting for transfers between devices, move_z(): return lax.ppermute(value, 'dp', dp_pairs(lax.axis_size('dp'), dz=step))  11.4 us
    ppermute x8, starting transfers between devices, move_y(): return lax.ppermute(value, 'dp', dp_pairs(lax.axis_size('dp'), dy=1))  8.1 us
    ppermute x4, waiting for transfers between devices, swap_z(): return lax.ppermute(value, 'dp', pairs)  6.96 us
  transfers between devices with their start and end apart: 45, of which 21 were waited for; matrix products, arithmetic and copies ran while one was open for 3% of the time, Pallas kernels for 21%

profile of v5, /device:TPU:0, one launch (start us, length us, event | category | flops | bytes accessed | tf_op | source)
XLA Modules:
  0.0 142.7 jit_solution(3664565212217623933)
XLA Ops:
  1.3 1.2 pack.1
  2.5 3.1 %collective-permute-start.2 = (bf16[24,1920]{1,0:T(8,128)(2,1)S(1)}, bf16[24,1920]{1,0:T(8,128)(2,1)S(1)}, u32[]{:S(2)}, u32[]{:S(2)}) collective-permute-start(bf16[24,1920]{1,0:T(8,128)(2,1)S(1)} %get-tuple-element.125), channel_id=1, source_target_pairs={{0,8},{2,10},{4,12},{6,14},{8,16},{10,18},{12,20},{14,22},{16,24},... | collective-permute-start | bytes 276488 | tf_op jit(solution)/shard_map/ppermute | solution.py:85
  5.6 2.6 %collective-permute-start.1 = (bf16[24,1920]{1,0:T(8,128)(2,1)S(1)}, bf16[24,1920]{1,0:T(8,128)(2,1)S(1)}, u32[]{:S(2)}, u32[]{:S(2)}) collective-permute-start(bf16[24,1920]{1,0:T(8,128)(2,1)S(1)} %get-tuple-element.125), channel_id=1, source_target_pairs={{0,16},{2,18},{4,20},{6,22},{8,24},{10,26},{12,28},{14,30},{16,0},... | collective-permute-start | bytes 276488 | tf_op jit(solution)/shard_map/ppermute | solution.py:85
  8.2 1.3 collective-permute-start
  9.6 1.5 %collective-permute-start.8 = (bf16[196,768]{1,0:T(8,128)(2,1)S(1)}, bf16[196,768]{1,0:T(8,128)(2,1)S(1)}, u32[]{:S(2)}, u32[]{:S(2)}) collective-permute-start(bf16[196,768]{1,0:T(8,128)(2,1)S(1)} %get-tuple-element.128.dm_ref.refs_0_), channel_id=1, source_target_pairs={{0,1},{1,0},{2,3},{3,2},{4,5},{5,4},{6,7},{7,6},{8,9},{9,8},{10,11... | collective-permute-start | bytes 903176 | tf_op jit(solution)/shard_map/ppermute | solution.py:103
  11.1 3.4 %prepare.1 = (bf16[224,768]{1,0:T(8,128)(2,1)S(1)}, bf16[768,224]{1,0:T(8,128)(2,1)S(1)}, bf16[768,768]{1,0:T(8,128)(2,1)S(1)}, bf16[768,768]{1,0:T(8,128)(2,1)S...) custom-call(bf16[196,768]{1,0:T(8,128)(2,1)} %x_ref.3, ...), custom_call_target="tpu_custom_call" | custom-call | flops 1 | bytes 1 | tf_op jit(solution)/shard_map/prepare/pallas_call | solution.py:66
  14.6 1.6 %collective-permute-start.4 = (bf16[96,1920]{1,0:T(8,128)(2,1)S(1)}, bf16[96,1920]{1,0:T(8,128)(2,1)S(1)}, u32[]{:S(2)}, u32[]{:S(2)}) collective-permute-start(bf16[96,1920]{1,0:T(8,128)(2,1)S(1)} %pad_maximum_fusion.1), channel_id=1, source_target_pairs={{0,1},{1,0},{2,3},{3,2},{4,5},{5,4},{6,7},{7,6},{8,9},{9,8},{10,11... | collective-permute-start | bytes 1105928 | tf_op jit(solution)/shard_map/ppermute | solution.py:103
  16.2 1.5 %collective-permute-start.3 = (bf16[96,1920]{1,0:T(8,128)(2,1)S(1)}, bf16[96,1920]{1,0:T(8,128)(2,1)S(1)}, u32[]{:S(2)}, u32[]{:S(2)}) collective-permute-start(bf16[96,1920]{1,0:T(8,128)(2,1)S(1)} %pad_maximum_fusion.1), channel_id=1, source_target_pairs={{0,4},{2,6},{4,0},{6,2},{8,12},{10,14},{12,8},{14,10},{16,20},{18,... | collective-permute-start | bytes 1105928 | tf_op jit(solution)/shard_map/ppermute | solution.py:94
  18.4 1.7 %collective-permute-start.11 = (bf16[24,1152]{1,0:T(8,128)(2,1)S(1)}, bf16[24,1152]{1,0:T(8,128)(2,1)S(1)}, u32[]{:S(2)}, u32[]{:S(2)}) collective-permute-start(bf16[24,1152]{1,0:T(8,128)(2,1)S(1)} %get-tuple-element.130), channel_id=1, source_target_pairs={{0,8},{2,10},{4,12},{6,14},{8,16},{10,18},{12,20},{14,22},{16,24},... | collective-permute-start | bytes 165896 | tf_op jit(solution)/shard_map/ppermute | solution.py:85
  20.1 1.7 %collective-permute-start.10 = (bf16[24,1152]{1,0:T(8,128)(2,1)S(1)}, bf16[24,1152]{1,0:T(8,128)(2,1)S(1)}, u32[]{:S(2)}, u32[]{:S(2)}) collective-permute-start(bf16[24,1152]{1,0:T(8,128)(2,1)S(1)} %get-tuple-element.130), channel_id=1, source_target_pairs={{0,16},{2,18},{4,20},{6,22},{8,24},{10,26},{12,28},{14,30},{16,0},... | collective-permute-start | bytes 165896 | tf_op jit(solution)/shard_map/ppermute | solution.py:85
  22.5 2.2 %collective-permute-done.11 = bf16[24,1152]{1,0:T(8,128)(2,1)S(1)} collective-permute-done((bf16[24,1152]{1,0:T(8,128)(2,1)S(1)}, bf16[24,1152]{1,0:T(8,128)(2,1)S(1)}, u32[]{:S(2)}, u32[]{:S(2)}) %collective-permute-start.11) | collective-permute-done | bytes 55328 | tf_op jit(solution)/shard_map/ppermute | solution.py:85
  24.7 1.5 %collective-permute-done.10 = bf16[24,1152]{1,0:T(8,128)(2,1)S(1)} collective-permute-done((bf16[24,1152]{1,0:T(8,128)(2,1)S(1)}, bf16[24,1152]{1,0:T(8,128)(2,1)S(1)}, u32[]{:S(2)}, u32[]{:S(2)}) %collective-permute-start.10) | collective-permute-done | bytes 55328 | tf_op jit(solution)/shard_map/ppermute | solution.py:85
  29.2 1.6 %collective-permute-start.6 = (bf16[96,960]{1,0:T(8,128)(2,1)S(1)}, bf16[96,960]{1,0:T(8,128)(2,1)S(1)}, u32[]{:S(2)}, u32[]{:S(2)}) collective-permute-start(bf16[96,960]{1,0:T(8,128)(2,1)S(1)} %slice.367), channel_id=1, source_target_pairs={{0,1},{1,0},{2,3},{3,2},{4,5},{5,4},{6,7},{7,6},{8,9},{9,8},{10,11... | collective-permute-start | bytes 552968 | tf_op jit(solution)/shard_map/ppermute | solution.py:103
  31.0 3.4 %collective-permute-done.13 = bf16[96,1152]{1,0:T(8,128)(2,1)S(1)} collective-permute-done((bf16[96,1152]{1,0:T(8,128)(2,1)S(1)}, bf16[96,1152]{1,0:T(8,128)(2,1)S(1)}, u32[]{:S(2)}, u32[]{:S(2)}) %collective-permute-start.13) | collective-permute-done | bytes 221216 | tf_op jit(solution)/shard_map/ppermute | solution.py:94
  34.8 1.6 %collective-permute-start.14 = (bf16[96,576]{1,0:T(8,128)(2,1)S(1)}, bf16[96,576]{1,0:T(8,128)(2,1)S(1)}, u32[]{:S(2)}, u32[]{:S(2)}) collective-permute-start(bf16[96,576]{1,0:T(8,128)(2,1)S(1)} %slice.286), channel_id=1, source_target_pairs={{0,4},{2,6},{4,0},{6,2},{8,12},{10,14},{12,8},{14,10},{16,20},{18,... | collective-permute-start | bytes 331784 | tf_op jit(solution)/shard_map/ppermute | solution.py:94
  37.5 2.2 %collective-permute-done.14 = bf16[96,576]{1,0:T(8,128)(2,1)S(1)} collective-permute-done((bf16[96,576]{1,0:T(8,128)(2,1)S(1)}, bf16[96,576]{1,0:T(8,128)(2,1)S(1)}, u32[]{:S(2)}, u32[]{:S(2)}) %collective-permute-start.14) | collective-permute-done | bytes 110624 | tf_op jit(solution)/shard_map/ppermute | solution.py:94
  39.7 1.5 %collective-permute-done.15 = bf16[96,576]{1,0:T(8,128)(2,1)S(1)} collective-permute-done((bf16[96,576]{1,0:T(8,128)(2,1)S(1)}, bf16[96,576]{1,0:T(8,128)(2,1)S(1)}, u32[]{:S(2)}, u32[]{:S(2)}) %collective-permute-start.15) | collective-permute-done | bytes 110624 | tf_op jit(solution)/shard_map/ppermute | solution.py:103
  41.4 2.4 %collective-permute-done.16.other_ref.other1_ref = bf16[384,1152]{1,0:T(8,128)(2,1)S(1)} collective-permute-done((bf16[384,1152]{1,0:T(8,128)(2,1)S(1)}, bf16[384,1152]{1,0:T(8,128)(2,1)S(1)}, u32[]{:S(2)}, u32[]{:S(2)}) %collective-permute-start.16) | collective-permute-done | bytes 884768 | tf_op jit(solution)/shard_map/ppermute | solution.py:98
  43.8 1.9 %attend1.1 = (bf16[224,1152]{1,0:T(8,128)(2,1)S(1)}, bf16[6,224,224]{2,1,0:T(8,128)(2,1)S(1)}, bf16[224,384]{1,0:T(8,128)(2,1)S(1)}) custom-call(bf16[224,768]{1,0:T(8,128)(2,1)S(1)} %get-tuple-element.139.a1_ref, bf16[384,1152]{1,0:T(8,128)(2,1)S(1)} %maximum_dynamic-update-slice_fusion.1.own_ref.own1_ref, ...), custom_call_target="tpu_custom_call" | custom-call | flops 1 | bytes 1 | tf_op jit(solution)/shard_map/attend1/pallas_call | solution.py:66
  45.8 3.9 %attend2.1 = (bf16[224,1152]{1,0:T(8,128)(2,1)S(1)}, bf16[6,224,224]{2,1,0:T(8,128)(2,1)S(1)}, bf16[768,196]{1,0:T(8,128)(2,1)S(1)}, f32[196,768]{1,0:T(8,128)S(1)}, bf16[196,768]{1,0:T(8,128)(2,1)S(1)}) custom-call(s32[1,2]{1,0:T(1,128)S(1)} %copy-done.5, bf16[224,768]{1,0:T(8,128)(2,1)S(1)} %get-tuple-element.139.a1_ref, ...), custom_call_target="tpu_custom_call" | custom-call | flops 1 | bytes 1 | tf_op jit(solution)/shard_map/attend2/pallas_call | solution.py:66
  51.5 1.4 act.3
  53.2 2.0 %feed.2 = (bf16[196,1536]{1,0:T(8,128)(2,1)S(1)}, bf16[196,1536]{1,0:T(8,128)(2,1)S(1)}, f32[196,768]{1,0:T(8,128)S(1)}) custom-call(bf16[196,768]{1,0:T(8,128)(2,1)S(1)} %get-tuple-element.141.a2_ref.refs_4_, bf16[768,1536]{1,0:T(8,128)(2,1)S(1)} %copy-done.1, f32[1,1536]{1,0:T(1,128)S(1)} %get-tuple-element.135.upb_ref, ...), custom_call_target="tpu_custom_call" | custom-call | flops 1 | bytes 1 | tf_op jit(solution)/shard_map/feed/pallas_call | solution.py:66
  55.2 3.9 %collective-permute-done.17.a2_ref.refs_5_ = bf16[196,768]{1,0:T(8,128)(2,1)S(1)} collective-permute-done((bf16[196,768]{1,0:T(8,128)(2,1)S(1)}, bf16[196,768]{1,0:T(8,128)(2,1)S(1)}, u32[]{:S(2)}, u32[]{:S(2)}) %collective-permute-start.17) | collective-permute-done | bytes 301088 | tf_op jit(solution)/shard_map/ppermute | solution.py:103
  59.1 2.0 %feed.3 = (bf16[196,1536]{1,0:T(8,128)(2,1)S(1)}, bf16[196,1536]{1,0:T(8,128)(2,1)S(1)}, bf16[196,768]{1,0:T(8,128)(2,1)S(1)}) custom-call(bf16[196,768]{1,0:T(8,128)(2,1)S(1)} %collective-permute-done.17.a2_ref.refs_5_, bf16[768,1536]{1,0:T(8,128)(2,1)S(1)} %copy-done.1, f32[1,1536]{1,0:T(1,128)S(1)} %get-tuple-element.135.upb_ref, ...), custom_call_target="tpu_custom_call" | custom-call | flops 1 | bytes 1 | tf_op jit(solution)/shard_map/feed/pallas_call | solution.py:66
  62.0 6.1 %feedw.1 = (bf16[192,1536]{1,0:T(8,128)(2,1)S(1)}, bf16[192,1536]{1,0:T(8,128)(2,1)S(1)}, bf16[192,1536]{1,0:T(8,128)(2,1)S(1)}, bf16[192,1536]{1,0:T(8,128)(2,1...) custom-call(bf16[768,768]{1,0:T(8,128)(2,1)S(1)} %get-tuple-element., ...), custom_call_target="tpu_custom_call" | custom-call | flops 1 | bytes 1 | tf_op jit(solution)/shard_map/feedw/pallas_call | solution.py:66
  68.1 1.6 %collective-permute-done.18.got_ref = bf16[196,768]{1,0:T(8,128)(2,1)S(1)} collective-permute-done((bf16[196,768]{1,0:T(8,128)(2,1)S(1)}, bf16[196,768]{1,0:T(8,128)(2,1)S(1)}, u32[]{:S(2)}, u32[]{:S(2)}) %collective-permute-start.18) | collective-permute-done | bytes 301088 | tf_op jit(solution)/shard_map/ppermute | solution.py:103
  70.2 1.5 %collective-permute-done.20 = bf16[192,1536]{1,0:T(8,128)(2,1)S(1)} collective-permute-done((bf16[192,1536]{1,0:T(8,128)(2,1)S(1)}, bf16[192,1536]{1,0:T(8,128)(2,1)S(1)}, u32[]{:S(2)}, u32[]{:S(2)}) %collective-permute-start.20) | collective-permute-done | bytes 589856 | tf_op jit(solution)/shard_map/ppermute | solution.py:98
  73.0 1.5 %collective-permute-start.21 = (bf16[196,768]{1,0:T(8,128)(2,1)S(1)}, bf16[196,768]{1,0:T(8,128)(2,1)S(1)}, u32[]{:S(2)}, u32[]{:S(2)}) collective-permute-start(bf16[196,768]{1,0:T(8,128)(2,1)S(1)} %get-tuple-element.170), channel_id=1, source_target_pairs={{0,1},{1,0},{2,3},{3,2},{4,5},{5,4},{6,7},{7,6},{8,9},{9,8},{10,11... | collective-permute-start | bytes 903176 | tf_op jit(solution)/shard_map/ppermute | solution.py:103
  74.6 2.1 %backnorm.1 = (f32[196,768]{1,0:T(8,128)S(1)}, bf16[224,768]{1,0:T(8,128)(2,1)S(1)}, bf16[196,768]{1,0:T(8,128)(2,1)S(1)}, f32[3,768]{1,0:T(4,128)S(1)}) custom-call(s32[1,2]{1,0:T(1,128)S(1)} %copy-done.5, f32[196,768]{1,0:T(8,128)S(1)} %get-tuple-element.143.da2_ref, bf16[196,768]{1,0:T(8,128)(2,1)S(1)} %collective-permute-done.18.got_ref, ...), custom_call_target="tpu_custom_call" | custom-call | flops 1 | bytes 1 | tf_op jit(solution)/shard_map/backnorm/pallas_call | solution.py:66
  76.6 3.3 %back1.1 = (bf16[224,1152]{1,0:T(8,128)(2,1)S(1)}, bf16[192,1920]{1,0:T(8,128)(2,1)S(1)}, bf16[192,1920]{1,0:T(8,128)(2,1)S(1)}, bf16[192,1920]{1,0:T(8,128)(2,1...) custom-call(bf16[224,768]{1,0:T(8,128)(2,1)S(1)} %get-tuple-element.173.do_ref, ...), custom_call_target="tpu_custom_call" | custom-call | flops 1 | bytes 1 | tf_op jit(solution)/shard_map/back1/pallas_call | solution.py:66
  80.0 2.4 %collective-permute-done.21.mgot_ref = bf16[196,768]{1,0:T(8,128)(2,1)S(1)} collective-permute-done((bf16[196,768]{1,0:T(8,128)(2,1)S(1)}, bf16[196,768]{1,0:T(8,128)(2,1)S(1)}, u32[]{:S(2)}, u32[]{:S(2)}) %collective-permute-start.21) | collective-permute-done | bytes 301088 | tf_op jit(solution)/shard_map/ppermute | solution.py:103
  82.8 3.0 %back2.1 = (bf16[224,1152]{1,0:T(8,128)(2,1)S(1)}, bf16[192,1152]{1,0:T(8,128)(2,1)S(1)}, bf16[192,1152]{1,0:T(8,128)(2,1)S(1)}, bf16[192,1152]{1,0:T(8,128)(2,1...) custom-call(bf16[224,768]{1,0:T(8,128)(2,1)S(1)} %get-tuple-element.173.do_ref, ...), custom_call_target="tpu_custom_call" | custom-call | flops 1 | bytes 1 | tf_op jit(solution)/shard_map/back2/pallas_call | solution.py:66
  85.8 1.4 collective-permute-done.22
  88.8 1.7 %collective-permute-start.33 = (bf16[192,1920]{1,0:T(8,128)(2,1)S(1)}, bf16[192,1920]{1,0:T(8,128)(2,1)S(1)}, u32[]{:S(2)}, u32[]{:S(2)}) collective-permute-start(bf16[192,1920]{1,0:T(8,128)(2,1)S(1)} %add_convert_fusion), channel_id=1, source_target_pairs={{0,1},{1,0},{2,3},{3,2},{4,5},{5,4},{6,7},{7,6},{8,9},{9,8},{10,11... | collective-permute-start | bytes 2211848 | tf_op jit(solution)/shard_map/ppermute | solution.py:103
  90.5 4.5 %finish.1 = (bf16[196,768]{1,0:T(8,128)(2,1)}, bf16[196,768]{1,0:T(8,128)(2,1)}, f32[16,1152]{1,0:T(8,128)S(1)}) custom-call(s32[1,2]{1,0:T(1,128)S(1)} %copy-done.5, bf16[224,1152]{1,0:T(8,128)(2,1)S(1)} %get-tuple-element.169.dq1_ref, bf16[224,1152]{1,0:T(8,128)(2,1)S(1)} %get-tuple-element.176.dq2_ref, ...), custom_call_target="tpu_custom_call" | custom-call | flops 1 | bytes 1 | tf_op jit(solution)/shard_map/finish/pallas_call | solution.py:66
  95.1 1.5 %collective-permute-start.35 = (bf16[96,1536]{1,0:T(8,128)(2,1)S(1)}, bf16[96,1536]{1,0:T(8,128)(2,1)S(1)}, u32[]{:S(2)}, u32[]{:S(2)}) collective-permute-start(bf16[96,1536]{1,0:T(8,128)(2,1)S(1)} %pad_maximum_fusion.2), channel_id=1, source_target_pairs={{0,8},{2,10},{4,12},{6,14},{8,0},{10,2},{12,4},{14,6},{16,24},{18,... | collective-permute-start | bytes 884744 | tf_op jit(solution)/shard_map/ppermute | solution.py:90
  96.8 1.1 collective-permute-start.28
  98.0 6.2 %collective-permute-done.42 = bf16[192,1536]{1,0:T(8,128)(2,1)S(1)} collective-permute-done((bf16[192,1536]{1,0:T(8,128)(2,1)S(1)}, bf16[192,1536]{1,0:T(8,128)(2,1)S(1)}, u32[]{:S(2)}, u32[]{:S(2)}) %collective-permute-start.42) | collective-permute-done | bytes 589856 | tf_op jit(solution)/shard_map/ppermute | solution.py:94
  104.3 1.6 %collective-permute-start.43 = (bf16[96,1536]{1,0:T(8,128)(2,1)S(1)}, bf16[96,1536]{1,0:T(8,128)(2,1)S(1)}, u32[]{:S(2)}, u32[]{:S(2)}) collective-permute-start(bf16[96,1536]{1,0:T(8,128)(2,1)S(1)} %pad_maximum_fusion.3), channel_id=1, source_target_pairs={{0,8},{2,10},{4,12},{6,14},{8,0},{10,2},{12,4},{14,6},{16,24},{18,... | collective-permute-start | bytes 884744 | tf_op jit(solution)/shard_map/ppermute | solution.py:90
  106.0 1.8 %collective-permute-start.36 = (bf16[48,1536]{1,0:T(8,128)(2,1)S(1)}, bf16[48,1536]{1,0:T(8,128)(2,1)S(1)}, u32[]{:S(2)}, u32[]{:S(2)}) collective-permute-start(bf16[48,1536]{1,0:T(8,128)(2,1)S(1)} %add_convert_fusion.9), channel_id=1, source_target_pairs={{0,16},{2,18},{4,20},{6,22},{8,24},{10,26},{12,28},{14,30},{16,0},... | collective-permute-start | bytes 442376 | tf_op jit(solution)/shard_map/ppermute | solution.py:90
  107.8 7.0 %collective-permute-done.43 = bf16[96,1536]{1,0:T(8,128)(2,1)S(1)} collective-permute-done((bf16[96,1536]{1,0:T(8,128)(2,1)S(1)}, bf16[96,1536]{1,0:T(8,128)(2,1)S(1)}, u32[]{:S(2)}, u32[]{:S(2)}) %collective-permute-start.43) | collective-permute-done | bytes 294944 | tf_op jit(solution)/shard_map/ppermute | solution.py:90
  117.6 1.2 collective-permute-start.34
  118.8 4.3 %collective-permute-done.29 = bf16[112,1152]{1,0:T(8,128)(2,1)S(1)} collective-permute-done((bf16[112,1152]{1,0:T(8,128)(2,1)S(1)}, bf16[112,1152]{1,0:T(8,128)(2,1)S(1)}, u32[]{:S(2)}, u32[]{:S(2)}) %collective-permute-start.29) | collective-permute-done | bytes 258080 | tf_op jit(solution)/shard_map/ppermute | solution.py:103
  123.3 2.2 %collective-permute-start.32 = (bf16[40,1152]{1,0:T(8,128)(2,1)S(1)}, bf16[40,1152]{1,0:T(8,128)(2,1)S(1)}, u32[]{:S(2)}, u32[]{:S(2)}) collective-permute-start(bf16[40,1152]{1,0:T(8,128)(2,1)S(1)} %get-tuple-element.244), channel_id=1, source_target_pairs={{0,24},{2,26},{4,28},{6,30},{8,0},{10,2},{12,4},{14,6},{16,8},{18,... | collective-permute-start | bytes 276488 | tf_op jit(solution)/shard_map/ppermute | solution.py:85
  125.5 1.8 %collective-permute-start.31 = (bf16[40,1152]{1,0:T(8,128)(2,1)S(1)}, bf16[40,1152]{1,0:T(8,128)(2,1)S(1)}, u32[]{:S(2)}, u32[]{:S(2)}) collective-permute-start(bf16[40,1152]{1,0:T(8,128)(2,1)S(1)} %get-tuple-element.245), channel_id=1, source_target_pairs={{0,16},{2,18},{4,20},{6,22},{8,24},{10,26},{12,28},{14,30},{16,0},... | collective-permute-start | bytes 276488 | tf_op jit(solution)/shard_map/ppermute | solution.py:85
  128.4 3.7 %collective-permute-start.39 = (bf16[24,1920]{1,0:T(8,128)(2,1)S(1)}, bf16[24,1920]{1,0:T(8,128)(2,1)S(1)}, u32[]{:S(2)}, u32[]{:S(2)}) collective-permute-start(bf16[24,1920]{1,0:T(8,128)(2,1)S(1)} %get-tuple-element.234), channel_id=1, source_target_pairs={{0,24},{2,26},{4,28},{6,30},{8,0},{10,2},{12,4},{14,6},{16,8},{18,... | collective-permute-start | bytes 276488 | tf_op jit(solution)/shard_map/ppermute | solution.py:85
  132.8 6.0 %collective-permute-done.31.refs_2_ = bf16[40,1152]{1,0:T(8,128)(2,1)S(1)} collective-permute-done((bf16[40,1152]{1,0:T(8,128)(2,1)S(1)}, bf16[40,1152]{1,0:T(8,128)(2,1)S(1)}, u32[]{:S(2)}, u32[]{:S(2)}) %collective-permute-start.31) | collective-permute-done | bytes 92192 | tf_op jit(solution)/shard_map/ppermute | solution.py:85
  139.8 1.5 %collective-permute-done.38 = bf16[24,1920]{1,0:T(8,128)(2,1)S(1)} collective-permute-done((bf16[24,1920]{1,0:T(8,128)(2,1)S(1)}, bf16[24,1920]{1,0:T(8,128)(2,1)S(1)}, u32[]{:S(2)}, u32[]{:S(2)}) %collective-permute-start.38) | collective-permute-done | bytes 92192 | tf_op jit(solution)/shard_map/ppermute | solution.py:85
  (121 shorter events, 21.4 us)
Async XLA Ops:
  2.5 12.0 %collective-permute-start.2 = (bf16[24,1920]{1,0:T(8,128)(2,1)S(1)}, bf16[24,1920]{1,0:T(8,128)(2,1)S(1)}, u32[]{:S(2)}, u32[]{:S(2)}) collective-permute-start(bf16[24,1920]{1,0:T(8,128)(2,1)S(1)} %get-tuple-element.125), channel_id=1, source_target_pairs={{0,8},{2,10},{4,12},{6,14},{8,16},{10,18},{12,20},{14,22},{16,24},... | collective-permute-start | bytes 276488 | tf_op jit(solution)/shard_map/ppermute | solution.py:85
  5.6 8.9 %collective-permute-start.1 = (bf16[24,1920]{1,0:T(8,128)(2,1)S(1)}, bf16[24,1920]{1,0:T(8,128)(2,1)S(1)}, u32[]{:S(2)}, u32[]{:S(2)}) collective-permute-start(bf16[24,1920]{1,0:T(8,128)(2,1)S(1)} %get-tuple-element.125), channel_id=1, source_target_pairs={{0,16},{2,18},{4,20},{6,22},{8,24},{10,26},{12,28},{14,30},{16,0},... | collective-permute-start | bytes 276488 | tf_op jit(solution)/shard_map/ppermute | solution.py:85
  8.2 6.4 %collective-permute-start = (bf16[24,1920]{1,0:T(8,128)(2,1)S(1)}, bf16[24,1920]{1,0:T(8,128)(2,1)S(1)}, u32[]{:S(2)}, u32[]{:S(2)}) collective-permute-start(bf16[24,1920]{1,0:T(8,128)(2,1)S(1)} %get-tuple-element.125), channel_id=1, source_target_pairs={{0,24},{2,26},{4,28},{6,30},{8,0},{10,2},{12,4},{14,6},{16,8},{18,... | collective-permute-start | bytes 276488 | tf_op jit(solution)/shard_map/ppermute | solution.py:85
  9.6 8.8 %collective-permute-start.8 = (bf16[196,768]{1,0:T(8,128)(2,1)S(1)}, bf16[196,768]{1,0:T(8,128)(2,1)S(1)}, u32[]{:S(2)}, u32[]{:S(2)}) collective-permute-start(bf16[196,768]{1,0:T(8,128)(2,1)S(1)} %get-tuple-element.128.dm_ref.refs_0_), channel_id=1, source_target_pairs={{0,1},{1,0},{2,3},{3,2},{4,5},{5,4},{6,7},{7,6},{8,9},{9,8},{10,11... | collective-permute-start | bytes 903176 | tf_op jit(solution)/shard_map/ppermute | solution.py:103
  14.6 13.4 %collective-permute-start.4 = (bf16[96,1920]{1,0:T(8,128)(2,1)S(1)}, bf16[96,1920]{1,0:T(8,128)(2,1)S(1)}, u32[]{:S(2)}, u32[]{:S(2)}) collective-permute-start(bf16[96,1920]{1,0:T(8,128)(2,1)S(1)} %pad_maximum_fusion.1), channel_id=1, source_target_pairs={{0,1},{1,0},{2,3},{3,2},{4,5},{5,4},{6,7},{7,6},{8,9},{9,8},{10,11... | collective-permute-start | bytes 1105928 | tf_op jit(solution)/shard_map/ppermute | solution.py:103
  16.2 12.9 %collective-permute-start.3 = (bf16[96,1920]{1,0:T(8,128)(2,1)S(1)}, bf16[96,1920]{1,0:T(8,128)(2,1)S(1)}, u32[]{:S(2)}, u32[]{:S(2)}) collective-permute-start(bf16[96,1920]{1,0:T(8,128)(2,1)S(1)} %pad_maximum_fusion.1), channel_id=1, source_target_pairs={{0,4},{2,6},{4,0},{6,2},{8,12},{10,14},{12,8},{14,10},{16,20},{18,... | collective-permute-start | bytes 1105928 | tf_op jit(solution)/shard_map/ppermute | solution.py:94
  18.4 6.4 %collective-permute-start.11 = (bf16[24,1152]{1,0:T(8,128)(2,1)S(1)}, bf16[24,1152]{1,0:T(8,128)(2,1)S(1)}, u32[]{:S(2)}, u32[]{:S(2)}) collective-permute-start(bf16[24,1152]{1,0:T(8,128)(2,1)S(1)} %get-tuple-element.130), channel_id=1, source_target_pairs={{0,8},{2,10},{4,12},{6,14},{8,16},{10,18},{12,20},{14,22},{16,24},... | collective-permute-start | bytes 165896 | tf_op jit(solution)/shard_map/ppermute | solution.py:85
  20.1 6.1 %collective-permute-start.10 = (bf16[24,1152]{1,0:T(8,128)(2,1)S(1)}, bf16[24,1152]{1,0:T(8,128)(2,1)S(1)}, u32[]{:S(2)}, u32[]{:S(2)}) collective-permute-start(bf16[24,1152]{1,0:T(8,128)(2,1)S(1)} %get-tuple-element.130), channel_id=1, source_target_pairs={{0,16},{2,18},{4,20},{6,22},{8,24},{10,26},{12,28},{14,30},{16,0},... | collective-permute-start | bytes 165896 | tf_op jit(solution)/shard_map/ppermute | solution.py:85
  21.8 4.6 %collective-permute-start.9 = (bf16[24,1152]{1,0:T(8,128)(2,1)S(1)}, bf16[24,1152]{1,0:T(8,128)(2,1)S(1)}, u32[]{:S(2)}, u32[]{:S(2)}) collective-permute-start(bf16[24,1152]{1,0:T(8,128)(2,1)S(1)} %get-tuple-element.130), channel_id=1, source_target_pairs={{0,24},{2,26},{4,28},{6,30},{8,0},{10,2},{12,4},{14,6},{16,8},{18,... | collective-permute-start | bytes 165896 | tf_op jit(solution)/shard_map/ppermute | solution.py:85
  26.4 8.0 %collective-permute-start.13 = (bf16[96,1152]{1,0:T(8,128)(2,1)S(1)}, bf16[96,1152]{1,0:T(8,128)(2,1)S(1)}, u32[]{:S(2)}, u32[]{:S(2)}) collective-permute-start(bf16[96,1152]{1,0:T(8,128)(2,1)S(1)} %pad_maximum_fusion.5), channel_id=1, source_target_pairs={{0,4},{2,6},{4,0},{6,2},{8,12},{10,14},{12,8},{14,10},{16,20},{18,... | collective-permute-start | bytes 663560 | tf_op jit(solution)/shard_map/ppermute | solution.py:94
  26.9 7.7 %collective-permute-start.12 = (bf16[96,1152]{1,0:T(8,128)(2,1)S(1)}, bf16[96,1152]{1,0:T(8,128)(2,1)S(1)}, u32[]{:S(2)}, u32[]{:S(2)}) collective-permute-start(bf16[96,1152]{1,0:T(8,128)(2,1)S(1)} %pad_maximum_fusion.5), channel_id=1, source_target_pairs={{0,1},{1,0},{2,3},{3,2},{4,5},{5,4},{6,7},{7,6},{8,9},{9,8},{10,11... | collective-permute-start | bytes 663560 | tf_op jit(solution)/shard_map/ppermute | solution.py:103
  28.1 9.1 %collective-permute-start.5 = (bf16[96,960]{1,0:T(8,128)(2,1)S(1)}, bf16[96,960]{1,0:T(8,128)(2,1)S(1)}, u32[]{:S(2)}, u32[]{:S(2)}) collective-permute-start(bf16[96,960]{1,0:T(8,128)(2,1)S(1)} %slice.366), channel_id=1, source_target_pairs={{0,4},{2,6},{4,0},{6,2},{8,12},{10,14},{12,8},{14,10},{16,20},{18,... | collective-permute-start | bytes 552968 | tf_op jit(solution)/shard_map/ppermute | solution.py:94
  29.2 8.0 %collective-permute-start.6 = (bf16[96,960]{1,0:T(8,128)(2,1)S(1)}, bf16[96,960]{1,0:T(8,128)(2,1)S(1)}, u32[]{:S(2)}, u32[]{:S(2)}) collective-permute-start(bf16[96,960]{1,0:T(8,128)(2,1)S(1)} %slice.367), channel_id=1, source_target_pairs={{0,1},{1,0},{2,3},{3,2},{4,5},{5,4},{6,7},{7,6},{8,9},{9,8},{10,11... | collective-permute-start | bytes 552968 | tf_op jit(solution)/shard_map/ppermute | solution.py:103
  34.8 4.9 %collective-permute-start.14 = (bf16[96,576]{1,0:T(8,128)(2,1)S(1)}, bf16[96,576]{1,0:T(8,128)(2,1)S(1)}, u32[]{:S(2)}, u32[]{:S(2)}) collective-permute-start(bf16[96,576]{1,0:T(8,128)(2,1)S(1)} %slice.286), channel_id=1, source_target_pairs={{0,4},{2,6},{4,0},{6,2},{8,12},{10,14},{12,8},{14,10},{16,20},{18,... | collective-permute-start | bytes 331784 | tf_op jit(solution)/shard_map/ppermute | solution.py:94
  36.3 4.9 %collective-permute-start.15 = (bf16[96,576]{1,0:T(8,128)(2,1)S(1)}, bf16[96,576]{1,0:T(8,128)(2,1)S(1)}, u32[]{:S(2)}, u32[]{:S(2)}) collective-permute-start(bf16[96,576]{1,0:T(8,128)(2,1)S(1)} %slice.287), channel_id=1, source_target_pairs={{0,1},{1,0},{2,3},{3,2},{4,5},{5,4},{6,7},{7,6},{8,9},{9,8},{10,11... | collective-permute-start | bytes 331784 | tf_op jit(solution)/shard_map/ppermute | solution.py:103
  37.3 8.4 %collective-permute-start.7 = (bf16[384,1920]{1,0:T(8,128)(2,1)S(1)}, bf16[384,1920]{1,0:T(8,128)(2,1)S(1)}, u32[]{:S(2)}, u32[]{:S(2)}) collective-permute-start(bf16[384,1920]{1,0:T(8,128)(2,1)S(1)} %maximum_dynamic-update-slice_fusion.own_ref.own2_ref), channel_id=1, source_target_pairs={{0,2},{2,0},{4,6},{6,4},{8,10},{10,8},{12,14},{14,12},{16,18},{18,... | collective-permute-start | bytes 4423688 | tf_op jit(solution)/shard_map/ppermute | solution.py:98
  37.5 8.3 %copy-start.2 = (bf16[196,768]{1,0:T(8,128)(2,1)S(1)}, bf16[196,768]{1,0:T(8,128)(2,1)}, u32[]{:S(2)}) copy-start(bf16[196,768]{1,0:T(8,128)(2,1)} %x_ref.3) | copy-start | bytes 903172
  37.5 8.3 %copy-start.5 = (s32[1,2]{1,0:T(1,128)S(1)}, s32[1,2]{1,0:T(1,128)}, u32[]{:S(2)}) copy-start(s32[1,2]{1,0:T(1,128)} %keep_ref.7) | copy-start | bytes 28
  41.3 2.5 %collective-permute-start.16 = (bf16[384,1152]{1,0:T(8,128)(2,1)S(1)}, bf16[384,1152]{1,0:T(8,128)(2,1)S(1)}, u32[]{:S(2)}, u32[]{:S(2)}) collective-permute-start(bf16[384,1152]{1,0:T(8,128)(2,1)S(1)} %maximum_dynamic-update-slice_fusion.1.own_ref.own1_ref), channel_id=1, source_target_pairs={{0,2},{2,0},{4,6},{6,4},{8,10},{10,8},{12,14},{14,12},{16,18},{18,... | collective-permute-start | bytes 2654216 | tf_op jit(solution)/shard_map/ppermute | solution.py:98
  49.7 9.4 %collective-permute-start.17 = (bf16[196,768]{1,0:T(8,128)(2,1)S(1)}, bf16[196,768]{1,0:T(8,128)(2,1)S(1)}, u32[]{:S(2)}, u32[]{:S(2)}) collective-permute-start(bf16[196,768]{1,0:T(8,128)(2,1)S(1)} %get-tuple-element.141.a2_ref.refs_4_), channel_id=1, source_target_pairs={{0,1},{1,0},{2,3},{3,2},{4,5},{5,4},{6,7},{7,6},{8,9},{9,8},{10,11... | collective-permute-start | bytes 903176 | tf_op jit(solution)/shard_map/ppermute | solution.py:103
  61.1 8.6 %collective-permute-start.18 = (bf16[196,768]{1,0:T(8,128)(2,1)S(1)}, bf16[196,768]{1,0:T(8,128)(2,1)S(1)}, u32[]{:S(2)}, u32[]{:S(2)}) collective-permute-start(bf16[196,768]{1,0:T(8,128)(2,1)S(1)} %get-tuple-element.147), channel_id=1, source_target_pairs={{0,1},{1,0},{2,3},{3,2},{4,5},{5,4},{6,7},{7,6},{8,9},{9,8},{10,11... | collective-permute-start | bytes 903176 | tf_op jit(solution)/shard_map/ppermute | solution.py:103
  68.1 6.5 %copy-start.3 = (bf16[196,768]{1,0:T(8,128)(2,1)S(1)}, bf16[196,768]{1,0:T(8,128)(2,1)}, u32[]{:S(2)}) copy-start(bf16[196,768]{1,0:T(8,128)(2,1)} %g_ref.1) | copy-start | bytes 903172
  69.7 2.0 %collective-permute-start.20 = (bf16[192,1536]{1,0:T(8,128)(2,1)S(1)}, bf16[192,1536]{1,0:T(8,128)(2,1)S(1)}, u32[]{:S(2)}, u32[]{:S(2)}) collective-permute-start(bf16[192,1536]{1,0:T(8,128)(2,1)S(1)} %get-tuple-element.163), channel_id=1, source_target_pairs={{0,2},{2,0},{4,6},{6,4},{8,10},{10,8},{12,14},{14,12},{16,18},{18,... | collective-permute-start | bytes 1769480 | tf_op jit(solution)/shard_map/ppermute | solution.py:98
  69.7 2.8 %collective-permute-start.19 = (bf16[192,1536]{1,0:T(8,128)(2,1)S(1)}, bf16[192,1536]{1,0:T(8,128)(2,1)S(1)}, u32[]{:S(2)}, u32[]{:S(2)}) collective-permute-start(bf16[192,1536]{1,0:T(8,128)(2,1)S(1)} %get-tuple-element.162), channel_id=1, source_target_pairs={{0,2},{2,0},{4,6},{6,4},{8,10},{10,8},{12,14},{14,12},{16,18},{18,... | collective-permute-start | bytes 1769480 | tf_op jit(solution)/shard_map/ppermute | solution.py:98
  71.8 15.4 %collective-permute-start.22 = (bf16[192,1536]{1,0:T(8,128)(2,1)S(1)}, bf16[192,1536]{1,0:T(8,128)(2,1)S(1)}, u32[]{:S(2)}, u32[]{:S(2)}) collective-permute-start(bf16[192,1536]{1,0:T(8,128)(2,1)S(1)} %add_convert_fusion.2), channel_id=1, source_target_pairs={{0,4},{2,6},{4,0},{6,2},{8,12},{10,14},{12,8},{14,10},{16,20},{18,... | collective-permute-start | bytes 1769480 | tf_op jit(solution)/shard_map/ppermute | solution.py:94
  72.5 14.7 %collective-permute-start.40 = (bf16[192,1536]{1,0:T(8,128)(2,1)S(1)}, bf16[192,1536]{1,0:T(8,128)(2,1)S(1)}, u32[]{:S(2)}, u32[]{:S(2)}) collective-permute-start(bf16[192,1536]{1,0:T(8,128)(2,1)S(1)} %get-tuple-element.222), channel_id=1, source_target_pairs={{0,2},{2,0},{4,6},{6,4},{8,10},{10,8},{12,14},{14,12},{16,18},{18,... | collective-permute-start | bytes 1769480 | tf_op jit(solution)/shard_map/ppermute | solution.py:98
  72.6 14.6 %collective-permute-start.41 = (bf16[192,1536]{1,0:T(8,128)(2,1)S(1)}, bf16[192,1536]{1,0:T(8,128)(2,1)S(1)}, u32[]{:S(2)}, u32[]{:S(2)}) collective-permute-start(bf16[192,1536]{1,0:T(8,128)(2,1)S(1)} %get-tuple-element.223), channel_id=1, source_target_pairs={{0,2},{2,0},{4,6},{6,4},{8,10},{10,8},{12,14},{14,12},{16,18},{18,... | collective-permute-start | bytes 1769480 | tf_op jit(solution)/shard_map/ppermute | solution.py:98
  73.0 9.3 %collective-permute-start.21 = (bf16[196,768]{1,0:T(8,128)(2,1)S(1)}, bf16[196,768]{1,0:T(8,128)(2,1)S(1)}, u32[]{:S(2)}, u32[]{:S(2)}) collective-permute-start(bf16[196,768]{1,0:T(8,128)(2,1)S(1)} %get-tuple-element.170), channel_id=1, source_target_pairs={{0,1},{1,0},{2,3},{3,2},{4,5},{5,4},{6,7},{7,6},{8,9},{9,8},{10,11... | collective-permute-start | bytes 903176 | tf_op jit(solution)/shard_map/ppermute | solution.py:103
  82.3 14.4 %collective-permute-start.26 = (bf16[192,1920]{1,0:T(8,128)(2,1)S(1)}, bf16[192,1920]{1,0:T(8,128)(2,1)S(1)}, u32[]{:S(2)}, u32[]{:S(2)}) collective-permute-start(bf16[192,1920]{1,0:T(8,128)(2,1)S(1)} %get-tuple-element.193), channel_id=1, source_target_pairs={{0,2},{2,0},{4,6},{6,4},{8,10},{10,8},{12,14},{14,12},{16,18},{18,... | collective-permute-start | bytes 2211848 | tf_op jit(solution)/shard_map/ppermute | solution.py:98
  82.3 6.3 %collective-permute-start.27 = (bf16[192,1920]{1,0:T(8,128)(2,1)S(1)}, bf16[192,1920]{1,0:T(8,128)(2,1)S(1)}, u32[]{:S(2)}, u32[]{:S(2)}) collective-permute-start(bf16[192,1920]{1,0:T(8,128)(2,1)S(1)} %get-tuple-element.194), channel_id=1, source_target_pairs={{0,2},{2,0},{4,6},{6,4},{8,10},{10,8},{12,14},{14,12},{16,18},{18,... | collective-permute-start | bytes 2211848 | tf_op jit(solution)/shard_map/ppermute | solution.py:98
  87.2 3.3 %collective-permute-start.23 = (bf16[192,1152]{1,0:T(8,128)(2,1)S(1)}, bf16[192,1152]{1,0:T(8,128)(2,1)S(1)}, u32[]{:S(2)}, u32[]{:S(2)}) collective-permute-start(bf16[192,1152]{1,0:T(8,128)(2,1)S(1)} %get-tuple-element.180), channel_id=1, source_target_pairs={{0,2},{2,0},{4,6},{6,4},{8,10},{10,8},{12,14},{14,12},{16,18},{18,... | collective-permute-start | bytes 1327112 | tf_op jit(solution)/shard_map/ppermute | solution.py:98
  87.3 3.3 %collective-permute-start.24 = (bf16[192,1152]{1,0:T(8,128)(2,1)S(1)}, bf16[192,1152]{1,0:T(8,128)(2,1)S(1)}, u32[]{:S(2)}, u32[]{:S(2)}) collective-permute-start(bf16[192,1152]{1,0:T(8,128)(2,1)S(1)} %get-tuple-element.181), channel_id=1, source_target_pairs={{0,2},{2,0},{4,6},{6,4},{8,10},{10,8},{12,14},{14,12},{16,18},{18,... | collective-permute-start | bytes 1327112 | tf_op jit(solution)/shard_map/ppermute | solution.py:98
  87.9 16.2 %collective-permute-start.42 = (bf16[192,1536]{1,0:T(8,128)(2,1)S(1)}, bf16[192,1536]{1,0:T(8,128)(2,1)S(1)}, u32[]{:S(2)}, u32[]{:S(2)}) collective-permute-start(bf16[192,1536]{1,0:T(8,128)(2,1)S(1)} %add_convert_fusion.1), channel_id=1, source_target_pairs={{0,4},{2,6},{4,0},{6,2},{8,12},{10,14},{12,8},{14,10},{16,20},{18,... | collective-permute-start | bytes 1769480 | tf_op jit(solution)/shard_map/ppermute | solution.py:94
  88.8 28.7 %collective-permute-start.33 = (bf16[192,1920]{1,0:T(8,128)(2,1)S(1)}, bf16[192,1920]{1,0:T(8,128)(2,1)S(1)}, u32[]{:S(2)}, u32[]{:S(2)}) collective-permute-start(bf16[192,1920]{1,0:T(8,128)(2,1)S(1)} %add_convert_fusion), channel_id=1, source_target_pairs={{0,1},{1,0},{2,3},{3,2},{4,5},{5,4},{6,7},{7,6},{8,9},{9,8},{10,11... | collective-permute-start | bytes 2211848 | tf_op jit(solution)/shard_map/ppermute | solution.py:103
  95.1 1.6 %collective-permute-start.25 = (f32[16,1152]{1,0:T(8,128)S(1)}, f32[16,1152]{1,0:T(8,128)S(1)}, u32[]{:S(2)}, u32[]{:S(2)}) collective-permute-start(f32[16,1152]{1,0:T(8,128)S(1)} %get-tuple-element.192), channel_id=1, source_target_pairs={{0,2},{2,0},{4,6},{6,4},{8,10},{10,8},{12,14},{14,12},{16,18},{18,... | collective-permute-start | bytes 221192 | tf_op jit(solution)/shard_map/ppermute | solution.py:98
  95.1 10.8 %collective-permute-start.35 = (bf16[96,1536]{1,0:T(8,128)(2,1)S(1)}, bf16[96,1536]{1,0:T(8,128)(2,1)S(1)}, u32[]{:S(2)}, u32[]{:S(2)}) collective-permute-start(bf16[96,1536]{1,0:T(8,128)(2,1)S(1)} %pad_maximum_fusion.2), channel_id=1, source_target_pairs={{0,8},{2,10},{4,12},{6,14},{8,0},{10,2},{12,4},{14,6},{16,24},{18,... | collective-permute-start | bytes 884744 | tf_op jit(solution)/shard_map/ppermute | solution.py:90
  96.8 19.8 %collective-permute-start.28 = (bf16[208,1152]{1,0:T(8,128)(2,1)S(1)}, bf16[208,1152]{1,0:T(8,128)(2,1)S(1)}, u32[]{:S(2)}, u32[]{:S(2)}) collective-permute-start(bf16[208,1152]{1,0:T(8,128)(2,1)S(1)} %pad_maximum_fusion), channel_id=1, source_target_pairs={{0,4},{2,6},{4,0},{6,2},{8,12},{10,14},{12,8},{14,10},{16,20},{18,... | collective-permute-start | bytes 1437704 | tf_op jit(solution)/shard_map/ppermute | solution.py:94
  104.3 10.5 %collective-permute-start.43 = (bf16[96,1536]{1,0:T(8,128)(2,1)S(1)}, bf16[96,1536]{1,0:T(8,128)(2,1)S(1)}, u32[]{:S(2)}, u32[]{:S(2)}) collective-permute-start(bf16[96,1536]{1,0:T(8,128)(2,1)S(1)} %pad_maximum_fusion.3), channel_id=1, source_target_pairs={{0,8},{2,10},{4,12},{6,14},{8,0},{10,2},{12,4},{14,6},{16,24},{18,... | collective-permute-start | bytes 884744 | tf_op jit(solution)/shard_map/ppermute | solution.py:90
  106.0 9.8 %collective-permute-start.36 = (bf16[48,1536]{1,0:T(8,128)(2,1)S(1)}, bf16[48,1536]{1,0:T(8,128)(2,1)S(1)}, u32[]{:S(2)}, u32[]{:S(2)}) collective-permute-start(bf16[48,1536]{1,0:T(8,128)(2,1)S(1)} %add_convert_fusion.9), channel_id=1, source_target_pairs={{0,16},{2,18},{4,20},{6,22},{8,24},{10,26},{12,28},{14,30},{16,0},... | collective-permute-start | bytes 442376 | tf_op jit(solution)/shard_map/ppermute | solution.py:90
  114.9 8.3 %collective-permute-start.44 = (bf16[48,1536]{1,0:T(8,128)(2,1)S(1)}, bf16[48,1536]{1,0:T(8,128)(2,1)S(1)}, u32[]{:S(2)}, u32[]{:S(2)}) collective-permute-start(bf16[48,1536]{1,0:T(8,128)(2,1)S(1)} %add_convert_fusion.6), channel_id=1, source_target_pairs={{0,16},{2,18},{4,20},{6,22},{8,24},{10,26},{12,28},{14,30},{16,0},... | collective-permute-start | bytes 442376 | tf_op jit(solution)/shard_map/ppermute | solution.py:90
  116.7 6.4 %collective-permute-start.29 = (bf16[112,1152]{1,0:T(8,128)(2,1)S(1)}, bf16[112,1152]{1,0:T(8,128)(2,1)S(1)}, u32[]{:S(2)}, u32[]{:S(2)}) collective-permute-start(bf16[112,1152]{1,0:T(8,128)(2,1)S(1)} %pad_maximum_fusion.4), channel_id=1, source_target_pairs={{0,1},{1,0},{2,3},{3,2},{4,5},{5,4},{6,7},{7,6},{8,9},{9,8},{10,11... | collective-permute-start | bytes 774152 | tf_op jit(solution)/shard_map/ppermute | solution.py:103
  117.6 10.6 %collective-permute-start.34 = (bf16[96,1920]{1,0:T(8,128)(2,1)S(1)}, bf16[96,1920]{1,0:T(8,128)(2,1)S(1)}, u32[]{:S(2)}, u32[]{:S(2)}) collective-permute-start(bf16[96,1920]{1,0:T(8,128)(2,1)S(1)} %add_convert_fusion.4), channel_id=1, source_target_pairs={{0,4},{2,6},{4,0},{6,2},{8,12},{10,14},{12,8},{14,10},{16,20},{18,... | collective-permute-start | bytes 1105928 | tf_op jit(solution)/shard_map/ppermute | solution.py:94
  123.3 8.9 %collective-permute-start.32 = (bf16[40,1152]{1,0:T(8,128)(2,1)S(1)}, bf16[40,1152]{1,0:T(8,128)(2,1)S(1)}, u32[]{:S(2)}, u32[]{:S(2)}) collective-permute-start(bf16[40,1152]{1,0:T(8,128)(2,1)S(1)} %get-tuple-element.244), channel_id=1, source_target_pairs={{0,24},{2,26},{4,28},{6,30},{8,0},{10,2},{12,4},{14,6},{16,8},{18,... | collective-permute-start | bytes 276488 | tf_op jit(solution)/shard_map/ppermute | solution.py:85
  125.5 13.3 %collective-permute-start.31 = (bf16[40,1152]{1,0:T(8,128)(2,1)S(1)}, bf16[40,1152]{1,0:T(8,128)(2,1)S(1)}, u32[]{:S(2)}, u32[]{:S(2)}) collective-permute-start(bf16[40,1152]{1,0:T(8,128)(2,1)S(1)} %get-tuple-element.245), channel_id=1, source_target_pairs={{0,16},{2,18},{4,20},{6,22},{8,24},{10,26},{12,28},{14,30},{16,0},... | collective-permute-start | bytes 276488 | tf_op jit(solution)/shard_map/ppermute | solution.py:85
  127.3 11.5 %collective-permute-start.30 = (bf16[40,1152]{1,0:T(8,128)(2,1)S(1)}, bf16[40,1152]{1,0:T(8,128)(2,1)S(1)}, u32[]{:S(2)}, u32[]{:S(2)}) collective-permute-start(bf16[40,1152]{1,0:T(8,128)(2,1)S(1)} %get-tuple-element.246), channel_id=1, source_target_pairs={{0,8},{2,10},{4,12},{6,14},{8,16},{10,18},{12,20},{14,22},{16,24},... | collective-permute-start | bytes 276488 | tf_op jit(solution)/shard_map/ppermute | solution.py:85
  128.4 11.4 %collective-permute-start.39 = (bf16[24,1920]{1,0:T(8,128)(2,1)S(1)}, bf16[24,1920]{1,0:T(8,128)(2,1)S(1)}, u32[]{:S(2)}, u32[]{:S(2)}) collective-permute-start(bf16[24,1920]{1,0:T(8,128)(2,1)S(1)} %get-tuple-element.234), channel_id=1, source_target_pairs={{0,24},{2,26},{4,28},{6,30},{8,0},{10,2},{12,4},{14,6},{16,8},{18,... | collective-permute-start | bytes 276488 | tf_op jit(solution)/shard_map/ppermute | solution.py:85
  132.1 9.1 %collective-permute-start.38 = (bf16[24,1920]{1,0:T(8,128)(2,1)S(1)}, bf16[24,1920]{1,0:T(8,128)(2,1)S(1)}, u32[]{:S(2)}, u32[]{:S(2)}) collective-permute-start(bf16[24,1920]{1,0:T(8,128)(2,1)S(1)} %get-tuple-element.235), channel_id=1, source_target_pairs={{0,16},{2,18},{4,20},{6,22},{8,24},{10,26},{12,28},{14,30},{16,0},... | collective-permute-start | bytes 276488 | tf_op jit(solution)/shard_map/ppermute | solution.py:85
  132.1 9.1 %collective-permute-start.37 = (bf16[24,1920]{1,0:T(8,128)(2,1)S(1)}, bf16[24,1920]{1,0:T(8,128)(2,1)S(1)}, u32[]{:S(2)}, u32[]{:S(2)}) collective-permute-start(bf16[24,1920]{1,0:T(8,128)(2,1)S(1)} %get-tuple-element.236), channel_id=1, source_target_pairs={{0,8},{2,10},{4,12},{6,14},{8,16},{10,18},{12,20},{14,22},{16,24},... | collective-permute-start | bytes 276488 | tf_op jit(solution)/shard_map/ppermute | solution.py:85
  (4 other events, 7.8 us)

commit v6 on v5

--- a/solution.py
+++ b/solution.py
@@ -32,7 +32,7 @@
 TREE = (True, True)
 FRONT = ('dm', 'z1', 'prep', 'act1', 'z2', 'n1', 'n2', 'act0', 'f2', 'f1', 'c1', 'attend1', 'c2')
 ORDER = ('dc', 'dy', 'm', 'norm', 'back2', 'bc', 'back1', 'finish', 'ac', 'sc', 'by', 'bx', 'ax', 'd0', 'd1', 'bz', 'uc', 'uy', 'ay', 'u0', 'u1', 'az')
-GATES = {'n1:s': ['prep', 'dm'], 'n2:s': ['z2'], 'f1:s': ['n1'], 'act1:s': ['dm'], 'attend1:s': ['dm', 'f1'], 'z1:s': ['dm'], 'back1:s': ['dc'], 'back2:s': ['m', 'dc', 'norm'], 'finish:s': ['bc'], 'ay:r': ['ac', 'back1', 'd1'], 'uc:s': ['dc'], 'bc:s': ['dy'], 'bx:r': ['dy'], 'bz:r': ['bc'], 'd0:s': ['finish'], 'd1:r': ['dy'], 'az:r': ['bz'], 'u1:r': ['by', 'bx'], 'uc:r': ['back2'], 'sc:r': ['ac']}
+GATES = {'n1:s': ['prep', 'dm'], 'n2:s': ['z2'], 'f1:s': ['n1'], 'act1:s': ['dm'], 'attend1:s': ['dm', 'f1'], 'z1:s': ['dm'], 'back1:s': ['dc'], 'back2:s': ['m', 'dc'], 'finish:s': ['bc'], 'ay:r': ['ac', 'back1', 'd1'], 'uc:s': ['dc'], 'bc:s': ['dy'], 'bx:r': ['dy'], 'bz:r': ['bc'], 'd0:s': ['finish'], 'd1:r': ['dy'], 'az:r': ['bz'], 'u1:r': ['by', 'bx'], 'uc:r': ['back2'], 'sc:r': ['ac'], 'ax:r': ['sc'], 'az:s': ['ay']}
 ROUTE = {"y": "b", "x": "b", "z": "b"}
 CHEAP = pl.CostEstimate(flops=1, bytes_accessed=1, transcendentals=0)
 SMALL = {"gain1": 0, "shift1": 6, "qbias": 12, "vbias": 18, "projb": 24, "gain2": 30, "shift2": 36, "downb": 42}

time: 143 us -> 142 us (level)
  no operation moved by 1% of the time
where the time goes in v6:
time: 142 us
  waiting for transfers between devices  49.2 us (35%)
  starting transfers between devices  48.4 us (34%)
  Pallas kernels  36.7 us (26%)
  other arithmetic  3.65 us (3%)
  local copies, waits for them, and re-layouts  2.73 us (2%)
    pallas_call x14, Pallas kernels, run(): call(*args[:smem], *map(pltpu.with_memory_space_constraint, args[smem:],...  36.7 us
    ppermute x12, starting transfers between devices, move_z(): return lax.ppermute(value, 'dp', dp_pairs(lax.axis_size('dp'), dz=step))  19.7 us
    ppermute x10, waiting for transfers between devices, move_x(): lax.ppermute(value, 'mp', [(i, (i + step) % count) for i in range(count)])  14.4 us
    ppermute x8, waiting for transfers between devices, move_y(): return lax.ppermute(value, 'dp', dp_pairs(lax.axis_size('dp'), dy=1))  13.2 us
    ppermute x10, starting transfers between devices, move_x(): lax.ppermute(value, 'mp', [(i, (i + step) % count) for i in range(count)])  12.6 us
    ppermute x12, waiting for transfers between devices, move_z(): return lax.ppermute(value, 'dp', dp_pairs(lax.axis_size('dp'), dz=step))  10.5 us
    ppermute x8, starting transfers between devices, move_y(): return lax.ppermute(value, 'dp', dp_pairs(lax.axis_size('dp'), dy=1))  8.1 us
    ppermute x4, waiting for transfers between devices, swap_z(): return lax.ppermute(value, 'dp', pairs)  6.96 us
  transfers between devices with their start and end apart: 45, of which 21 were waited for; matrix products, arithmetic and copies ran while one was open for 3% of the time, Pallas kernels for 21%

profile of v6, /device:TPU:0, one launch (start us, length us, event | category | flops | bytes accessed | tf_op | source)
XLA Modules:
  0.0 141.8 jit_solution(11386754034225595463)
XLA Ops:
  1.3 1.2 pack.1
  2.5 3.1 %collective-permute-start.2 = (bf16[24,1920]{1,0:T(8,128)(2,1)S(1)}, bf16[24,1920]{1,0:T(8,128)(2,1)S(1)}, u32[]{:S(2)}, u32[]{:S(2)}) collective-permute-start(bf16[24,1920]{1,0:T(8,128)(2,1)S(1)} %get-tuple-element.129), channel_id=1, source_target_pairs={{0,8},{2,10},{4,12},{6,14},{8,16},{10,18},{12,20},{14,22},{16,24},... | collective-permute-start | bytes 276488 | tf_op jit(solution)/shard_map/ppermute | solution.py:85
  5.6 2.6 %collective-permute-start.1 = (bf16[24,1920]{1,0:T(8,128)(2,1)S(1)}, bf16[24,1920]{1,0:T(8,128)(2,1)S(1)}, u32[]{:S(2)}, u32[]{:S(2)}) collective-permute-start(bf16[24,1920]{1,0:T(8,128)(2,1)S(1)} %get-tuple-element.129), channel_id=1, source_target_pairs={{0,16},{2,18},{4,20},{6,22},{8,24},{10,26},{12,28},{14,30},{16,0},... | collective-permute-start | bytes 276488 | tf_op jit(solution)/shard_map/ppermute | solution.py:85
  8.2 1.3 collective-permute-start
  9.6 1.5 %collective-permute-start.8 = (bf16[196,768]{1,0:T(8,128)(2,1)S(1)}, bf16[196,768]{1,0:T(8,128)(2,1)S(1)}, u32[]{:S(2)}, u32[]{:S(2)}) collective-permute-start(bf16[196,768]{1,0:T(8,128)(2,1)S(1)} %get-tuple-element.132.dm_ref.refs_0_), channel_id=1, source_target_pairs={{0,1},{1,0},{2,3},{3,2},{4,5},{5,4},{6,7},{7,6},{8,9},{9,8},{10,11... | collective-permute-start | bytes 903176 | tf_op jit(solution)/shard_map/ppermute | solution.py:103
  11.1 3.4 %prepare.1 = (bf16[224,768]{1,0:T(8,128)(2,1)S(1)}, bf16[768,224]{1,0:T(8,128)(2,1)S(1)}, bf16[768,768]{1,0:T(8,128)(2,1)S(1)}, bf16[768,768]{1,0:T(8,128)(2,1)S...) custom-call(bf16[196,768]{1,0:T(8,128)(2,1)} %x_ref.3, ...), custom_call_target="tpu_custom_call" | custom-call | flops 1 | bytes 1 | tf_op jit(solution)/shard_map/prepare/pallas_call | solution.py:66
  14.6 1.6 %collective-permute-start.4 = (bf16[96,1920]{1,0:T(8,128)(2,1)S(1)}, bf16[96,1920]{1,0:T(8,128)(2,1)S(1)}, u32[]{:S(2)}, u32[]{:S(2)}) collective-permute-start(bf16[96,1920]{1,0:T(8,128)(2,1)S(1)} %pad_maximum_fusion.1), channel_id=1, source_target_pairs={{0,1},{1,0},{2,3},{3,2},{4,5},{5,4},{6,7},{7,6},{8,9},{9,8},{10,11... | collective-permute-start | bytes 1105928 | tf_op jit(solution)/shard_map/ppermute | solution.py:103
  16.2 1.5 %collective-permute-start.3 = (bf16[96,1920]{1,0:T(8,128)(2,1)S(1)}, bf16[96,1920]{1,0:T(8,128)(2,1)S(1)}, u32[]{:S(2)}, u32[]{:S(2)}) collective-permute-start(bf16[96,1920]{1,0:T(8,128)(2,1)S(1)} %pad_maximum_fusion.1), channel_id=1, source_target_pairs={{0,4},{2,6},{4,0},{6,2},{8,12},{10,14},{12,8},{14,10},{16,20},{18,... | collective-permute-start | bytes 1105928 | tf_op jit(solution)/shard_map/ppermute | solution.py:94
  18.4 1.7 %collective-permute-start.11 = (bf16[24,1152]{1,0:T(8,128)(2,1)S(1)}, bf16[24,1152]{1,0:T(8,128)(2,1)S(1)}, u32[]{:S(2)}, u32[]{:S(2)}) collective-permute-start(bf16[24,1152]{1,0:T(8,128)(2,1)S(1)} %get-tuple-element.134), channel_id=1, source_target_pairs={{0,8},{2,10},{4,12},{6,14},{8,16},{10,18},{12,20},{14,22},{16,24},... | collective-permute-start | bytes 165896 | tf_op jit(solution)/shard_map/ppermute | solution.py:85
  20.1 1.7 %collective-permute-start.10 = (bf16[24,1152]{1,0:T(8,128)(2,1)S(1)}, bf16[24,1152]{1,0:T(8,128)(2,1)S(1)}, u32[]{:S(2)}, u32[]{:S(2)}) collective-permute-start(bf16[24,1152]{1,0:T(8,128)(2,1)S(1)} %get-tuple-element.134), channel_id=1, source_target_pairs={{0,16},{2,18},{4,20},{6,22},{8,24},{10,26},{12,28},{14,30},{16,0},... | collective-permute-start | bytes 165896 | tf_op jit(solution)/shard_map/ppermute | solution.py:85
  22.5 2.2 %collective-permute-done.11 = bf16[24,1152]{1,0:T(8,128)(2,1)S(1)} collective-permute-done((bf16[24,1152]{1,0:T(8,128)(2,1)S(1)}, bf16[24,1152]{1,0:T(8,128)(2,1)S(1)}, u32[]{:S(2)}, u32[]{:S(2)}) %collective-permute-start.11) | collective-permute-done | bytes 55328 | tf_op jit(solution)/shard_map/ppermute | solution.py:85
  24.7 1.5 %collective-permute-done.10 = bf16[24,1152]{1,0:T(8,128)(2,1)S(1)} collective-permute-done((bf16[24,1152]{1,0:T(8,128)(2,1)S(1)}, bf16[24,1152]{1,0:T(8,128)(2,1)S(1)}, u32[]{:S(2)}, u32[]{:S(2)}) %collective-permute-start.10) | collective-permute-done | bytes 55328 | tf_op jit(solution)/shard_map/ppermute | solution.py:85
  29.2 1.6 %collective-permute-start.6 = (bf16[96,960]{1,0:T(8,128)(2,1)S(1)}, bf16[96,960]{1,0:T(8,128)(2,1)S(1)}, u32[]{:S(2)}, u32[]{:S(2)}) collective-permute-start(bf16[96,960]{1,0:T(8,128)(2,1)S(1)} %slice.367), channel_id=1, source_target_pairs={{0,1},{1,0},{2,3},{3,2},{4,5},{5,4},{6,7},{7,6},{8,9},{9,8},{10,11... | collective-permute-start | bytes 552968 | tf_op jit(solution)/shard_map/ppermute | solution.py:103
  31.0 3.4 %collective-permute-done.13 = bf16[96,1152]{1,0:T(8,128)(2,1)S(1)} collective-permute-done((bf16[96,1152]{1,0:T(8,128)(2,1)S(1)}, bf16[96,1152]{1,0:T(8,128)(2,1)S(1)}, u32[]{:S(2)}, u32[]{:S(2)}) %collective-permute-start.13) | collective-permute-done | bytes 221216 | tf_op jit(solution)/shard_map/ppermute | solution.py:94
  34.8 1.6 %collective-permute-start.14 = (bf16[96,576]{1,0:T(8,128)(2,1)S(1)}, bf16[96,576]{1,0:T(8,128)(2,1)S(1)}, u32[]{:S(2)}, u32[]{:S(2)}) collective-permute-start(bf16[96,576]{1,0:T(8,128)(2,1)S(1)} %slice.286), channel_id=1, source_target_pairs={{0,4},{2,6},{4,0},{6,2},{8,12},{10,14},{12,8},{14,10},{16,20},{18,... | collective-permute-start | bytes 331784 | tf_op jit(solution)/shard_map/ppermute | solution.py:94
  37.5 2.2 %collective-permute-done.14 = bf16[96,576]{1,0:T(8,128)(2,1)S(1)} collective-permute-done((bf16[96,576]{1,0:T(8,128)(2,1)S(1)}, bf16[96,576]{1,0:T(8,128)(2,1)S(1)}, u32[]{:S(2)}, u32[]{:S(2)}) %collective-permute-start.14) | collective-permute-done | bytes 110624 | tf_op jit(solution)/shard_map/ppermute | solution.py:94
  39.7 1.5 %collective-permute-done.15 = bf16[96,576]{1,0:T(8,128)(2,1)S(1)} collective-permute-done((bf16[96,576]{1,0:T(8,128)(2,1)S(1)}, bf16[96,576]{1,0:T(8,128)(2,1)S(1)}, u32[]{:S(2)}, u32[]{:S(2)}) %collective-permute-start.15) | collective-permute-done | bytes 110624 | tf_op jit(solution)/shard_map/ppermute | solution.py:103
  41.4 2.4 %collective-permute-done.16.other_ref.other1_ref = bf16[384,1152]{1,0:T(8,128)(2,1)S(1)} collective-permute-done((bf16[384,1152]{1,0:T(8,128)(2,1)S(1)}, bf16[384,1152]{1,0:T(8,128)(2,1)S(1)}, u32[]{:S(2)}, u32[]{:S(2)}) %collective-permute-start.16) | collective-permute-done | bytes 884768 | tf_op jit(solution)/shard_map/ppermute | solution.py:98
  43.8 1.9 %attend1.1 = (bf16[224,1152]{1,0:T(8,128)(2,1)S(1)}, bf16[6,224,224]{2,1,0:T(8,128)(2,1)S(1)}, bf16[224,384]{1,0:T(8,128)(2,1)S(1)}) custom-call(bf16[224,768]{1,0:T(8,128)(2,1)S(1)} %get-tuple-element.143.a1_ref, bf16[384,1152]{1,0:T(8,128)(2,1)S(1)} %maximum_dynamic-update-slice_fusion.1.own_ref.own1_ref, ...), custom_call_target="tpu_custom_call" | custom-call | flops 1 | bytes 1 | tf_op jit(solution)/shard_map/attend1/pallas_call | solution.py:66
  45.8 3.9 %attend2.1 = (bf16[224,1152]{1,0:T(8,128)(2,1)S(1)}, bf16[6,224,224]{2,1,0:T(8,128)(2,1)S(1)}, bf16[768,196]{1,0:T(8,128)(2,1)S(1)}, f32[196,768]{1,0:T(8,128)S(1)}, bf16[196,768]{1,0:T(8,128)(2,1)S(1)}) custom-call(s32[1,2]{1,0:T(1,128)S(1)} %copy-done.5, bf16[224,768]{1,0:T(8,128)(2,1)S(1)} %get-tuple-element.143.a1_ref, ...), custom_call_target="tpu_custom_call" | custom-call | flops 1 | bytes 1 | tf_op jit(solution)/shard_map/attend2/pallas_call | solution.py:66
  51.5 1.4 %act.3 = (f32[196,1536]{1,0:T(8,128)S(1)}, f32[1,768]{1,0:T(1,128)}) custom-call(bf16[196,768]{1,0:T(8,128)(2,1)S(1)} %collective-permute-done.8.dm_ref.refs_1_, bf16[1536,768]{1,0:T(8,128)(2,1)S(1)} %copy-done), custom_call_target="tpu_custom_call" | custom-call | flops 1 | bytes 1 | tf_op jit(solution)/shard_map/act/pallas_call | solution.py:66
  53.2 2.0 %feed.2 = (bf16[196,1536]{1,0:T(8,128)(2,1)S(1)}, bf16[196,1536]{1,0:T(8,128)(2,1)S(1)}, f32[196,768]{1,0:T(8,128)S(1)}) custom-call(bf16[196,768]{1,0:T(8,128)(2,1)S(1)} %get-tuple-element.145.a2_ref.refs_4_, bf16[768,1536]{1,0:T(8,128)(2,1)S(1)} %copy-done.1, f32[1,1536]{1,0:T(1,128)S(1)} %get-tuple-element.139.upb_ref, ...), custom_call_target="tpu_custom_call" | custom-call | flops 1 | bytes 1 | tf_op jit(solution)/shard_map/feed/pallas_call | solution.py:66
  55.2 3.9 %collective-permute-done.17.a2_ref.refs_5_ = bf16[196,768]{1,0:T(8,128)(2,1)S(1)} collective-permute-done((bf16[196,768]{1,0:T(8,128)(2,1)S(1)}, bf16[196,768]{1,0:T(8,128)(2,1)S(1)}, u32[]{:S(2)}, u32[]{:S(2)}) %collective-permute-start.17) | collective-permute-done | bytes 301088 | tf_op jit(solution)/shard_map/ppermute | solution.py:103
  59.1 2.0 %feed.3 = (bf16[196,1536]{1,0:T(8,128)(2,1)S(1)}, bf16[196,1536]{1,0:T(8,128)(2,1)S(1)}, bf16[196,768]{1,0:T(8,128)(2,1)S(1)}) custom-call(bf16[196,768]{1,0:T(8,128)(2,1)S(1)} %collective-permute-done.17.a2_ref.refs_5_, bf16[768,1536]{1,0:T(8,128)(2,1)S(1)} %copy-done.1, f32[1,1536]{1,0:T(1,128)S(1)} %get-tuple-element.139.upb_ref, ...), custom_call_target="tpu_custom_call" | custom-call | flops 1 | bytes 1 | tf_op jit(solution)/shard_map/feed/pallas_call | solution.py:66
  62.0 6.1 %feedw.1 = (bf16[192,1536]{1,0:T(8,128)(2,1)S(1)}, bf16[192,1536]{1,0:T(8,128)(2,1)S(1)}, bf16[192,1536]{1,0:T(8,128)(2,1)S(1)}, bf16[192,1536]{1,0:T(8,128)(2,1...) custom-call(bf16[768,768]{1,0:T(8,128)(2,1)S(1)} %get-tuple-element., ...), custom_call_target="tpu_custom_call" | custom-call | flops 1 | bytes 1 | tf_op jit(solution)/shard_map/feedw/pallas_call | solution.py:66
  68.1 1.6 %collective-permute-done.18.got_ref = bf16[196,768]{1,0:T(8,128)(2,1)S(1)} collective-permute-done((bf16[196,768]{1,0:T(8,128)(2,1)S(1)}, bf16[196,768]{1,0:T(8,128)(2,1)S(1)}, u32[]{:S(2)}, u32[]{:S(2)}) %collective-permute-start.18) | collective-permute-done | bytes 301088 | tf_op jit(solution)/shard_map/ppermute | solution.py:103
  70.2 1.5 %collective-permute-done.20 = bf16[192,1536]{1,0:T(8,128)(2,1)S(1)} collective-permute-done((bf16[192,1536]{1,0:T(8,128)(2,1)S(1)}, bf16[192,1536]{1,0:T(8,128)(2,1)S(1)}, u32[]{:S(2)}, u32[]{:S(2)}) %collective-permute-start.20) | collective-permute-done | bytes 589856 | tf_op jit(solution)/shard_map/ppermute | solution.py:98
  73.0 1.5 %collective-permute-start.21 = (bf16[196,768]{1,0:T(8,128)(2,1)S(1)}, bf16[196,768]{1,0:T(8,128)(2,1)S(1)}, u32[]{:S(2)}, u32[]{:S(2)}) collective-permute-start(bf16[196,768]{1,0:T(8,128)(2,1)S(1)} %get-tuple-element.174), channel_id=1, source_target_pairs={{0,1},{1,0},{2,3},{3,2},{4,5},{5,4},{6,7},{7,6},{8,9},{9,8},{10,11... | collective-permute-start | bytes 903176 | tf_op jit(solution)/shard_map/ppermute | solution.py:103
  74.6 2.1 %backnorm.1 = (f32[196,768]{1,0:T(8,128)S(1)}, bf16[224,768]{1,0:T(8,128)(2,1)S(1)}, bf16[196,768]{1,0:T(8,128)(2,1)S(1)}, f32[3,768]{1,0:T(4,128)S(1)}) custom-call(s32[1,2]{1,0:T(1,128)S(1)} %copy-done.5, f32[196,768]{1,0:T(8,128)S(1)} %get-tuple-element.147.da2_ref, bf16[196,768]{1,0:T(8,128)(2,1)S(1)} %collective-permute-done.18.got_ref, ...), custom_call_target="tpu_custom_call" | custom-call | flops 1 | bytes 1 | tf_op jit(solution)/shard_map/backnorm/pallas_call | solution.py:66
  76.6 3.3 %back1.1 = (bf16[224,1152]{1,0:T(8,128)(2,1)S(1)}, bf16[192,1920]{1,0:T(8,128)(2,1)S(1)}, bf16[192,1920]{1,0:T(8,128)(2,1)S(1)}, bf16[192,1920]{1,0:T(8,128)(2,1...) custom-call(bf16[224,768]{1,0:T(8,128)(2,1)S(1)} %get-tuple-element.175.do_ref, ...), custom_call_target="tpu_custom_call" | custom-call | flops 1 | bytes 1 | tf_op jit(solution)/shard_map/back1/pallas_call | solution.py:66
  80.0 2.4 %collective-permute-done.21.mgot_ref = bf16[196,768]{1,0:T(8,128)(2,1)S(1)} collective-permute-done((bf16[196,768]{1,0:T(8,128)(2,1)S(1)}, bf16[196,768]{1,0:T(8,128)(2,1)S(1)}, u32[]{:S(2)}, u32[]{:S(2)}) %collective-permute-start.21) | collective-permute-done | bytes 301088 | tf_op jit(solution)/shard_map/ppermute | solution.py:103
  82.8 3.0 %back2.1 = (bf16[224,1152]{1,0:T(8,128)(2,1)S(1)}, bf16[192,1152]{1,0:T(8,128)(2,1)S(1)}, bf16[192,1152]{1,0:T(8,128)(2,1)S(1)}, bf16[192,1152]{1,0:T(8,128)(2,1...) custom-call(bf16[224,768]{1,0:T(8,128)(2,1)S(1)} %get-tuple-element.175.do_ref, ...), custom_call_target="tpu_custom_call" | custom-call | flops 1 | bytes 1 | tf_op jit(solution)/shard_map/back2/pallas_call | solution.py:66
  85.8 1.4 collective-permute-done.22
  88.8 1.7 %collective-permute-start.33 = (bf16[192,1920]{1,0:T(8,128)(2,1)S(1)}, bf16[192,1920]{1,0:T(8,128)(2,1)S(1)}, u32[]{:S(2)}, u32[]{:S(2)}) collective-permute-start(bf16[192,1920]{1,0:T(8,128)(2,1)S(1)} %add_convert_fusion), channel_id=1, source_target_pairs={{0,1},{1,0},{2,3},{3,2},{4,5},{5,4},{6,7},{7,6},{8,9},{9,8},{10,11... | collective-permute-start | bytes 2211848 | tf_op jit(solution)/shard_map/ppermute | solution.py:103
  90.5 4.5 %finish.1 = (bf16[196,768]{1,0:T(8,128)(2,1)}, bf16[196,768]{1,0:T(8,128)(2,1)}, f32[16,1152]{1,0:T(8,128)S(1)}) custom-call(s32[1,2]{1,0:T(1,128)S(1)} %copy-done.5, bf16[224,1152]{1,0:T(8,128)(2,1)S(1)} %get-tuple-element.173.dq1_ref, bf16[224,1152]{1,0:T(8,128)(2,1)S(1)} %get-tuple-element.178.dq2_ref, ...), custom_call_target="tpu_custom_call" | custom-call | flops 1 | bytes 1 | tf_op jit(solution)/shard_map/finish/pallas_call | solution.py:66
  95.1 1.5 %collective-permute-start.35 = (bf16[96,1536]{1,0:T(8,128)(2,1)S(1)}, bf16[96,1536]{1,0:T(8,128)(2,1)S(1)}, u32[]{:S(2)}, u32[]{:S(2)}) collective-permute-start(bf16[96,1536]{1,0:T(8,128)(2,1)S(1)} %pad_maximum_fusion.2), channel_id=1, source_target_pairs={{0,8},{2,10},{4,12},{6,14},{8,0},{10,2},{12,4},{14,6},{16,24},{18,... | collective-permute-start | bytes 884744 | tf_op jit(solution)/shard_map/ppermute | solution.py:90
  96.8 1.1 collective-permute-start.28
  98.0 6.2 %collective-permute-done.42 = bf16[192,1536]{1,0:T(8,128)(2,1)S(1)} collective-permute-done((bf16[192,1536]{1,0:T(8,128)(2,1)S(1)}, bf16[192,1536]{1,0:T(8,128)(2,1)S(1)}, u32[]{:S(2)}, u32[]{:S(2)}) %collective-permute-start.42) | collective-permute-done | bytes 589856 | tf_op jit(solution)/shard_map/ppermute | solution.py:94
  104.3 1.6 %collective-permute-start.43 = (bf16[96,1536]{1,0:T(8,128)(2,1)S(1)}, bf16[96,1536]{1,0:T(8,128)(2,1)S(1)}, u32[]{:S(2)}, u32[]{:S(2)}) collective-permute-start(bf16[96,1536]{1,0:T(8,128)(2,1)S(1)} %pad_maximum_fusion.3), channel_id=1, source_target_pairs={{0,8},{2,10},{4,12},{6,14},{8,0},{10,2},{12,4},{14,6},{16,24},{18,... | collective-permute-start | bytes 884744 | tf_op jit(solution)/shard_map/ppermute | solution.py:90
  106.0 1.8 %collective-permute-start.36 = (bf16[48,1536]{1,0:T(8,128)(2,1)S(1)}, bf16[48,1536]{1,0:T(8,128)(2,1)S(1)}, u32[]{:S(2)}, u32[]{:S(2)}) collective-permute-start(bf16[48,1536]{1,0:T(8,128)(2,1)S(1)} %add_convert_fusion.9), channel_id=1, source_target_pairs={{0,16},{2,18},{4,20},{6,22},{8,24},{10,26},{12,28},{14,30},{16,0},... | collective-permute-start | bytes 442376 | tf_op jit(solution)/shard_map/ppermute | solution.py:90
  107.8 7.0 %collective-permute-done.43 = bf16[96,1536]{1,0:T(8,128)(2,1)S(1)} collective-permute-done((bf16[96,1536]{1,0:T(8,128)(2,1)S(1)}, bf16[96,1536]{1,0:T(8,128)(2,1)S(1)}, u32[]{:S(2)}, u32[]{:S(2)}) %collective-permute-start.43) | collective-permute-done | bytes 294944 | tf_op jit(solution)/shard_map/ppermute | solution.py:90
  117.6 1.2 collective-permute-start.34
  118.8 4.3 %collective-permute-done.29 = bf16[112,1152]{1,0:T(8,128)(2,1)S(1)} collective-permute-done((bf16[112,1152]{1,0:T(8,128)(2,1)S(1)}, bf16[112,1152]{1,0:T(8,128)(2,1)S(1)}, u32[]{:S(2)}, u32[]{:S(2)}) %collective-permute-start.29) | collective-permute-done | bytes 258080 | tf_op jit(solution)/shard_map/ppermute | solution.py:103
  123.3 2.2 %collective-permute-start.32 = (bf16[40,1152]{1,0:T(8,128)(2,1)S(1)}, bf16[40,1152]{1,0:T(8,128)(2,1)S(1)}, u32[]{:S(2)}, u32[]{:S(2)}) collective-permute-start(bf16[40,1152]{1,0:T(8,128)(2,1)S(1)} %get-tuple-element.252), channel_id=1, source_target_pairs={{0,24},{2,26},{4,28},{6,30},{8,0},{10,2},{12,4},{14,6},{16,8},{18,... | collective-permute-start | bytes 276488 | tf_op jit(solution)/shard_map/ppermute | solution.py:85
  125.5 1.8 %collective-permute-start.31 = (bf16[40,1152]{1,0:T(8,128)(2,1)S(1)}, bf16[40,1152]{1,0:T(8,128)(2,1)S(1)}, u32[]{:S(2)}, u32[]{:S(2)}) collective-permute-start(bf16[40,1152]{1,0:T(8,128)(2,1)S(1)} %get-tuple-element.253), channel_id=1, source_target_pairs={{0,16},{2,18},{4,20},{6,22},{8,24},{10,26},{12,28},{14,30},{16,0},... | collective-permute-start | bytes 276488 | tf_op jit(solution)/shard_map/ppermute | solution.py:85
  128.4 1.6 %collective-permute-start.37 = (bf16[24,1920]{1,0:T(8,128)(2,1)S(1)}, bf16[24,1920]{1,0:T(8,128)(2,1)S(1)}, u32[]{:S(2)}, u32[]{:S(2)}) collective-permute-start(bf16[24,1920]{1,0:T(8,128)(2,1)S(1)} %get-tuple-element.215), channel_id=1, source_target_pairs={{0,8},{2,10},{4,12},{6,14},{8,16},{10,18},{12,20},{14,22},{16,24},... | collective-permute-start | bytes 276488 | tf_op jit(solution)/shard_map/ppermute | solution.py:85
  130.0 2.7 %collective-permute-start.38 = (bf16[24,1920]{1,0:T(8,128)(2,1)S(1)}, bf16[24,1920]{1,0:T(8,128)(2,1)S(1)}, u32[]{:S(2)}, u32[]{:S(2)}) collective-permute-start(bf16[24,1920]{1,0:T(8,128)(2,1)S(1)} %get-tuple-element.216), channel_id=1, source_target_pairs={{0,16},{2,18},{4,20},{6,22},{8,24},{10,26},{12,28},{14,30},{16,0},... | collective-permute-start | bytes 276488 | tf_op jit(solution)/shard_map/ppermute | solution.py:85
  132.8 5.6 %collective-permute-done.31.refs_2_ = bf16[40,1152]{1,0:T(8,128)(2,1)S(1)} collective-permute-done((bf16[40,1152]{1,0:T(8,128)(2,1)S(1)}, bf16[40,1152]{1,0:T(8,128)(2,1)S(1)}, u32[]{:S(2)}, u32[]{:S(2)}) %collective-permute-start.31) | collective-permute-done | bytes 92192 | tf_op jit(solution)/shard_map/ppermute | solution.py:85
  (121 shorter events, 21.7 us)
Async XLA Ops:
  2.5 12.0 %collective-permute-start.2 = (bf16[24,1920]{1,0:T(8,128)(2,1)S(1)}, bf16[24,1920]{1,0:T(8,128)(2,1)S(1)}, u32[]{:S(2)}, u32[]{:S(2)}) collective-permute-start(bf16[24,1920]{1,0:T(8,128)(2,1)S(1)} %get-tuple-element.129), channel_id=1, source_target_pairs={{0,8},{2,10},{4,12},{6,14},{8,16},{10,18},{12,20},{14,22},{16,24},... | collective-permute-start | bytes 276488 | tf_op jit(solution)/shard_map/ppermute | solution.py:85
  5.6 8.9 %collective-permute-start.1 = (bf16[24,1920]{1,0:T(8,128)(2,1)S(1)}, bf16[24,1920]{1,0:T(8,128)(2,1)S(1)}, u32[]{:S(2)}, u32[]{:S(2)}) collective-permute-start(bf16[24,1920]{1,0:T(8,128)(2,1)S(1)} %get-tuple-element.129), channel_id=1, source_target_pairs={{0,16},{2,18},{4,20},{6,22},{8,24},{10,26},{12,28},{14,30},{16,0},... | collective-permute-start | bytes 276488 | tf_op jit(solution)/shard_map/ppermute | solution.py:85
  8.2 6.4 %collective-permute-start = (bf16[24,1920]{1,0:T(8,128)(2,1)S(1)}, bf16[24,1920]{1,0:T(8,128)(2,1)S(1)}, u32[]{:S(2)}, u32[]{:S(2)}) collective-permute-start(bf16[24,1920]{1,0:T(8,128)(2,1)S(1)} %get-tuple-element.129), channel_id=1, source_target_pairs={{0,24},{2,26},{4,28},{6,30},{8,0},{10,2},{12,4},{14,6},{16,8},{18,... | collective-permute-start | bytes 276488 | tf_op jit(solution)/shard_map/ppermute | solution.py:85
  9.6 8.8 %collective-permute-start.8 = (bf16[196,768]{1,0:T(8,128)(2,1)S(1)}, bf16[196,768]{1,0:T(8,128)(2,1)S(1)}, u32[]{:S(2)}, u32[]{:S(2)}) collective-permute-start(bf16[196,768]{1,0:T(8,128)(2,1)S(1)} %get-tuple-element.132.dm_ref.refs_0_), channel_id=1, source_target_pairs={{0,1},{1,0},{2,3},{3,2},{4,5},{5,4},{6,7},{7,6},{8,9},{9,8},{10,11... | collective-permute-start | bytes 903176 | tf_op jit(solution)/shard_map/ppermute | solution.py:103
  14.6 13.4 %collective-permute-start.4 = (bf16[96,1920]{1,0:T(8,128)(2,1)S(1)}, bf16[96,1920]{1,0:T(8,128)(2,1)S(1)}, u32[]{:S(2)}, u32[]{:S(2)}) collective-permute-start(bf16[96,1920]{1,0:T(8,128)(2,1)S(1)} %pad_maximum_fusion.1), channel_id=1, source_target_pairs={{0,1},{1,0},{2,3},{3,2},{4,5},{5,4},{6,7},{7,6},{8,9},{9,8},{10,11... | collective-permute-start | bytes 1105928 | tf_op jit(solution)/shard_map/ppermute | solution.py:103
  16.2 12.9 %collective-permute-start.3 = (bf16[96,1920]{1,0:T(8,128)(2,1)S(1)}, bf16[96,1920]{1,0:T(8,128)(2,1)S(1)}, u32[]{:S(2)}, u32[]{:S(2)}) collective-permute-start(bf16[96,1920]{1,0:T(8,128)(2,1)S(1)} %pad_maximum_fusion.1), channel_id=1, source_target_pairs={{0,4},{2,6},{4,0},{6,2},{8,12},{10,14},{12,8},{14,10},{16,20},{18,... | collective-permute-start | bytes 1105928 | tf_op jit(solution)/shard_map/ppermute | solution.py:94
  18.4 6.4 %collective-permute-start.11 = (bf16[24,1152]{1,0:T(8,128)(2,1)S(1)}, bf16[24,1152]{1,0:T(8,128)(2,1)S(1)}, u32[]{:S(2)}, u32[]{:S(2)}) collective-permute-start(bf16[24,1152]{1,0:T(8,128)(2,1)S(1)} %get-tuple-element.134), channel_id=1, source_target_pairs={{0,8},{2,10},{4,12},{6,14},{8,16},{10,18},{12,20},{14,22},{16,24},... | collective-permute-start | bytes 165896 | tf_op jit(solution)/shard_map/ppermute | solution.py:85
  20.1 6.1 %collective-permute-start.10 = (bf16[24,1152]{1,0:T(8,128)(2,1)S(1)}, bf16[24,1152]{1,0:T(8,128)(2,1)S(1)}, u32[]{:S(2)}, u32[]{:S(2)}) collective-permute-start(bf16[24,1152]{1,0:T(8,128)(2,1)S(1)} %get-tuple-element.134), channel_id=1, source_target_pairs={{0,16},{2,18},{4,20},{6,22},{8,24},{10,26},{12,28},{14,30},{16,0},... | collective-permute-start | bytes 165896 | tf_op jit(solution)/shard_map/ppermute | solution.py:85
  21.8 4.6 %collective-permute-start.9 = (bf16[24,1152]{1,0:T(8,128)(2,1)S(1)}, bf16[24,1152]{1,0:T(8,128)(2,1)S(1)}, u32[]{:S(2)}, u32[]{:S(2)}) collective-permute-start(bf16[24,1152]{1,0:T(8,128)(2,1)S(1)} %get-tuple-element.134), channel_id=1, source_target_pairs={{0,24},{2,26},{4,28},{6,30},{8,0},{10,2},{12,4},{14,6},{16,8},{18,... | collective-permute-start | bytes 165896 | tf_op jit(solution)/shard_map/ppermute | solution.py:85
  26.4 8.0 %collective-permute-start.13 = (bf16[96,1152]{1,0:T(8,128)(2,1)S(1)}, bf16[96,1152]{1,0:T(8,128)(2,1)S(1)}, u32[]{:S(2)}, u32[]{:S(2)}) collective-permute-start(bf16[96,1152]{1,0:T(8,128)(2,1)S(1)} %pad_maximum_fusion.5), channel_id=1, source_target_pairs={{0,4},{2,6},{4,0},{6,2},{8,12},{10,14},{12,8},{14,10},{16,20},{18,... | collective-permute-start | bytes 663560 | tf_op jit(solution)/shard_map/ppermute | solution.py:94
  26.9 7.7 %collective-permute-start.12 = (bf16[96,1152]{1,0:T(8,128)(2,1)S(1)}, bf16[96,1152]{1,0:T(8,128)(2,1)S(1)}, u32[]{:S(2)}, u32[]{:S(2)}) collective-permute-start(bf16[96,1152]{1,0:T(8,128)(2,1)S(1)} %pad_maximum_fusion.5), channel_id=1, source_target_pairs={{0,1},{1,0},{2,3},{3,2},{4,5},{5,4},{6,7},{7,6},{8,9},{9,8},{10,11... | collective-permute-start | bytes 663560 | tf_op jit(solution)/shard_map/ppermute | solution.py:103
  28.1 9.1 %collective-permute-start.5 = (bf16[96,960]{1,0:T(8,128)(2,1)S(1)}, bf16[96,960]{1,0:T(8,128)(2,1)S(1)}, u32[]{:S(2)}, u32[]{:S(2)}) collective-permute-start(bf16[96,960]{1,0:T(8,128)(2,1)S(1)} %slice.366), channel_id=1, source_target_pairs={{0,4},{2,6},{4,0},{6,2},{8,12},{10,14},{12,8},{14,10},{16,20},{18,... | collective-permute-start | bytes 552968 | tf_op jit(solution)/shard_map/ppermute | solution.py:94
  29.2 8.0 %collective-permute-start.6 = (bf16[96,960]{1,0:T(8,128)(2,1)S(1)}, bf16[96,960]{1,0:T(8,128)(2,1)S(1)}, u32[]{:S(2)}, u32[]{:S(2)}) collective-permute-start(bf16[96,960]{1,0:T(8,128)(2,1)S(1)} %slice.367), channel_id=1, source_target_pairs={{0,1},{1,0},{2,3},{3,2},{4,5},{5,4},{6,7},{7,6},{8,9},{9,8},{10,11... | collective-permute-start | bytes 552968 | tf_op jit(solution)/shard_map/ppermute | solution.py:103
  34.8 4.9 %collective-permute-start.14 = (bf16[96,576]{1,0:T(8,128)(2,1)S(1)}, bf16[96,576]{1,0:T(8,128)(2,1)S(1)}, u32[]{:S(2)}, u32[]{:S(2)}) collective-permute-start(bf16[96,576]{1,0:T(8,128)(2,1)S(1)} %slice.286), channel_id=1, source_target_pairs={{0,4},{2,6},{4,0},{6,2},{8,12},{10,14},{12,8},{14,10},{16,20},{18,... | collective-permute-start | bytes 331784 | tf_op jit(solution)/shard_map/ppermute | solution.py:94
  36.3 4.9 %collective-permute-start.15 = (bf16[96,576]{1,0:T(8,128)(2,1)S(1)}, bf16[96,576]{1,0:T(8,128)(2,1)S(1)}, u32[]{:S(2)}, u32[]{:S(2)}) collective-permute-start(bf16[96,576]{1,0:T(8,128)(2,1)S(1)} %slice.287), channel_id=1, source_target_pairs={{0,1},{1,0},{2,3},{3,2},{4,5},{5,4},{6,7},{7,6},{8,9},{9,8},{10,11... | collective-permute-start | bytes 331784 | tf_op jit(solution)/shard_map/ppermute | solution.py:103
  37.3 8.4 %collective-permute-start.7 = (bf16[384,1920]{1,0:T(8,128)(2,1)S(1)}, bf16[384,1920]{1,0:T(8,128)(2,1)S(1)}, u32[]{:S(2)}, u32[]{:S(2)}) collective-permute-start(bf16[384,1920]{1,0:T(8,128)(2,1)S(1)} %maximum_dynamic-update-slice_fusion.own_ref.own2_ref), channel_id=1, source_target_pairs={{0,2},{2,0},{4,6},{6,4},{8,10},{10,8},{12,14},{14,12},{16,18},{18,... | collective-permute-start | bytes 4423688 | tf_op jit(solution)/shard_map/ppermute | solution.py:98
  37.5 8.3 %copy-start.2 = (bf16[196,768]{1,0:T(8,128)(2,1)S(1)}, bf16[196,768]{1,0:T(8,128)(2,1)}, u32[]{:S(2)}) copy-start(bf16[196,768]{1,0:T(8,128)(2,1)} %x_ref.3) | copy-start | bytes 903172
  37.5 8.3 %copy-start.5 = (s32[1,2]{1,0:T(1,128)S(1)}, s32[1,2]{1,0:T(1,128)}, u32[]{:S(2)}) copy-start(s32[1,2]{1,0:T(1,128)} %keep_ref.7) | copy-start | bytes 28
  41.3 2.5 %collective-permute-start.16 = (bf16[384,1152]{1,0:T(8,128)(2,1)S(1)}, bf16[384,1152]{1,0:T(8,128)(2,1)S(1)}, u32[]{:S(2)}, u32[]{:S(2)}) collective-permute-start(bf16[384,1152]{1,0:T(8,128)(2,1)S(1)} %maximum_dynamic-update-slice_fusion.1.own_ref.own1_ref), channel_id=1, source_target_pairs={{0,2},{2,0},{4,6},{6,4},{8,10},{10,8},{12,14},{14,12},{16,18},{18,... | collective-permute-start | bytes 2654216 | tf_op jit(solution)/shard_map/ppermute | solution.py:98
  49.7 9.4 %collective-permute-start.17 = (bf16[196,768]{1,0:T(8,128)(2,1)S(1)}, bf16[196,768]{1,0:T(8,128)(2,1)S(1)}, u32[]{:S(2)}, u32[]{:S(2)}) collective-permute-start(bf16[196,768]{1,0:T(8,128)(2,1)S(1)} %get-tuple-element.145.a2_ref.refs_4_), channel_id=1, source_target_pairs={{0,1},{1,0},{2,3},{3,2},{4,5},{5,4},{6,7},{7,6},{8,9},{9,8},{10,11... | collective-permute-start | bytes 903176 | tf_op jit(solution)/shard_map/ppermute | solution.py:103
  61.1 8.6 %collective-permute-start.18 = (bf16[196,768]{1,0:T(8,128)(2,1)S(1)}, bf16[196,768]{1,0:T(8,128)(2,1)S(1)}, u32[]{:S(2)}, u32[]{:S(2)}) collective-permute-start(bf16[196,768]{1,0:T(8,128)(2,1)S(1)} %get-tuple-element.151), channel_id=1, source_target_pairs={{0,1},{1,0},{2,3},{3,2},{4,5},{5,4},{6,7},{7,6},{8,9},{9,8},{10,11... | collective-permute-start | bytes 903176 | tf_op jit(solution)/shard_map/ppermute | solution.py:103
  68.1 6.5 %copy-start.3 = (bf16[196,768]{1,0:T(8,128)(2,1)S(1)}, bf16[196,768]{1,0:T(8,128)(2,1)}, u32[]{:S(2)}) copy-start(bf16[196,768]{1,0:T(8,128)(2,1)} %g_ref.1) | copy-start | bytes 903172
  69.7 2.0 %collective-permute-start.20 = (bf16[192,1536]{1,0:T(8,128)(2,1)S(1)}, bf16[192,1536]{1,0:T(8,128)(2,1)S(1)}, u32[]{:S(2)}, u32[]{:S(2)}) collective-permute-start(bf16[192,1536]{1,0:T(8,128)(2,1)S(1)} %get-tuple-element.167), channel_id=1, source_target_pairs={{0,2},{2,0},{4,6},{6,4},{8,10},{10,8},{12,14},{14,12},{16,18},{18,... | collective-permute-start | bytes 1769480 | tf_op jit(solution)/shard_map/ppermute | solution.py:98
  69.7 2.8 %collective-permute-start.19 = (bf16[192,1536]{1,0:T(8,128)(2,1)S(1)}, bf16[192,1536]{1,0:T(8,128)(2,1)S(1)}, u32[]{:S(2)}, u32[]{:S(2)}) collective-permute-start(bf16[192,1536]{1,0:T(8,128)(2,1)S(1)} %get-tuple-element.166), channel_id=1, source_target_pairs={{0,2},{2,0},{4,6},{6,4},{8,10},{10,8},{12,14},{14,12},{16,18},{18,... | collective-permute-start | bytes 1769480 | tf_op jit(solution)/shard_map/ppermute | solution.py:98
  71.8 15.4 %collective-permute-start.22 = (bf16[192,1536]{1,0:T(8,128)(2,1)S(1)}, bf16[192,1536]{1,0:T(8,128)(2,1)S(1)}, u32[]{:S(2)}, u32[]{:S(2)}) collective-permute-start(bf16[192,1536]{1,0:T(8,128)(2,1)S(1)} %add_convert_fusion.2), channel_id=1, source_target_pairs={{0,4},{2,6},{4,0},{6,2},{8,12},{10,14},{12,8},{14,10},{16,20},{18,... | collective-permute-start | bytes 1769480 | tf_op jit(solution)/shard_map/ppermute | solution.py:94
  72.5 14.7 %collective-permute-start.40 = (bf16[192,1536]{1,0:T(8,128)(2,1)S(1)}, bf16[192,1536]{1,0:T(8,128)(2,1)S(1)}, u32[]{:S(2)}, u32[]{:S(2)}) collective-permute-start(bf16[192,1536]{1,0:T(8,128)(2,1)S(1)} %get-tuple-element.230), channel_id=1, source_target_pairs={{0,2},{2,0},{4,6},{6,4},{8,10},{10,8},{12,14},{14,12},{16,18},{18,... | collective-permute-start | bytes 1769480 | tf_op jit(solution)/shard_map/ppermute | solution.py:98
  72.6 14.6 %collective-permute-start.41 = (bf16[192,1536]{1,0:T(8,128)(2,1)S(1)}, bf16[192,1536]{1,0:T(8,128)(2,1)S(1)}, u32[]{:S(2)}, u32[]{:S(2)}) collective-permute-start(bf16[192,1536]{1,0:T(8,128)(2,1)S(1)} %get-tuple-element.231), channel_id=1, source_target_pairs={{0,2},{2,0},{4,6},{6,4},{8,10},{10,8},{12,14},{14,12},{16,18},{18,... | collective-permute-start | bytes 1769480 | tf_op jit(solution)/shard_map/ppermute | solution.py:98
  73.0 9.3 %collective-permute-start.21 = (bf16[196,768]{1,0:T(8,128)(2,1)S(1)}, bf16[196,768]{1,0:T(8,128)(2,1)S(1)}, u32[]{:S(2)}, u32[]{:S(2)}) collective-permute-start(bf16[196,768]{1,0:T(8,128)(2,1)S(1)} %get-tuple-element.174), channel_id=1, source_target_pairs={{0,1},{1,0},{2,3},{3,2},{4,5},{5,4},{6,7},{7,6},{8,9},{9,8},{10,11... | collective-permute-start | bytes 903176 | tf_op jit(solution)/shard_map/ppermute | solution.py:103
  82.3 14.4 %collective-permute-start.26 = (bf16[192,1920]{1,0:T(8,128)(2,1)S(1)}, bf16[192,1920]{1,0:T(8,128)(2,1)S(1)}, u32[]{:S(2)}, u32[]{:S(2)}) collective-permute-start(bf16[192,1920]{1,0:T(8,128)(2,1)S(1)} %get-tuple-element.197), channel_id=1, source_target_pairs={{0,2},{2,0},{4,6},{6,4},{8,10},{10,8},{12,14},{14,12},{16,18},{18,... | collective-permute-start | bytes 2211848 | tf_op jit(solution)/shard_map/ppermute | solution.py:98
  82.3 6.3 %collective-permute-start.27 = (bf16[192,1920]{1,0:T(8,128)(2,1)S(1)}, bf16[192,1920]{1,0:T(8,128)(2,1)S(1)}, u32[]{:S(2)}, u32[]{:S(2)}) collective-permute-start(bf16[192,1920]{1,0:T(8,128)(2,1)S(1)} %get-tuple-element.198), channel_id=1, source_target_pairs={{0,2},{2,0},{4,6},{6,4},{8,10},{10,8},{12,14},{14,12},{16,18},{18,... | collective-permute-start | bytes 2211848 | tf_op jit(solution)/shard_map/ppermute | solution.py:98
  87.2 3.3 %collective-permute-start.23 = (bf16[192,1152]{1,0:T(8,128)(2,1)S(1)}, bf16[192,1152]{1,0:T(8,128)(2,1)S(1)}, u32[]{:S(2)}, u32[]{:S(2)}) collective-permute-start(bf16[192,1152]{1,0:T(8,128)(2,1)S(1)} %get-tuple-element.183), channel_id=1, source_target_pairs={{0,2},{2,0},{4,6},{6,4},{8,10},{10,8},{12,14},{14,12},{16,18},{18,... | collective-permute-start | bytes 1327112 | tf_op jit(solution)/shard_map/ppermute | solution.py:98
  87.3 3.3 %collective-permute-start.24 = (bf16[192,1152]{1,0:T(8,128)(2,1)S(1)}, bf16[192,1152]{1,0:T(8,128)(2,1)S(1)}, u32[]{:S(2)}, u32[]{:S(2)}) collective-permute-start(bf16[192,1152]{1,0:T(8,128)(2,1)S(1)} %get-tuple-element.184), channel_id=1, source_target_pairs={{0,2},{2,0},{4,6},{6,4},{8,10},{10,8},{12,14},{14,12},{16,18},{18,... | collective-permute-start | bytes 1327112 | tf_op jit(solution)/shard_map/ppermute | solution.py:98
  87.9 16.2 %collective-permute-start.42 = (bf16[192,1536]{1,0:T(8,128)(2,1)S(1)}, bf16[192,1536]{1,0:T(8,128)(2,1)S(1)}, u32[]{:S(2)}, u32[]{:S(2)}) collective-permute-start(bf16[192,1536]{1,0:T(8,128)(2,1)S(1)} %add_convert_fusion.1), channel_id=1, source_target_pairs={{0,4},{2,6},{4,0},{6,2},{8,12},{10,14},{12,8},{14,10},{16,20},{18,... | collective-permute-start | bytes 1769480 | tf_op jit(solution)/shard_map/ppermute | solution.py:94
  88.8 27.8 %collective-permute-start.33 = (bf16[192,1920]{1,0:T(8,128)(2,1)S(1)}, bf16[192,1920]{1,0:T(8,128)(2,1)S(1)}, u32[]{:S(2)}, u32[]{:S(2)}) collective-permute-start(bf16[192,1920]{1,0:T(8,128)(2,1)S(1)} %add_convert_fusion), channel_id=1, source_target_pairs={{0,1},{1,0},{2,3},{3,2},{4,5},{5,4},{6,7},{7,6},{8,9},{9,8},{10,11... | collective-permute-start | bytes 2211848 | tf_op jit(solution)/shard_map/ppermute | solution.py:103
  95.1 1.6 %collective-permute-start.25 = (f32[16,1152]{1,0:T(8,128)S(1)}, f32[16,1152]{1,0:T(8,128)S(1)}, u32[]{:S(2)}, u32[]{:S(2)}) collective-permute-start(f32[16,1152]{1,0:T(8,128)S(1)} %get-tuple-element.196), channel_id=1, source_target_pairs={{0,2},{2,0},{4,6},{6,4},{8,10},{10,8},{12,14},{14,12},{16,18},{18,... | collective-permute-start | bytes 221192 | tf_op jit(solution)/shard_map/ppermute | solution.py:98
  95.1 10.8 %collective-permute-start.35 = (bf16[96,1536]{1,0:T(8,128)(2,1)S(1)}, bf16[96,1536]{1,0:T(8,128)(2,1)S(1)}, u32[]{:S(2)}, u32[]{:S(2)}) collective-permute-start(bf16[96,1536]{1,0:T(8,128)(2,1)S(1)} %pad_maximum_fusion.2), channel_id=1, source_target_pairs={{0,8},{2,10},{4,12},{6,14},{8,0},{10,2},{12,4},{14,6},{16,24},{18,... | collective-permute-start | bytes 884744 | tf_op jit(solution)/shard_map/ppermute | solution.py:90
  96.8 19.8 %collective-permute-start.28 = (bf16[208,1152]{1,0:T(8,128)(2,1)S(1)}, bf16[208,1152]{1,0:T(8,128)(2,1)S(1)}, u32[]{:S(2)}, u32[]{:S(2)}) collective-permute-start(bf16[208,1152]{1,0:T(8,128)(2,1)S(1)} %pad_maximum_fusion), channel_id=1, source_target_pairs={{0,4},{2,6},{4,0},{6,2},{8,12},{10,14},{12,8},{14,10},{16,20},{18,... | collective-permute-start | bytes 1437704 | tf_op jit(solution)/shard_map/ppermute | solution.py:94
  104.3 10.5 %collective-permute-start.43 = (bf16[96,1536]{1,0:T(8,128)(2,1)S(1)}, bf16[96,1536]{1,0:T(8,128)(2,1)S(1)}, u32[]{:S(2)}, u32[]{:S(2)}) collective-permute-start(bf16[96,1536]{1,0:T(8,128)(2,1)S(1)} %pad_maximum_fusion.3), channel_id=1, source_target_pairs={{0,8},{2,10},{4,12},{6,14},{8,0},{10,2},{12,4},{14,6},{16,24},{18,... | collective-permute-start | bytes 884744 | tf_op jit(solution)/shard_map/ppermute | solution.py:90
  106.0 9.8 %collective-permute-start.36 = (bf16[48,1536]{1,0:T(8,128)(2,1)S(1)}, bf16[48,1536]{1,0:T(8,128)(2,1)S(1)}, u32[]{:S(2)}, u32[]{:S(2)}) collective-permute-start(bf16[48,1536]{1,0:T(8,128)(2,1)S(1)} %add_convert_fusion.9), channel_id=1, source_target_pairs={{0,16},{2,18},{4,20},{6,22},{8,24},{10,26},{12,28},{14,30},{16,0},... | collective-permute-start | bytes 442376 | tf_op jit(solution)/shard_map/ppermute | solution.py:90
  114.9 8.3 %collective-permute-start.44 = (bf16[48,1536]{1,0:T(8,128)(2,1)S(1)}, bf16[48,1536]{1,0:T(8,128)(2,1)S(1)}, u32[]{:S(2)}, u32[]{:S(2)}) collective-permute-start(bf16[48,1536]{1,0:T(8,128)(2,1)S(1)} %add_convert_fusion.6), channel_id=1, source_target_pairs={{0,16},{2,18},{4,20},{6,22},{8,24},{10,26},{12,28},{14,30},{16,0},... | collective-permute-start | bytes 442376 | tf_op jit(solution)/shard_map/ppermute | solution.py:90
  116.7 6.4 %collective-permute-start.29 = (bf16[112,1152]{1,0:T(8,128)(2,1)S(1)}, bf16[112,1152]{1,0:T(8,128)(2,1)S(1)}, u32[]{:S(2)}, u32[]{:S(2)}) collective-permute-start(bf16[112,1152]{1,0:T(8,128)(2,1)S(1)} %pad_maximum_fusion.4), channel_id=1, source_target_pairs={{0,1},{1,0},{2,3},{3,2},{4,5},{5,4},{6,7},{7,6},{8,9},{9,8},{10,11... | collective-permute-start | bytes 774152 | tf_op jit(solution)/shard_map/ppermute | solution.py:103
  117.6 10.6 %collective-permute-start.34 = (bf16[96,1920]{1,0:T(8,128)(2,1)S(1)}, bf16[96,1920]{1,0:T(8,128)(2,1)S(1)}, u32[]{:S(2)}, u32[]{:S(2)}) collective-permute-start(bf16[96,1920]{1,0:T(8,128)(2,1)S(1)} %add_convert_fusion.4), channel_id=1, source_target_pairs={{0,4},{2,6},{4,0},{6,2},{8,12},{10,14},{12,8},{14,10},{16,20},{18,... | collective-permute-start | bytes 1105928 | tf_op jit(solution)/shard_map/ppermute | solution.py:94
  123.3 9.4 %collective-permute-start.32 = (bf16[40,1152]{1,0:T(8,128)(2,1)S(1)}, bf16[40,1152]{1,0:T(8,128)(2,1)S(1)}, u32[]{:S(2)}, u32[]{:S(2)}) collective-permute-start(bf16[40,1152]{1,0:T(8,128)(2,1)S(1)} %get-tuple-element.252), channel_id=1, source_target_pairs={{0,24},{2,26},{4,28},{6,30},{8,0},{10,2},{12,4},{14,6},{16,8},{18,... | collective-permute-start | bytes 276488 | tf_op jit(solution)/shard_map/ppermute | solution.py:85
  125.5 12.9 %collective-permute-start.31 = (bf16[40,1152]{1,0:T(8,128)(2,1)S(1)}, bf16[40,1152]{1,0:T(8,128)(2,1)S(1)}, u32[]{:S(2)}, u32[]{:S(2)}) collective-permute-start(bf16[40,1152]{1,0:T(8,128)(2,1)S(1)} %get-tuple-element.253), channel_id=1, source_target_pairs={{0,16},{2,18},{4,20},{6,22},{8,24},{10,26},{12,28},{14,30},{16,0},... | collective-permute-start | bytes 276488 | tf_op jit(solution)/shard_map/ppermute | solution.py:85
  127.3 11.1 %collective-permute-start.30 = (bf16[40,1152]{1,0:T(8,128)(2,1)S(1)}, bf16[40,1152]{1,0:T(8,128)(2,1)S(1)}, u32[]{:S(2)}, u32[]{:S(2)}) collective-permute-start(bf16[40,1152]{1,0:T(8,128)(2,1)S(1)} %get-tuple-element.254), channel_id=1, source_target_pairs={{0,8},{2,10},{4,12},{6,14},{8,16},{10,18},{12,20},{14,22},{16,24},... | collective-permute-start | bytes 276488 | tf_op jit(solution)/shard_map/ppermute | solution.py:85
  128.4 11.0 %collective-permute-start.37 = (bf16[24,1920]{1,0:T(8,128)(2,1)S(1)}, bf16[24,1920]{1,0:T(8,128)(2,1)S(1)}, u32[]{:S(2)}, u32[]{:S(2)}) collective-permute-start(bf16[24,1920]{1,0:T(8,128)(2,1)S(1)} %get-tuple-element.215), channel_id=1, source_target_pairs={{0,8},{2,10},{4,12},{6,14},{8,16},{10,18},{12,20},{14,22},{16,24},... | collective-permute-start | bytes 276488 | tf_op jit(solution)/shard_map/ppermute | solution.py:85
  130.0 10.3 %collective-permute-start.38 = (bf16[24,1920]{1,0:T(8,128)(2,1)S(1)}, bf16[24,1920]{1,0:T(8,128)(2,1)S(1)}, u32[]{:S(2)}, u32[]{:S(2)}) collective-permute-start(bf16[24,1920]{1,0:T(8,128)(2,1)S(1)} %get-tuple-element.216), channel_id=1, source_target_pairs={{0,16},{2,18},{4,20},{6,22},{8,24},{10,26},{12,28},{14,30},{16,0},... | collective-permute-start | bytes 276488 | tf_op jit(solution)/shard_map/ppermute | solution.py:85
  132.7 7.6 %collective-permute-start.39 = (bf16[24,1920]{1,0:T(8,128)(2,1)S(1)}, bf16[24,1920]{1,0:T(8,128)(2,1)S(1)}, u32[]{:S(2)}, u32[]{:S(2)}) collective-permute-start(bf16[24,1920]{1,0:T(8,128)(2,1)S(1)} %get-tuple-element.217), channel_id=1, source_target_pairs={{0,24},{2,26},{4,28},{6,30},{8,0},{10,2},{12,4},{14,6},{16,8},{18,... | collective-permute-start | bytes 276488 | tf_op jit(solution)/shard_map/ppermute | solution.py:85
  (4 other events, 7.8 us)

commit v7 on v6

--- a/solution.py
+++ b/solution.py
@@ -32,7 +32,7 @@
 TREE = (True, True)
 FRONT = ('dm', 'z1', 'prep', 'act1', 'z2', 'n1', 'n2', 'act0', 'f2', 'f1', 'c1', 'attend1', 'c2')
 ORDER = ('dc', 'dy', 'm', 'norm', 'back2', 'bc', 'back1', 'finish', 'ac', 'sc', 'by', 'bx', 'ax', 'd0', 'd1', 'bz', 'uc', 'uy', 'ay', 'u0', 'u1', 'az')
-GATES = {'n1:s': ['prep', 'dm'], 'n2:s': ['z2'], 'f1:s': ['n1'], 'act1:s': ['dm'], 'attend1:s': ['dm', 'f1'], 'z1:s': ['dm'], 'back1:s': ['dc'], 'back2:s': ['m', 'dc'], 'finish:s': ['bc'], 'ay:r': ['ac', 'back1', 'd1'], 'uc:s': ['dc'], 'bc:s': ['dy'], 'bx:r': ['dy'], 'bz:r': ['bc'], 'd0:s': ['finish'], 'd1:r': ['dy'], 'az:r': ['bz'], 'u1:r': ['by', 'bx'], 'uc:r': ['back2'], 'sc:r': ['ac'], 'ax:r': ['sc'], 'az:s': ['ay']}
+GATES = {'n1:s': ['prep', 'dm'], 'n2:s': ['z2'], 'f1:s': ['n1'], 'act1:s': ['dm'], 'attend1:s': ['dm', 'f1'], 'z1:s': ['dm'], 'back1:s': ['dc'], 'back2:s': ['m', 'dc'], 'finish:s': ['bc', 'm'], 'ay:r': ['ac', 'back1', 'd1'], 'uc:s': ['dc'], 'bc:s': ['dy'], 'bx:r': ['dy'], 'bz:r': ['bc'], 'd0:s': ['finish'], 'd1:r': ['dy'], 'az:r': ['bz'], 'u1:r': ['by', 'bx'], 'uc:r': ['back2'], 'sc:r': ['ac'], 'ax:r': ['sc'], 'az:s': ['ay']}
 ROUTE = {"y": "b", "x": "b", "z": "b"}
 CHEAP = pl.CostEstimate(flops=1, bytes_accessed=1, transcendentals=0)
 SMALL = {"gain1": 0, "shift1": 6, "qbias": 12, "vbias": 18, "projb": 24, "gain2": 30, "shift2": 36, "downb": 42}
@@ -631,9 +631,9 @@
 
 
 def finish_kernel(
-    wide, keep_ref, dq1_ref, dq2_ref, own1_ref, other1_ref, own2_ref, other2_ref, att_ref, x_ref, dmid_ref,
-    params_ref, mid_ref, m_ref, mgot_ref, downb_ref, upb_ref, sums0_ref, sums1_ref, sums2_ref, tab1_ref, tab2_ref,
-    dx_ref, result_ref, small_ref,
+    wide, dq1_ref, dq2_ref, own1_ref, other1_ref, own2_ref, other2_ref, att_ref, x_ref,
+    downb_ref, upb_ref, sums0_ref, sums1_ref, sums2_ref, tab1_ref, tab2_ref,
+    da1_ref, small_ref,
 ):
     spread = spread_rows()
     dq1, dq2 = dot_tn(spread, dq1_ref[...]).astype(BF16), dot_tn(spread, dq2_ref[...]).astype(BF16)
@@ -644,12 +644,8 @@
     high = moved.astype(BF16)
     low = (moved - high.astype(F32)).astype(BF16)
     da1 = dot_nn(high, att_ref[...]) + dot_nn(low, att_ref[...])
-    unit, factor = norm_parts(x_ref[...].astype(F32))
-    dx_ref[...] = (dmid_ref[...] + norm_back(da1, unit, factor, params_ref[0:1])).astype(BF16)
-    rate = rate_of(keep_ref, 1)
-    total = m_ref[...] + mgot_ref[...].astype(F32) + params_ref[5:6]
-    result_ref[...] = (mid_ref[...] + rate * total).astype(BF16)
-
+    da1_ref[...] = da1
+    unit, _ = norm_parts(x_ref[...].astype(F32))
     small_ref[...] = jnp.zeros(small_ref.shape, F32)
 
     def put(name, value):
@@ -692,18 +688,21 @@
     return kernel_call(
         "finish",
         partial(finish_kernel, wide),
-        21,
-        [shape_of((AREA, D), BF16), shape_of((AREA, D), BF16), shape_of((rows, TIER), F32)],
-        smem=1, out_far=(0, 1),
+        15,
+        [shape_of((AREA, D), F32), shape_of((rows, TIER), F32)],
     )(*args)
 
 
 def outputs_kernel(
-    n_parts, rows, *refs
+    n_parts, rows, keep_ref, da1_ref, x_ref, dmid_ref, params_ref, mid_ref, m_ref, mgot_ref, *refs
 ):
     parts, refs = refs[:n_parts], refs[n_parts:]
-    gain1_ref, shift1_ref, qv_ref, relh_ref, relw_ref, projb_ref, gain2_ref, shift2_ref, upb_ref, downb_ref = refs[:10]
-    table_ref, up_ref = refs[10:]
+    *refs, dx_ref, result_ref, table_ref, up_ref = refs
+    unit, factor = norm_parts(x_ref[...].astype(F32))
+    dx_ref[...] = (dmid_ref[...] + norm_back(da1_ref[...], unit, factor, params_ref[0:1])).astype(BF16)
+    feed_sum = m_ref[...] + mgot_ref[...].astype(F32) + params_ref[5:6]
+    result_ref[...] = (mid_ref[...] + rate_of(keep_ref, 1) * feed_sum).astype(BF16)
+    gain1_ref, shift1_ref, qv_ref, relh_ref, relw_ref, projb_ref, gain2_ref, shift2_ref, upb_ref, downb_ref = refs
     total = parts[0][...]
     for part in parts[1:]:
         total = total + part[part.shape[0] - rows :].astype(F32)
@@ -736,17 +735,19 @@
     upb_ref[...] = up_ref[place, : upb_ref.shape[0]]
 
 
-def outputs(parts, size, ups):
+def outputs(parts, size, ups, *rows):
     row = shape_of((D,), F32)
     table = shape_of((TABLE, HEAD), F32)
     return kernel_call(
         "outputs",
         partial(outputs_kernel, len(parts), parts[0].shape[0]),
-        len(parts),
-        [row, row, shape_of((2, D), F32), table, table, row, row, row, shape_of((size,), F32), row],
+        8 + len(parts),
+        [row, row, shape_of((2, D), F32), table, table, row, row, row, shape_of((size,), F32), row]
+        + [shape_of((AREA, D), BF16)] * 2,
+        smem=1,
         scratch=[pltpu.VMEM((HEAD // 2, LANES), F32), pltpu.VMEM((ups, LANES), F32)],
-        out_far=range(10),
-    )(*parts)
+        out_far=range(12),
+    )(*rows, *parts)
 
 
 def per_device(
@@ -866,7 +867,7 @@
         return got
 
     def small_cores():
-        flat = gated(made["finish"][2], "sc", "s")
+        flat = gated(made["finish"][1], "sc", "s")
         got = gated(move_c(flat), "sc", "r")
         chains["s"] = flat + got
         return got
@@ -885,11 +886,10 @@
             return moved[0] if wide == 2 else add_up(*moved)
         if name == "finish":
             first, second = made["back1"], made["back2"]
-            mid = gated(middle, "finish", "s")
+            row_map = gated(att_map, "finish", "s")
             return finish(
-                wide, small_rows, keep_mask, first[0], second[0], own1, other1, own2, other2, att_map, tokens,
-                made["norm"][0], params, mid, outs[0], made["m"], downb, upb_sum, made["norm"][3], first[3], second[3],
-                first[4], second[4],
+                wide, small_rows, first[0], second[0], own1, other1, own2, other2, row_map, tokens,
+                downb, upb_sum, made["norm"][3], first[3], second[3], first[4], second[4],
             )
         chain, axis = name
         if chain == "s":
@@ -907,7 +907,6 @@
         made[name] = task(name)
         while name[-1] == "1" and name[0] in "du" and chains[name[0]][1][:1].isdigit():
             along(name[0], chains[name[0]][1][0])
-    grad_in, result, _ = made["finish"]
     small = chains["s"]
     down_grad, up_grad, rows1, rows2 = (add_up(*chains[name][0]) for name in "duab")
     proj_grad = rows1[:, TIER:]
@@ -919,8 +918,9 @@
     ]
     qkv_grad = jnp.concatenate(pieces, axis=1)
 
-    gain1, shift1, qv_grad, relh_grad, relw_grad, projb, gain2, shift2, up_bias_grad, downb = outputs(
-        small, hidden // lax.axis_size("dp"), wide * lax.axis_size("dp")
+    gain1, shift1, qv_grad, relh_grad, relw_grad, projb, gain2, shift2, up_bias_grad, downb, grad_in, result = outputs(
+        small, hidden // lax.axis_size("dp"), wide * lax.axis_size("dp"),
+        keep_mask, made["finish"][0], tokens, made["norm"][0], params, middle, outs[0], made["m"],
     )
     return (
         result, grad_in, gain1, shift1, qkv_grad, qv_grad, relh_grad, relw_grad, proj_grad, projb, gain2, shift2,

time: 142 us -> 144 us (1.014)
  waiting for transfers between devices: 49.2 us -> 51.4 us
    ppermute x8, waiting for transfers between devices: 13.2 us -> 14.7 us  [move_y(): return lax.ppermute(value, 'dp', dp_pairs(lax.axis_size('dp'), dy=1))]
  transfers between devices with their start and end apart: 45 -> 45, of which waited for: 21 -> 20; matrix products, arithmetic and copies ran while one was open for 3% -> 3% of each run, Pallas kernels for 21% -> 20%
where the time goes in v7:
time: 144 us
  waiting for transfers between devices  51.4 us (36%)
  starting transfers between devices  48.5 us (34%)
  Pallas kernels  36.2 us (25%)
  other arithmetic  3.64 us (3%)
  local copies, waits for them, and re-layouts  2.73 us (2%)
    pallas_call x14, Pallas kernels, run(): call(*args[:smem], *map(pltpu.with_memory_space_constraint, args[smem:],...  36.2 us
    ppermute x12, starting transfers between devices, move_z(): return lax.ppermute(value, 'dp', dp_pairs(lax.axis_size('dp'), dz=step))  19.9 us
    ppermute x10, waiting for transfers between devices, move_x(): lax.ppermute(value, 'mp', [(i, (i + step) % count) for i in range(count)])  15.2 us
    ppermute x8, waiting for transfers between devices, move_y(): return lax.ppermute(value, 'dp', dp_pairs(lax.axis_size('dp'), dy=1))  14.7 us
    ppermute x10, starting transfers between devices, move_x(): lax.ppermute(value, 'mp', [(i, (i + step) % count) for i in range(count)])  12.6 us
    ppermute x12, waiting for transfers between devices, move_z(): return lax.ppermute(value, 'dp', dp_pairs(lax.axis_size('dp'), dz=step))  10.6 us
    ppermute x8, starting transfers between devices, move_y(): return lax.ppermute(value, 'dp', dp_pairs(lax.axis_size('dp'), dy=1))  7.68 us
    ppermute x4, waiting for transfers between devices, swap_z(): return lax.ppermute(value, 'dp', pairs)  6.87 us
  transfers between devices with their start and end apart: 45, of which 20 were waited for; matrix products, arithmetic and copies ran while one was open for 3% of the time, Pallas kernels for 20%

profile of v7, /device:TPU:0, one launch (start us, length us, event | category | flops | bytes accessed | tf_op | source)
XLA Modules:
  0.0 143.6 jit_solution(9322442517871714663)
XLA Ops:
  1.3 1.2 pack.1
  2.6 3.1 %collective-permute-start.2 = (bf16[24,1920]{1,0:T(8,128)(2,1)S(1)}, bf16[24,1920]{1,0:T(8,128)(2,1)S(1)}, u32[]{:S(2)}, u32[]{:S(2)}) collective-permute-start(bf16[24,1920]{1,0:T(8,128)(2,1)S(1)} %get-tuple-element.130), channel_id=1, source_target_pairs={{0,8},{2,10},{4,12},{6,14},{8,16},{10,18},{12,20},{14,22},{16,24},... | collective-permute-start | bytes 276488 | tf_op jit(solution)/shard_map/ppermute | solution.py:85
  5.6 2.6 %collective-permute-start.1 = (bf16[24,1920]{1,0:T(8,128)(2,1)S(1)}, bf16[24,1920]{1,0:T(8,128)(2,1)S(1)}, u32[]{:S(2)}, u32[]{:S(2)}) collective-permute-start(bf16[24,1920]{1,0:T(8,128)(2,1)S(1)} %get-tuple-element.130), channel_id=1, source_target_pairs={{0,16},{2,18},{4,20},{6,22},{8,24},{10,26},{12,28},{14,30},{16,0},... | collective-permute-start | bytes 276488 | tf_op jit(solution)/shard_map/ppermute | solution.py:85
  8.2 1.3 collective-permute-start
  9.6 1.5 %collective-permute-start.8 = (bf16[196,768]{1,0:T(8,128)(2,1)S(1)}, bf16[196,768]{1,0:T(8,128)(2,1)S(1)}, u32[]{:S(2)}, u32[]{:S(2)}) collective-permute-start(bf16[196,768]{1,0:T(8,128)(2,1)S(1)} %get-tuple-element.133.dm_ref.refs_0_), channel_id=1, source_target_pairs={{0,1},{1,0},{2,3},{3,2},{4,5},{5,4},{6,7},{7,6},{8,9},{9,8},{10,11... | collective-permute-start | bytes 903176 | tf_op jit(solution)/shard_map/ppermute | solution.py:103
  11.1 3.4 %prepare.1 = (bf16[224,768]{1,0:T(8,128)(2,1)S(1)}, bf16[768,224]{1,0:T(8,128)(2,1)S(1)}, bf16[768,768]{1,0:T(8,128)(2,1)S(1)}, bf16[768,768]{1,0:T(8,128)(2,1)S...) custom-call(bf16[196,768]{1,0:T(8,128)(2,1)} %x_ref.5, ...), custom_call_target="tpu_custom_call" | custom-call | flops 1 | bytes 1 | tf_op jit(solution)/shard_map/prepare/pallas_call | solution.py:66
  14.6 1.6 %collective-permute-start.4 = (bf16[96,1920]{1,0:T(8,128)(2,1)S(1)}, bf16[96,1920]{1,0:T(8,128)(2,1)S(1)}, u32[]{:S(2)}, u32[]{:S(2)}) collective-permute-start(bf16[96,1920]{1,0:T(8,128)(2,1)S(1)} %pad_maximum_fusion.1), channel_id=1, source_target_pairs={{0,1},{1,0},{2,3},{3,2},{4,5},{5,4},{6,7},{7,6},{8,9},{9,8},{10,11... | collective-permute-start | bytes 1105928 | tf_op jit(solution)/shard_map/ppermute | solution.py:103
  16.2 1.5 %collective-permute-start.3 = (bf16[96,1920]{1,0:T(8,128)(2,1)S(1)}, bf16[96,1920]{1,0:T(8,128)(2,1)S(1)}, u32[]{:S(2)}, u32[]{:S(2)}) collective-permute-start(bf16[96,1920]{1,0:T(8,128)(2,1)S(1)} %pad_maximum_fusion.1), channel_id=1, source_target_pairs={{0,4},{2,6},{4,0},{6,2},{8,12},{10,14},{12,8},{14,10},{16,20},{18,... | collective-permute-start | bytes 1105928 | tf_op jit(solution)/shard_map/ppermute | solution.py:94
  18.4 1.7 %collective-permute-start.11 = (bf16[24,1152]{1,0:T(8,128)(2,1)S(1)}, bf16[24,1152]{1,0:T(8,128)(2,1)S(1)}, u32[]{:S(2)}, u32[]{:S(2)}) collective-permute-start(bf16[24,1152]{1,0:T(8,128)(2,1)S(1)} %get-tuple-element.135), channel_id=1, source_target_pairs={{0,8},{2,10},{4,12},{6,14},{8,16},{10,18},{12,20},{14,22},{16,24},... | collective-permute-start | bytes 165896 | tf_op jit(solution)/shard_map/ppermute | solution.py:85
  20.1 1.7 %collective-permute-start.10 = (bf16[24,1152]{1,0:T(8,128)(2,1)S(1)}, bf16[24,1152]{1,0:T(8,128)(2,1)S(1)}, u32[]{:S(2)}, u32[]{:S(2)}) collective-permute-start(bf16[24,1152]{1,0:T(8,128)(2,1)S(1)} %get-tuple-element.135), channel_id=1, source_target_pairs={{0,16},{2,18},{4,20},{6,22},{8,24},{10,26},{12,28},{14,30},{16,0},... | collective-permute-start | bytes 165896 | tf_op jit(solution)/shard_map/ppermute | solution.py:85
  22.5 2.2 %collective-permute-done.11 = bf16[24,1152]{1,0:T(8,128)(2,1)S(1)} collective-permute-done((bf16[24,1152]{1,0:T(8,128)(2,1)S(1)}, bf16[24,1152]{1,0:T(8,128)(2,1)S(1)}, u32[]{:S(2)}, u32[]{:S(2)}) %collective-permute-start.11) | collective-permute-done | bytes 55328 | tf_op jit(solution)/shard_map/ppermute | solution.py:85
  24.7 1.5 %collective-permute-done.10 = bf16[24,1152]{1,0:T(8,128)(2,1)S(1)} collective-permute-done((bf16[24,1152]{1,0:T(8,128)(2,1)S(1)}, bf16[24,1152]{1,0:T(8,128)(2,1)S(1)}, u32[]{:S(2)}, u32[]{:S(2)}) %collective-permute-start.10) | collective-permute-done | bytes 55328 | tf_op jit(solution)/shard_map/ppermute | solution.py:85
  29.2 1.6 %collective-permute-start.6 = (bf16[96,960]{1,0:T(8,128)(2,1)S(1)}, bf16[96,960]{1,0:T(8,128)(2,1)S(1)}, u32[]{:S(2)}, u32[]{:S(2)}) collective-permute-start(bf16[96,960]{1,0:T(8,128)(2,1)S(1)} %slice.367), channel_id=1, source_target_pairs={{0,1},{1,0},{2,3},{3,2},{4,5},{5,4},{6,7},{7,6},{8,9},{9,8},{10,11... | collective-permute-start | bytes 552968 | tf_op jit(solution)/shard_map/ppermute | solution.py:103
  31.0 3.4 %collective-permute-done.13 = bf16[96,1152]{1,0:T(8,128)(2,1)S(1)} collective-permute-done((bf16[96,1152]{1,0:T(8,128)(2,1)S(1)}, bf16[96,1152]{1,0:T(8,128)(2,1)S(1)}, u32[]{:S(2)}, u32[]{:S(2)}) %collective-permute-start.13) | collective-permute-done | bytes 221216 | tf_op jit(solution)/shard_map/ppermute | solution.py:94
  34.8 1.6 %collective-permute-start.14 = (bf16[96,576]{1,0:T(8,128)(2,1)S(1)}, bf16[96,576]{1,0:T(8,128)(2,1)S(1)}, u32[]{:S(2)}, u32[]{:S(2)}) collective-permute-start(bf16[96,576]{1,0:T(8,128)(2,1)S(1)} %slice.286), channel_id=1, source_target_pairs={{0,4},{2,6},{4,0},{6,2},{8,12},{10,14},{12,8},{14,10},{16,20},{18,... | collective-permute-start | bytes 331784 | tf_op jit(solution)/shard_map/ppermute | solution.py:94
  37.5 2.2 %collective-permute-done.14 = bf16[96,576]{1,0:T(8,128)(2,1)S(1)} collective-permute-done((bf16[96,576]{1,0:T(8,128)(2,1)S(1)}, bf16[96,576]{1,0:T(8,128)(2,1)S(1)}, u32[]{:S(2)}, u32[]{:S(2)}) %collective-permute-start.14) | collective-permute-done | bytes 110624 | tf_op jit(solution)/shard_map/ppermute | solution.py:94
  39.7 1.5 %collective-permute-done.15 = bf16[96,576]{1,0:T(8,128)(2,1)S(1)} collective-permute-done((bf16[96,576]{1,0:T(8,128)(2,1)S(1)}, bf16[96,576]{1,0:T(8,128)(2,1)S(1)}, u32[]{:S(2)}, u32[]{:S(2)}) %collective-permute-start.15) | collective-permute-done | bytes 110624 | tf_op jit(solution)/shard_map/ppermute | solution.py:103
  41.4 2.4 %collective-permute-done.16.other_ref.other1_ref = bf16[384,1152]{1,0:T(8,128)(2,1)S(1)} collective-permute-done((bf16[384,1152]{1,0:T(8,128)(2,1)S(1)}, bf16[384,1152]{1,0:T(8,128)(2,1)S(1)}, u32[]{:S(2)}, u32[]{:S(2)}) %collective-permute-start.16) | collective-permute-done | bytes 884768 | tf_op jit(solution)/shard_map/ppermute | solution.py:98
  43.8 1.9 %attend1.1 = (bf16[224,1152]{1,0:T(8,128)(2,1)S(1)}, bf16[6,224,224]{2,1,0:T(8,128)(2,1)S(1)}, bf16[224,384]{1,0:T(8,128)(2,1)S(1)}) custom-call(bf16[224,768]{1,0:T(8,128)(2,1)S(1)} %get-tuple-element.144.a1_ref, bf16[384,1152]{1,0:T(8,128)(2,1)S(1)} %maximum_dynamic-update-slice_fusion.1.own_ref.own1_ref, ...), custom_call_target="tpu_custom_call" | custom-call | flops 1 | bytes 1 | tf_op jit(solution)/shard_map/attend1/pallas_call | solution.py:66
  45.8 3.9 %attend2.1 = (bf16[224,1152]{1,0:T(8,128)(2,1)S(1)}, bf16[6,224,224]{2,1,0:T(8,128)(2,1)S(1)}, bf16[768,196]{1,0:T(8,128)(2,1)S(1)}, f32[196,768]{1,0:T(8,128)S(1)}, bf16[196,768]{1,0:T(8,128)(2,1)S(1)}) custom-call(s32[1,2]{1,0:T(1,128)S(1)} %copy-done.5, bf16[224,768]{1,0:T(8,128)(2,1)S(1)} %get-tuple-element.144.a1_ref, ...), custom_call_target="tpu_custom_call" | custom-call | flops 1 | bytes 1 | tf_op jit(solution)/shard_map/attend2/pallas_call | solution.py:66
  51.5 1.4 act.3
  53.2 2.0 %feed.2 = (bf16[196,1536]{1,0:T(8,128)(2,1)S(1)}, bf16[196,1536]{1,0:T(8,128)(2,1)S(1)}, f32[196,768]{1,0:T(8,128)S(1)}) custom-call(bf16[196,768]{1,0:T(8,128)(2,1)S(1)} %get-tuple-element.146.a2_ref.refs_4_, bf16[768,1536]{1,0:T(8,128)(2,1)S(1)} %copy-done.1, f32[1,1536]{1,0:T(1,128)S(1)} %get-tuple-element.140.upb_ref, ...), custom_call_target="tpu_custom_call" | custom-call | flops 1 | bytes 1 | tf_op jit(solution)/shard_map/feed/pallas_call | solution.py:66
  55.2 3.9 %collective-permute-done.17.a2_ref.refs_5_ = bf16[196,768]{1,0:T(8,128)(2,1)S(1)} collective-permute-done((bf16[196,768]{1,0:T(8,128)(2,1)S(1)}, bf16[196,768]{1,0:T(8,128)(2,1)S(1)}, u32[]{:S(2)}, u32[]{:S(2)}) %collective-permute-start.17) | collective-permute-done | bytes 301088 | tf_op jit(solution)/shard_map/ppermute | solution.py:103
  59.1 2.0 %feed.3 = (bf16[196,1536]{1,0:T(8,128)(2,1)S(1)}, bf16[196,1536]{1,0:T(8,128)(2,1)S(1)}, bf16[196,768]{1,0:T(8,128)(2,1)S(1)}) custom-call(bf16[196,768]{1,0:T(8,128)(2,1)S(1)} %collective-permute-done.17.a2_ref.refs_5_, bf16[768,1536]{1,0:T(8,128)(2,1)S(1)} %copy-done.1, f32[1,1536]{1,0:T(1,128)S(1)} %get-tuple-element.140.upb_ref, ...), custom_call_target="tpu_custom_call" | custom-call | flops 1 | bytes 1 | tf_op jit(solution)/shard_map/feed/pallas_call | solution.py:66
  62.0 6.1 %feedw.1 = (bf16[192,1536]{1,0:T(8,128)(2,1)S(1)}, bf16[192,1536]{1,0:T(8,128)(2,1)S(1)}, bf16[192,1536]{1,0:T(8,128)(2,1)S(1)}, bf16[192,1536]{1,0:T(8,128)(2,1...) custom-call(bf16[768,768]{1,0:T(8,128)(2,1)S(1)} %get-tuple-element., ...), custom_call_target="tpu_custom_call" | custom-call | flops 1 | bytes 1 | tf_op jit(solution)/shard_map/feedw/pallas_call | solution.py:66
  68.1 1.5 %collective-permute-done.18.got_ref = bf16[196,768]{1,0:T(8,128)(2,1)S(1)} collective-permute-done((bf16[196,768]{1,0:T(8,128)(2,1)S(1)}, bf16[196,768]{1,0:T(8,128)(2,1)S(1)}, u32[]{:S(2)}, u32[]{:S(2)}) %collective-permute-start.18) | collective-permute-done | bytes 301088 | tf_op jit(solution)/shard_map/ppermute | solution.py:103
  70.1 1.5 %collective-permute-done.20 = bf16[192,1536]{1,0:T(8,128)(2,1)S(1)} collective-permute-done((bf16[192,1536]{1,0:T(8,128)(2,1)S(1)}, bf16[192,1536]{1,0:T(8,128)(2,1)S(1)}, u32[]{:S(2)}, u32[]{:S(2)}) %collective-permute-start.20) | collective-permute-done | bytes 589856 | tf_op jit(solution)/shard_map/ppermute | solution.py:98
  73.0 1.6 %collective-permute-start.21 = (bf16[196,768]{1,0:T(8,128)(2,1)S(1)}, bf16[196,768]{1,0:T(8,128)(2,1)S(1)}, u32[]{:S(2)}, u32[]{:S(2)}) collective-permute-start(bf16[196,768]{1,0:T(8,128)(2,1)S(1)} %get-tuple-element.175), channel_id=1, source_target_pairs={{0,1},{1,0},{2,3},{3,2},{4,5},{5,4},{6,7},{7,6},{8,9},{9,8},{10,11... | collective-permute-start | bytes 903176 | tf_op jit(solution)/shard_map/ppermute | solution.py:103
  74.6 2.1 %backnorm.1 = (f32[196,768]{1,0:T(8,128)S(1)}, bf16[224,768]{1,0:T(8,128)(2,1)S(1)}, bf16[196,768]{1,0:T(8,128)(2,1)S(1)}, f32[3,768]{1,0:T(4,128)S(1)}) custom-call(s32[1,2]{1,0:T(1,128)S(1)} %copy-done.5, f32[196,768]{1,0:T(8,128)S(1)} %get-tuple-element.148.da2_ref, bf16[196,768]{1,0:T(8,128)(2,1)S(1)} %collective-permute-done.18.got_ref, ...), custom_call_target="tpu_custom_call" | custom-call | flops 1 | bytes 1 | tf_op jit(solution)/shard_map/backnorm/pallas_call | solution.py:66
  76.7 3.3 %back1.1 = (bf16[224,1152]{1,0:T(8,128)(2,1)S(1)}, bf16[192,1920]{1,0:T(8,128)(2,1)S(1)}, bf16[192,1920]{1,0:T(8,128)(2,1)S(1)}, bf16[192,1920]{1,0:T(8,128)(2,1...) custom-call(bf16[224,768]{1,0:T(8,128)(2,1)S(1)} %get-tuple-element.176.do_ref, ...), custom_call_target="tpu_custom_call" | custom-call | flops 1 | bytes 1 | tf_op jit(solution)/shard_map/back1/pallas_call | solution.py:66
  80.0 2.3 %collective-permute-done.21.mgot_ref = bf16[196,768]{1,0:T(8,128)(2,1)S(1)} collective-permute-done((bf16[196,768]{1,0:T(8,128)(2,1)S(1)}, bf16[196,768]{1,0:T(8,128)(2,1)S(1)}, u32[]{:S(2)}, u32[]{:S(2)}) %collective-permute-start.21) | collective-permute-done | bytes 301088 | tf_op jit(solution)/shard_map/ppermute | solution.py:103
  82.8 3.0 %back2.1 = (bf16[224,1152]{1,0:T(8,128)(2,1)S(1)}, bf16[192,1152]{1,0:T(8,128)(2,1)S(1)}, bf16[192,1152]{1,0:T(8,128)(2,1)S(1)}, bf16[192,1152]{1,0:T(8,128)(2,1...) custom-call(bf16[224,768]{1,0:T(8,128)(2,1)S(1)} %get-tuple-element.176.do_ref, ...), custom_call_target="tpu_custom_call" | custom-call | flops 1 | bytes 1 | tf_op jit(solution)/shard_map/back2/pallas_call | solution.py:66
  85.8 1.4 collective-permute-done.22
  88.8 1.7 %collective-permute-start.33 = (bf16[192,1920]{1,0:T(8,128)(2,1)S(1)}, bf16[192,1920]{1,0:T(8,128)(2,1)S(1)}, u32[]{:S(2)}, u32[]{:S(2)}) collective-permute-start(bf16[192,1920]{1,0:T(8,128)(2,1)S(1)} %add_convert_fusion), channel_id=1, source_target_pairs={{0,1},{1,0},{2,3},{3,2},{4,5},{5,4},{6,7},{7,6},{8,9},{9,8},{10,11... | collective-permute-start | bytes 2211848 | tf_op jit(solution)/shard_map/ppermute | solution.py:103
  90.6 2.9 %finish.1 = (f32[196,768]{1,0:T(8,128)S(1)}, f32[16,1152]{1,0:T(8,128)S(1)}) custom-call(bf16[224,1152]{1,0:T(8,128)(2,1)S(1)} %get-tuple-element.174.dq1_ref, bf16[224,1152]{1,0:T(8,128)(2,1)S(1)} %get-tuple-element.179.dq2_ref, bf16[384,1152]{1,0:T(8,128)(2,1)S(1)} %maximum_dynamic-update-slice_fusion.1.own_ref.own1_ref, ...), custom_call_target="tpu_custom_call" | custom-call | flops 1 | bytes 1 | tf_op jit(solution)/shard_map/finish/pallas_call | solution.py:66
  93.5 1.6 %collective-permute-start.35 = (bf16[96,1536]{1,0:T(8,128)(2,1)S(1)}, bf16[96,1536]{1,0:T(8,128)(2,1)S(1)}, u32[]{:S(2)}, u32[]{:S(2)}) collective-permute-start(bf16[96,1536]{1,0:T(8,128)(2,1)S(1)} %pad_maximum_fusion.2), channel_id=1, source_target_pairs={{0,8},{2,10},{4,12},{6,14},{8,0},{10,2},{12,4},{14,6},{16,24},{18,... | collective-permute-start | bytes 884744 | tf_op jit(solution)/shard_map/ppermute | solution.py:90
  95.3 1.1 collective-permute-start.28
  96.4 7.7 %collective-permute-done.42 = bf16[192,1536]{1,0:T(8,128)(2,1)S(1)} collective-permute-done((bf16[192,1536]{1,0:T(8,128)(2,1)S(1)}, bf16[192,1536]{1,0:T(8,128)(2,1)S(1)}, u32[]{:S(2)}, u32[]{:S(2)}) %collective-permute-start.42) | collective-permute-done | bytes 589856 | tf_op jit(solution)/shard_map/ppermute | solution.py:94
  104.3 1.7 %collective-permute-start.43 = (bf16[96,1536]{1,0:T(8,128)(2,1)S(1)}, bf16[96,1536]{1,0:T(8,128)(2,1)S(1)}, u32[]{:S(2)}, u32[]{:S(2)}) collective-permute-start(bf16[96,1536]{1,0:T(8,128)(2,1)S(1)} %pad_maximum_fusion.3), channel_id=1, source_target_pairs={{0,8},{2,10},{4,12},{6,14},{8,0},{10,2},{12,4},{14,6},{16,24},{18,... | collective-permute-start | bytes 884744 | tf_op jit(solution)/shard_map/ppermute | solution.py:90
  106.0 1.8 %collective-permute-start.36 = (bf16[48,1536]{1,0:T(8,128)(2,1)S(1)}, bf16[48,1536]{1,0:T(8,128)(2,1)S(1)}, u32[]{:S(2)}, u32[]{:S(2)}) collective-permute-start(bf16[48,1536]{1,0:T(8,128)(2,1)S(1)} %add_convert_fusion.9), channel_id=1, source_target_pairs={{0,16},{2,18},{4,20},{6,22},{8,24},{10,26},{12,28},{14,30},{16,0},... | collective-permute-start | bytes 442376 | tf_op jit(solution)/shard_map/ppermute | solution.py:90
  107.9 6.9 %collective-permute-done.43 = bf16[96,1536]{1,0:T(8,128)(2,1)S(1)} collective-permute-done((bf16[96,1536]{1,0:T(8,128)(2,1)S(1)}, bf16[96,1536]{1,0:T(8,128)(2,1)S(1)}, u32[]{:S(2)}, u32[]{:S(2)}) %collective-permute-start.43) | collective-permute-done | bytes 294944 | tf_op jit(solution)/shard_map/ppermute | solution.py:90
  118.4 5.2 %collective-permute-done.29 = bf16[112,1152]{1,0:T(8,128)(2,1)S(1)} collective-permute-done((bf16[112,1152]{1,0:T(8,128)(2,1)S(1)}, bf16[112,1152]{1,0:T(8,128)(2,1)S(1)}, u32[]{:S(2)}, u32[]{:S(2)}) %collective-permute-start.29) | collective-permute-done | bytes 258080 | tf_op jit(solution)/shard_map/ppermute | solution.py:103
  123.7 2.3 %collective-permute-start.32 = (bf16[40,1152]{1,0:T(8,128)(2,1)S(1)}, bf16[40,1152]{1,0:T(8,128)(2,1)S(1)}, u32[]{:S(2)}, u32[]{:S(2)}) collective-permute-start(bf16[40,1152]{1,0:T(8,128)(2,1)S(1)} %get-tuple-element.254), channel_id=1, source_target_pairs={{0,24},{2,26},{4,28},{6,30},{8,0},{10,2},{12,4},{14,6},{16,8},{18,... | collective-permute-start | bytes 276488 | tf_op jit(solution)/shard_map/ppermute | solution.py:85
  126.0 1.7 %collective-permute-start.31 = (bf16[40,1152]{1,0:T(8,128)(2,1)S(1)}, bf16[40,1152]{1,0:T(8,128)(2,1)S(1)}, u32[]{:S(2)}, u32[]{:S(2)}) collective-permute-start(bf16[40,1152]{1,0:T(8,128)(2,1)S(1)} %get-tuple-element.255), channel_id=1, source_target_pairs={{0,16},{2,18},{4,20},{6,22},{8,24},{10,26},{12,28},{14,30},{16,0},... | collective-permute-start | bytes 276488 | tf_op jit(solution)/shard_map/ppermute | solution.py:85
  128.7 1.8 %collective-permute-start.37 = (bf16[24,1920]{1,0:T(8,128)(2,1)S(1)}, bf16[24,1920]{1,0:T(8,128)(2,1)S(1)}, u32[]{:S(2)}, u32[]{:S(2)}) collective-permute-start(bf16[24,1920]{1,0:T(8,128)(2,1)S(1)} %get-tuple-element.217), channel_id=1, source_target_pairs={{0,8},{2,10},{4,12},{6,14},{8,16},{10,18},{12,20},{14,22},{16,24},... | collective-permute-start | bytes 276488 | tf_op jit(solution)/shard_map/ppermute | solution.py:85
  130.5 2.6 %collective-permute-start.38 = (bf16[24,1920]{1,0:T(8,128)(2,1)S(1)}, bf16[24,1920]{1,0:T(8,128)(2,1)S(1)}, u32[]{:S(2)}, u32[]{:S(2)}) collective-permute-start(bf16[24,1920]{1,0:T(8,128)(2,1)S(1)} %get-tuple-element.218), channel_id=1, source_target_pairs={{0,16},{2,18},{4,20},{6,22},{8,24},{10,26},{12,28},{14,30},{16,0},... | collective-permute-start | bytes 276488 | tf_op jit(solution)/shard_map/ppermute | solution.py:85
  133.4 6.6 %collective-permute-done.31.refs_2_ = bf16[40,1152]{1,0:T(8,128)(2,1)S(1)} collective-permute-done((bf16[40,1152]{1,0:T(8,128)(2,1)S(1)}, bf16[40,1152]{1,0:T(8,128)(2,1)S(1)}, u32[]{:S(2)}, u32[]{:S(2)}) %collective-permute-start.31) | collective-permute-done | bytes 92192 | tf_op jit(solution)/shard_map/ppermute | solution.py:85
  140.1 2.1 %outputs.1 = (f32[768]{0:T(1024)}, f32[768]{0:T(1024)}, f32[2,768]{1,0:T(2,128)}, f32[27,64]{1,0:T(8,128)}, f32[27,64]{1,0:T(8,128)}, /*index=5*/f32[768]{0:T(10...) custom-call(s32[1,2]{1,0:T(1,128)S(1)} %copy-done.5, ...), custom_call_target="tpu_custom_call" | custom-call | flops 1 | bytes 1 | tf_op jit(solution)/shard_map/outputs/pallas_call | solution.py:66
  (121 shorter events, 20.8 us)
Async XLA Ops:
  2.6 12.0 %collective-permute-start.2 = (bf16[24,1920]{1,0:T(8,128)(2,1)S(1)}, bf16[24,1920]{1,0:T(8,128)(2,1)S(1)}, u32[]{:S(2)}, u32[]{:S(2)}) collective-permute-start(bf16[24,1920]{1,0:T(8,128)(2,1)S(1)} %get-tuple-element.130), channel_id=1, source_target_pairs={{0,8},{2,10},{4,12},{6,14},{8,16},{10,18},{12,20},{14,22},{16,24},... | collective-permute-start | bytes 276488 | tf_op jit(solution)/shard_map/ppermute | solution.py:85
  5.6 8.9 %collective-permute-start.1 = (bf16[24,1920]{1,0:T(8,128)(2,1)S(1)}, bf16[24,1920]{1,0:T(8,128)(2,1)S(1)}, u32[]{:S(2)}, u32[]{:S(2)}) collective-permute-start(bf16[24,1920]{1,0:T(8,128)(2,1)S(1)} %get-tuple-element.130), channel_id=1, source_target_pairs={{0,16},{2,18},{4,20},{6,22},{8,24},{10,26},{12,28},{14,30},{16,0},... | collective-permute-start | bytes 276488 | tf_op jit(solution)/shard_map/ppermute | solution.py:85
  8.2 6.4 %collective-permute-start = (bf16[24,1920]{1,0:T(8,128)(2,1)S(1)}, bf16[24,1920]{1,0:T(8,128)(2,1)S(1)}, u32[]{:S(2)}, u32[]{:S(2)}) collective-permute-start(bf16[24,1920]{1,0:T(8,128)(2,1)S(1)} %get-tuple-element.130), channel_id=1, source_target_pairs={{0,24},{2,26},{4,28},{6,30},{8,0},{10,2},{12,4},{14,6},{16,8},{18,... | collective-permute-start | bytes 276488 | tf_op jit(solution)/shard_map/ppermute | solution.py:85
  9.6 8.8 %collective-permute-start.8 = (bf16[196,768]{1,0:T(8,128)(2,1)S(1)}, bf16[196,768]{1,0:T(8,128)(2,1)S(1)}, u32[]{:S(2)}, u32[]{:S(2)}) collective-permute-start(bf16[196,768]{1,0:T(8,128)(2,1)S(1)} %get-tuple-element.133.dm_ref.refs_0_), channel_id=1, source_target_pairs={{0,1},{1,0},{2,3},{3,2},{4,5},{5,4},{6,7},{7,6},{8,9},{9,8},{10,11... | collective-permute-start | bytes 903176 | tf_op jit(solution)/shard_map/ppermute | solution.py:103
  14.6 13.4 %collective-permute-start.4 = (bf16[96,1920]{1,0:T(8,128)(2,1)S(1)}, bf16[96,1920]{1,0:T(8,128)(2,1)S(1)}, u32[]{:S(2)}, u32[]{:S(2)}) collective-permute-start(bf16[96,1920]{1,0:T(8,128)(2,1)S(1)} %pad_maximum_fusion.1), channel_id=1, source_target_pairs={{0,1},{1,0},{2,3},{3,2},{4,5},{5,4},{6,7},{7,6},{8,9},{9,8},{10,11... | collective-permute-start | bytes 1105928 | tf_op jit(solution)/shard_map/ppermute | solution.py:103
  16.2 12.9 %collective-permute-start.3 = (bf16[96,1920]{1,0:T(8,128)(2,1)S(1)}, bf16[96,1920]{1,0:T(8,128)(2,1)S(1)}, u32[]{:S(2)}, u32[]{:S(2)}) collective-permute-start(bf16[96,1920]{1,0:T(8,128)(2,1)S(1)} %pad_maximum_fusion.1), channel_id=1, source_target_pairs={{0,4},{2,6},{4,0},{6,2},{8,12},{10,14},{12,8},{14,10},{16,20},{18,... | collective-permute-start | bytes 1105928 | tf_op jit(solution)/shard_map/ppermute | solution.py:94
  18.4 6.4 %collective-permute-start.11 = (bf16[24,1152]{1,0:T(8,128)(2,1)S(1)}, bf16[24,1152]{1,0:T(8,128)(2,1)S(1)}, u32[]{:S(2)}, u32[]{:S(2)}) collective-permute-start(bf16[24,1152]{1,0:T(8,128)(2,1)S(1)} %get-tuple-element.135), channel_id=1, source_target_pairs={{0,8},{2,10},{4,12},{6,14},{8,16},{10,18},{12,20},{14,22},{16,24},... | collective-permute-start | bytes 165896 | tf_op jit(solution)/shard_map/ppermute | solution.py:85
  20.1 6.1 %collective-permute-start.10 = (bf16[24,1152]{1,0:T(8,128)(2,1)S(1)}, bf16[24,1152]{1,0:T(8,128)(2,1)S(1)}, u32[]{:S(2)}, u32[]{:S(2)}) collective-permute-start(bf16[24,1152]{1,0:T(8,128)(2,1)S(1)} %get-tuple-element.135), channel_id=1, source_target_pairs={{0,16},{2,18},{4,20},{6,22},{8,24},{10,26},{12,28},{14,30},{16,0},... | collective-permute-start | bytes 165896 | tf_op jit(solution)/shard_map/ppermute | solution.py:85
  21.8 4.6 %collective-permute-start.9 = (bf16[24,1152]{1,0:T(8,128)(2,1)S(1)}, bf16[24,1152]{1,0:T(8,128)(2,1)S(1)}, u32[]{:S(2)}, u32[]{:S(2)}) collective-permute-start(bf16[24,1152]{1,0:T(8,128)(2,1)S(1)} %get-tuple-element.135), channel_id=1, source_target_pairs={{0,24},{2,26},{4,28},{6,30},{8,0},{10,2},{12,4},{14,6},{16,8},{18,... | collective-permute-start | bytes 165896 | tf_op jit(solution)/shard_map/ppermute | solution.py:85
  26.4 8.0 %collective-permute-start.13 = (bf16[96,1152]{1,0:T(8,128)(2,1)S(1)}, bf16[96,1152]{1,0:T(8,128)(2,1)S(1)}, u32[]{:S(2)}, u32[]{:S(2)}) collective-permute-start(bf16[96,1152]{1,0:T(8,128)(2,1)S(1)} %pad_maximum_fusion.5), channel_id=1, source_target_pairs={{0,4},{2,6},{4,0},{6,2},{8,12},{10,14},{12,8},{14,10},{16,20},{18,... | collective-permute-start | bytes 663560 | tf_op jit(solution)/shard_map/ppermute | solution.py:94
  26.9 7.7 %collective-permute-start.12 = (bf16[96,1152]{1,0:T(8,128)(2,1)S(1)}, bf16[96,1152]{1,0:T(8,128)(2,1)S(1)}, u32[]{:S(2)}, u32[]{:S(2)}) collective-permute-start(bf16[96,1152]{1,0:T(8,128)(2,1)S(1)} %pad_maximum_fusion.5), channel_id=1, source_target_pairs={{0,1},{1,0},{2,3},{3,2},{4,5},{5,4},{6,7},{7,6},{8,9},{9,8},{10,11... | collective-permute-start | bytes 663560 | tf_op jit(solution)/shard_map/ppermute | solution.py:103
  28.1 9.1 %collective-permute-start.5 = (bf16[96,960]{1,0:T(8,128)(2,1)S(1)}, bf16[96,960]{1,0:T(8,128)(2,1)S(1)}, u32[]{:S(2)}, u32[]{:S(2)}) collective-permute-start(bf16[96,960]{1,0:T(8,128)(2,1)S(1)} %slice.366), channel_id=1, source_target_pairs={{0,4},{2,6},{4,0},{6,2},{8,12},{10,14},{12,8},{14,10},{16,20},{18,... | collective-permute-start | bytes 552968 | tf_op jit(solution)/shard_map/ppermute | solution.py:94
  29.2 8.0 %collective-permute-start.6 = (bf16[96,960]{1,0:T(8,128)(2,1)S(1)}, bf16[96,960]{1,0:T(8,128)(2,1)S(1)}, u32[]{:S(2)}, u32[]{:S(2)}) collective-permute-start(bf16[96,960]{1,0:T(8,128)(2,1)S(1)} %slice.367), channel_id=1, source_target_pairs={{0,1},{1,0},{2,3},{3,2},{4,5},{5,4},{6,7},{7,6},{8,9},{9,8},{10,11... | collective-permute-start | bytes 552968 | tf_op jit(solution)/shard_map/ppermute | solution.py:103
  34.8 4.9 %collective-permute-start.14 = (bf16[96,576]{1,0:T(8,128)(2,1)S(1)}, bf16[96,576]{1,0:T(8,128)(2,1)S(1)}, u32[]{:S(2)}, u32[]{:S(2)}) collective-permute-start(bf16[96,576]{1,0:T(8,128)(2,1)S(1)} %slice.286), channel_id=1, source_target_pairs={{0,4},{2,6},{4,0},{6,2},{8,12},{10,14},{12,8},{14,10},{16,20},{18,... | collective-permute-start | bytes 331784 | tf_op jit(solution)/shard_map/ppermute | solution.py:94
  36.3 4.9 %collective-permute-start.15 = (bf16[96,576]{1,0:T(8,128)(2,1)S(1)}, bf16[96,576]{1,0:T(8,128)(2,1)S(1)}, u32[]{:S(2)}, u32[]{:S(2)}) collective-permute-start(bf16[96,576]{1,0:T(8,128)(2,1)S(1)} %slice.287), channel_id=1, source_target_pairs={{0,1},{1,0},{2,3},{3,2},{4,5},{5,4},{6,7},{7,6},{8,9},{9,8},{10,11... | collective-permute-start | bytes 331784 | tf_op jit(solution)/shard_map/ppermute | solution.py:103
  37.3 8.4 %collective-permute-start.7 = (bf16[384,1920]{1,0:T(8,128)(2,1)S(1)}, bf16[384,1920]{1,0:T(8,128)(2,1)S(1)}, u32[]{:S(2)}, u32[]{:S(2)}) collective-permute-start(bf16[384,1920]{1,0:T(8,128)(2,1)S(1)} %maximum_dynamic-update-slice_fusion.own_ref.own2_ref), channel_id=1, source_target_pairs={{0,2},{2,0},{4,6},{6,4},{8,10},{10,8},{12,14},{14,12},{16,18},{18,... | collective-permute-start | bytes 4423688 | tf_op jit(solution)/shard_map/ppermute | solution.py:98
  37.5 8.3 %copy-start.2 = (bf16[196,768]{1,0:T(8,128)(2,1)S(1)}, bf16[196,768]{1,0:T(8,128)(2,1)}, u32[]{:S(2)}) copy-start(bf16[196,768]{1,0:T(8,128)(2,1)} %x_ref.5) | copy-start | bytes 903172
  37.5 8.3 %copy-start.5 = (s32[1,2]{1,0:T(1,128)S(1)}, s32[1,2]{1,0:T(1,128)}, u32[]{:S(2)}) copy-start(s32[1,2]{1,0:T(1,128)} %keep_ref.7) | copy-start | bytes 28
  41.3 2.5 %collective-permute-start.16 = (bf16[384,1152]{1,0:T(8,128)(2,1)S(1)}, bf16[384,1152]{1,0:T(8,128)(2,1)S(1)}, u32[]{:S(2)}, u32[]{:S(2)}) collective-permute-start(bf16[384,1152]{1,0:T(8,128)(2,1)S(1)} %maximum_dynamic-update-slice_fusion.1.own_ref.own1_ref), channel_id=1, source_target_pairs={{0,2},{2,0},{4,6},{6,4},{8,10},{10,8},{12,14},{14,12},{16,18},{18,... | collective-permute-start | bytes 2654216 | tf_op jit(solution)/shard_map/ppermute | solution.py:98
  49.7 9.4 %collective-permute-start.17 = (bf16[196,768]{1,0:T(8,128)(2,1)S(1)}, bf16[196,768]{1,0:T(8,128)(2,1)S(1)}, u32[]{:S(2)}, u32[]{:S(2)}) collective-permute-start(bf16[196,768]{1,0:T(8,128)(2,1)S(1)} %get-tuple-element.146.a2_ref.refs_4_), channel_id=1, source_target_pairs={{0,1},{1,0},{2,3},{3,2},{4,5},{5,4},{6,7},{7,6},{8,9},{9,8},{10,11... | collective-permute-start | bytes 903176 | tf_op jit(solution)/shard_map/ppermute | solution.py:103
  61.1 8.5 %collective-permute-start.18 = (bf16[196,768]{1,0:T(8,128)(2,1)S(1)}, bf16[196,768]{1,0:T(8,128)(2,1)S(1)}, u32[]{:S(2)}, u32[]{:S(2)}) collective-permute-start(bf16[196,768]{1,0:T(8,128)(2,1)S(1)} %get-tuple-element.152), channel_id=1, source_target_pairs={{0,1},{1,0},{2,3},{3,2},{4,5},{5,4},{6,7},{7,6},{8,9},{9,8},{10,11... | collective-permute-start | bytes 903176 | tf_op jit(solution)/shard_map/ppermute | solution.py:103
  68.1 6.5 %copy-start.3 = (bf16[196,768]{1,0:T(8,128)(2,1)S(1)}, bf16[196,768]{1,0:T(8,128)(2,1)}, u32[]{:S(2)}) copy-start(bf16[196,768]{1,0:T(8,128)(2,1)} %g_ref.1) | copy-start | bytes 903172
  69.6 2.0 %collective-permute-start.20 = (bf16[192,1536]{1,0:T(8,128)(2,1)S(1)}, bf16[192,1536]{1,0:T(8,128)(2,1)S(1)}, u32[]{:S(2)}, u32[]{:S(2)}) collective-permute-start(bf16[192,1536]{1,0:T(8,128)(2,1)S(1)} %get-tuple-element.168), channel_id=1, source_target_pairs={{0,2},{2,0},{4,6},{6,4},{8,10},{10,8},{12,14},{14,12},{16,18},{18,... | collective-permute-start | bytes 1769480 | tf_op jit(solution)/shard_map/ppermute | solution.py:98
  69.6 2.8 %collective-permute-start.19 = (bf16[192,1536]{1,0:T(8,128)(2,1)S(1)}, bf16[192,1536]{1,0:T(8,128)(2,1)S(1)}, u32[]{:S(2)}, u32[]{:S(2)}) collective-permute-start(bf16[192,1536]{1,0:T(8,128)(2,1)S(1)} %get-tuple-element.167), channel_id=1, source_target_pairs={{0,2},{2,0},{4,6},{6,4},{8,10},{10,8},{12,14},{14,12},{16,18},{18,... | collective-permute-start | bytes 1769480 | tf_op jit(solution)/shard_map/ppermute | solution.py:98
  71.8 15.4 %collective-permute-start.22 = (bf16[192,1536]{1,0:T(8,128)(2,1)S(1)}, bf16[192,1536]{1,0:T(8,128)(2,1)S(1)}, u32[]{:S(2)}, u32[]{:S(2)}) collective-permute-start(bf16[192,1536]{1,0:T(8,128)(2,1)S(1)} %add_convert_fusion.2), channel_id=1, source_target_pairs={{0,4},{2,6},{4,0},{6,2},{8,12},{10,14},{12,8},{14,10},{16,20},{18,... | collective-permute-start | bytes 1769480 | tf_op jit(solution)/shard_map/ppermute | solution.py:94
  72.5 14.7 %collective-permute-start.40 = (bf16[192,1536]{1,0:T(8,128)(2,1)S(1)}, bf16[192,1536]{1,0:T(8,128)(2,1)S(1)}, u32[]{:S(2)}, u32[]{:S(2)}) collective-permute-start(bf16[192,1536]{1,0:T(8,128)(2,1)S(1)} %get-tuple-element.232), channel_id=1, source_target_pairs={{0,2},{2,0},{4,6},{6,4},{8,10},{10,8},{12,14},{14,12},{16,18},{18,... | collective-permute-start | bytes 1769480 | tf_op jit(solution)/shard_map/ppermute | solution.py:98
  72.6 14.6 %collective-permute-start.41 = (bf16[192,1536]{1,0:T(8,128)(2,1)S(1)}, bf16[192,1536]{1,0:T(8,128)(2,1)S(1)}, u32[]{:S(2)}, u32[]{:S(2)}) collective-permute-start(bf16[192,1536]{1,0:T(8,128)(2,1)S(1)} %get-tuple-element.233), channel_id=1, source_target_pairs={{0,2},{2,0},{4,6},{6,4},{8,10},{10,8},{12,14},{14,12},{16,18},{18,... | collective-permute-start | bytes 1769480 | tf_op jit(solution)/shard_map/ppermute | solution.py:98
  73.0 9.3 %collective-permute-start.21 = (bf16[196,768]{1,0:T(8,128)(2,1)S(1)}, bf16[196,768]{1,0:T(8,128)(2,1)S(1)}, u32[]{:S(2)}, u32[]{:S(2)}) collective-permute-start(bf16[196,768]{1,0:T(8,128)(2,1)S(1)} %get-tuple-element.175), channel_id=1, source_target_pairs={{0,1},{1,0},{2,3},{3,2},{4,5},{5,4},{6,7},{7,6},{8,9},{9,8},{10,11... | collective-permute-start | bytes 903176 | tf_op jit(solution)/shard_map/ppermute | solution.py:103
  82.3 12.9 %collective-permute-start.26 = (bf16[192,1920]{1,0:T(8,128)(2,1)S(1)}, bf16[192,1920]{1,0:T(8,128)(2,1)S(1)}, u32[]{:S(2)}, u32[]{:S(2)}) collective-permute-start(bf16[192,1920]{1,0:T(8,128)(2,1)S(1)} %get-tuple-element.197), channel_id=1, source_target_pairs={{0,2},{2,0},{4,6},{6,4},{8,10},{10,8},{12,14},{14,12},{16,18},{18,... | collective-permute-start | bytes 2211848 | tf_op jit(solution)/shard_map/ppermute | solution.py:98
  82.3 6.3 %collective-permute-start.27 = (bf16[192,1920]{1,0:T(8,128)(2,1)S(1)}, bf16[192,1920]{1,0:T(8,128)(2,1)S(1)}, u32[]{:S(2)}, u32[]{:S(2)}) collective-permute-start(bf16[192,1920]{1,0:T(8,128)(2,1)S(1)} %get-tuple-element.198), channel_id=1, source_target_pairs={{0,2},{2,0},{4,6},{6,4},{8,10},{10,8},{12,14},{14,12},{16,18},{18,... | collective-permute-start | bytes 2211848 | tf_op jit(solution)/shard_map/ppermute | solution.py:98
  87.2 3.4 %collective-permute-start.23 = (bf16[192,1152]{1,0:T(8,128)(2,1)S(1)}, bf16[192,1152]{1,0:T(8,128)(2,1)S(1)}, u32[]{:S(2)}, u32[]{:S(2)}) collective-permute-start(bf16[192,1152]{1,0:T(8,128)(2,1)S(1)} %get-tuple-element.183), channel_id=1, source_target_pairs={{0,2},{2,0},{4,6},{6,4},{8,10},{10,8},{12,14},{14,12},{16,18},{18,... | collective-permute-start | bytes 1327112 | tf_op jit(solution)/shard_map/ppermute | solution.py:98
  87.2 3.3 %collective-permute-start.24 = (bf16[192,1152]{1,0:T(8,128)(2,1)S(1)}, bf16[192,1152]{1,0:T(8,128)(2,1)S(1)}, u32[]{:S(2)}, u32[]{:S(2)}) collective-permute-start(bf16[192,1152]{1,0:T(8,128)(2,1)S(1)} %get-tuple-element.184), channel_id=1, source_target_pairs={{0,2},{2,0},{4,6},{6,4},{8,10},{10,8},{12,14},{14,12},{16,18},{18,... | collective-permute-start | bytes 1327112 | tf_op jit(solution)/shard_map/ppermute | solution.py:98
  87.9 16.2 %collective-permute-start.42 = (bf16[192,1536]{1,0:T(8,128)(2,1)S(1)}, bf16[192,1536]{1,0:T(8,128)(2,1)S(1)}, u32[]{:S(2)}, u32[]{:S(2)}) collective-permute-start(bf16[192,1536]{1,0:T(8,128)(2,1)S(1)} %add_convert_fusion.1), channel_id=1, source_target_pairs={{0,4},{2,6},{4,0},{6,2},{8,12},{10,14},{12,8},{14,10},{16,20},{18,... | collective-permute-start | bytes 1769480 | tf_op jit(solution)/shard_map/ppermute | solution.py:94
  88.8 27.8 %collective-permute-start.33 = (bf16[192,1920]{1,0:T(8,128)(2,1)S(1)}, bf16[192,1920]{1,0:T(8,128)(2,1)S(1)}, u32[]{:S(2)}, u32[]{:S(2)}) collective-permute-start(bf16[192,1920]{1,0:T(8,128)(2,1)S(1)} %add_convert_fusion), channel_id=1, source_target_pairs={{0,1},{1,0},{2,3},{3,2},{4,5},{5,4},{6,7},{7,6},{8,9},{9,8},{10,11... | collective-permute-start | bytes 2211848 | tf_op jit(solution)/shard_map/ppermute | solution.py:103
  93.4 1.8 %collective-permute-start.25 = (f32[16,1152]{1,0:T(8,128)S(1)}, f32[16,1152]{1,0:T(8,128)S(1)}, u32[]{:S(2)}, u32[]{:S(2)}) collective-permute-start(f32[16,1152]{1,0:T(8,128)S(1)} %get-tuple-element.196), channel_id=1, source_target_pairs={{0,2},{2,0},{4,6},{6,4},{8,10},{10,8},{12,14},{14,12},{16,18},{18,... | collective-permute-start | bytes 221192 | tf_op jit(solution)/shard_map/ppermute | solution.py:98
  93.5 12.5 %collective-permute-start.35 = (bf16[96,1536]{1,0:T(8,128)(2,1)S(1)}, bf16[96,1536]{1,0:T(8,128)(2,1)S(1)}, u32[]{:S(2)}, u32[]{:S(2)}) collective-permute-start(bf16[96,1536]{1,0:T(8,128)(2,1)S(1)} %pad_maximum_fusion.2), channel_id=1, source_target_pairs={{0,8},{2,10},{4,12},{6,14},{8,0},{10,2},{12,4},{14,6},{16,24},{18,... | collective-permute-start | bytes 884744 | tf_op jit(solution)/shard_map/ppermute | solution.py:90
  95.3 21.4 %collective-permute-start.28 = (bf16[208,1152]{1,0:T(8,128)(2,1)S(1)}, bf16[208,1152]{1,0:T(8,128)(2,1)S(1)}, u32[]{:S(2)}, u32[]{:S(2)}) collective-permute-start(bf16[208,1152]{1,0:T(8,128)(2,1)S(1)} %pad_maximum_fusion), channel_id=1, source_target_pairs={{0,4},{2,6},{4,0},{6,2},{8,12},{10,14},{12,8},{14,10},{16,20},{18,... | collective-permute-start | bytes 1437704 | tf_op jit(solution)/shard_map/ppermute | solution.py:94
  104.3 10.5 %collective-permute-start.43 = (bf16[96,1536]{1,0:T(8,128)(2,1)S(1)}, bf16[96,1536]{1,0:T(8,128)(2,1)S(1)}, u32[]{:S(2)}, u32[]{:S(2)}) collective-permute-start(bf16[96,1536]{1,0:T(8,128)(2,1)S(1)} %pad_maximum_fusion.3), channel_id=1, source_target_pairs={{0,8},{2,10},{4,12},{6,14},{8,0},{10,2},{12,4},{14,6},{16,24},{18,... | collective-permute-start | bytes 884744 | tf_op jit(solution)/shard_map/ppermute | solution.py:90
  106.0 9.8 %collective-permute-start.36 = (bf16[48,1536]{1,0:T(8,128)(2,1)S(1)}, bf16[48,1536]{1,0:T(8,128)(2,1)S(1)}, u32[]{:S(2)}, u32[]{:S(2)}) collective-permute-start(bf16[48,1536]{1,0:T(8,128)(2,1)S(1)} %add_convert_fusion.9), channel_id=1, source_target_pairs={{0,16},{2,18},{4,20},{6,22},{8,24},{10,26},{12,28},{14,30},{16,0},... | collective-permute-start | bytes 442376 | tf_op jit(solution)/shard_map/ppermute | solution.py:90
  114.8 8.7 %collective-permute-start.44 = (bf16[48,1536]{1,0:T(8,128)(2,1)S(1)}, bf16[48,1536]{1,0:T(8,128)(2,1)S(1)}, u32[]{:S(2)}, u32[]{:S(2)}) collective-permute-start(bf16[48,1536]{1,0:T(8,128)(2,1)S(1)} %add_convert_fusion.6), channel_id=1, source_target_pairs={{0,16},{2,18},{4,20},{6,22},{8,24},{10,26},{12,28},{14,30},{16,0},... | collective-permute-start | bytes 442376 | tf_op jit(solution)/shard_map/ppermute | solution.py:90
  116.8 6.8 %collective-permute-start.29 = (bf16[112,1152]{1,0:T(8,128)(2,1)S(1)}, bf16[112,1152]{1,0:T(8,128)(2,1)S(1)}, u32[]{:S(2)}, u32[]{:S(2)}) collective-permute-start(bf16[112,1152]{1,0:T(8,128)(2,1)S(1)} %pad_maximum_fusion.4), channel_id=1, source_target_pairs={{0,1},{1,0},{2,3},{3,2},{4,5},{5,4},{6,7},{7,6},{8,9},{9,8},{10,11... | collective-permute-start | bytes 774152 | tf_op jit(solution)/shard_map/ppermute | solution.py:103
  117.7 10.9 %collective-permute-start.34 = (bf16[96,1920]{1,0:T(8,128)(2,1)S(1)}, bf16[96,1920]{1,0:T(8,128)(2,1)S(1)}, u32[]{:S(2)}, u32[]{:S(2)}) collective-permute-start(bf16[96,1920]{1,0:T(8,128)(2,1)S(1)} %add_convert_fusion.4), channel_id=1, source_target_pairs={{0,4},{2,6},{4,0},{6,2},{8,12},{10,14},{12,8},{14,10},{16,20},{18,... | collective-permute-start | bytes 1105928 | tf_op jit(solution)/shard_map/ppermute | solution.py:94
  123.7 9.4 %collective-permute-start.32 = (bf16[40,1152]{1,0:T(8,128)(2,1)S(1)}, bf16[40,1152]{1,0:T(8,128)(2,1)S(1)}, u32[]{:S(2)}, u32[]{:S(2)}) collective-permute-start(bf16[40,1152]{1,0:T(8,128)(2,1)S(1)} %get-tuple-element.254), channel_id=1, source_target_pairs={{0,24},{2,26},{4,28},{6,30},{8,0},{10,2},{12,4},{14,6},{16,8},{18,... | collective-permute-start | bytes 276488 | tf_op jit(solution)/shard_map/ppermute | solution.py:85
  126.0 14.0 %collective-permute-start.31 = (bf16[40,1152]{1,0:T(8,128)(2,1)S(1)}, bf16[40,1152]{1,0:T(8,128)(2,1)S(1)}, u32[]{:S(2)}, u32[]{:S(2)}) collective-permute-start(bf16[40,1152]{1,0:T(8,128)(2,1)S(1)} %get-tuple-element.255), channel_id=1, source_target_pairs={{0,16},{2,18},{4,20},{6,22},{8,24},{10,26},{12,28},{14,30},{16,0},... | collective-permute-start | bytes 276488 | tf_op jit(solution)/shard_map/ppermute | solution.py:85
  127.7 12.3 %collective-permute-start.30 = (bf16[40,1152]{1,0:T(8,128)(2,1)S(1)}, bf16[40,1152]{1,0:T(8,128)(2,1)S(1)}, u32[]{:S(2)}, u32[]{:S(2)}) collective-permute-start(bf16[40,1152]{1,0:T(8,128)(2,1)S(1)} %get-tuple-element.256), channel_id=1, source_target_pairs={{0,8},{2,10},{4,12},{6,14},{8,16},{10,18},{12,20},{14,22},{16,24},... | collective-permute-start | bytes 276488 | tf_op jit(solution)/shard_map/ppermute | solution.py:85
  128.7 13.5 %collective-permute-start.37 = (bf16[24,1920]{1,0:T(8,128)(2,1)S(1)}, bf16[24,1920]{1,0:T(8,128)(2,1)S(1)}, u32[]{:S(2)}, u32[]{:S(2)}) collective-permute-start(bf16[24,1920]{1,0:T(8,128)(2,1)S(1)} %get-tuple-element.217), channel_id=1, source_target_pairs={{0,8},{2,10},{4,12},{6,14},{8,16},{10,18},{12,20},{14,22},{16,24},... | collective-permute-start | bytes 276488 | tf_op jit(solution)/shard_map/ppermute | solution.py:85
  130.5 11.7 %collective-permute-start.38 = (bf16[24,1920]{1,0:T(8,128)(2,1)S(1)}, bf16[24,1920]{1,0:T(8,128)(2,1)S(1)}, u32[]{:S(2)}, u32[]{:S(2)}) collective-permute-start(bf16[24,1920]{1,0:T(8,128)(2,1)S(1)} %get-tuple-element.218), channel_id=1, source_target_pairs={{0,16},{2,18},{4,20},{6,22},{8,24},{10,26},{12,28},{14,30},{16,0},... | collective-permute-start | bytes 276488 | tf_op jit(solution)/shard_map/ppermute | solution.py:85
  133.1 9.0 %collective-permute-start.39 = (bf16[24,1920]{1,0:T(8,128)(2,1)S(1)}, bf16[24,1920]{1,0:T(8,128)(2,1)S(1)}, u32[]{:S(2)}, u32[]{:S(2)}) collective-permute-start(bf16[24,1920]{1,0:T(8,128)(2,1)S(1)} %get-tuple-element.219), channel_id=1, source_target_pairs={{0,24},{2,26},{4,28},{6,30},{8,0},{10,2},{12,4},{14,6},{16,8},{18,... | collective-permute-start | bytes 276488 | tf_op jit(solution)/shard_map/ppermute | solution.py:85
  (4 other events, 7.8 us)
